TPU v7x, 128 devices: a whole 4x4x4 slice. The times are simulated.
128 devices in a mesh: dp: 8 (over x, core), fsdp: 16 (over y, z).
Axes of the slice: x: 4, y: 4, z: 4, core: 2. Of those that a mesh axis runs over, the one named last changes fastest.
Arguments:
- activations: bfloat16 [1024, 8192], P('dp'), may hold values from -6 to 6
- out_grads: bfloat16 [2, 1024, 22016], P(None, 'dp'), may hold values from -4 to 4
- bases: bfloat16 [2, 8192, 1024], P(None, 'fsdp'), may hold values from -0.0625 to 0.0625
- first_moment: float32 [2, 1024, 22016], P(None, 'fsdp', 'dp'), may hold values from -6 to 6
- second_moment: float32 [2, 1024, 22016], P(None, 'fsdp', 'dp'), may hold values from 0.5 to 8
Outputs:
- weight_update: bfloat16 [2, 8192, 22016], P(None, 'fsdp', 'dp')
- new_first: float32 [2, 1024, 22016], P(None, 'fsdp', 'dp')
- new_second: float32 [2, 1024, 22016], P(None, 'fsdp', 'dp')
All inputs are finite; a program needn't handle non-finite values.
Results may differ from a plain program's by a relative error of at most 0.02.
Values may be sent and summed in bfloat16 or wider, within the bound.
No kernel may reach another device: no remote copies, remote signals or barrier semaphores. Data moves between devices by JAX's collectives and lax.ppermute only.
A program may use at most 192 MiB of HBM per device.

v0:
```python
import jax
import jax.numpy as jnp
from jax import lax
from jax.sharding import PartitionSpec as P


def on_device(activations, out_grads, bases, first_moment, second_moment):
    groups = lax.axis_size("fsdp")
    rank_width = bases.shape[2]
    rank_part = rank_width // groups
    feature_part = bases.shape[1]
    gathered = lax.all_gather(bases, "fsdp", axis=1, tiled=True)
    own_columns = lax.dynamic_slice_in_dim(
        gathered, lax.axis_index("fsdp") * rank_part, rank_part, 2
    )
    projected = jnp.einsum(
        "kdr,td->krt", own_columns, activations, preferred_element_type=jnp.float32
    ).astype(jnp.bfloat16)
    partial_grad = jnp.einsum(
        "krt,ktf->krf", projected, out_grads, preferred_element_type=jnp.float32
    )
    gradient = lax.psum_scatter(
        partial_grad.astype(jnp.bfloat16), "dp", scatter_dimension=2, tiled=True
    ).astype(jnp.float32)
    new_first = 0.9 * first_moment + 0.1 * gradient
    new_second = 0.999 * second_moment + 0.001 * gradient * gradient
    first_fix = 1.0 - 0.9**1000.0
    second_fix = 1.0 - 0.999**1000.0
    direction = (new_first / first_fix / (jnp.sqrt(new_second / second_fix) + 1e-08)).astype(
        jnp.bfloat16
    )
    starting = jnp.zeros((2, feature_part, direction.shape[2]), jnp.float32)
    shard_piece = lax.all_gather(direction, "fsdp", axis=1, tiled=True)
    columns = lax.slice_in_dim(bases, 0, shard_piece.shape[1], axis=2)
    expanded = starting + jnp.einsum(
        "kdr,krf->kdf", columns, shard_piece, preferred_element_type=jnp.float32
    )
    return (expanded.astype(jnp.bfloat16), new_first, new_second)


def solution(mesh):
    return jax.shard_map(
        on_device,
        mesh=mesh,
        in_specs=(
            P("dp", None),
            P(None, "dp", None),
            P(None, "fsdp", None),
            P(None, "fsdp", "dp"),
            P(None, "fsdp", "dp"),
        ),
        out_specs=(P(None, "fsdp", "dp"), P(None, "fsdp", "dp"), P(None, "fsdp", "dp")),
        check_vma=False,
    )
```

profile of v0, /device:TPU:0, one launch (start us, length us, event | category | flops | bytes accessed | tf_op | source)
XLA Modules:
  0.0 421.5 jit_solution(17840059396491522338)
XLA Ops:
  7.2 0.0 copy-start
  7.2 0.0 all-gather.3.cloned.1.call-start
  7.2 0.7 all-gather.3.cloned.1.call-update
  7.9 0.0 reduce-scatter.4.cloned.1.call-start
  8.0 202.0 %all-gather.3.cloned.1.call-done = bf16[2,8192,1024]{2,1,0:T(8,128)(2,1)} async-done(((bf16[2,512,1024]{2,1,0:T(8,128)(2,1)}), bf16[2,8192,1024]{2,1,0:T(8,128)(2,1)}) %all-gather.3.cloned.1.call-update) | async-done | bytes 33554448 | tf_op jit(solution)/shard_map/all_gather | solution.py:12
  209.9 0.0 copy-done
  209.9 4.6 %fusion.6 = bf16[2,64,128]{2,1,0:T(8,128)(2,1)S(1)} fusion(bf16[128,8192]{1,0:T(8,128)(2,1)S(1)} %copy-done, bf16[2,8192,1024]{2,1,0:T(8,128)(2,1)} %all-gather.3.cloned.1.call-done, s32[]{:T(128)S(6)} %select_n.3), kind=kOutput, calls=%fused_computation.11 | convolution fusion | flops 268451840 | bytes 6324228 | tf_op jit(solution)/shard_map/kdr,td->krt/dot_general | solution.py:16
  214.5 8.4 %convolution_convert_fusion = bf16[2,64,22016]{2,1,0:T(8,128)(2,1)} fusion(bf16[2,64,128]{2,1,0:T(8,128)(2,1)S(1)} %fusion.6, bf16[2,128,22016]{2,1,0:T(8,128)(2,1)} %param.6), kind=kOutput, calls=%fused_computation | convolution fusion | flops 724238336 | bytes 16941056 | tf_op jit(solution)/shard_map/krt,ktf->krf/dot_general | solution.py:19
  222.9 23.4 %copy.8 = bf16[2,64,22016]{1,0,2:T(2,128)(2,1)} copy(bf16[2,64,22016]{2,1,0:T(8,128)(2,1)} %convolution_convert_fusion) | data formatting | bytes 11272192
  246.3 18.5 %reshape.7 = bf16[22016,128]{1,0:T(8,128)(2,1)} reshape(bf16[22016,2,64]{2,1,0:T(2,128)(2,1)} %bitcast.13) | data formatting | bytes 11272192
  264.8 0.0 reduce-scatter.4.cloned.1.call-update
  264.8 0.2 all-gather.5.cloned.1.call-start
  265.0 40.6 %reduce-scatter.4.cloned.1.call-done = bf16[2752,128]{1,0:T(8,128)(2,1)} async-done(((bf16[22016,128]{1,0:T(8,128)(2,1)}), bf16[2752,128]{1,0:T(8,128)(2,1)}) %reduce-scatter.4.cloned.1.call-update) | async-done | bytes 704528
  305.6 2.9 reshape.8
  308.5 1.8 copy.9
  310.3 4.1 divide_convert_fusion
  314.4 0.0 all-gather.5.cloned.1.call-update
  314.5 85.1 %all-gather.5.cloned.1.call-done = bf16[2,1024,2752]{2,1,0:T(8,128)(2,1)} async-done(((bf16[2,64,2752]{2,1,0:T(8,128)(2,1)}), bf16[2,1024,2752]{2,1,0:T(8,128)(2,1)}) %all-gather.5.cloned.1.call-update) | async-done | bytes 11272208 | tf_op jit(solution)/shard_map/all_gather | solution.py:33
  399.6 0.0 copy-start.1
  399.6 15.3 %fusion = bf16[2,512,2752]{1,2,0:T(8,128)(2,1)} fusion(bf16[2,1024,2752]{2,1,0:T(8,128)(2,1)} %all-gather.5.cloned.1.call-done, bf16[2,512,1024]{2,1,0:T(8,128)(2,1)} %param.7), kind=kOutput, calls=%fused_computation.2 | convolution fusion | flops 5774180352 | bytes 19005440 | tf_op jit(solution)/shard_map/kdr,krf->kdf/dot_general | solution.py:35
  414.9 0.0 copy-done.1
Async XLA Ops:
  7.2 202.8 %copy-start = (bf16[128,8192]{1,0:T(8,128)(2,1)S(1)}, bf16[128,8192]{1,0:T(8,128)(2,1)}, u32[]{:S(2)}) copy-start(bf16[128,8192]{1,0:T(8,128)(2,1)} %param.5) | copy-start | bytes 6291460
  7.2 202.7 %all-gather.3.cloned.1.call-start = ((), (), s32[]{:S(2)}) async-start(), calls=%async_computation.1 | async-start | bytes 35651584 | tf_op jit(solution)/shard_map/all_gather | solution.py:12
  7.9 297.7 %reduce-scatter.4.cloned.1.call-start = ((), (), s32[]{:S(2)}) async-start(), calls=%async_computation.3 | async-start | bytes 6340608
  264.8 134.8 %all-gather.5.cloned.1.call-start = ((), (), s32[]{:S(2)}) async-start(), calls=%async_computation.2 | async-start | bytes 12255232 | tf_op jit(solution)/shard_map/all_gather | solution.py:33
  399.6 15.3 %copy-start.1 = (bf16[128,8192]{1,0:T(8,128)(2,1)S(1)}, bf16[128,8192]{1,0:T(8,128)(2,1)}, u32[]{:S(2)}) copy-start(bf16[128,8192]{1,0:T(8,128)(2,1)} %param.5) | copy-start | bytes 6291460
Sparse Core Ops, SparseCore 0:
  10.2 199.6 all-gather.2
  264.9 40.6 reduce-scatter.3
  314.6 84.9 all-gather.4
where the time goes:
time: 423 us; the launch traced here: 421 us
  waiting for transfers between devices  328 us (78%)
  local copies, waits for them, and re-layouts  46.7 us (11%)
  matrix products  28.3 us (7%)
  between operations  13.8 us (3%)
    all_gather x1, waiting for transfers between devices, on_device(): gathered = lax.all_gather(bases, 'fsdp', axis=1, tiled=True)  202 us
    all_gather x1, waiting for transfers between devices, on_device(): shard_piece = lax.all_gather(direction, 'fsdp', axis=1, tiled=True)  85.1 us
    unnamed x8, local copies, waits for them, and re-layouts  46.7 us
    unnamed x4, waiting for transfers between devices  41.3 us
    dot_general x1, matrix products, on_device(): jnp.einsum('kdr,krf->kdf', columns, shard_piece, preferred_element_type=j...  15.3 us
  transfers between devices with their start and end apart: 3, of which 3 were waited for; matrix products, arithmetic and copies ran while one was open for 0% of the time, Pallas kernels for 0%

commit v1 on v0

v1 whole, which is shorter than its diff:
```python
import jax
import jax.numpy as jnp
from jax import lax
from jax.experimental import pallas as pl
from jax.experimental.pallas import tpu as pltpu
from jax.sharding import Mesh, PartitionSpec as P

BF16 = jnp.bfloat16
F32 = jnp.float32
SIDE = 4
VMEM = 56 * 1024 * 1024


def receive(value, axis, distance):
    return lax.ppermute(value, axis, [((i + distance) % SIDE, i) for i in range(SIDE)])


def send(value, axis, distance):
    return receive(value, axis, -distance)


def swap_cores(value):
    return lax.ppermute(value, "c", [(0, 1), (1, 0)])


def partial_kernel(where_ref, proj_ref, grads_ref, mine_ref, other_ref):
    half = mine_ref.shape[2]
    both = lax.dot_general(
        proj_ref[...], grads_ref[0], (((0,), (0,)), ((), ())), preferred_element_type=F32
    ).astype(BF16)
    low, high = both[:, :half], both[:, half:]

    @pl.when(where_ref[1] == 0)
    def _():
        mine_ref[0] = low
        other_ref[0] = high

    @pl.when(where_ref[1] == 1)
    def _():
        mine_ref[0] = high
        other_ref[0] = low


def partial_grads(where, proj, grads, which):
    tokens, rank_part = proj.shape
    pair = grads.shape[2] // SIDE
    out = jax.ShapeDtypeStruct((SIDE, rank_part, pair // 2), BF16)
    return pl.pallas_call(
        partial_kernel,
        grid_spec=pltpu.PrefetchScalarGridSpec(
            num_scalar_prefetch=1,
            grid=(SIDE,),
            in_specs=[
                pl.BlockSpec((tokens, rank_part), lambda i, w: (0, 0)),
                pl.BlockSpec((1, tokens, pair), lambda i, w: (which, 0, (w[0] + i) % SIDE)),
            ],
            out_specs=[pl.BlockSpec((1, rank_part, pair // 2), lambda i, w: (i, 0, 0))] * 2,
        ),
        out_shape=[out, out],
        compiler_params=pltpu.CompilerParams(vmem_limit_bytes=VMEM),
        cost_estimate=pl.CostEstimate(
            flops=2 * tokens * rank_part * pair * SIDE,
            bytes_accessed=2 * tokens * pair * SIDE + 2 * rank_part * pair * SIDE,
            transcendentals=0,
        ),
    )(where, proj, grads)


def expand_kernel(*refs):
    columns_a, columns_b = refs[0], refs[1]
    pieces_a, pieces_b = refs[2:7], refs[7:12]
    out_ref = refs[-1]
    base = 0
    for columns, pieces in ((columns_a, pieces_a), (columns_b, pieces_b)):
        width = pieces[0].shape[1]
        for low in range(0, width, 256):
            high = min(low + 256, width)
            total, at = None, 0
            for piece in pieces:
                depth = piece.shape[0]
                term = jnp.dot(
                    columns[0, :, at : at + depth], piece[:, low:high], preferred_element_type=F32
                )
                total = term if total is None else total + term
                at += depth
            out_ref[0, :, base + low : base + high] = total.astype(BF16)
        base += width


def expand(columns_a, columns_b, pieces_a, pieces_b, which, before=None):
    _, rows, ranks = columns_a.shape
    width = pieces_a[0].shape[1] + pieces_b[0].shape[1]
    tile = 256
    pieces = [*pieces_a, *pieces_b]
    in_specs = [pl.BlockSpec((1, tile, ranks), lambda i: (which, i, 0))] * 2
    in_specs += [pl.BlockSpec(p.shape, lambda i: (0, 0)) for p in pieces]
    args = [columns_a, columns_b, *pieces]
    aliases = {}
    if before is not None:
        in_specs.append(pl.BlockSpec(memory_space=pl.ANY))
        aliases = {len(args): 0}
        args.append(before)
    return pl.pallas_call(
        expand_kernel,
        grid=(rows // tile,),
        in_specs=in_specs,
        out_specs=pl.BlockSpec((1, tile, width), lambda i: (which, i, 0)),
        out_shape=jax.ShapeDtypeStruct((2, rows, width), BF16),
        input_output_aliases=aliases,
        compiler_params=pltpu.CompilerParams(vmem_limit_bytes=VMEM),
        cost_estimate=pl.CostEstimate(
            flops=2 * rows * ranks * width,
            bytes_accessed=2 * (rows * ranks + ranks * width + rows * width),
            transcendentals=0,
        ),
    )(*args)


def ring_gather(value, first, second):
    row = jnp.concatenate([value] + [receive(value, first, d) for d in (1, 2, 3)], axis=0)
    half = row.shape[0] // 2
    after = receive(row, second, 1)
    before = receive(row, second, -1)
    far_top = receive(after[:half], second, 1)
    far_bottom = receive(before[half:], second, -1)
    return row, after, far_top, far_bottom, before


def on_device(activations, out_grads, bases, first_moment, second_moment):
    x, c, y, z = (lax.axis_index(n) for n in ("x", "c", "y", "z"))
    where = jnp.stack([x, c]).astype(jnp.int32)
    features, ranks = bases.shape[1:]
    part = ranks // (SIDE * SIDE)
    tokens = activations.shape[0]

    column = jnp.arange(ranks)
    slow, fast, inner = column // (SIDE * part), column // part % SIDE, column % part
    source_b = (((y + slow) % SIDE) * SIDE + (z + fast) % SIDE) * part + inner
    source_a = (((y + fast) % SIDE) * SIDE + (z + slow) % SIDE) * part + inner
    place_b = (column[:, None] == source_b[None, :]).astype(BF16)
    place_a = (column[:, None] == source_a[None, :]).astype(BF16)

    own = lax.dynamic_slice_in_dim(activations, (y * SIDE + z) * features, features, 1)
    partial = jnp.einsum("td,kdr->ktr", own, bases, preferred_element_type=F32).astype(BF16)
    partial = jnp.einsum("ktr,rs->kts", partial, place_b, preferred_element_type=F32).astype(BF16)
    for axis in ("y", "z"):
        width = partial.shape[2] // SIDE
        blocks = [partial[:, :, i * width : (i + 1) * width] for i in range(SIDE)]
        total = blocks[0].astype(F32)
        for i in (1, 3, 2):
            total = total + send(blocks[i], axis, i).astype(F32)
        partial = total.astype(BF16)

    columns_a = jnp.einsum("kdr,rs->kds", bases, place_a, preferred_element_type=F32).astype(BF16)
    columns_b = jnp.einsum("kdr,rs->kds", bases, place_b, preferred_element_type=F32).astype(BF16)

    first_fix = 1.0 - 0.9**1000.0
    second_fix = 1.0 - 0.999**1000.0
    firsts, seconds = [], []
    update = None
    for which in range(2):
        mine, other = partial_grads(where, partial[which], out_grads, which)
        other = swap_cores(other)
        sums = [mine[i].astype(F32) + other[i].astype(F32) for i in range(SIDE)]
        gradient = sums[0]
        for i in (1, 3, 2):
            gradient = gradient + send(sums[i].astype(BF16), "x", i).astype(F32)
        new_first = 0.9 * first_moment[which] + 0.1 * gradient
        new_second = 0.999 * second_moment[which] + 0.001 * gradient * gradient
        direction = (
            new_first / first_fix / (jnp.sqrt(new_second / second_fix) + 1e-08)
        ).astype(BF16)
        firsts.append(new_first)
        seconds.append(new_second)
        cut = (direction.shape[1] // 2 + 127) // 128 * 128
        pieces_a = ring_gather(direction[:, :cut], "y", "z")
        pieces_b = ring_gather(direction[:, cut:], "z", "y")
        update = expand(columns_a, columns_b, pieces_a, pieces_b, which, update)
    return update, jnp.stack(firsts), jnp.stack(seconds)


def solution(mesh):
    grid = Mesh(mesh.devices.reshape(4, 2, 4, 4), ("x", "c", "y", "z"))
    dp, fsdp = ("x", "c"), ("y", "z")
    return jax.shard_map(
        on_device,
        mesh=grid,
        in_specs=(
            P(dp, None),
            P(None, dp, None),
            P(None, fsdp, None),
            P(None, fsdp, dp),
            P(None, fsdp, dp),
        ),
        out_specs=(P(None, fsdp, dp), P(None, fsdp, dp), P(None, fsdp, dp)),
        check_vma=False,
    )
```

time: 423 us -> 203 us (0.48)
  waiting for transfers between devices: 328 us -> 56.2 us
  starting transfers between devices: 0.3 us -> 62.3 us
  Pallas kernels: 0 us -> 29.8 us
  matrix products: 28.3 us -> 9.88 us
  local copies, waits for them, and re-layouts: 46.7 us -> 30.2 us
  between operations: 13.8 us -> 0.99 us
  other arithmetic: 4.08 us -> 12.5 us
    all_gather x2 -> x0, waiting for transfers between devices: 287 us -> none  [the longest x1 202 us: on_device(): gathered = lax.all_gather(bases, 'fsdp', axis=1, tiled=True)]
    ppermute x0 -> x42, starting transfers between devices: none -> 62.3 us  [the longest x40 61.8 us: receive(): lax.ppermute(value, axis, [((i + distance) % SIDE, i) for i in range(SIDE)])]
    ppermute x0 -> x42, waiting for transfers between devices: none -> 56.2 us  [the longest x40 56.2 us: receive(): lax.ppermute(value, axis, [((i + distance) % SIDE, i) for i in range(SIDE)])]
    unnamed x4 -> x0, waiting for transfers between devices: 41.3 us -> none
    unnamed x8 -> x43, local copies, waits for them, and re-layouts: 46.7 us -> 13.1 us
    pallas_call x0 -> x4, Pallas kernels: none -> 29.8 us  [the longest x2 16.8 us: expand(): pl.pallas_call(expand_kernel, grid=(rows // tile,), in_specs=in_specs, ou...]
    dot_general x3, matrix products: 28.3 us -> 9.88 us  [the longest x1 3.85 us: on_device(): jnp.einsum('kdr,rs->kds', bases, place_a, preferred_element_type=F32)]
    slice x0 -> x14, local copies, waits for them, and re-layouts: none -> 8.16 us  [the longest x4 3.09 us: ring_gather(): far_top = receive(after[:half], second, 1)]
  transfers between devices with their start and end apart: 3 -> 42, of which waited for: 3 -> 15; matrix products, arithmetic and copies ran while one was open for 0% -> 16% of each run, Pallas kernels for 0% -> 7%
where the time goes in v1:
time: 203 us; the launch traced here: 202 us
  starting transfers between devices  62.3 us (31%)
  waiting for transfers between devices  56.2 us (28%)
  local copies, waits for them, and re-layouts  30.2 us (15%)
  Pallas kernels  29.8 us (15%)
  other arithmetic  12.5 us (6%)
  matrix products  9.88 us (5%)
    ppermute x40, starting transfers between devices, receive(): lax.ppermute(value, axis, [((i + distance) % SIDE, i) for i in range(SIDE)])  61.8 us
    ppermute x40, waiting for transfers between devices, receive(): lax.ppermute(value, axis, [((i + distance) % SIDE, i) for i in range(SIDE)])  56.2 us
    pallas_call x2, Pallas kernels, expand(): pl.pallas_call(expand_kernel, grid=(rows // tile,), in_specs=in_specs, ou...  16.8 us
    unnamed x43, local copies, waits for them, and re-layouts  13.1 us
    pallas_call x2, Pallas kernels, partial_grads(): pl.pallas_call(partial_kernel, grid_spec=pltpu.PrefetchScalarGridSpec(num...  13.1 us
    ppermute x4, local copies, waits for them, and re-layouts, receive(): lax.ppermute(value, axis, [((i + distance) % SIDE, i) for i in range(SIDE)])  6.06 us
    concatenate x4, other arithmetic, ring_gather(): jnp.concatenate([value] + [receive(value, first, d) for d in (1, 2, 3)],...  5.41 us
    another operation x3, other arithmetic, on_device(): return (update, jnp.stack(firsts), jnp.stack(seconds))  4.13 us
  transfers between devices with their start and end apart: 42, of which 15 were waited for; matrix products, arithmetic and copies ran while one was open for 16% of the time, Pallas kernels for 7%

profile of v1, /device:TPU:0, one launch (start us, length us, event | category | flops | bytes accessed | tf_op | source)
XLA Modules:
  0.0 201.9 jit_solution(10637531053625074966)
XLA Ops:
  0.7 1.6 copy-done
  2.2 2.2 %fusion.15 = bf16[2,128,1024]{2,1,0:T(8,128)(2,1)S(1)} fusion(s32[1024]{0:T(1024)S(1)} %fusion.59, bf16[2,512,1024]{2,1,0:T(8,128)(2,1)S(1)} %copy-done, bf16[128,8192]{1,0:T(8,128)(2,1)} %param.5, s32[]{:T(128)S(6)} %select_n.98), kind=kOutput, calls=%fused_computation.14 | convolution fusion | flops 806879232 | bytes 2756612 | tf_op jit(solution)/shard_map/ktr,rs->kts/dot_general | solution.py:145
  4.5 1.7 collective-permute-start
  6.2 2.9 %collective-permute-start.2 = (bf16[2,128,256]{2,1,0:T(8,128)(2,1)S(1)}, bf16[2,128,256]{2,1,0:T(8,128)(2,1)S(1)}, u32[]{:S(2)}, u32[]{:S(2)}) collective-permute-start(bf16[2,128,256]{2,1,0:T(8,128)(2,1)S(1)} %get-tuple-element.34), channel_id=1, source_target_pairs={{8,0},{12,4},{0,8},{4,12},{9,1},{13,5},{1,9},{5,13},{10,2},{14,6},... | collective-permute-start | bytes 393224 | tf_op jit(solution)/shard_map/ppermute | solution.py:15
  11.2 4.0 %collective-permute-done.2 = bf16[2,128,256]{2,1,0:T(8,128)(2,1)S(1)} collective-permute-done((bf16[2,128,256]{2,1,0:T(8,128)(2,1)S(1)}, bf16[2,128,256]{2,1,0:T(8,128)(2,1)S(1)}, u32[]{:S(2)}, u32[]{:S(2)}) %collective-permute-start.2) | collective-permute-done | bytes 131104 | tf_op jit(solution)/shard_map/ppermute | solution.py:15
  15.3 2.0 collective-permute-start.3
  17.3 3.6 %collective-permute-start.5 = (bf16[2,128,64]{2,1,0:T(8,128)(2,1)S(1)}, bf16[2,128,64]{2,1,0:T(8,128)(2,1)S(1)}, u32[]{:S(2)}, u32[]{:S(2)}) collective-permute-start(bf16[2,128,64]{2,1,0:T(8,128)(2,1)S(1)} %get-tuple-element.37), channel_id=1, source_target_pairs={{2,0},{3,1},{0,2},{1,3},{6,4},{7,5},{4,6},{5,7},{10,8},{11,9},{8,1... | collective-permute-start | bytes 98312 | tf_op jit(solution)/shard_map/ppermute | solution.py:15
  25.8 6.5 %shard_map.77 = (bf16[4,64,2752]{2,1,0:T(8,128)(2,1)}, bf16[4,64,2752]{2,1,0:T(8,128)(2,1)}) custom-call(s32[2]{0:T(128)} %pad_add_fusion.where_ref, bf16[128,64]{1,0:T(8,128)(2,1)} %get-tuple-element.39.proj_ref, bf16[2,128,22016]{2,1,0:T(8,128)(2,1)} %grads_ref.3), custom_call_target="tpu_custom_call" | custom-call | flops 360710144 | bytes 8454144 | tf_op jit(solution)/shard_map/pallas_call | solution.py:48
  32.3 6.6 %shard_map.76 = (bf16[4,64,2752]{2,1,0:T(8,128)(2,1)}, bf16[4,64,2752]{2,1,0:T(8,128)(2,1)}) custom-call(s32[2]{0:T(128)} %pad_add_fusion.where_ref, bf16[128,64]{1,0:T(8,128)(2,1)} %get-tuple-element.40.proj_ref, bf16[2,128,22016]{2,1,0:T(8,128)(2,1)} %grads_ref.3), custom_call_target="tpu_custom_call" | custom-call | flops 360710144 | bytes 8454144 | tf_op jit(solution)/shard_map/pallas_call | solution.py:48
  39.7 1.5 collective-permute-start.25
  41.2 2.8 %collective-permute-start.27 = (bf16[64,2752]{1,0:T(8,128)(2,1)S(1)}, bf16[64,2752]{1,0:T(8,128)(2,1)S(1)}, u32[]{:S(2)}, u32[]{:S(2)}) collective-permute-start(bf16[64,2752]{1,0:T(8,128)(2,1)S(1)} %get-tuple-element.24), channel_id=1, source_target_pairs={{64,0},{96,32},{0,64},{32,96},{65,1},{97,33},{1,65},{33,97},{66,2}... | collective-permute-start | bytes 1056776 | tf_op jit(solution)/shard_map/ppermute | solution.py:15
  44.0 1.4 collective-permute-start.26
  47.2 5.9 %collective-permute-done.25 = bf16[64,2752]{1,0:T(8,128)(2,1)S(1)} collective-permute-done((bf16[64,2752]{1,0:T(8,128)(2,1)S(1)}, bf16[64,2752]{1,0:T(8,128)(2,1)S(1)}, u32[]{:S(2)}, u32[]{:S(2)}) %collective-permute-start.25) | collective-permute-done | bytes 352288 | tf_op jit(solution)/shard_map/ppermute | solution.py:15
  53.8 7.2 %collective-permute-done.27 = bf16[64,2752]{1,0:T(8,128)(2,1)S(1)} collective-permute-done((bf16[64,2752]{1,0:T(8,128)(2,1)S(1)}, bf16[64,2752]{1,0:T(8,128)(2,1)S(1)}, u32[]{:S(2)}, u32[]{:S(2)}) %collective-permute-start.27) | collective-permute-done | bytes 352288 | tf_op jit(solution)/shard_map/ppermute | solution.py:15
  61.0 5.8 %collective-permute-done.7 = bf16[64,2752]{1,0:T(8,128)(2,1)S(1)} collective-permute-done((bf16[64,2752]{1,0:T(8,128)(2,1)S(1)}, bf16[64,2752]{1,0:T(8,128)(2,1)S(1)}, u32[]{:S(2)}, u32[]{:S(2)}) %collective-permute-start.7) | collective-permute-done | bytes 352288 | tf_op jit(solution)/shard_map/ppermute | solution.py:15
  66.7 8.7 %collective-permute-done.9 = bf16[64,2752]{1,0:T(8,128)(2,1)S(1)} collective-permute-done((bf16[64,2752]{1,0:T(8,128)(2,1)S(1)}, bf16[64,2752]{1,0:T(8,128)(2,1)S(1)}, u32[]{:S(2)}, u32[]{:S(2)}) %collective-permute-start.9) | collective-permute-done | bytes 352288 | tf_op jit(solution)/shard_map/ppermute | solution.py:15
  75.5 1.7 fusion.33
  77.2 1.7 divide_convert_fusion
  79.2 3.5 %collective-permute-start.36 = (bf16[64,1344]{1,0:T(8,128)(2,1)S(1)}, bf16[64,1344]{1,0:T(8,128)(2,1)S(1)}, u32[]{:S(2)}, u32[]{:S(2)}) collective-permute-start(bf16[64,1344]{1,0:T(8,128)(2,1)S(1)} %slice.195), channel_id=1, source_target_pairs={{2,0},{3,1},{0,2},{1,3},{6,4},{7,5},{4,6},{5,7},{10,8},{11,9},{8,1... | collective-permute-start | bytes 516104 | tf_op jit(solution)/shard_map/ppermute | solution.py:15
  85.3 1.6 collective-permute-start.19
  88.5 3.6 %collective-permute-done.36 = bf16[64,1344]{1,0:T(8,128)(2,1)S(1)} collective-permute-done((bf16[64,1344]{1,0:T(8,128)(2,1)S(1)}, bf16[64,1344]{1,0:T(8,128)(2,1)S(1)}, u32[]{:S(2)}, u32[]{:S(2)}) %collective-permute-start.36) | collective-permute-done | bytes 172064 | tf_op jit(solution)/shard_map/ppermute | solution.py:15
  92.1 2.6 %collective-permute-start.29 = (bf16[64,1408]{1,0:T(8,128)(2,1)}, bf16[64,1408]{1,0:T(8,128)(2,1)}, u32[]{:S(2)}, u32[]{:S(2)}) collective-permute-start(bf16[64,1408]{1,0:T(8,128)(2,1)} %slice.192), channel_id=1, source_target_pairs={{8,0},{12,4},{0,8},{4,12},{9,1},{13,5},{1,9},{5,13},{10,2},{14,6},... | collective-permute-start | bytes 540680 | tf_op jit(solution)/shard_map/ppermute | solution.py:15
  94.6 1.4 collective-permute-start.28
  100.8 1.8 collective-permute-start.40
  102.6 2.1 %pad_maximum_fusion.4.refs_2_ = bf16[256,1408]{1,0:T(8,128)(2,1)} fusion(bf16[64,1408]{1,0:T(8,128)(2,1)} %collective-permute-done.30, bf16[64,1408]{1,0:T(8,128)(2,1)} %collective-permute-done.29, bf16[64,1408]{1,0:T(8,128)(2,1)} %collective-permute-done.28, bf16[64,1408]{1,0:T(8,128)(2,1)} %slice.192), kind=kLoop, calls=%fused_computation.23 | loop fusion | flops 2883584 | bytes 1441792 | tf_op jit(solution)/shard_map/concatenate | solution.py:120
  104.7 1.5 collective-permute-start.38
  106.2 3.8 %convert_bitcast_fusion.refs_1_ = bf16[2,512,1024]{2,1,0:T(8,128)(2,1)} fusion(bf16[2,512,1024]{2,1,0:T(8,128)(2,1)S(1)} %copy-done, s32[1024]{0:T(1024)S(1)} %fusion.59), kind=kOutput, calls=%fused_computation.7 | convolution fusion | flops 2149580800 | bytes 4198400 | tf_op jit(solution)/shard_map/kdr,rs->kds/dot_general | solution.py:155
  111.9 2.0 %collective-permute-start.10 = (bf16[64,1408]{1,0:T(8,128)(2,1)}, bf16[64,1408]{1,0:T(8,128)(2,1)}, u32[]{:S(2)}, u32[]{:S(2)}) collective-permute-start(bf16[64,1408]{1,0:T(8,128)(2,1)} %slice.181), channel_id=1, source_target_pairs={{4,0},{8,4},{12,8},{0,12},{5,1},{9,5},{13,9},{1,13},{6,2},{10,6},{... | collective-permute-start | bytes 540680 | tf_op jit(solution)/shard_map/ppermute | solution.py:15
  116.3 7.8 %collective-permute-done.11 = bf16[64,1408]{1,0:T(8,128)(2,1)} collective-permute-done((bf16[64,1408]{1,0:T(8,128)(2,1)}, bf16[64,1408]{1,0:T(8,128)(2,1)}, u32[]{:S(2)}, u32[]{:S(2)}) %collective-permute-start.11) | collective-permute-done | bytes 180256 | tf_op jit(solution)/shard_map/ppermute | solution.py:15
  124.1 2.1 %collective-permute-start.22 = (bf16[256,1344]{0,1:T(8,128)(2,1)}, bf16[256,1344]{0,1:T(8,128)(2,1)}, u32[]{:S(2)}, u32[]{:S(2)}) collective-permute-start(bf16[256,1344]{0,1:T(8,128)(2,1)} %copy.16), channel_id=1, source_target_pairs={{12,0},{0,4},{4,8},{8,12},{13,1},{1,5},{5,9},{9,13},{14,2},{2,6},{... | collective-permute-start | bytes 2064392 | tf_op jit(solution)/shard_map/ppermute | solution.py:15
  126.1 2.0 collective-permute-done.10
  128.1 2.7 %collective-permute-start.20 = (bf16[256,1344]{0,1:T(8,128)(2,1)}, bf16[256,1344]{0,1:T(8,128)(2,1)}, u32[]{:S(2)}, u32[]{:S(2)}) collective-permute-start(bf16[256,1344]{0,1:T(8,128)(2,1)} %copy.16), channel_id=1, source_target_pairs={{4,0},{8,4},{12,8},{0,12},{5,1},{9,5},{13,9},{1,13},{6,2},{10,6},{... | collective-permute-start | bytes 2064392 | tf_op jit(solution)/shard_map/ppermute | solution.py:15
  130.8 1.9 collective-permute-start.31
  132.7 2.1 %pad_maximum_fusion.2.refs_2_ = bf16[256,1408]{1,0:T(8,128)(2,1)} fusion(bf16[64,1408]{1,0:T(8,128)(2,1)} %copy-done.20, bf16[64,1408]{1,0:T(8,128)(2,1)} %collective-permute-done.11, bf16[64,1408]{1,0:T(8,128)(2,1)} %collective-permute-done.10, bf16[64,1408]{1,0:T(8,128)(2,1)} %slice.181), kind=kLoop, calls=%fused_computation.21 | loop fusion | flops 2883584 | bytes 1441792 | tf_op jit(solution)/shard_map/concatenate | solution.py:120
  135.0 3.1 %collective-permute-start.13 = (bf16[256,1408]{1,0:T(8,128)(2,1)}, bf16[256,1408]{1,0:T(8,128)(2,1)}, u32[]{:S(2)}, u32[]{:S(2)}) collective-permute-start(bf16[256,1408]{1,0:T(8,128)(2,1)} %pad_maximum_fusion.2.refs_2_), channel_id=1, source_target_pairs={{1,0},{2,1},{3,2},{0,3},{5,4},{6,5},{7,6},{4,7},{9,8},{10,9},{11,1... | collective-permute-start | bytes 2162696 | tf_op jit(solution)/shard_map/ppermute | solution.py:15
  138.1 3.8 %convert_bitcast_fusion.1.refs_0_ = bf16[2,512,1024]{2,1,0:T(8,128)(2,1)} fusion(bf16[2,512,1024]{2,1,0:T(8,128)(2,1)S(1)} %copy-done, s32[1024]{0:T(1024)S(1)} %fusion.50), kind=kOutput, calls=%fused_computation.10 | convolution fusion | flops 2149580800 | bytes 4198400 | tf_op jit(solution)/shard_map/kdr,rs->kds/dot_general | solution.py:154
  141.9 1.4 copy.23.refs_11_
  144.2 1.5 copy.24.refs_8_
  147.6 3.2 %collective-permute-start.39 = (bf16[128,1344]{1,0:T(8,128)(2,1)}, bf16[128,1344]{1,0:T(8,128)(2,1)}, u32[]{:S(2)}, u32[]{:S(2)}) collective-permute-start(bf16[128,1344]{1,0:T(8,128)(2,1)} %slice.196), channel_id=1, source_target_pairs={{4,0},{8,4},{12,8},{0,12},{5,1},{9,5},{13,9},{1,13},{6,2},{10,6},{... | collective-permute-start | bytes 1032200 | tf_op jit(solution)/shard_map/ppermute | solution.py:15
  152.0 1.4 copy.19.refs_11_
  153.5 1.7 copy.26.refs_8_
  157.6 3.4 %collective-permute-done.13.refs_3_ = bf16[256,1408]{1,0:T(8,128)(2,1)} collective-permute-done((bf16[256,1408]{1,0:T(8,128)(2,1)}, bf16[256,1408]{1,0:T(8,128)(2,1)}, u32[]{:S(2)}, u32[]{:S(2)}) %collective-permute-start.13) | collective-permute-done | bytes 720928 | tf_op jit(solution)/shard_map/ppermute | solution.py:15
  162.8 3.8 %collective-permute-start.32 = (bf16[128,1408]{1,0:T(8,128)(2,1)S(1)}, bf16[128,1408]{1,0:T(8,128)(2,1)S(1)}, u32[]{:S(2)}, u32[]{:S(2)}) collective-permute-start(bf16[128,1408]{1,0:T(8,128)(2,1)S(1)} %slice.193), channel_id=1, source_target_pairs={{1,0},{2,1},{3,2},{0,3},{5,4},{6,5},{7,6},{4,7},{9,8},{10,9},{11,1... | collective-permute-start | bytes 1081352 | tf_op jit(solution)/shard_map/ppermute | solution.py:15
  166.5 3.2 %collective-permute-start.14 = (bf16[128,1408]{1,0:T(8,128)(2,1)S(1)}, bf16[128,1408]{1,0:T(8,128)(2,1)S(1)}, u32[]{:S(2)}, u32[]{:S(2)}) collective-permute-start(bf16[128,1408]{1,0:T(8,128)(2,1)S(1)} %slice.182), channel_id=1, source_target_pairs={{1,0},{2,1},{3,2},{0,3},{5,4},{6,5},{7,6},{4,7},{9,8},{10,9},{11,1... | collective-permute-start | bytes 1081352 | tf_op jit(solution)/shard_map/ppermute | solution.py:15
  171.0 3.3 %collective-permute-done.32.refs_4_ = bf16[128,1408]{1,0:T(8,128)(2,1)S(1)} collective-permute-done((bf16[128,1408]{1,0:T(8,128)(2,1)S(1)}, bf16[128,1408]{1,0:T(8,128)(2,1)S(1)}, u32[]{:S(2)}, u32[]{:S(2)}) %collective-permute-start.32) | collective-permute-done | bytes 360480 | tf_op jit(solution)/shard_map/ppermute | solution.py:15
  175.0 8.4 %shard_map.78.refs_12_ = bf16[2,512,2752]{2,1,0:T(8,128)(2,1)} custom-call(bf16[2,512,1024]{2,1,0:T(8,128)(2,1)} %convert_bitcast_fusion.1.refs_0_, bf16[2,512,1024]{2,1,0:T(8,128)(2,1)} %convert_bitcast_fusion.refs_1_, bf16[256,1408]{1,0:T(8,128)(2,1)} %pad_maximum_fusion.4.refs_2_, bf16[256,1408]{1,0:T(8,128)(2,1)} %collective-permute-done.31.refs_3_, ...), custom_call_target="tpu_custom_call" | custom-call | flops 2885681152 | bytes 9502720 | tf_op jit(solution)/shard_map/pallas_call | solution.py:103
  185.1 8.4 %shard_map.79 = bf16[2,512,2752]{2,1,0:T(8,128)(2,1)} custom-call(bf16[2,512,1024]{2,1,0:T(8,128)(2,1)} %convert_bitcast_fusion.1.refs_0_, bf16[2,512,1024]{2,1,0:T(8,128)(2,1)} %convert_bitcast_fusion.refs_1_, bf16[256,1408]{1,0:T(8,128)(2,1)} %pad_maximum_fusion.2.refs_2_, ...), custom_call_target="tpu_custom_call", output_to_operand_aliasing={{}: (12, {})} | custom-call | flops 2885681152 | bytes 9502720 | tf_op jit(solution)/shard_map/pallas_call | solution.py:103
  193.6 8.3 %copy.28 = bf16[2,512,2752]{1,2,0:T(8,128)(2,1)} copy(bf16[2,512,2752]{2,1,0:T(8,128)(2,1)} %shard_map.79) | data formatting | bytes 11272192
  (122 shorter events, 35.8 us)
Async XLA Ops:
  4.5 6.7 %collective-permute-start = (bf16[2,128,256]{2,1,0:T(8,128)(2,1)S(1)}, bf16[2,128,256]{2,1,0:T(8,128)(2,1)S(1)}, u32[]{:S(2)}, u32[]{:S(2)}) collective-permute-start(bf16[2,128,256]{2,1,0:T(8,128)(2,1)S(1)} %get-tuple-element.33), channel_id=1, source_target_pairs={{12,0},{0,4},{4,8},{8,12},{13,1},{1,5},{5,9},{9,13},{14,2},{2,6},{... | collective-permute-start | bytes 393224 | tf_op jit(solution)/shard_map/ppermute | solution.py:15
  6.2 8.9 %collective-permute-start.2 = (bf16[2,128,256]{2,1,0:T(8,128)(2,1)S(1)}, bf16[2,128,256]{2,1,0:T(8,128)(2,1)S(1)}, u32[]{:S(2)}, u32[]{:S(2)}) collective-permute-start(bf16[2,128,256]{2,1,0:T(8,128)(2,1)S(1)} %get-tuple-element.34), channel_id=1, source_target_pairs={{8,0},{12,4},{0,8},{4,12},{9,1},{13,5},{1,9},{5,13},{10,2},{14,6},... | collective-permute-start | bytes 393224 | tf_op jit(solution)/shard_map/ppermute | solution.py:15
  9.1 6.0 %collective-permute-start.1 = (bf16[2,128,256]{2,1,0:T(8,128)(2,1)S(1)}, bf16[2,128,256]{2,1,0:T(8,128)(2,1)S(1)}, u32[]{:S(2)}, u32[]{:S(2)}) collective-permute-start(bf16[2,128,256]{2,1,0:T(8,128)(2,1)S(1)} %get-tuple-element.35), channel_id=1, source_target_pairs={{4,0},{8,4},{12,8},{0,12},{5,1},{9,5},{13,9},{1,13},{6,2},{10,6},{... | collective-permute-start | bytes 393224 | tf_op jit(solution)/shard_map/ppermute | solution.py:15
  15.3 7.2 %collective-permute-start.3 = (bf16[2,128,64]{2,1,0:T(8,128)(2,1)S(1)}, bf16[2,128,64]{2,1,0:T(8,128)(2,1)S(1)}, u32[]{:S(2)}, u32[]{:S(2)}) collective-permute-start(bf16[2,128,64]{2,1,0:T(8,128)(2,1)S(1)} %get-tuple-element.36), channel_id=1, source_target_pairs={{3,0},{0,1},{1,2},{2,3},{7,4},{4,5},{5,6},{6,7},{11,8},{8,9},{9,10... | collective-permute-start | bytes 98312 | tf_op jit(solution)/shard_map/ppermute | solution.py:15
  17.3 6.5 %collective-permute-start.5 = (bf16[2,128,64]{2,1,0:T(8,128)(2,1)S(1)}, bf16[2,128,64]{2,1,0:T(8,128)(2,1)S(1)}, u32[]{:S(2)}, u32[]{:S(2)}) collective-permute-start(bf16[2,128,64]{2,1,0:T(8,128)(2,1)S(1)} %get-tuple-element.37), channel_id=1, source_target_pairs={{2,0},{3,1},{0,2},{1,3},{6,4},{7,5},{4,6},{5,7},{10,8},{11,9},{8,1... | collective-permute-start | bytes 98312 | tf_op jit(solution)/shard_map/ppermute | solution.py:15
  20.9 4.3 %collective-permute-start.4 = (bf16[2,128,64]{2,1,0:T(8,128)(2,1)S(1)}, bf16[2,128,64]{2,1,0:T(8,128)(2,1)S(1)}, u32[]{:S(2)}, u32[]{:S(2)}) collective-permute-start(bf16[2,128,64]{2,1,0:T(8,128)(2,1)S(1)} %get-tuple-element.38), channel_id=1, source_target_pairs={{1,0},{2,1},{3,2},{0,3},{5,4},{6,5},{7,6},{4,7},{9,8},{10,9},{11,1... | collective-permute-start | bytes 98312 | tf_op jit(solution)/shard_map/ppermute | solution.py:15
  32.3 7.1 %collective-permute-start.24 = (bf16[4,64,2752]{2,1,0:T(8,128)(2,1)}, bf16[4,64,2752]{2,1,0:T(8,128)(2,1)S(1)}, u32[]{:S(2)}, u32[]{:S(2)}) collective-permute-start(bf16[4,64,2752]{2,1,0:T(8,128)(2,1)} %get-tuple-element.10), channel_id=1, source_target_pairs={{0,16},{16,0},{1,17},{17,1},{2,18},{18,2},{3,19},{19,3},{4,20},{20... | collective-permute-start | bytes 4227080 | tf_op jit(solution)/shard_map/ppermute | solution.py:23
  38.9 6.5 %collective-permute-start.6 = (bf16[4,64,2752]{2,1,0:T(8,128)(2,1)}, bf16[4,64,2752]{2,1,0:T(8,128)(2,1)S(1)}, u32[]{:S(2)}, u32[]{:S(2)}) collective-permute-start(bf16[4,64,2752]{2,1,0:T(8,128)(2,1)} %get-tuple-element.8), channel_id=1, source_target_pairs={{0,16},{16,0},{1,17},{17,1},{2,18},{18,2},{3,19},{19,3},{4,20},{20... | collective-permute-start | bytes 4227080 | tf_op jit(solution)/shard_map/ppermute | solution.py:23
  39.7 13.4 %collective-permute-start.25 = (bf16[64,2752]{1,0:T(8,128)(2,1)S(1)}, bf16[64,2752]{1,0:T(8,128)(2,1)S(1)}, u32[]{:S(2)}, u32[]{:S(2)}) collective-permute-start(bf16[64,2752]{1,0:T(8,128)(2,1)S(1)} %get-tuple-element.23), channel_id=1, source_target_pairs={{96,0},{0,32},{32,64},{64,96},{97,1},{1,33},{33,65},{65,97},{98,2}... | collective-permute-start | bytes 1056776 | tf_op jit(solution)/shard_map/ppermute | solution.py:15
  41.2 19.8 %collective-permute-start.27 = (bf16[64,2752]{1,0:T(8,128)(2,1)S(1)}, bf16[64,2752]{1,0:T(8,128)(2,1)S(1)}, u32[]{:S(2)}, u32[]{:S(2)}) collective-permute-start(bf16[64,2752]{1,0:T(8,128)(2,1)S(1)} %get-tuple-element.24), channel_id=1, source_target_pairs={{64,0},{96,32},{0,64},{32,96},{65,1},{97,33},{1,65},{33,97},{66,2}... | collective-permute-start | bytes 1056776 | tf_op jit(solution)/shard_map/ppermute | solution.py:15
  44.0 17.0 %collective-permute-start.26 = (bf16[64,2752]{1,0:T(8,128)(2,1)S(1)}, bf16[64,2752]{1,0:T(8,128)(2,1)S(1)}, u32[]{:S(2)}, u32[]{:S(2)}) collective-permute-start(bf16[64,2752]{1,0:T(8,128)(2,1)S(1)} %get-tuple-element.25), channel_id=1, source_target_pairs={{32,0},{64,32},{96,64},{0,96},{33,1},{65,33},{97,65},{1,97},{34,2}... | collective-permute-start | bytes 1056776 | tf_op jit(solution)/shard_map/ppermute | solution.py:15
  45.4 30.1 %copy-start.4 = (f32[2,64,2752]{2,1,0:T(8,128)S(1)}, f32[2,64,2752]{2,1,0:T(8,128)}, u32[]{:S(2)}) copy-start(f32[2,64,2752]{2,1,0:T(8,128)} %param.9) | copy-start | bytes 4227076
  45.7 21.1 %collective-permute-start.7 = (bf16[64,2752]{1,0:T(8,128)(2,1)S(1)}, bf16[64,2752]{1,0:T(8,128)(2,1)S(1)}, u32[]{:S(2)}, u32[]{:S(2)}) collective-permute-start(bf16[64,2752]{1,0:T(8,128)(2,1)S(1)} %get-tuple-element.26), channel_id=1, source_target_pairs={{96,0},{0,32},{32,64},{64,96},{97,1},{1,33},{33,65},{65,97},{98,2}... | collective-permute-start | bytes 1056776 | tf_op jit(solution)/shard_map/ppermute | solution.py:15
  46.3 29.2 %collective-permute-start.9 = (bf16[64,2752]{1,0:T(8,128)(2,1)S(1)}, bf16[64,2752]{1,0:T(8,128)(2,1)S(1)}, u32[]{:S(2)}, u32[]{:S(2)}) collective-permute-start(bf16[64,2752]{1,0:T(8,128)(2,1)S(1)} %get-tuple-element.27), channel_id=1, source_target_pairs={{64,0},{96,32},{0,64},{32,96},{65,1},{97,33},{1,65},{33,97},{66,2}... | collective-permute-start | bytes 1056776 | tf_op jit(solution)/shard_map/ppermute | solution.py:15
  53.1 24.2 %copy-start.14 = (f32[2,64,2752]{2,1,0:T(8,128)S(1)}, f32[2,64,2752]{2,1,0:T(8,128)}, u32[]{:S(2)}) copy-start(f32[2,64,2752]{2,1,0:T(8,128)} %param.8) | copy-start | bytes 4227076
  53.1 22.4 %collective-permute-start.8 = (bf16[64,2752]{1,0:T(8,128)(2,1)S(1)}, bf16[64,2752]{1,0:T(8,128)(2,1)S(1)}, u32[]{:S(2)}, u32[]{:S(2)}) collective-permute-start(bf16[64,2752]{1,0:T(8,128)(2,1)S(1)} %get-tuple-element.28), channel_id=1, source_target_pairs={{32,0},{64,32},{96,64},{0,96},{33,1},{65,33},{97,65},{1,97},{34,2}... | collective-permute-start | bytes 1056776 | tf_op jit(solution)/shard_map/ppermute | solution.py:15
  79.0 8.3 %collective-permute-start.37 = (bf16[64,1344]{1,0:T(8,128)(2,1)S(1)}, bf16[64,1344]{1,0:T(8,128)(2,1)S(1)}, u32[]{:S(2)}, u32[]{:S(2)}) collective-permute-start(bf16[64,1344]{1,0:T(8,128)(2,1)S(1)} %slice.195), channel_id=1, source_target_pairs={{3,0},{0,1},{1,2},{2,3},{7,4},{4,5},{5,6},{6,7},{11,8},{8,9},{9,10... | collective-permute-start | bytes 516104 | tf_op jit(solution)/shard_map/ppermute | solution.py:15
  79.2 12.9 %collective-permute-start.36 = (bf16[64,1344]{1,0:T(8,128)(2,1)S(1)}, bf16[64,1344]{1,0:T(8,128)(2,1)S(1)}, u32[]{:S(2)}, u32[]{:S(2)}) collective-permute-start(bf16[64,1344]{1,0:T(8,128)(2,1)S(1)} %slice.195), channel_id=1, source_target_pairs={{2,0},{3,1},{0,2},{1,3},{6,4},{7,5},{4,6},{5,7},{10,8},{11,9},{8,1... | collective-permute-start | bytes 516104 | tf_op jit(solution)/shard_map/ppermute | solution.py:15
  82.7 11.9 %collective-permute-start.35 = (bf16[64,1344]{1,0:T(8,128)(2,1)S(1)}, bf16[64,1344]{1,0:T(8,128)(2,1)S(1)}, u32[]{:S(2)}, u32[]{:S(2)}) collective-permute-start(bf16[64,1344]{1,0:T(8,128)(2,1)S(1)} %slice.195), channel_id=1, source_target_pairs={{1,0},{2,1},{3,2},{0,3},{5,4},{6,5},{7,6},{4,7},{9,8},{10,9},{11,1... | collective-permute-start | bytes 516104 | tf_op jit(solution)/shard_map/ppermute | solution.py:15
  85.3 19.4 %collective-permute-start.19 = (bf16[64,1344]{1,0:T(8,128)(2,1)}, bf16[64,1344]{1,0:T(8,128)(2,1)}, u32[]{:S(2)}, u32[]{:S(2)}) collective-permute-start(bf16[64,1344]{1,0:T(8,128)(2,1)} %slice.184), channel_id=1, source_target_pairs={{3,0},{0,1},{1,2},{2,3},{7,4},{4,5},{5,6},{6,7},{11,8},{8,9},{9,10... | collective-permute-start | bytes 516104 | tf_op jit(solution)/shard_map/ppermute | solution.py:15
  86.8 19.3 %collective-permute-start.18 = (bf16[64,1344]{1,0:T(8,128)(2,1)}, bf16[64,1344]{1,0:T(8,128)(2,1)}, u32[]{:S(2)}, u32[]{:S(2)}) collective-permute-start(bf16[64,1344]{1,0:T(8,128)(2,1)} %slice.184), channel_id=1, source_target_pairs={{2,0},{3,1},{0,2},{1,3},{6,4},{7,5},{4,6},{5,7},{10,8},{11,9},{8,1... | collective-permute-start | bytes 516104 | tf_op jit(solution)/shard_map/ppermute | solution.py:15
  87.3 9.9 %collective-permute-start.30 = (bf16[64,1408]{1,0:T(8,128)(2,1)}, bf16[64,1408]{1,0:T(8,128)(2,1)}, u32[]{:S(2)}, u32[]{:S(2)}) collective-permute-start(bf16[64,1408]{1,0:T(8,128)(2,1)} %slice.192), channel_id=1, source_target_pairs={{12,0},{0,4},{4,8},{8,12},{13,1},{1,5},{5,9},{9,13},{14,2},{2,6},{... | collective-permute-start | bytes 540680 | tf_op jit(solution)/shard_map/ppermute | solution.py:15
  92.1 7.3 %collective-permute-start.29 = (bf16[64,1408]{1,0:T(8,128)(2,1)}, bf16[64,1408]{1,0:T(8,128)(2,1)}, u32[]{:S(2)}, u32[]{:S(2)}) collective-permute-start(bf16[64,1408]{1,0:T(8,128)(2,1)} %slice.192), channel_id=1, source_target_pairs={{8,0},{12,4},{0,8},{4,12},{9,1},{13,5},{1,9},{5,13},{10,2},{14,6},... | collective-permute-start | bytes 540680 | tf_op jit(solution)/shard_map/ppermute | solution.py:15
  94.6 6.2 %collective-permute-start.28 = (bf16[64,1408]{1,0:T(8,128)(2,1)}, bf16[64,1408]{1,0:T(8,128)(2,1)}, u32[]{:S(2)}, u32[]{:S(2)}) collective-permute-start(bf16[64,1408]{1,0:T(8,128)(2,1)} %slice.192), channel_id=1, source_target_pairs={{4,0},{8,4},{12,8},{0,12},{5,1},{9,5},{13,9},{1,13},{6,2},{10,6},{... | collective-permute-start | bytes 540680 | tf_op jit(solution)/shard_map/ppermute | solution.py:15
  96.1 13.9 %copy-start.2 = (bf16[256,1344]{1,0:T(8,128)(2,1)}, bf16[256,1344]{1,0:T(8,128)(2,1)S(1)}, u32[]{:S(2)}) copy-start(bf16[256,1344]{1,0:T(8,128)(2,1)S(1)} %pad_maximum_fusion.5.refs_7_) | copy-start | bytes 2064388
  97.2 12.8 %collective-permute-start.17 = (bf16[64,1344]{1,0:T(8,128)(2,1)}, bf16[64,1344]{1,0:T(8,128)(2,1)S(1)}, u32[]{:S(2)}, u32[]{:S(2)}) collective-permute-start(bf16[64,1344]{1,0:T(8,128)(2,1)} %slice.184), channel_id=1, source_target_pairs={{1,0},{2,1},{3,2},{0,3},{5,4},{6,5},{7,6},{4,7},{9,8},{10,9},{11,1... | collective-permute-start | bytes 516104 | tf_op jit(solution)/shard_map/ppermute | solution.py:15
  99.4 11.9 %collective-permute-start.12 = (bf16[64,1408]{1,0:T(8,128)(2,1)}, bf16[64,1408]{1,0:T(8,128)(2,1)S(1)}, u32[]{:S(2)}, u32[]{:S(2)}) collective-permute-start(bf16[64,1408]{1,0:T(8,128)(2,1)} %slice.181), channel_id=1, source_target_pairs={{12,0},{0,4},{4,8},{8,12},{13,1},{1,5},{5,9},{9,13},{14,2},{2,6},{... | collective-permute-start | bytes 540680 | tf_op jit(solution)/shard_map/ppermute | solution.py:15
  100.8 30.0 %collective-permute-start.40 = (bf16[256,1344]{0,1:T(8,128)(2,1)}, bf16[256,1344]{0,1:T(8,128)(2,1)}, u32[]{:S(2)}, u32[]{:S(2)}) collective-permute-start(bf16[256,1344]{0,1:T(8,128)(2,1)} %copy.20), channel_id=1, source_target_pairs={{12,0},{0,4},{4,8},{8,12},{13,1},{1,5},{5,9},{9,13},{14,2},{2,6},{... | collective-permute-start | bytes 2064392 | tf_op jit(solution)/shard_map/ppermute | solution.py:15
  104.7 30.1 %collective-permute-start.38 = (bf16[256,1344]{0,1:T(8,128)(2,1)}, bf16[256,1344]{0,1:T(8,128)(2,1)}, u32[]{:S(2)}, u32[]{:S(2)}) collective-permute-start(bf16[256,1344]{0,1:T(8,128)(2,1)} %copy.20), channel_id=1, source_target_pairs={{4,0},{8,4},{12,8},{0,12},{5,1},{9,5},{13,9},{1,13},{6,2},{10,6},{... | collective-permute-start | bytes 2064392 | tf_op jit(solution)/shard_map/ppermute | solution.py:15
  106.2 28.8 %collective-permute-start.33 = (bf16[256,1408]{1,0:T(8,128)(2,1)}, bf16[256,1408]{1,0:T(8,128)(2,1)}, u32[]{:S(2)}, u32[]{:S(2)}) collective-permute-start(bf16[256,1408]{1,0:T(8,128)(2,1)} %pad_maximum_fusion.4.refs_2_), channel_id=1, source_target_pairs={{3,0},{0,1},{1,2},{2,3},{7,4},{4,5},{5,6},{6,7},{11,8},{8,9},{9,10... | collective-permute-start | bytes 2162696 | tf_op jit(solution)/shard_map/ppermute | solution.py:15
  110.0 14.1 %collective-permute-start.11 = (bf16[64,1408]{1,0:T(8,128)(2,1)}, bf16[64,1408]{1,0:T(8,128)(2,1)}, u32[]{:S(2)}, u32[]{:S(2)}) collective-permute-start(bf16[64,1408]{1,0:T(8,128)(2,1)} %slice.181), channel_id=1, source_target_pairs={{8,0},{12,4},{0,8},{4,12},{9,1},{13,5},{1,9},{5,13},{10,2},{14,6},... | collective-permute-start | bytes 540680 | tf_op jit(solution)/shard_map/ppermute | solution.py:15
  111.9 16.2 %collective-permute-start.10 = (bf16[64,1408]{1,0:T(8,128)(2,1)}, bf16[64,1408]{1,0:T(8,128)(2,1)}, u32[]{:S(2)}, u32[]{:S(2)}) collective-permute-start(bf16[64,1408]{1,0:T(8,128)(2,1)} %slice.181), channel_id=1, source_target_pairs={{4,0},{8,4},{12,8},{0,12},{5,1},{9,5},{13,9},{1,13},{6,2},{10,6},{... | collective-permute-start | bytes 540680 | tf_op jit(solution)/shard_map/ppermute | solution.py:15
  115.1 26.8 %copy-start.3 = (bf16[256,1344]{1,0:T(8,128)(2,1)}, bf16[256,1344]{1,0:T(8,128)(2,1)S(1)}, u32[]{:S(2)}) copy-start(bf16[256,1344]{1,0:T(8,128)(2,1)S(1)} %pad_maximum_fusion.3.refs_7_) | copy-start | bytes 2064388
  124.1 23.4 %collective-permute-start.22 = (bf16[256,1344]{0,1:T(8,128)(2,1)}, bf16[256,1344]{0,1:T(8,128)(2,1)}, u32[]{:S(2)}, u32[]{:S(2)}) collective-permute-start(bf16[256,1344]{0,1:T(8,128)(2,1)} %copy.16), channel_id=1, source_target_pairs={{12,0},{0,4},{4,8},{8,12},{13,1},{1,5},{5,9},{9,13},{14,2},{2,6},{... | collective-permute-start | bytes 2064392 | tf_op jit(solution)/shard_map/ppermute | solution.py:15
  128.1 19.5 %collective-permute-start.20 = (bf16[256,1344]{0,1:T(8,128)(2,1)}, bf16[256,1344]{0,1:T(8,128)(2,1)}, u32[]{:S(2)}, u32[]{:S(2)}) collective-permute-start(bf16[256,1344]{0,1:T(8,128)(2,1)} %copy.16), channel_id=1, source_target_pairs={{4,0},{8,4},{12,8},{0,12},{5,1},{9,5},{13,9},{1,13},{6,2},{10,6},{... | collective-permute-start | bytes 2064392 | tf_op jit(solution)/shard_map/ppermute | solution.py:15
  130.8 20.0 %collective-permute-start.31 = (bf16[256,1408]{1,0:T(8,128)(2,1)}, bf16[256,1408]{1,0:T(8,128)(2,1)}, u32[]{:S(2)}, u32[]{:S(2)}) collective-permute-start(bf16[256,1408]{1,0:T(8,128)(2,1)} %pad_maximum_fusion.4.refs_2_), channel_id=1, source_target_pairs={{1,0},{2,1},{3,2},{0,3},{5,4},{6,5},{7,6},{4,7},{9,8},{10,9},{11,1... | collective-permute-start | bytes 2162696 | tf_op jit(solution)/shard_map/ppermute | solution.py:15
  134.8 21.7 %collective-permute-start.15 = (bf16[256,1408]{1,0:T(8,128)(2,1)}, bf16[256,1408]{1,0:T(8,128)(2,1)}, u32[]{:S(2)}, u32[]{:S(2)}) collective-permute-start(bf16[256,1408]{1,0:T(8,128)(2,1)} %pad_maximum_fusion.2.refs_2_), channel_id=1, source_target_pairs={{3,0},{0,1},{1,2},{2,3},{7,4},{4,5},{5,6},{6,7},{11,8},{8,9},{9,10... | collective-permute-start | bytes 2162696 | tf_op jit(solution)/shard_map/ppermute | solution.py:15
  135.0 26.1 %collective-permute-start.13 = (bf16[256,1408]{1,0:T(8,128)(2,1)}, bf16[256,1408]{1,0:T(8,128)(2,1)}, u32[]{:S(2)}, u32[]{:S(2)}) collective-permute-start(bf16[256,1408]{1,0:T(8,128)(2,1)} %pad_maximum_fusion.2.refs_2_), channel_id=1, source_target_pairs={{1,0},{2,1},{3,2},{0,3},{5,4},{6,5},{7,6},{4,7},{9,8},{10,9},{11,1... | collective-permute-start | bytes 2162696 | tf_op jit(solution)/shard_map/ppermute | solution.py:15
  147.5 15.3 %collective-permute-start.41 = (bf16[128,1344]{1,0:T(8,128)(2,1)}, bf16[128,1344]{1,0:T(8,128)(2,1)}, u32[]{:S(2)}, u32[]{:S(2)}) collective-permute-start(bf16[128,1344]{1,0:T(8,128)(2,1)} %slice.197), channel_id=1, source_target_pairs={{12,0},{0,4},{4,8},{8,12},{13,1},{1,5},{5,9},{9,13},{14,2},{2,6},{... | collective-permute-start | bytes 1032200 | tf_op jit(solution)/shard_map/ppermute | solution.py:15
  147.6 19.0 %collective-permute-start.39 = (bf16[128,1344]{1,0:T(8,128)(2,1)}, bf16[128,1344]{1,0:T(8,128)(2,1)}, u32[]{:S(2)}, u32[]{:S(2)}) collective-permute-start(bf16[128,1344]{1,0:T(8,128)(2,1)} %slice.196), channel_id=1, source_target_pairs={{4,0},{8,4},{12,8},{0,12},{5,1},{9,5},{13,9},{1,13},{6,2},{10,6},{... | collective-permute-start | bytes 1032200 | tf_op jit(solution)/shard_map/ppermute | solution.py:15
  150.8 15.8 %collective-permute-start.34 = (bf16[128,1408]{1,0:T(8,128)(2,1)S(1)}, bf16[128,1408]{1,0:T(8,128)(2,1)}, u32[]{:S(2)}, u32[]{:S(2)}) collective-permute-start(bf16[128,1408]{1,0:T(8,128)(2,1)S(1)} %slice.194), channel_id=1, source_target_pairs={{3,0},{0,1},{1,2},{2,3},{7,4},{4,5},{5,6},{6,7},{11,8},{8,9},{9,10... | collective-permute-start | bytes 1081352 | tf_op jit(solution)/shard_map/ppermute | solution.py:15
  155.2 14.6 %copy-start.8 = (bf16[256,1344]{1,0:T(8,128)(2,1)}, bf16[256,1344]{1,0:T(8,128)(2,1)S(1)}, u32[]{:S(2)}) copy-start(bf16[256,1344]{1,0:T(8,128)(2,1)S(1)} %copy.26.refs_8_) | copy-start | bytes 2064388
  155.2 14.6 %copy-start.9 = (f32[1,64,2752]{2,1,0:T(8,128)S(1)}, f32[1,64,2752]{2,1,0:T(8,128)}, u32[]{:S(2)}) copy-start(f32[1,64,2752]{2,1,0:T(8,128)} %get-tuple-element.30) | copy-start | bytes 2113540
  156.5 26.8 %collective-permute-start.23 = (bf16[128,1344]{1,0:T(8,128)(2,1)S(1)}, bf16[128,1344]{1,0:T(8,128)(2,1)S(1)}, u32[]{:S(2)}, u32[]{:S(2)}) collective-permute-start(bf16[128,1344]{1,0:T(8,128)(2,1)S(1)} %slice.186), channel_id=1, source_target_pairs={{12,0},{0,4},{4,8},{8,12},{13,1},{1,5},{5,9},{9,13},{14,2},{2,6},{... | collective-permute-start | bytes 1032200 | tf_op jit(solution)/shard_map/ppermute | solution.py:15
  161.0 22.4 %collective-permute-start.21 = (bf16[128,1344]{1,0:T(8,128)(2,1)S(1)}, bf16[128,1344]{1,0:T(8,128)(2,1)S(1)}, u32[]{:S(2)}, u32[]{:S(2)}) collective-permute-start(bf16[128,1344]{1,0:T(8,128)(2,1)S(1)} %slice.185), channel_id=1, source_target_pairs={{4,0},{8,4},{12,8},{0,12},{5,1},{9,5},{13,9},{1,13},{6,2},{10,6},{... | collective-permute-start | bytes 1032200 | tf_op jit(solution)/shard_map/ppermute | solution.py:15
  162.8 11.5 %collective-permute-start.32 = (bf16[128,1408]{1,0:T(8,128)(2,1)S(1)}, bf16[128,1408]{1,0:T(8,128)(2,1)S(1)}, u32[]{:S(2)}, u32[]{:S(2)}) collective-permute-start(bf16[128,1408]{1,0:T(8,128)(2,1)S(1)} %slice.193), channel_id=1, source_target_pairs={{1,0},{2,1},{3,2},{0,3},{5,4},{6,5},{7,6},{4,7},{9,8},{10,9},{11,1... | collective-permute-start | bytes 1081352 | tf_op jit(solution)/shard_map/ppermute | solution.py:15
  166.5 16.9 %collective-permute-start.16 = (bf16[128,1408]{1,0:T(8,128)(2,1)S(1)}, bf16[128,1408]{1,0:T(8,128)(2,1)S(1)}, u32[]{:S(2)}, u32[]{:S(2)}) collective-permute-start(bf16[128,1408]{1,0:T(8,128)(2,1)S(1)} %slice.183), channel_id=1, source_target_pairs={{3,0},{0,1},{1,2},{2,3},{7,4},{4,5},{5,6},{6,7},{11,8},{8,9},{9,10... | collective-permute-start | bytes 1081352 | tf_op jit(solution)/shard_map/ppermute | solution.py:15
  166.5 16.9 %collective-permute-start.14 = (bf16[128,1408]{1,0:T(8,128)(2,1)S(1)}, bf16[128,1408]{1,0:T(8,128)(2,1)S(1)}, u32[]{:S(2)}, u32[]{:S(2)}) collective-permute-start(bf16[128,1408]{1,0:T(8,128)(2,1)S(1)} %slice.182), channel_id=1, source_target_pairs={{1,0},{2,1},{3,2},{0,3},{5,4},{6,5},{7,6},{4,7},{9,8},{10,9},{11,1... | collective-permute-start | bytes 1081352 | tf_op jit(solution)/shard_map/ppermute | solution.py:15
  (15 other events, 53.1 us)

commit v2 on v1

v2 whole, which is shorter than its diff:
```python
import jax
import jax.numpy as jnp
from jax import lax
from jax.experimental import pallas as pl
from jax.experimental.pallas import tpu as pltpu
from jax.sharding import Mesh, PartitionSpec as P

BF16 = jnp.bfloat16
F32 = jnp.float32
SIDE = 4
LANES = 128
VMEM = 56 * 1024 * 1024
PARAMS = pltpu.CompilerParams(vmem_limit_bytes=VMEM)
ANYWHERE = pl.BlockSpec(memory_space=pl.ANY)


def receive(value, axis, distance):
    return lax.ppermute(value, axis, [((i + distance) % SIDE, i) for i in range(SIDE)])


def send(value, axis, distance):
    return receive(value, axis, -distance)


def swap_cores(value):
    return lax.ppermute(value, "c", [(0, 1), (1, 0)])


def cost(flops, moved):
    return pl.CostEstimate(flops=flops, bytes_accessed=moved, transcendentals=0)


def arrange_kernel(where_ref, bases_ref, _, by_y_ref, by_z_ref):
    y, z = where_ref[2], where_ref[3]
    ranks = bases_ref.shape[2]
    part = ranks // (SIDE * SIDE)
    block = ranks // SIDE
    for out_ref, y_outer in ((by_y_ref, True), (by_z_ref, False)):
        for low in range(0, ranks, block):
            source = lax.broadcasted_iota(jnp.int32, (ranks, block), 0)
            column = lax.broadcasted_iota(jnp.int32, (ranks, block), 1) + low
            outer, inner = column // (SIDE * part), (column // part) & (SIDE - 1)
            dy, dz = (outer, inner) if y_outer else (inner, outer)
            wanted = (((y + dy) & (SIDE - 1)) * SIDE + ((z + dz) & (SIDE - 1))) * part
            wanted = wanted + (column & (part - 1))
            place = jnp.where(source == wanted, 1.0, 0.0).astype(BF16)
            for k in range(bases_ref.shape[0]):
                out_ref[k, :, low : low + block] = jnp.dot(
                    bases_ref[k], place, preferred_element_type=F32
                ).astype(BF16)


def arrange(where, bases, after):
    out = jax.ShapeDtypeStruct(bases.shape, BF16)
    whole = pl.BlockSpec(bases.shape, lambda i, w: (0, 0, 0))
    return pl.pallas_call(
        arrange_kernel,
        grid_spec=pltpu.PrefetchScalarGridSpec(
            num_scalar_prefetch=1, grid=(1,), in_specs=[whole, ANYWHERE], out_specs=[whole] * 2
        ),
        out_shape=[out, out],
        compiler_params=PARAMS,
        cost_estimate=cost(4 * bases.size * bases.shape[2], 6 * bases.size),
    )(where, bases, after)


def partial_kernel(where_ref, proj_ref, grads_ref, _, mine_ref, other_ref):
    half = mine_ref.shape[2]
    both = lax.dot_general(
        proj_ref[...], grads_ref[0], (((0,), (0,)), ((), ())), preferred_element_type=F32
    ).astype(BF16)
    low, high = both[:, :half], both[:, half:]

    @pl.when(where_ref[1] == 0)
    def _():
        mine_ref[0] = low
        other_ref[0] = high

    @pl.when(where_ref[1] == 1)
    def _():
        mine_ref[0] = high
        other_ref[0] = low


def partial_grads(where, proj, grads, which, after):
    tokens, rank_part = proj.shape
    pair = grads.shape[2] // SIDE
    out = jax.ShapeDtypeStruct((SIDE, rank_part, pair // 2), BF16)
    return pl.pallas_call(
        partial_kernel,
        grid_spec=pltpu.PrefetchScalarGridSpec(
            num_scalar_prefetch=1,
            grid=(SIDE,),
            in_specs=[
                pl.BlockSpec((tokens, rank_part), lambda i, w: (0, 0)),
                pl.BlockSpec((1, tokens, pair), lambda i, w: (which, 0, (w[0] + i) % SIDE)),
                ANYWHERE,
            ],
            out_specs=[pl.BlockSpec((1, rank_part, pair // 2), lambda i, w: (i, 0, 0))] * 2,
        ),
        out_shape=[out, out],
        compiler_params=PARAMS,
        cost_estimate=cost(
            2 * tokens * rank_part * pair * SIDE, 2 * tokens * pair * SIDE + 2 * rank_part * pair * SIDE
        ),
    )(where, proj, grads, after)


def direction_kernel(*refs):
    mine_ref, other_ref, one_ref, two_ref, first_ref, second_ref = refs[:6]
    new_first_ref, new_second_ref, left_ref, right_ref = refs[-4:]
    gradient = mine_ref[0].astype(F32) + other_ref[0].astype(F32)
    gradient = gradient + one_ref[...].astype(F32) + two_ref[...].astype(F32)
    new_first = 0.9 * first_ref[0] + 0.1 * gradient
    new_second = 0.999 * second_ref[0] + 0.001 * gradient * gradient
    new_first_ref[0] = new_first
    new_second_ref[0] = new_second
    first_fix = 1.0 - 0.9**1000.0
    second_fix = 1.0 - 0.999**1000.0
    direction = (new_first / first_fix / (jnp.sqrt(new_second / second_fix) + 1e-08)).astype(BF16)
    cut = left_ref.shape[1]
    rest = direction.shape[1] - cut
    left_ref[...] = direction[:, :cut]
    right_ref[:, :rest] = direction[:, cut:]
    right_ref[:, rest:] = jnp.zeros((right_ref.shape[0], cut - rest), BF16)


def directions(mine, other, one, two, first_moment, second_moment, which, before):
    _, rows, width = first_moment.shape
    cut = (width // 2 + LANES - 1) // LANES * LANES
    tile = 16
    zero = pl.BlockSpec((1, tile, width), lambda i: (0, i, 0))
    flat = pl.BlockSpec((tile, width), lambda i: (i, 0))
    own = pl.BlockSpec((1, tile, width), lambda i: (which, i, 0))
    half = pl.BlockSpec((tile, cut), lambda i: (i, 0))
    in_specs = [zero, zero, flat, flat, own, own]
    args = [mine, other, one, two, first_moment, second_moment]
    aliases = {}
    if before:
        aliases = {len(args) + i: i for i in range(len(before))}
        in_specs += [ANYWHERE] * len(before)
        args += before
    piece = jax.ShapeDtypeStruct((rows, cut), BF16)
    full = jax.ShapeDtypeStruct(first_moment.shape, F32)
    return pl.pallas_call(
        direction_kernel,
        grid=(rows // tile,),
        in_specs=in_specs,
        out_specs=[own, own, half, half],
        out_shape=[full, full, piece, piece],
        input_output_aliases=aliases,
        compiler_params=PARAMS,
        cost_estimate=cost(30 * rows * width, 26 * rows * width),
    )(*args)


def stack_kernel(*refs):
    rows = refs[0].shape[0]
    for i, ref in enumerate(refs[:-1]):
        refs[-1][i * rows : (i + 1) * rows, :] = ref[...]


def stack(pieces):
    rows, width = pieces[0].shape
    return pl.pallas_call(
        stack_kernel,
        out_shape=jax.ShapeDtypeStruct((rows * len(pieces), width), BF16),
        compiler_params=PARAMS,
        cost_estimate=cost(0, 4 * rows * width * len(pieces)),
    )(*pieces)


def expand_kernel(columns_ref, *refs):
    pieces, out_ref = refs[:SIDE], refs[-1]
    width = pieces[0].shape[1]
    for low in range(0, width, 256):
        high = min(low + 256, width)
        total, at = None, 0
        for piece in pieces:
            depth = piece.shape[0]
            term = jnp.dot(
                columns_ref[0, :, at : at + depth], piece[:, low:high], preferred_element_type=F32
            )
            total = term if total is None else total + term
            at += depth
        out_ref[0, low:high, :] = total.T.astype(BF16)


def expand(columns, pieces, width, which, place, before):
    count, rows, ranks = columns.shape
    cut = pieces[0].shape[1]
    in_specs = [pl.BlockSpec((1, rows, ranks), lambda i: (which, 0, 0))]
    in_specs += [pl.BlockSpec(p.shape, lambda i: (0, 0)) for p in pieces]
    args = [columns, *pieces]
    aliases = {}
    if before is not None:
        in_specs.append(ANYWHERE)
        aliases = {len(args): 0}
        args.append(before)
    return pl.pallas_call(
        expand_kernel,
        grid=(1,),
        in_specs=in_specs,
        out_specs=pl.BlockSpec((1, cut, rows), lambda i: (which, place, 0)),
        out_shape=jax.ShapeDtypeStruct((count, width, rows), BF16),
        input_output_aliases=aliases,
        compiler_params=PARAMS,
        cost_estimate=cost(2 * rows * ranks * cut, 2 * (rows * ranks + ranks * cut + rows * cut)),
    )(*args)


def ring_gather(value, first, second, way):
    row = stack([value] + [receive(value, first, d) for d in (1, 2, 3)])
    after = receive(row, second, 1)
    before = receive(row, second, -1)
    far = receive(after if way == 1 else before, second, way)
    return row, after, far, before


def on_device(activations, out_grads, bases, first_moment, second_moment):
    where = jnp.stack([lax.axis_index(n) for n in ("x", "c", "y", "z")]).astype(jnp.int32)
    y, z = where[2], where[3]
    features, ranks = bases.shape[1:]
    part = ranks // (SIDE * SIDE)
    width = first_moment.shape[2]

    column = jnp.arange(ranks)
    slow, fast, inner = column // (SIDE * part), column // part % SIDE, column % part
    source = (((y + slow) % SIDE) * SIDE + (z + fast) % SIDE) * part + inner
    place = (column[:, None] == source[None, :]).astype(BF16)
    own = lax.dynamic_slice_in_dim(activations, (y * SIDE + z) * features, features, 1)
    partial = jnp.einsum("td,kdr->ktr", own, bases, preferred_element_type=F32).astype(BF16)
    partial = jnp.einsum("ktr,rs->kts", partial, place, preferred_element_type=F32).astype(BF16)
    first_sent = None
    for axis in ("y", "z"):
        size = partial.shape[2] // SIDE
        blocks = [partial[:, :, i * size : (i + 1) * size] for i in range(SIDE)]
        first_sent = blocks[2] if first_sent is None else first_sent
        total = blocks[0].astype(F32)
        for i in (1, 3, 2):
            total = total + send(blocks[i], axis, i).astype(F32)
        partial = total.astype(BF16)
    columns_y, columns_z = arrange(where, bases, first_sent)

    moments, update = [], None
    after = columns_y
    for which in range(2):
        way = 1 if which == 0 else -1
        mine, other = partial_grads(where, partial[which], out_grads, which, after)
        other = swap_cores(other)
        sums = [mine[i].astype(F32) + other[i].astype(F32) for i in range(SIDE)]
        near = send(sums[-way % SIDE].astype(BF16), "x", -way)
        far = sums[2].astype(BF16)
        after = far
        passed = send(far, "x", way).astype(F32) + sums[way % SIDE]
        passed = send(passed.astype(BF16), "x", way)
        *moments, left, right = directions(
            mine, other, near, passed, first_moment, second_moment, which, moments
        )
        for half, first, second, columns in (
            (0, "y", "z", columns_z),
            (1, "z", "y", columns_y),
        ):
            pieces = ring_gather((left, right)[half], first, second, way)
            update = expand(columns, pieces, width, which, half, update)
    return jnp.swapaxes(update, 1, 2), *moments


def solution(mesh):
    grid = Mesh(mesh.devices.reshape(4, 2, 4, 4), ("x", "c", "y", "z"))
    dp, fsdp = ("x", "c"), ("y", "z")
    return jax.shard_map(
        on_device,
        mesh=grid,
        in_specs=(
            P(dp, None),
            P(None, dp, None),
            P(None, fsdp, None),
            P(None, fsdp, dp),
            P(None, fsdp, dp),
        ),
        out_specs=(P(None, fsdp, dp), P(None, fsdp, dp), P(None, fsdp, dp)),
        check_vma=False,
    )
```

time: 203 us -> 190 us (0.936)
  Pallas kernels: 29.8 us -> 58.3 us
  local copies, waits for them, and re-layouts: 30.2 us -> 8.1 us
  starting transfers between devices: 62.3 us -> 48.1 us
  waiting for transfers between devices: 56.2 us -> 66.4 us
  other arithmetic: 12.5 us -> 4.68 us
  matrix products: 9.88 us -> 2.91 us
    pallas_call x2 -> x11, Pallas kernels: 16.8 us -> 45.2 us  [the longest x4 20.5 us: expand(): pl.pallas_call(expand_kernel, grid=(1,), in_specs=in_specs, out_specs=pl....]
    ppermute x40 -> x36, starting transfers between devices: 61.8 us -> 47.9 us  [receive(): lax.ppermute(value, axis, [((i + distance) % SIDE, i) for i in range(SIDE)])]
    slice x14 -> x2, local copies, waits for them, and re-layouts: 8.16 us -> 0.13 us  [on_device(): blocks = [partial[:, :, i * size:(i + 1) * size] for i in range(SIDE)]]
    dot_general x3 -> x1, matrix products: 9.88 us -> 2.91 us  [on_device(): jnp.einsum('ktr,rs->kts', partial, place, preferred_element_type=F32)]
    ppermute x40 -> x36, waiting for transfers between devices: 56.2 us -> 63 us  [receive(): lax.ppermute(value, axis, [((i + distance) % SIDE, i) for i in range(SIDE)])]
    ppermute x4 -> x0, local copies, waits for them, and re-layouts: 6.06 us -> none  [receive(): lax.ppermute(value, axis, [((i + distance) % SIDE, i) for i in range(SIDE)])]
    unnamed x43 -> x66, local copies, waits for them, and re-layouts: 13.1 us -> 7.35 us
    concatenate x4 -> x0, other arithmetic: 5.41 us -> none  [ring_gather(): jnp.concatenate([value] + [receive(value, first, d) for d in (1, 2, 3)],...]
  transfers between devices with their start and end apart: 42 -> 38, of which waited for: 15 -> 16; matrix products, arithmetic and copies ran while one was open for 16% -> 1% of each run, Pallas kernels for 7% -> 21%
where the time goes in v2:
time: 190 us; the launch traced here: 189 us
  waiting for transfers between devices  66.4 us (35%)
  Pallas kernels  58.3 us (31%)
  starting transfers between devices  48.1 us (25%)
  local copies, waits for them, and re-layouts  8.1 us (4%)
  other arithmetic  4.68 us (2%)
  matrix products  2.91 us (2%)
    ppermute x36, waiting for transfers between devices, receive(): lax.ppermute(value, axis, [((i + distance) % SIDE, i) for i in range(SIDE)])  63 us
    ppermute x36, starting transfers between devices, receive(): lax.ppermute(value, axis, [((i + distance) % SIDE, i) for i in range(SIDE)])  47.9 us
    pallas_call x4, Pallas kernels, expand(): pl.pallas_call(expand_kernel, grid=(1,), in_specs=in_specs, out_specs=pl....  20.5 us
    pallas_call x2, Pallas kernels, partial_grads(): pl.pallas_call(partial_kernel, grid_spec=pltpu.PrefetchScalarGridSpec(num...  13 us
    pallas_call x4, Pallas kernels, stack(): pl.pallas_call(stack_kernel, out_shape=jax.ShapeDtypeStruct((rows * len(p...  8.53 us
    pallas_call x1, Pallas kernels, arrange(): pl.pallas_call(arrange_kernel, grid_spec=pltpu.PrefetchScalarGridSpec(num...  8.13 us
    pallas_call x2, Pallas kernels, directions(): pl.pallas_call(direction_kernel, grid=(rows // tile,), in_specs=in_specs,...  8.05 us
    unnamed x66, local copies, waits for them, and re-layouts  7.35 us
  transfers between devices with their start and end apart: 38, of which 16 were waited for; matrix products, arithmetic and copies ran while one was open for 1% of the time, Pallas kernels for 21%

profile of v2, /device:TPU:0, one launch (start us, length us, event | category | flops | bytes accessed | tf_op | source)
XLA Modules:
  0.0 189.3 jit_solution(15660520338457516780)
XLA Ops:
  0.7 1.6 copy-done
  2.2 2.9 %fusion.4 = bf16[2,128,1024]{2,1,0:T(8,128)(2,1)S(1)} fusion(s32[1024]{0:T(1024)S(1)} %fusion.27, bf16[2,512,1024]{2,1,0:T(8,128)(2,1)} %bases_ref.1, bf16[128,8192]{1,0:T(8,128)(2,1)S(1)} %copy-done, s32[]{:T(128)S(6)} %select_n.54), kind=kOutput, calls=%fused_computation.4 | convolution fusion | flops 806879232 | bytes 2756612 | tf_op jit(solution)/shard_map/ktr,rs->kts/dot_general | solution.py:233
  5.2 3.4 %collective-permute-start.2 = (bf16[2,128,256]{2,1,0:T(8,128)(2,1)S(1)}, bf16[2,128,256]{2,1,0:T(8,128)(2,1)S(1)}, u32[]{:S(2)}, u32[]{:S(2)}) collective-permute-start(bf16[2,128,256]{2,1,0:T(8,128)(2,1)S(1)} %get-tuple-element.37._), channel_id=1, source_target_pairs={{8,0},{12,4},{0,8},{4,12},{9,1},{13,5},{1,9},{5,13},{10,2},{14,6},... | collective-permute-start | bytes 393224 | tf_op jit(solution)/shard_map/ppermute | solution.py:18
  9.2 2.6 %collective-permute-start.1 = (bf16[2,128,256]{2,1,0:T(8,128)(2,1)S(1)}, bf16[2,128,256]{2,1,0:T(8,128)(2,1)S(1)}, u32[]{:S(2)}, u32[]{:S(2)}) collective-permute-start(bf16[2,128,256]{2,1,0:T(8,128)(2,1)S(1)} %get-tuple-element.36), channel_id=1, source_target_pairs={{4,0},{8,4},{12,8},{0,12},{5,1},{9,5},{13,9},{1,13},{6,2},{10,6},{... | collective-permute-start | bytes 393224 | tf_op jit(solution)/shard_map/ppermute | solution.py:18
  12.9 2.3 %collective-permute-done = bf16[2,128,256]{2,1,0:T(8,128)(2,1)S(1)} collective-permute-done((bf16[2,128,256]{2,1,0:T(8,128)(2,1)S(1)}, bf16[2,128,256]{2,1,0:T(8,128)(2,1)S(1)}, u32[]{:S(2)}, u32[]{:S(2)}) %collective-permute-start) | collective-permute-done | bytes 131104 | tf_op jit(solution)/shard_map/ppermute | solution.py:18
  15.4 2.0 %collective-permute-start.3 = (bf16[2,128,64]{2,1,0:T(8,128)(2,1)S(1)}, bf16[2,128,64]{2,1,0:T(8,128)(2,1)S(1)}, u32[]{:S(2)}, u32[]{:S(2)}) collective-permute-start(bf16[2,128,64]{2,1,0:T(8,128)(2,1)S(1)} %get-tuple-element.38), channel_id=1, source_target_pairs={{3,0},{0,1},{1,2},{2,3},{7,4},{4,5},{5,6},{6,7},{11,8},{8,9},{9,10... | collective-permute-start | bytes 98312 | tf_op jit(solution)/shard_map/ppermute | solution.py:18
  17.4 2.2 %collective-permute-start.4 = (bf16[2,128,64]{2,1,0:T(8,128)(2,1)S(1)}, bf16[2,128,64]{2,1,0:T(8,128)(2,1)S(1)}, u32[]{:S(2)}, u32[]{:S(2)}) collective-permute-start(bf16[2,128,64]{2,1,0:T(8,128)(2,1)S(1)} %get-tuple-element.40), channel_id=1, source_target_pairs={{1,0},{2,1},{3,2},{0,3},{5,4},{6,5},{7,6},{4,7},{9,8},{10,9},{11,1... | collective-permute-start | bytes 98312 | tf_op jit(solution)/shard_map/ppermute | solution.py:18
  19.6 1.8 collective-permute-start.5
  21.4 8.1 %shard_map.76 = (bf16[2,512,1024]{2,1,0:T(8,128)(2,1)}, bf16[2,512,1024]{2,1,0:T(8,128)(2,1)}) custom-call(s32[4]{0:T(128)} %pad_add_fusion.where_ref, bf16[2,512,1024]{2,1,0:T(8,128)(2,1)} %bases_ref.1, bf16[2,128,256]{2,1,0:T(8,128)(2,1)} %copy-done.32), custom_call_target="tpu_custom_call" | custom-call | flops 4294967296 | bytes 6291456 | tf_op jit(solution)/shard_map/pallas_call | solution.py:56
  30.2 6.5 %shard_map.77 = (bf16[4,64,2752]{2,1,0:T(8,128)(2,1)}, bf16[4,64,2752]{2,1,0:T(8,128)(2,1)}) custom-call(s32[4]{0:T(128)} %pad_add_fusion.where_ref, bf16[128,64]{1,0:T(8,128)(2,1)} %get-tuple-element.41.proj_ref, bf16[2,128,22016]{2,1,0:T(8,128)(2,1)} %grads_ref.3, bf16[2,512,1024]{2,1,0:T(8,128)(2,1)} %get-tuple-element.17._.columns_ref), custom_call_target="tpu_custom_call" | custom-call | flops 360710144 | bytes 8454144 | tf_op jit(solution)/shard_map/pallas_call | solution.py:89
  36.7 3.4 %collective-permute-done.6.refs_1_ = bf16[4,64,2752]{2,1,0:T(8,128)(2,1)S(1)} collective-permute-done((bf16[4,64,2752]{2,1,0:T(8,128)(2,1)}, bf16[4,64,2752]{2,1,0:T(8,128)(2,1)S(1)}, u32[]{:S(2)}, u32[]{:S(2)}) %collective-permute-start.6) | collective-permute-done | bytes 1409056 | tf_op jit(solution)/shard_map/ppermute | solution.py:26
  40.1 2.5 %fusion.13 = (bf16[64,2752]{1,0:T(8,128)(2,1)S(1)}, bf16[64,2752]{1,0:T(8,128)(2,1)}) fusion(bf16[4,64,2752]{2,1,0:T(8,128)(2,1)S(1)} %collective-permute-done.6.refs_1_, bf16[4,64,2752]{2,1,0:T(8,128)(2,1)} %get-tuple-element.18.refs_0_), kind=kLoop, calls=%fused_computation.18 | loop fusion | flops 1409024 | bytes 2113536 | tf_op jit(solution)/shard_map/convert_element_type | solution.py:252
  42.6 6.6 %shard_map.78 = (bf16[4,64,2752]{2,1,0:T(8,128)(2,1)}, bf16[4,64,2752]{2,1,0:T(8,128)(2,1)}) custom-call(s32[4]{0:T(128)} %pad_add_fusion.where_ref, bf16[128,64]{1,0:T(8,128)(2,1)} %get-tuple-element.42.proj_ref, bf16[2,128,22016]{2,1,0:T(8,128)(2,1)} %grads_ref.3, bf16[64,2752]{1,0:T(8,128)(2,1)} %get-tuple-element.32._), custom_call_target="tpu_custom_call" | custom-call | flops 360710144 | bytes 8454144 | tf_op jit(solution)/shard_map/pallas_call | solution.py:89
  49.4 1.5 collective-permute-start.12
  50.9 1.7 collective-permute-start.11
  52.6 8.6 %collective-permute-done.12 = bf16[64,2752]{1,0:T(8,128)(2,1)S(1)} collective-permute-done((bf16[64,2752]{1,0:T(8,128)(2,1)S(1)}, bf16[64,2752]{1,0:T(8,128)(2,1)S(1)}, u32[]{:S(2)}, u32[]{:S(2)}) %collective-permute-start.12) | collective-permute-done | bytes 352288 | tf_op jit(solution)/shard_map/ppermute | solution.py:18
  62.9 3.0 %collective-permute-start.9 = (bf16[64,2752]{1,0:T(8,128)(2,1)S(1)}, bf16[64,2752]{1,0:T(8,128)(2,1)S(1)}, u32[]{:S(2)}, u32[]{:S(2)}) collective-permute-start(bf16[64,2752]{1,0:T(8,128)(2,1)S(1)} %get-tuple-element.33), channel_id=1, source_target_pairs={{32,0},{64,32},{96,64},{0,96},{33,1},{65,33},{97,65},{1,97},{34,2}... | collective-permute-start | bytes 1056776 | tf_op jit(solution)/shard_map/ppermute | solution.py:18
  65.9 7.6 %collective-permute-done.13.refs_3_ = bf16[64,2752]{1,0:T(8,128)(2,1)S(1)} collective-permute-done((bf16[64,2752]{1,0:T(8,128)(2,1)S(1)}, bf16[64,2752]{1,0:T(8,128)(2,1)S(1)}, u32[]{:S(2)}, u32[]{:S(2)}) %collective-permute-start.13) | collective-permute-done | bytes 352288 | tf_op jit(solution)/shard_map/ppermute | solution.py:18
  74.3 4.0 %shard_map.79 = (f32[2,64,2752]{2,1,0:T(8,128)}, f32[2,64,2752]{2,1,0:T(8,128)}, bf16[64,1408]{1,0:T(8,128)(2,1)}, bf16[64,1408]{1,0:T(8,128)(2,1)}) custom-call(bf16[4,64,2752]{2,1,0:T(8,128)(2,1)} %get-tuple-element.18.refs_0_, bf16[4,64,2752]{2,1,0:T(8,128)(2,1)} %copy-done.3, bf16[64,2752]{1,0:T(8,128)(2,1)} %copy-done.19, bf16[64,2752]{1,0:T(8,128)(2,1)} %copy-done.20, ...), custom_call_target="tpu_custom_call" | custom-call | flops 5283840 | bytes 4579328 | tf_op jit(solution)/shard_map/pallas_call | solution.py:145
  78.3 3.2 %collective-permute-start.32 = (bf16[64,1408]{1,0:T(8,128)(2,1)}, bf16[64,1408]{1,0:T(8,128)(2,1)S(1)}, u32[]{:S(2)}, u32[]{:S(2)}) collective-permute-start(bf16[64,1408]{1,0:T(8,128)(2,1)} %get-tuple-element.28.refs_0_), channel_id=1, source_target_pairs={{4,0},{8,4},{12,8},{0,12},{5,1},{9,5},{13,9},{1,13},{6,2},{10,6},{... | collective-permute-start | bytes 540680 | tf_op jit(solution)/shard_map/ppermute | solution.py:18
  82.4 5.9 %collective-permute-done.32.refs_1_ = bf16[64,1408]{1,0:T(8,128)(2,1)S(1)} collective-permute-done((bf16[64,1408]{1,0:T(8,128)(2,1)}, bf16[64,1408]{1,0:T(8,128)(2,1)S(1)}, u32[]{:S(2)}, u32[]{:S(2)}) %collective-permute-start.32) | collective-permute-done | bytes 180256 | tf_op jit(solution)/shard_map/ppermute | solution.py:18
  88.2 1.8 collective-permute-done.33.refs_2_
  90.0 1.6 collective-permute-done.34.refs_3_
  92.3 2.2 %shard_map.84.refs_0_ = bf16[256,1408]{1,0:T(8,128)(2,1)} custom-call(bf16[64,1408]{1,0:T(8,128)(2,1)} %get-tuple-element.28.refs_0_, bf16[64,1408]{1,0:T(8,128)(2,1)} %copy-done.29, bf16[64,1408]{1,0:T(8,128)(2,1)} %copy-done.30, bf16[64,1408]{1,0:T(8,128)(2,1)} %copy-done.31), custom_call_target="tpu_custom_call" | custom-call | bytes 1441792 | tf_op jit(solution)/shard_map/pallas_call | solution.py:165
  95.3 3.3 %collective-permute-start.10 = (bf16[64,2752]{1,0:T(8,128)(2,1)S(1)}, bf16[64,2752]{1,0:T(8,128)(2,1)S(1)}, u32[]{:S(2)}, u32[]{:S(2)}) collective-permute-start(bf16[64,2752]{1,0:T(8,128)(2,1)S(1)} %fusion.9), channel_id=1, source_target_pairs={{32,0},{64,32},{96,64},{0,96},{33,1},{65,33},{97,65},{1,97},{34,2}... | collective-permute-start | bytes 1056776 | tf_op jit(solution)/shard_map/ppermute | solution.py:18
  98.6 1.3 collective-permute-start.37
  99.9 1.9 %collective-permute-start.26 = (bf16[64,1408]{1,0:T(8,128)(2,1)}, bf16[64,1408]{1,0:T(8,128)(2,1)S(1)}, u32[]{:S(2)}, u32[]{:S(2)}) collective-permute-start(bf16[64,1408]{1,0:T(8,128)(2,1)} %get-tuple-element.27.refs_0_), channel_id=1, source_target_pairs={{1,0},{2,1},{3,2},{0,3},{5,4},{6,5},{7,6},{4,7},{9,8},{10,9},{11,1... | collective-permute-start | bytes 540680 | tf_op jit(solution)/shard_map/ppermute | solution.py:18
  101.9 3.7 %collective-permute-done.8.refs_2_ = bf16[64,2752]{1,0:T(8,128)(2,1)S(1)} collective-permute-done((bf16[64,2752]{1,0:T(8,128)(2,1)S(1)}, bf16[64,2752]{1,0:T(8,128)(2,1)S(1)}, u32[]{:S(2)}, u32[]{:S(2)}) %collective-permute-start.8) | collective-permute-done | bytes 352288 | tf_op jit(solution)/shard_map/ppermute | solution.py:18
  105.5 2.4 %collective-permute-start.27 = (bf16[64,1408]{1,0:T(8,128)(2,1)}, bf16[64,1408]{1,0:T(8,128)(2,1)S(1)}, u32[]{:S(2)}, u32[]{:S(2)}) collective-permute-start(bf16[64,1408]{1,0:T(8,128)(2,1)} %get-tuple-element.27.refs_0_), channel_id=1, source_target_pairs={{2,0},{3,1},{0,2},{1,3},{6,4},{7,5},{4,6},{5,7},{10,8},{11,9},{8,1... | collective-permute-start | bytes 540680 | tf_op jit(solution)/shard_map/ppermute | solution.py:18
  108.7 4.0 %shard_map.80 = (f32[2,64,2752]{2,1,0:T(8,128)}, f32[2,64,2752]{2,1,0:T(8,128)}, bf16[64,1408]{1,0:T(8,128)(2,1)}, bf16[64,1408]{1,0:T(8,128)(2,1)}) custom-call(bf16[4,64,2752]{2,1,0:T(8,128)(2,1)} %get-tuple-element.20.refs_0_, bf16[4,64,2752]{2,1,0:T(8,128)(2,1)} %copy-done.2, ...), custom_call_target="tpu_custom_call", output_to_operand_aliasing={{0}: (6, {}), {1}: (7, {})} | custom-call | flops 5283840 | bytes 4579328 | tf_op jit(solution)/shard_map/pallas_call | solution.py:145
  112.7 4.8 %collective-permute-done.26.refs_1_ = bf16[64,1408]{1,0:T(8,128)(2,1)S(1)} collective-permute-done((bf16[64,1408]{1,0:T(8,128)(2,1)}, bf16[64,1408]{1,0:T(8,128)(2,1)S(1)}, u32[]{:S(2)}, u32[]{:S(2)}) %collective-permute-start.26) | collective-permute-done | bytes 180256 | tf_op jit(solution)/shard_map/ppermute | solution.py:18
  118.3 3.6 %collective-permute-done.27.refs_2_ = bf16[64,1408]{1,0:T(8,128)(2,1)S(1)} collective-permute-done((bf16[64,1408]{1,0:T(8,128)(2,1)}, bf16[64,1408]{1,0:T(8,128)(2,1)S(1)}, u32[]{:S(2)}, u32[]{:S(2)}) %collective-permute-start.27) | collective-permute-done | bytes 180256 | tf_op jit(solution)/shard_map/ppermute | solution.py:18
  121.9 2.0 %collective-permute-done.28.refs_3_ = bf16[64,1408]{1,0:T(8,128)(2,1)S(1)} collective-permute-done((bf16[64,1408]{1,0:T(8,128)(2,1)}, bf16[64,1408]{1,0:T(8,128)(2,1)S(1)}, u32[]{:S(2)}, u32[]{:S(2)}) %collective-permute-start.28) | collective-permute-done | bytes 180256 | tf_op jit(solution)/shard_map/ppermute | solution.py:18
  124.4 1.7 collective-permute-start.15
  126.1 2.2 %shard_map.83.refs_0_ = bf16[256,1408]{1,0:T(8,128)(2,1)} custom-call(bf16[64,1408]{1,0:T(8,128)(2,1)} %get-tuple-element.27.refs_0_, bf16[64,1408]{1,0:T(8,128)(2,1)} %copy-done.22, bf16[64,1408]{1,0:T(8,128)(2,1)} %copy-done.23, bf16[64,1408]{1,0:T(8,128)(2,1)} %copy-done.25), custom_call_target="tpu_custom_call" | custom-call | bytes 1441792 | tf_op jit(solution)/shard_map/pallas_call | solution.py:165
  129.1 2.4 %collective-permute-start.29 = (bf16[256,1408]{1,0:T(8,128)(2,1)}, bf16[256,1408]{1,0:T(8,128)(2,1)S(1)}, u32[]{:S(2)}, u32[]{:S(2)}) collective-permute-start(bf16[256,1408]{1,0:T(8,128)(2,1)} %shard_map.83.refs_0_), channel_id=1, source_target_pairs={{4,0},{8,4},{12,8},{0,12},{5,1},{9,5},{13,9},{1,13},{6,2},{10,6},{... | collective-permute-start | bytes 2162696 | tf_op jit(solution)/shard_map/ppermute | solution.py:18
  132.2 2.1 %shard_map.82.refs_0_ = bf16[256,1408]{1,0:T(8,128)(2,1)} custom-call(bf16[64,1408]{1,0:T(8,128)(2,1)} %get-tuple-element.26.refs_0_, bf16[64,1408]{1,0:T(8,128)(2,1)} %copy-done.26, bf16[64,1408]{1,0:T(8,128)(2,1)} %copy-done.27, bf16[64,1408]{1,0:T(8,128)(2,1)} %copy-done.28), custom_call_target="tpu_custom_call" | custom-call | bytes 1441792 | tf_op jit(solution)/shard_map/pallas_call | solution.py:165
  135.6 4.7 %collective-permute-done.16.refs_3_ = bf16[64,1408]{1,0:T(8,128)(2,1)} collective-permute-done((bf16[64,1408]{1,0:T(8,128)(2,1)S(1)}, bf16[64,1408]{1,0:T(8,128)(2,1)}, u32[]{:S(2)}, u32[]{:S(2)}) %collective-permute-start.16) | collective-permute-done | bytes 180256 | tf_op jit(solution)/shard_map/ppermute | solution.py:18
  140.4 1.4 collective-permute-start.36
  141.7 2.1 %shard_map.81.refs_0_ = bf16[256,1408]{1,0:T(8,128)(2,1)} custom-call(bf16[64,1408]{1,0:T(8,128)(2,1)} %get-tuple-element.24.refs_0_, bf16[64,1408]{1,0:T(8,128)(2,1)} %copy-done.24, bf16[64,1408]{1,0:T(8,128)(2,1)} %collective-permute-done.15.refs_2_, bf16[64,1408]{1,0:T(8,128)(2,1)} %collective-permute-done.16.refs_3_), custom_call_target="tpu_custom_call" | custom-call | bytes 1441792 | tf_op jit(solution)/shard_map/pallas_call | solution.py:165
  144.7 3.3 %collective-permute-start.30 = (bf16[256,1408]{1,0:T(8,128)(2,1)S(1)}, bf16[256,1408]{1,0:T(8,128)(2,1)S(1)}, u32[]{:S(2)}, u32[]{:S(2)}) collective-permute-start(bf16[256,1408]{1,0:T(8,128)(2,1)S(1)} %collective-permute-done.29.refs_1_), channel_id=1, source_target_pairs={{4,0},{8,4},{12,8},{0,12},{5,1},{9,5},{13,9},{1,13},{6,2},{10,6},{... | collective-permute-start | bytes 2162696 | tf_op jit(solution)/shard_map/ppermute | solution.py:18
  148.0 6.6 %collective-permute-done.31.refs_3_ = bf16[256,1408]{1,0:T(8,128)(2,1)S(1)} collective-permute-done((bf16[256,1408]{1,0:T(8,128)(2,1)S(1)}, bf16[256,1408]{1,0:T(8,128)(2,1)S(1)}, u32[]{:S(2)}, u32[]{:S(2)}) %collective-permute-start.31) | collective-permute-done | bytes 720928 | tf_op jit(solution)/shard_map/ppermute | solution.py:18
  154.7 2.6 %collective-permute-start.23 = (bf16[256,1408]{1,0:T(8,128)(2,1)S(1)}, bf16[256,1408]{1,0:T(8,128)(2,1)S(1)}, u32[]{:S(2)}, u32[]{:S(2)}) collective-permute-start(bf16[256,1408]{1,0:T(8,128)(2,1)S(1)} %copy-done.5), channel_id=1, source_target_pairs={{1,0},{2,1},{3,2},{0,3},{5,4},{6,5},{7,6},{4,7},{9,8},{10,9},{11,1... | collective-permute-start | bytes 2162696 | tf_op jit(solution)/shard_map/ppermute | solution.py:18
  157.7 8.4 %collective-permute-done.18.refs_3_ = bf16[256,1408]{1,0:T(8,128)(2,1)S(1)} collective-permute-done((bf16[256,1408]{1,0:T(8,128)(2,1)}, bf16[256,1408]{1,0:T(8,128)(2,1)S(1)}, u32[]{:S(2)}, u32[]{:S(2)}) %collective-permute-start.18) | collective-permute-done | bytes 720928 | tf_op jit(solution)/shard_map/ppermute | solution.py:18
  166.1 5.3 %shard_map.85.refs_4_ = bf16[2,2752,512]{2,1,0:T(8,128)(2,1)} custom-call(bf16[2,512,1024]{2,1,0:T(8,128)(2,1)} %get-tuple-element.25.columns_ref, bf16[256,1408]{1,0:T(8,128)(2,1)} %shard_map.84.refs_0_, bf16[256,1408]{1,0:T(8,128)(2,1)} %copy-done.15, bf16[256,1408]{1,0:T(8,128)(2,1)} %collective-permute-done.36.refs_2_, bf16[256,1408]{1,0:T(8,128)(2,1)} %copy-done.16), custom_call_target="tpu_custom_call" | custom-call | flops 1476395008 | bytes 5373952 | tf_op jit(solution)/shard_map/pallas_call | solution.py:200
  172.4 5.1 %shard_map.86.refs_4_ = bf16[2,2752,512]{2,1,0:T(8,128)(2,1)} custom-call(bf16[2,512,1024]{2,1,0:T(8,128)(2,1)} %get-tuple-element.17._.columns_ref, bf16[256,1408]{1,0:T(8,128)(2,1)} %shard_map.83.refs_0_, bf16[256,1408]{1,0:T(8,128)(2,1)} %copy-done.8, bf16[256,1408]{1,0:T(8,128)(2,1)} %copy-done.14, ...), custom_call_target="tpu_custom_call", output_to_operand_aliasing={{}: (5, {})} | custom-call | flops 1476395008 | bytes 5373952 | tf_op jit(solution)/shard_map/pallas_call | solution.py:200
  178.3 5.1 %shard_map.87.refs_4_ = bf16[2,2752,512]{2,1,0:T(8,128)(2,1)} custom-call(bf16[2,512,1024]{2,1,0:T(8,128)(2,1)} %get-tuple-element.25.columns_ref, bf16[256,1408]{1,0:T(8,128)(2,1)} %shard_map.82.refs_0_, bf16[256,1408]{1,0:T(8,128)(2,1)} %copy-done.12, bf16[256,1408]{1,0:T(8,128)(2,1)} %collective-permute-done.25.refs_2_, ...), custom_call_target="tpu_custom_call", output_to_operand_aliasing={{}: (5, {})} | custom-call | flops 1476395008 | bytes 5373952 | tf_op jit(solution)/shard_map/pallas_call | solution.py:200
  184.3 5.1 %shard_map.88 = bf16[2,2752,512]{2,1,0:T(8,128)(2,1)} custom-call(bf16[2,512,1024]{2,1,0:T(8,128)(2,1)} %get-tuple-element.17._.columns_ref, bf16[256,1408]{1,0:T(8,128)(2,1)} %shard_map.81.refs_0_, bf16[256,1408]{1,0:T(8,128)(2,1)} %copy-done.13, bf16[256,1408]{1,0:T(8,128)(2,1)} %collective-permute-done.19.refs_2_, ...), custom_call_target="tpu_custom_call", output_to_operand_aliasing={{}: (5, {})} | custom-call | flops 1476395008 | bytes 5373952 | tf_op jit(solution)/shard_map/pallas_call | solution.py:200
  (119 shorter events, 16.6 us)
Async XLA Ops:
  5.2 16.3 %copy-start.32 = (bf16[2,128,256]{2,1,0:T(8,128)(2,1)}, bf16[2,128,256]{2,1,0:T(8,128)(2,1)S(1)}, u32[]{:S(2)}) copy-start(bf16[2,128,256]{2,1,0:T(8,128)(2,1)S(1)} %get-tuple-element.37._) | copy-start | bytes 393220
  5.2 7.7 %collective-permute-start.2 = (bf16[2,128,256]{2,1,0:T(8,128)(2,1)S(1)}, bf16[2,128,256]{2,1,0:T(8,128)(2,1)S(1)}, u32[]{:S(2)}, u32[]{:S(2)}) collective-permute-start(bf16[2,128,256]{2,1,0:T(8,128)(2,1)S(1)} %get-tuple-element.37._), channel_id=1, source_target_pairs={{8,0},{12,4},{0,8},{4,12},{9,1},{13,5},{1,9},{5,13},{10,2},{14,6},... | collective-permute-start | bytes 393224 | tf_op jit(solution)/shard_map/ppermute | solution.py:18
  8.5 6.7 %collective-permute-start = (bf16[2,128,256]{2,1,0:T(8,128)(2,1)S(1)}, bf16[2,128,256]{2,1,0:T(8,128)(2,1)S(1)}, u32[]{:S(2)}, u32[]{:S(2)}) collective-permute-start(bf16[2,128,256]{2,1,0:T(8,128)(2,1)S(1)} %get-tuple-element.35), channel_id=1, source_target_pairs={{12,0},{0,4},{4,8},{8,12},{13,1},{1,5},{5,9},{9,13},{14,2},{2,6},{... | collective-permute-start | bytes 393224 | tf_op jit(solution)/shard_map/ppermute | solution.py:18
  9.2 6.0 %collective-permute-start.1 = (bf16[2,128,256]{2,1,0:T(8,128)(2,1)S(1)}, bf16[2,128,256]{2,1,0:T(8,128)(2,1)S(1)}, u32[]{:S(2)}, u32[]{:S(2)}) collective-permute-start(bf16[2,128,256]{2,1,0:T(8,128)(2,1)S(1)} %get-tuple-element.36), channel_id=1, source_target_pairs={{4,0},{8,4},{12,8},{0,12},{5,1},{9,5},{13,9},{1,13},{6,2},{10,6},{... | collective-permute-start | bytes 393224 | tf_op jit(solution)/shard_map/ppermute | solution.py:18
  15.4 14.1 %collective-permute-start.3 = (bf16[2,128,64]{2,1,0:T(8,128)(2,1)S(1)}, bf16[2,128,64]{2,1,0:T(8,128)(2,1)S(1)}, u32[]{:S(2)}, u32[]{:S(2)}) collective-permute-start(bf16[2,128,64]{2,1,0:T(8,128)(2,1)S(1)} %get-tuple-element.38), channel_id=1, source_target_pairs={{3,0},{0,1},{1,2},{2,3},{7,4},{4,5},{5,6},{6,7},{11,8},{8,9},{9,10... | collective-permute-start | bytes 98312 | tf_op jit(solution)/shard_map/ppermute | solution.py:18
  17.4 12.1 %collective-permute-start.4 = (bf16[2,128,64]{2,1,0:T(8,128)(2,1)S(1)}, bf16[2,128,64]{2,1,0:T(8,128)(2,1)S(1)}, u32[]{:S(2)}, u32[]{:S(2)}) collective-permute-start(bf16[2,128,64]{2,1,0:T(8,128)(2,1)S(1)} %get-tuple-element.40), channel_id=1, source_target_pairs={{1,0},{2,1},{3,2},{0,3},{5,4},{6,5},{7,6},{4,7},{9,8},{10,9},{11,1... | collective-permute-start | bytes 98312 | tf_op jit(solution)/shard_map/ppermute | solution.py:18
  19.6 9.9 %collective-permute-start.5 = (bf16[2,128,64]{2,1,0:T(8,128)(2,1)S(1)}, bf16[2,128,64]{2,1,0:T(8,128)(2,1)S(1)}, u32[]{:S(2)}, u32[]{:S(2)}) collective-permute-start(bf16[2,128,64]{2,1,0:T(8,128)(2,1)S(1)} %get-tuple-element.39), channel_id=1, source_target_pairs={{2,0},{3,1},{0,2},{1,3},{6,4},{7,5},{4,6},{5,7},{10,8},{11,9},{8,1... | collective-permute-start | bytes 98312 | tf_op jit(solution)/shard_map/ppermute | solution.py:18
  36.7 3.4 %collective-permute-start.6 = (bf16[4,64,2752]{2,1,0:T(8,128)(2,1)}, bf16[4,64,2752]{2,1,0:T(8,128)(2,1)S(1)}, u32[]{:S(2)}, u32[]{:S(2)}) collective-permute-start(bf16[4,64,2752]{2,1,0:T(8,128)(2,1)} %get-tuple-element.19), channel_id=1, source_target_pairs={{0,16},{16,0},{1,17},{17,1},{2,18},{18,2},{3,19},{19,3},{4,20},{20... | collective-permute-start | bytes 4227080 | tf_op jit(solution)/shard_map/ppermute | solution.py:26
  40.1 21.1 %copy-start.3 = (bf16[4,64,2752]{2,1,0:T(8,128)(2,1)}, bf16[4,64,2752]{2,1,0:T(8,128)(2,1)S(1)}, u32[]{:S(2)}) copy-start(bf16[4,64,2752]{2,1,0:T(8,128)(2,1)S(1)} %collective-permute-done.6.refs_1_) | copy-start | bytes 4227076
  49.2 13.5 %copy-start.1 = (bf16[4,64,2752]{2,1,0:T(8,128)(2,1)S(1)}, bf16[4,64,2752]{2,1,0:T(8,128)(2,1)}, u32[]{:S(2)}) copy-start(bf16[4,64,2752]{2,1,0:T(8,128)(2,1)} %get-tuple-element.20.refs_0_) | copy-start | bytes 4227076
  49.2 13.5 %collective-permute-start.7 = (bf16[4,64,2752]{2,1,0:T(8,128)(2,1)}, bf16[4,64,2752]{2,1,0:T(8,128)(2,1)S(1)}, u32[]{:S(2)}, u32[]{:S(2)}) collective-permute-start(bf16[4,64,2752]{2,1,0:T(8,128)(2,1)} %get-tuple-element.21), channel_id=1, source_target_pairs={{0,16},{16,0},{1,17},{17,1},{2,18},{18,2},{3,19},{19,3},{4,20},{20... | collective-permute-start | bytes 4227080 | tf_op jit(solution)/shard_map/ppermute | solution.py:26
  49.4 11.9 %collective-permute-start.12 = (bf16[64,2752]{1,0:T(8,128)(2,1)S(1)}, bf16[64,2752]{1,0:T(8,128)(2,1)S(1)}, u32[]{:S(2)}, u32[]{:S(2)}) collective-permute-start(bf16[64,2752]{1,0:T(8,128)(2,1)S(1)} %copy-done.7), channel_id=1, source_target_pairs={{96,0},{0,32},{32,64},{64,96},{97,1},{1,33},{33,65},{65,97},{98,2}... | collective-permute-start | bytes 1056776 | tf_op jit(solution)/shard_map/ppermute | solution.py:18
  50.9 15.1 %collective-permute-start.11 = (bf16[64,2752]{1,0:T(8,128)(2,1)S(1)}, bf16[64,2752]{1,0:T(8,128)(2,1)S(1)}, u32[]{:S(2)}, u32[]{:S(2)}) collective-permute-start(bf16[64,2752]{1,0:T(8,128)(2,1)S(1)} %get-tuple-element.31), channel_id=1, source_target_pairs={{32,0},{64,32},{96,64},{0,96},{33,1},{65,33},{97,65},{1,97},{34,2}... | collective-permute-start | bytes 1056776 | tf_op jit(solution)/shard_map/ppermute | solution.py:18
  62.4 11.1 %collective-permute-start.13 = (bf16[64,2752]{1,0:T(8,128)(2,1)S(1)}, bf16[64,2752]{1,0:T(8,128)(2,1)S(1)}, u32[]{:S(2)}, u32[]{:S(2)}) collective-permute-start(bf16[64,2752]{1,0:T(8,128)(2,1)S(1)} %fusion.8), channel_id=1, source_target_pairs={{96,0},{0,32},{32,64},{64,96},{97,1},{1,33},{33,65},{65,97},{98,2}... | collective-permute-start | bytes 1056776 | tf_op jit(solution)/shard_map/ppermute | solution.py:18
  62.8 32.4 %copy-start.2 = (bf16[4,64,2752]{2,1,0:T(8,128)(2,1)}, bf16[4,64,2752]{2,1,0:T(8,128)(2,1)S(1)}, u32[]{:S(2)}) copy-start(bf16[4,64,2752]{2,1,0:T(8,128)(2,1)S(1)} %collective-permute-done.7.refs_1_) | copy-start | bytes 4227076
  62.9 32.3 %collective-permute-start.9 = (bf16[64,2752]{1,0:T(8,128)(2,1)S(1)}, bf16[64,2752]{1,0:T(8,128)(2,1)S(1)}, u32[]{:S(2)}, u32[]{:S(2)}) collective-permute-start(bf16[64,2752]{1,0:T(8,128)(2,1)S(1)} %get-tuple-element.33), channel_id=1, source_target_pairs={{32,0},{64,32},{96,64},{0,96},{33,1},{65,33},{97,65},{1,97},{34,2}... | collective-permute-start | bytes 1056776 | tf_op jit(solution)/shard_map/ppermute | solution.py:18
  78.3 10.0 %collective-permute-start.32 = (bf16[64,1408]{1,0:T(8,128)(2,1)}, bf16[64,1408]{1,0:T(8,128)(2,1)S(1)}, u32[]{:S(2)}, u32[]{:S(2)}) collective-permute-start(bf16[64,1408]{1,0:T(8,128)(2,1)} %get-tuple-element.28.refs_0_), channel_id=1, source_target_pairs={{4,0},{8,4},{12,8},{0,12},{5,1},{9,5},{13,9},{1,13},{6,2},{10,6},{... | collective-permute-start | bytes 540680 | tf_op jit(solution)/shard_map/ppermute | solution.py:18
  81.4 8.6 %collective-permute-start.33 = (bf16[64,1408]{1,0:T(8,128)(2,1)}, bf16[64,1408]{1,0:T(8,128)(2,1)S(1)}, u32[]{:S(2)}, u32[]{:S(2)}) collective-permute-start(bf16[64,1408]{1,0:T(8,128)(2,1)} %get-tuple-element.28.refs_0_), channel_id=1, source_target_pairs={{8,0},{12,4},{0,8},{4,12},{9,1},{13,5},{1,9},{5,13},{10,2},{14,6},... | collective-permute-start | bytes 540680 | tf_op jit(solution)/shard_map/ppermute | solution.py:18
  81.8 9.8 %collective-permute-start.34 = (bf16[64,1408]{1,0:T(8,128)(2,1)}, bf16[64,1408]{1,0:T(8,128)(2,1)S(1)}, u32[]{:S(2)}, u32[]{:S(2)}) collective-permute-start(bf16[64,1408]{1,0:T(8,128)(2,1)} %get-tuple-element.28.refs_0_), channel_id=1, source_target_pairs={{12,0},{0,4},{4,8},{8,12},{13,1},{1,5},{5,9},{9,13},{14,2},{2,6},{... | collective-permute-start | bytes 540680 | tf_op jit(solution)/shard_map/ppermute | solution.py:18
  94.4 29.4 %collective-permute-start.35 = (bf16[256,1408]{1,0:T(8,128)(2,1)}, bf16[256,1408]{1,0:T(8,128)(2,1)S(1)}, u32[]{:S(2)}, u32[]{:S(2)}) collective-permute-start(bf16[256,1408]{1,0:T(8,128)(2,1)} %shard_map.84.refs_0_), channel_id=1, source_target_pairs={{1,0},{2,1},{3,2},{0,3},{5,4},{6,5},{7,6},{4,7},{9,8},{10,9},{11,1... | collective-permute-start | bytes 2162696 | tf_op jit(solution)/shard_map/ppermute | solution.py:18
  95.2 10.3 %collective-permute-start.8 = (bf16[64,2752]{1,0:T(8,128)(2,1)S(1)}, bf16[64,2752]{1,0:T(8,128)(2,1)S(1)}, u32[]{:S(2)}, u32[]{:S(2)}) collective-permute-start(bf16[64,2752]{1,0:T(8,128)(2,1)S(1)} %get-tuple-element.34), channel_id=1, source_target_pairs={{96,0},{0,32},{32,64},{64,96},{97,1},{1,33},{33,65},{65,97},{98,2}... | collective-permute-start | bytes 1056776 | tf_op jit(solution)/shard_map/ppermute | solution.py:18
  95.3 12.6 %collective-permute-start.10 = (bf16[64,2752]{1,0:T(8,128)(2,1)S(1)}, bf16[64,2752]{1,0:T(8,128)(2,1)S(1)}, u32[]{:S(2)}, u32[]{:S(2)}) collective-permute-start(bf16[64,2752]{1,0:T(8,128)(2,1)S(1)} %fusion.9), channel_id=1, source_target_pairs={{32,0},{64,32},{96,64},{0,96},{33,1},{65,33},{97,65},{1,97},{34,2}... | collective-permute-start | bytes 1056776 | tf_op jit(solution)/shard_map/ppermute | solution.py:18
  98.6 45.2 %collective-permute-start.37 = (bf16[256,1408]{1,0:T(8,128)(2,1)S(1)}, bf16[256,1408]{1,0:T(8,128)(2,1)S(1)}, u32[]{:S(2)}, u32[]{:S(2)}) collective-permute-start(bf16[256,1408]{1,0:T(8,128)(2,1)S(1)} %copy-done.6), channel_id=1, source_target_pairs={{3,0},{0,1},{1,2},{2,3},{7,4},{4,5},{5,6},{6,7},{11,8},{8,9},{9,10... | collective-permute-start | bytes 2162696 | tf_op jit(solution)/shard_map/ppermute | solution.py:18
  99.9 17.7 %collective-permute-start.26 = (bf16[64,1408]{1,0:T(8,128)(2,1)}, bf16[64,1408]{1,0:T(8,128)(2,1)S(1)}, u32[]{:S(2)}, u32[]{:S(2)}) collective-permute-start(bf16[64,1408]{1,0:T(8,128)(2,1)} %get-tuple-element.27.refs_0_), channel_id=1, source_target_pairs={{1,0},{2,1},{3,2},{0,3},{5,4},{6,5},{7,6},{4,7},{9,8},{10,9},{11,1... | collective-permute-start | bytes 540680 | tf_op jit(solution)/shard_map/ppermute | solution.py:18
  105.5 16.4 %collective-permute-start.27 = (bf16[64,1408]{1,0:T(8,128)(2,1)}, bf16[64,1408]{1,0:T(8,128)(2,1)S(1)}, u32[]{:S(2)}, u32[]{:S(2)}) collective-permute-start(bf16[64,1408]{1,0:T(8,128)(2,1)} %get-tuple-element.27.refs_0_), channel_id=1, source_target_pairs={{2,0},{3,1},{0,2},{1,3},{6,4},{7,5},{4,6},{5,7},{10,8},{11,9},{8,1... | collective-permute-start | bytes 540680 | tf_op jit(solution)/shard_map/ppermute | solution.py:18
  107.9 15.9 %collective-permute-start.28 = (bf16[64,1408]{1,0:T(8,128)(2,1)}, bf16[64,1408]{1,0:T(8,128)(2,1)S(1)}, u32[]{:S(2)}, u32[]{:S(2)}) collective-permute-start(bf16[64,1408]{1,0:T(8,128)(2,1)} %get-tuple-element.27.refs_0_), channel_id=1, source_target_pairs={{3,0},{0,1},{1,2},{2,3},{7,4},{4,5},{5,6},{6,7},{11,8},{8,9},{9,10... | collective-permute-start | bytes 540680 | tf_op jit(solution)/shard_map/ppermute | solution.py:18
  112.7 18.8 %copy-start.21 = (bf16[64,1408]{1,0:T(8,128)(2,1)S(1)}, bf16[64,1408]{1,0:T(8,128)(2,1)}, u32[]{:S(2)}) copy-start(bf16[64,1408]{1,0:T(8,128)(2,1)} %get-tuple-element.24.refs_0_) | copy-start | bytes 540676
  117.6 6.8 %collective-permute-start.20 = (bf16[64,1408]{1,0:T(8,128)(2,1)}, bf16[64,1408]{1,0:T(8,128)(2,1)S(1)}, u32[]{:S(2)}, u32[]{:S(2)}) collective-permute-start(bf16[64,1408]{1,0:T(8,128)(2,1)} %get-tuple-element.26.refs_0_), channel_id=1, source_target_pairs={{4,0},{8,4},{12,8},{0,12},{5,1},{9,5},{13,9},{1,13},{6,2},{10,6},{... | collective-permute-start | bytes 540680 | tf_op jit(solution)/shard_map/ppermute | solution.py:18
  121.9 7.2 %collective-permute-start.21 = (bf16[64,1408]{1,0:T(8,128)(2,1)}, bf16[64,1408]{1,0:T(8,128)(2,1)S(1)}, u32[]{:S(2)}, u32[]{:S(2)}) collective-permute-start(bf16[64,1408]{1,0:T(8,128)(2,1)} %get-tuple-element.26.refs_0_), channel_id=1, source_target_pairs={{8,0},{12,4},{0,8},{4,12},{9,1},{13,5},{1,9},{5,13},{10,2},{14,6},... | collective-permute-start | bytes 540680 | tf_op jit(solution)/shard_map/ppermute | solution.py:18
  123.9 7.6 %collective-permute-start.22 = (bf16[64,1408]{1,0:T(8,128)(2,1)}, bf16[64,1408]{1,0:T(8,128)(2,1)S(1)}, u32[]{:S(2)}, u32[]{:S(2)}) collective-permute-start(bf16[64,1408]{1,0:T(8,128)(2,1)} %get-tuple-element.26.refs_0_), channel_id=1, source_target_pairs={{12,0},{0,4},{4,8},{8,12},{13,1},{1,5},{5,9},{9,13},{14,2},{2,6},{... | collective-permute-start | bytes 540680 | tf_op jit(solution)/shard_map/ppermute | solution.py:18
  123.9 16.5 %copy-start.15 = (bf16[256,1408]{1,0:T(8,128)(2,1)}, bf16[256,1408]{1,0:T(8,128)(2,1)S(1)}, u32[]{:S(2)}) copy-start(bf16[256,1408]{1,0:T(8,128)(2,1)S(1)} %collective-permute-done.35.refs_1_) | copy-start | bytes 2162692
  123.9 10.4 %collective-permute-start.14 = (bf16[64,1408]{1,0:T(8,128)(2,1)}, bf16[64,1408]{1,0:T(8,128)(2,1)S(1)}, u32[]{:S(2)}, u32[]{:S(2)}) collective-permute-start(bf16[64,1408]{1,0:T(8,128)(2,1)} %get-tuple-element.24.refs_0_), channel_id=1, source_target_pairs={{1,0},{2,1},{3,2},{0,3},{5,4},{6,5},{7,6},{4,7},{9,8},{10,9},{11,1... | collective-permute-start | bytes 540680 | tf_op jit(solution)/shard_map/ppermute | solution.py:18
  124.4 10.0 %collective-permute-start.15 = (bf16[64,1408]{1,0:T(8,128)(2,1)}, bf16[64,1408]{1,0:T(8,128)(2,1)}, u32[]{:S(2)}, u32[]{:S(2)}) collective-permute-start(bf16[64,1408]{1,0:T(8,128)(2,1)} %get-tuple-element.24.refs_0_), channel_id=1, source_target_pairs={{2,0},{3,1},{0,2},{1,3},{6,4},{7,5},{4,6},{5,7},{10,8},{11,9},{8,1... | collective-permute-start | bytes 540680 | tf_op jit(solution)/shard_map/ppermute | solution.py:18
  129.1 15.6 %collective-permute-start.29 = (bf16[256,1408]{1,0:T(8,128)(2,1)}, bf16[256,1408]{1,0:T(8,128)(2,1)S(1)}, u32[]{:S(2)}, u32[]{:S(2)}) collective-permute-start(bf16[256,1408]{1,0:T(8,128)(2,1)} %shard_map.83.refs_0_), channel_id=1, source_target_pairs={{4,0},{8,4},{12,8},{0,12},{5,1},{9,5},{13,9},{1,13},{6,2},{10,6},{... | collective-permute-start | bytes 2162696 | tf_op jit(solution)/shard_map/ppermute | solution.py:18
  131.5 8.9 %collective-permute-start.16 = (bf16[64,1408]{1,0:T(8,128)(2,1)S(1)}, bf16[64,1408]{1,0:T(8,128)(2,1)}, u32[]{:S(2)}, u32[]{:S(2)}) collective-permute-start(bf16[64,1408]{1,0:T(8,128)(2,1)S(1)} %copy-done.21), channel_id=1, source_target_pairs={{3,0},{0,1},{1,2},{2,3},{7,4},{4,5},{5,6},{6,7},{11,8},{8,9},{9,10... | collective-permute-start | bytes 540680 | tf_op jit(solution)/shard_map/ppermute | solution.py:18
  134.3 20.4 %copy-start.5 = (bf16[256,1408]{1,0:T(8,128)(2,1)S(1)}, bf16[256,1408]{1,0:T(8,128)(2,1)}, u32[]{:S(2)}) copy-start(bf16[256,1408]{1,0:T(8,128)(2,1)} %shard_map.82.refs_0_) | copy-start | bytes 2162692
  134.3 20.4 %collective-permute-start.31 = (bf16[256,1408]{1,0:T(8,128)(2,1)S(1)}, bf16[256,1408]{1,0:T(8,128)(2,1)S(1)}, u32[]{:S(2)}, u32[]{:S(2)}) collective-permute-start(bf16[256,1408]{1,0:T(8,128)(2,1)S(1)} %copy-done.4), channel_id=1, source_target_pairs={{12,0},{0,4},{4,8},{8,12},{13,1},{1,5},{5,9},{9,13},{14,2},{2,6},{... | collective-permute-start | bytes 2162696 | tf_op jit(solution)/shard_map/ppermute | solution.py:18
  134.4 22.9 %collective-permute-start.24 = (bf16[256,1408]{1,0:T(8,128)(2,1)}, bf16[256,1408]{1,0:T(8,128)(2,1)S(1)}, u32[]{:S(2)}, u32[]{:S(2)}) collective-permute-start(bf16[256,1408]{1,0:T(8,128)(2,1)} %shard_map.82.refs_0_), channel_id=1, source_target_pairs={{3,0},{0,1},{1,2},{2,3},{7,4},{4,5},{5,6},{6,7},{11,8},{8,9},{9,10... | collective-permute-start | bytes 2162696 | tf_op jit(solution)/shard_map/ppermute | solution.py:18
  140.4 16.9 %collective-permute-start.36 = (bf16[256,1408]{1,0:T(8,128)(2,1)S(1)}, bf16[256,1408]{1,0:T(8,128)(2,1)}, u32[]{:S(2)}, u32[]{:S(2)}) collective-permute-start(bf16[256,1408]{1,0:T(8,128)(2,1)S(1)} %collective-permute-done.35.refs_1_), channel_id=1, source_target_pairs={{1,0},{2,1},{3,2},{0,3},{5,4},{6,5},{7,6},{4,7},{9,8},{10,9},{11,1... | collective-permute-start | bytes 2162696 | tf_op jit(solution)/shard_map/ppermute | solution.py:18
  143.8 22.3 %collective-permute-start.18 = (bf16[256,1408]{1,0:T(8,128)(2,1)}, bf16[256,1408]{1,0:T(8,128)(2,1)S(1)}, u32[]{:S(2)}, u32[]{:S(2)}) collective-permute-start(bf16[256,1408]{1,0:T(8,128)(2,1)} %shard_map.81.refs_0_), channel_id=1, source_target_pairs={{12,0},{0,4},{4,8},{8,12},{13,1},{1,5},{5,9},{9,13},{14,2},{2,6},{... | collective-permute-start | bytes 2162696 | tf_op jit(solution)/shard_map/ppermute | solution.py:18
  144.7 26.8 %copy-start.8 = (bf16[256,1408]{1,0:T(8,128)(2,1)}, bf16[256,1408]{1,0:T(8,128)(2,1)S(1)}, u32[]{:S(2)}) copy-start(bf16[256,1408]{1,0:T(8,128)(2,1)S(1)} %collective-permute-done.29.refs_1_) | copy-start | bytes 2162692
  144.7 26.8 %collective-permute-start.30 = (bf16[256,1408]{1,0:T(8,128)(2,1)S(1)}, bf16[256,1408]{1,0:T(8,128)(2,1)S(1)}, u32[]{:S(2)}, u32[]{:S(2)}) collective-permute-start(bf16[256,1408]{1,0:T(8,128)(2,1)S(1)} %collective-permute-done.29.refs_1_), channel_id=1, source_target_pairs={{4,0},{8,4},{12,8},{0,12},{5,1},{9,5},{13,9},{1,13},{6,2},{10,6},{... | collective-permute-start | bytes 2162696 | tf_op jit(solution)/shard_map/ppermute | solution.py:18
  154.7 16.8 %copy-start.10 = (bf16[256,1408]{1,0:T(8,128)(2,1)}, bf16[256,1408]{1,0:T(8,128)(2,1)S(1)}, u32[]{:S(2)}) copy-start(bf16[256,1408]{1,0:T(8,128)(2,1)S(1)} %collective-permute-done.31.refs_3_) | copy-start | bytes 2162692
  154.7 22.8 %collective-permute-start.23 = (bf16[256,1408]{1,0:T(8,128)(2,1)S(1)}, bf16[256,1408]{1,0:T(8,128)(2,1)S(1)}, u32[]{:S(2)}, u32[]{:S(2)}) collective-permute-start(bf16[256,1408]{1,0:T(8,128)(2,1)S(1)} %copy-done.5), channel_id=1, source_target_pairs={{1,0},{2,1},{3,2},{0,3},{5,4},{6,5},{7,6},{4,7},{9,8},{10,9},{11,1... | collective-permute-start | bytes 2162696 | tf_op jit(solution)/shard_map/ppermute | solution.py:18
  157.3 14.2 %copy-start.9 = (bf16[256,1408]{1,0:T(8,128)(2,1)}, bf16[256,1408]{1,0:T(8,128)(2,1)S(1)}, u32[]{:S(2)}) copy-start(bf16[256,1408]{1,0:T(8,128)(2,1)S(1)} %collective-permute-done.24.refs_3_) | copy-start | bytes 2162692
  157.3 20.1 %collective-permute-start.25 = (bf16[256,1408]{1,0:T(8,128)(2,1)S(1)}, bf16[256,1408]{1,0:T(8,128)(2,1)}, u32[]{:S(2)}, u32[]{:S(2)}) collective-permute-start(bf16[256,1408]{1,0:T(8,128)(2,1)S(1)} %collective-permute-done.24.refs_3_), channel_id=1, source_target_pairs={{3,0},{0,1},{1,2},{2,3},{7,4},{4,5},{5,6},{6,7},{11,8},{8,9},{9,10... | collective-permute-start | bytes 2162696 | tf_op jit(solution)/shard_map/ppermute | solution.py:18
  157.3 26.1 %collective-permute-start.17 = (bf16[256,1408]{1,0:T(8,128)(2,1)}, bf16[256,1408]{1,0:T(8,128)(2,1)S(1)}, u32[]{:S(2)}, u32[]{:S(2)}) collective-permute-start(bf16[256,1408]{1,0:T(8,128)(2,1)} %shard_map.81.refs_0_), channel_id=1, source_target_pairs={{4,0},{8,4},{12,8},{0,12},{5,1},{9,5},{13,9},{1,13},{6,2},{10,6},{... | collective-permute-start | bytes 2162696 | tf_op jit(solution)/shard_map/ppermute | solution.py:18
  166.1 17.3 %collective-permute-start.19 = (bf16[256,1408]{1,0:T(8,128)(2,1)S(1)}, bf16[256,1408]{1,0:T(8,128)(2,1)}, u32[]{:S(2)}, u32[]{:S(2)}) collective-permute-start(bf16[256,1408]{1,0:T(8,128)(2,1)S(1)} %collective-permute-done.18.refs_3_), channel_id=1, source_target_pairs={{12,0},{0,4},{4,8},{8,12},{13,1},{1,5},{5,9},{9,13},{14,2},{2,6},{... | collective-permute-start | bytes 2162696 | tf_op jit(solution)/shard_map/ppermute | solution.py:18
  (23 other events, 78.3 us)

commit v3 on v2

v3 whole, which is shorter than its diff:
```python
import functools

import jax
import jax.numpy as jnp
from jax import lax
from jax.experimental import pallas as pl
from jax.experimental.pallas import tpu as pltpu
from jax.sharding import Mesh, PartitionSpec as P

BF16 = jnp.bfloat16
F32 = jnp.float32
SIDE = 4
LANES = 128
VMEM = 56 * 1024 * 1024
PARAMS = pltpu.CompilerParams(vmem_limit_bytes=VMEM)
ANYWHERE = pl.BlockSpec(memory_space=pl.ANY)


def receive(value, axis, distance):
    return lax.ppermute(value, axis, [((i + distance) % SIDE, i) for i in range(SIDE)])


def send(value, axis, distance):
    return receive(value, axis, -distance)


def swap_cores(value):
    return lax.ppermute(value, "c", [(0, 1), (1, 0)])


def held(shape, dtype=BF16):
    return pltpu.HBM(shape, dtype)


def cost(flops, moved):
    return pl.CostEstimate(flops=flops, bytes_accessed=moved, transcendentals=0)


def arrange_kernel(where_ref, bases_ref, _, by_y_ref, by_z_ref):
    y, z = where_ref[2], where_ref[3]
    ranks = bases_ref.shape[2]
    part = ranks // (SIDE * SIDE)
    block = ranks // SIDE
    for out_ref, y_outer in ((by_y_ref, True), (by_z_ref, False)):
        for low in range(0, ranks, block):
            source = lax.broadcasted_iota(jnp.int32, (ranks, block), 0)
            column = lax.broadcasted_iota(jnp.int32, (ranks, block), 1) + low
            outer, inner = column // (SIDE * part), (column // part) & (SIDE - 1)
            dy, dz = (outer, inner) if y_outer else (inner, outer)
            wanted = (((y + dy) & (SIDE - 1)) * SIDE + ((z + dz) & (SIDE - 1))) * part
            wanted = wanted + (column & (part - 1))
            place = jnp.where(source == wanted, 1.0, 0.0).astype(BF16)
            out_ref[:, low : low + block] = jnp.dot(
                bases_ref[0], place, preferred_element_type=F32
            ).astype(BF16)


def arrange(where, bases, which, after):
    _, rows, ranks = bases.shape
    return pl.pallas_call(
        arrange_kernel,
        grid_spec=pltpu.PrefetchScalarGridSpec(
            num_scalar_prefetch=1,
            grid=(1,),
            in_specs=[pl.BlockSpec((1, rows, ranks), lambda i, w: (which, 0, 0)), ANYWHERE],
            out_specs=[pl.BlockSpec((rows, ranks), lambda i, w: (0, 0))] * 2,
        ),
        out_shape=[held((rows, ranks))] * 2,
        compiler_params=PARAMS,
        cost_estimate=cost(4 * rows * ranks * ranks, 6 * rows * ranks),
    )(where, bases, after)


def partial_kernel(where_ref, proj_ref, grads_ref, _, mine_ref, other_ref):
    half = mine_ref.shape[2]
    both = lax.dot_general(
        proj_ref[...], grads_ref[0], (((0,), (0,)), ((), ())), preferred_element_type=F32
    ).astype(BF16)
    low, high = both[:, :half], both[:, half:]

    @pl.when(where_ref[1] == 0)
    def _():
        mine_ref[0] = low
        other_ref[0] = high

    @pl.when(where_ref[1] == 1)
    def _():
        mine_ref[0] = high
        other_ref[0] = low


def partial_grads(where, proj, grads, which, after):
    tokens, rank_part = proj.shape
    pair = grads.shape[2] // SIDE
    out = held((SIDE, rank_part, pair // 2))
    return pl.pallas_call(
        partial_kernel,
        grid_spec=pltpu.PrefetchScalarGridSpec(
            num_scalar_prefetch=1,
            grid=(SIDE,),
            in_specs=[
                pl.BlockSpec((tokens, rank_part), lambda i, w: (0, 0)),
                pl.BlockSpec((1, tokens, pair), lambda i, w: (which, 0, (w[0] + i) % SIDE)),
                ANYWHERE,
            ],
            out_specs=[pl.BlockSpec((1, rank_part, pair // 2), lambda i, w: (i, 0, 0))] * 2,
        ),
        out_shape=[out, out],
        compiler_params=PARAMS,
        cost_estimate=cost(
            2 * tokens * rank_part * pair * SIDE, 2 * tokens * pair * SIDE + 2 * rank_part * pair * SIDE
        ),
    )(where, proj, grads, after)


def sums_kernel(mine_ref, other_ref, near_ref, far_ref, via_ref, *, order):
    for i, ref in zip(order, (near_ref, far_ref, via_ref)):
        total = mine_ref[i].astype(F32) + other_ref[i].astype(F32)
        ref[...] = total.astype(ref.dtype)


def sums(mine, other, order):
    _, rows, width = mine.shape
    return pl.pallas_call(
        functools.partial(sums_kernel, order=order),
        out_shape=[held((rows, width)), held((rows, width)), held((rows, width), F32)],
        compiler_params=PARAMS,
        cost_estimate=cost(3 * rows * width, 20 * rows * width),
    )(mine, other)


def relay_kernel(one_ref, two_ref, _, out_ref):
    out_ref[...] = (one_ref[...].astype(F32) + two_ref[...]).astype(BF16)


def relay(one, two, after):
    rows, width = one.shape
    whole = pl.BlockSpec((rows, width), lambda: (0, 0))
    return pl.pallas_call(
        relay_kernel,
        in_specs=[whole, whole, ANYWHERE],
        out_specs=whole,
        out_shape=held((rows, width)),
        compiler_params=PARAMS,
        cost_estimate=cost(rows * width, 8 * rows * width),
    )(one, two, after)


def direction_kernel(*refs, pieces):
    mine_ref, other_ref, one_ref, two_ref, first_ref, second_ref = refs[:6]
    new_first_ref, new_second_ref = refs[-2 - pieces : -pieces]
    gradient = mine_ref[0].astype(F32) + other_ref[0].astype(F32)
    gradient = gradient + one_ref[...].astype(F32) + two_ref[...].astype(F32)
    new_first = 0.9 * first_ref[0] + 0.1 * gradient
    new_second = 0.999 * second_ref[0] + 0.001 * gradient * gradient
    new_first_ref[0] = new_first
    new_second_ref[0] = new_second
    first_fix = 1.0 - 0.9**1000.0
    second_fix = 1.0 - 0.999**1000.0
    direction = (new_first / first_fix / (jnp.sqrt(new_second / second_fix) + 1e-08)).astype(BF16)
    low = 0
    for ref in refs[-pieces:]:
        size = min(ref.shape[1], direction.shape[1] - low)
        ref[:, :size] = direction[:, low : low + size]
        if size < ref.shape[1]:
            ref[:, size:] = jnp.zeros((ref.shape[0], ref.shape[1] - size), BF16)
        low += size


def directions(mine, other, one, two, first_moment, second_moment, which, pieces, before, after):
    _, rows, width = first_moment.shape
    cut = (width // pieces + LANES - 1) // LANES * LANES
    tile = 16
    zero = pl.BlockSpec((1, tile, width), lambda i: (0, i, 0))
    flat = pl.BlockSpec((tile, width), lambda i: (i, 0))
    own = pl.BlockSpec((1, tile, width), lambda i: (which, i, 0))
    half = pl.BlockSpec((tile, cut), lambda i: (i, 0))
    in_specs = [zero, zero, flat, flat, own, own]
    args = [mine, other, one, two, first_moment, second_moment]
    aliases = {len(args) + i: i for i in range(len(before))}
    args += [*before, after]
    in_specs += [ANYWHERE] * (len(before) + 1)
    piece = held((rows, cut))
    full = jax.ShapeDtypeStruct(first_moment.shape, F32)
    return pl.pallas_call(
        functools.partial(direction_kernel, pieces=pieces),
        grid=(rows // tile,),
        in_specs=in_specs,
        out_specs=[own, own] + [half] * pieces,
        out_shape=[full, full] + [piece] * pieces,
        input_output_aliases=aliases,
        compiler_params=PARAMS,
        cost_estimate=cost(30 * rows * width, 26 * rows * width),
    )(*args)


def stack_kernel(*refs):
    rows = refs[0].shape[0]
    for i, ref in enumerate(refs[:-1]):
        refs[-1][i * rows : (i + 1) * rows, :] = ref[...]


def stack(pieces):
    rows, width = pieces[0].shape
    return pl.pallas_call(
        stack_kernel,
        out_shape=held((rows * len(pieces), width)),
        compiler_params=PARAMS,
        cost_estimate=cost(0, 4 * rows * width * len(pieces)),
    )(*pieces)


def expand_kernel(columns_ref, *refs, count):
    pieces, out_ref = refs[:count], refs[-1]
    width = pieces[0].shape[1]
    for low in range(0, width, 256):
        high = min(low + 256, width)
        total, at = None, 0
        for piece in pieces:
            depth = piece.shape[0]
            term = jnp.dot(
                columns_ref[:, at : at + depth], piece[:, low:high], preferred_element_type=F32
            )
            total = term if total is None else total + term
            at += depth
        out_ref[0, low:high, :] = total.T.astype(BF16)


def expand_half(columns, pieces, which, place, update):
    rows, ranks = columns.shape
    cut = pieces[0].shape[1]
    in_specs = [pl.BlockSpec((rows, ranks), lambda i: (0, 0))]
    in_specs += [pl.BlockSpec(p.shape, lambda i: (0, 0)) for p in pieces]
    return pl.pallas_call(
        functools.partial(expand_kernel, count=len(pieces)),
        grid=(1,),
        in_specs=[*in_specs, ANYWHERE],
        out_specs=pl.BlockSpec((1, cut, rows), lambda i: (which, place, 0)),
        out_shape=jax.ShapeDtypeStruct(update.shape, BF16),
        input_output_aliases={len(in_specs): 0},
        compiler_params=PARAMS,
        cost_estimate=cost(2 * rows * ranks * cut, 2 * (rows * ranks + ranks * cut + rows * cut)),
    )(columns, *pieces, update)


def expand_whole_kernel(bases_ref, gathered_ref, out_ref):
    out_ref[0] = (
        jnp.dot(bases_ref[0], gathered_ref[...], preferred_element_type=F32).T.astype(BF16)
    )


def expand_whole(bases, gathered, which, width):
    count, rows, ranks = bases.shape
    tile = 256
    return pl.pallas_call(
        expand_whole_kernel,
        grid=(gathered.shape[1] // tile,),
        in_specs=[
            pl.BlockSpec((1, rows, ranks), lambda i: (which, 0, 0)),
            pl.BlockSpec((ranks, tile), lambda i: (0, i)),
        ],
        out_specs=pl.BlockSpec((1, tile, rows), lambda i: (which, i, 0)),
        out_shape=jax.ShapeDtypeStruct((count, width, rows), BF16),
        compiler_params=PARAMS,
        cost_estimate=cost(
            2 * rows * ranks * width, 2 * (rows * ranks + ranks * width + rows * width)
        ),
    )(bases, gathered)


def ring_gather(value, first, second):
    row = stack([value] + [receive(value, first, d) for d in (1, 2, 3)])
    half = row.shape[0] // 2
    after = receive(row, second, 1)
    before = receive(row, second, -1)
    far_top = receive(after[:half], second, 1)
    far_bottom = receive(before[half:], second, -1)
    return row, after, far_top, far_bottom, before


def on_device(activations, out_grads, bases, first_moment, second_moment):
    where = jnp.stack([lax.axis_index(n) for n in ("x", "c", "y", "z")]).astype(jnp.int32)
    y, z = where[2], where[3]
    features, ranks = bases.shape[1:]
    part = ranks // (SIDE * SIDE)
    width = first_moment.shape[2]

    column = jnp.arange(ranks)
    slow, fast, inner = column // (SIDE * part), column // part % SIDE, column % part
    source = (((y + slow) % SIDE) * SIDE + (z + fast) % SIDE) * part + inner
    place = (column[:, None] == source[None, :]).astype(BF16)
    own = lax.dynamic_slice_in_dim(activations, (y * SIDE + z) * features, features, 1)
    partial = jnp.einsum("td,kdr->ktr", own, bases, preferred_element_type=F32).astype(BF16)
    partial = jnp.einsum("ktr,rs->kts", partial, place, preferred_element_type=F32).astype(BF16)
    for axis in ("y", "z"):
        size = partial.shape[2] // SIDE
        blocks = [partial[:, :, i * size : (i + 1) * size] for i in range(SIDE)]
        total = blocks[0].astype(F32)
        for i in (1, 3, 2):
            total = total + send(blocks[i], axis, i).astype(F32)
        partial = total.astype(BF16)

    mine, other = partial_grads(where, partial[0], out_grads, 0, where)
    other = swap_cores(other)
    near, far, via = sums(mine, other, (3, 2, 1))
    columns_y, columns_z = arrange(where, bases, 1, far)
    near = send(near, "x", -1)
    passed = relay(send(far, "x", 1), via, columns_y)
    mine_1, other_1 = partial_grads(where, partial[1], out_grads, 1, passed)
    passed = send(passed, "x", 1)
    *moments, whole = directions(
        mine, other, near, passed, first_moment, second_moment, 0, 1, [], mine_1
    )
    gathered = lax.all_gather(whole, ("y", "z"), axis=0, tiled=True)

    other_1 = swap_cores(other_1)
    near, far, via = sums(mine_1, other_1, (1, 2, 3))
    near = send(near, "x", 1)
    passed = send(relay(send(far, "x", -1), via, far), "x", -1)
    *moments, left, right = directions(
        mine_1, other_1, near, passed, first_moment, second_moment, 1, 2, moments, passed
    )
    pieces_left = ring_gather(left, "y", "z")
    pieces_right = ring_gather(right, "z", "y")
    update = expand_whole(bases, gathered, 0, width)
    update = expand_half(columns_z, pieces_left, 1, 0, update)
    update = expand_half(columns_y, pieces_right, 1, 1, update)
    return jnp.swapaxes(update, 1, 2), *moments


def solution(mesh):
    grid = Mesh(mesh.devices.reshape(4, 2, 4, 4), ("x", "c", "y", "z"))
    dp, fsdp = ("x", "c"), ("y", "z")
    return jax.shard_map(
        on_device,
        mesh=grid,
        in_specs=(
            P(dp, None),
            P(None, dp, None),
            P(None, fsdp, None),
            P(None, fsdp, dp),
            P(None, fsdp, dp),
        ),
        out_specs=(P(None, fsdp, dp), P(None, fsdp, dp), P(None, fsdp, dp)),
        check_vma=False,
    )
```

time: 190 us -> 194 us (1.021)
  starting transfers between devices: 48.1 us -> 33.6 us
  between operations: 0.88 us -> 14.2 us
  local copies, waits for them, and re-layouts: 8.1 us -> 14.6 us
  Pallas kernels: 58.3 us -> 62.6 us
  other arithmetic: 4.68 us -> 0.72 us
    ppermute x36 -> x26, starting transfers between devices: 47.9 us -> 33.5 us  [receive(): lax.ppermute(value, axis, [((i + distance) % SIDE, i) for i in range(SIDE)])]
    pallas_call x10 -> x11, Pallas kernels: 37.1 us -> 44.4 us  [the longest x1 11 us: expand_whole(): pl.pallas_call(expand_whole_kernel, grid=(gathered.shape[1] // tile,), in...]
    ppermute x36 -> x26, waiting for transfers between devices: 63 us -> 58 us  [receive(): lax.ppermute(value, axis, [((i + distance) % SIDE, i) for i in range(SIDE)])]
    convert_element_type x4 -> x0, other arithmetic: 3.9 us -> none  [the longest x1 2.49 us: on_device(): near = send(sums[-way % SIDE].astype(BF16), 'x', -way)]
    unnamed x66 -> x40, local copies, waits for them, and re-layouts: 7.35 us -> 10.7 us
    ppermute x2, waiting for transfers between devices: 3.43 us -> 6.64 us  [swap_cores(): return lax.ppermute(value, 'c', [(0, 1), (1, 0)])]
    slice x0 -> x4, local copies, waits for them, and re-layouts: none -> 3.17 us  [the longest x2 1.59 us: ring_gather(): far_bottom = receive(before[half:], second, -1)]
    pallas_call x1, Pallas kernels: 8.13 us -> 5.24 us  [arrange(): pl.pallas_call(arrange_kernel, grid_spec=pltpu.PrefetchScalarGridSpec(num...]
  transfers between devices with their start and end apart: 38 -> 29, of which waited for: 16 -> 14; matrix products, arithmetic and copies ran while one was open for 1% -> 2% of each run, Pallas kernels for 21% -> 23%
where the time goes in v3:
time: 194 us; the launch traced here: 193 us
  waiting for transfers between devices  64.6 us (33%)
  Pallas kernels  62.6 us (32%)
  starting transfers between devices  33.6 us (17%)
  local copies, waits for them, and re-layouts  14.6 us (8%)
  between operations  14.2 us (7%)
  matrix products  2.9 us (1%)
    ppermute x26, waiting for transfers between devices, receive(): lax.ppermute(value, axis, [((i + distance) % SIDE, i) for i in range(SIDE)])  58 us
    ppermute x26, starting transfers between devices, receive(): lax.ppermute(value, axis, [((i + distance) % SIDE, i) for i in range(SIDE)])  33.5 us
    pallas_call x2, Pallas kernels, partial_grads(): pl.pallas_call(partial_kernel, grid_spec=pltpu.PrefetchScalarGridSpec(num...  13 us
    pallas_call x1, Pallas kernels, expand_whole(): pl.pallas_call(expand_whole_kernel, grid=(gathered.shape[1] // tile,), in...  11 us
    pallas_call x2, Pallas kernels, expand_half(): pl.pallas_call(functools.partial(expand_kernel, count=len(pieces)), grid=...  10.8 us
    unnamed x40, local copies, waits for them, and re-layouts  10.7 us
    pallas_call x2, Pallas kernels, directions(): pl.pallas_call(functools.partial(direction_kernel, pieces=pieces), grid=(...  8.18 us
    ppermute x2, waiting for transfers between devices, swap_cores(): return lax.ppermute(value, 'c', [(0, 1), (1, 0)])  6.64 us
  transfers between devices with their start and end apart: 29, of which 14 were waited for; matrix products, arithmetic and copies ran while one was open for 2% of the time, Pallas kernels for 23%

profile of v3, /device:TPU:0, one launch (start us, length us, event | category | flops | bytes accessed | tf_op | source)
XLA Modules:
  0.0 193.2 jit_solution(7453575853399185985)
XLA Ops:
  7.3 1.5 copy-done
  8.8 2.9 %fusion.4 = bf16[2,128,1024]{2,1,0:T(8,128)(2,1)S(1)} fusion(s32[1024]{0:T(1024)S(1)} %fusion.21, bf16[2,512,1024]{2,1,0:T(8,128)(2,1)} %bases_ref.3, bf16[128,8192]{1,0:T(8,128)(2,1)S(1)} %copy-done, s32[]{:T(128)S(6)} %select_n.54), kind=kOutput, calls=%fused_computation.4 | convolution fusion | flops 806879232 | bytes 2756612 | tf_op jit(solution)/shard_map/ktr,rs->kts/dot_general | solution.py:294
  11.7 1.7 collective-permute-start
  13.4 1.6 collective-permute-start.1
  15.0 2.1 %collective-permute-start.2 = (bf16[2,128,256]{2,1,0:T(8,128)(2,1)S(1)}, bf16[2,128,256]{2,1,0:T(8,128)(2,1)S(1)}, u32[]{:S(2)}, u32[]{:S(2)}) collective-permute-start(bf16[2,128,256]{2,1,0:T(8,128)(2,1)S(1)} %get-tuple-element.42), channel_id=1, source_target_pairs={{8,0},{12,4},{0,8},{4,12},{9,1},{13,5},{1,9},{5,13},{10,2},{14,6},... | collective-permute-start | bytes 393224 | tf_op jit(solution)/shard_map/ppermute | solution.py:20
  17.1 1.3 collective-permute-done
  18.4 2.2 %collective-permute-done.1 = bf16[2,128,256]{2,1,0:T(8,128)(2,1)S(1)} collective-permute-done((bf16[2,128,256]{2,1,0:T(8,128)(2,1)S(1)}, bf16[2,128,256]{2,1,0:T(8,128)(2,1)S(1)}, u32[]{:S(2)}, u32[]{:S(2)}) %collective-permute-start.1) | collective-permute-done | bytes 131104 | tf_op jit(solution)/shard_map/ppermute | solution.py:20
  20.6 1.8 collective-permute-done.2
  22.5 2.0 %collective-permute-start.3 = (bf16[2,128,64]{2,1,0:T(8,128)(2,1)S(1)}, bf16[2,128,64]{2,1,0:T(8,128)(2,1)S(1)}, u32[]{:S(2)}, u32[]{:S(2)}) collective-permute-start(bf16[2,128,64]{2,1,0:T(8,128)(2,1)S(1)} %get-tuple-element.44), channel_id=1, source_target_pairs={{3,0},{0,1},{1,2},{2,3},{7,4},{4,5},{5,6},{6,7},{11,8},{8,9},{9,10... | collective-permute-start | bytes 98312 | tf_op jit(solution)/shard_map/ppermute | solution.py:20
  24.5 2.2 %collective-permute-start.4 = (bf16[2,128,64]{2,1,0:T(8,128)(2,1)S(1)}, bf16[2,128,64]{2,1,0:T(8,128)(2,1)S(1)}, u32[]{:S(2)}, u32[]{:S(2)}) collective-permute-start(bf16[2,128,64]{2,1,0:T(8,128)(2,1)S(1)} %get-tuple-element.46), channel_id=1, source_target_pairs={{1,0},{2,1},{3,2},{0,3},{5,4},{6,5},{7,6},{4,7},{9,8},{10,9},{11,1... | collective-permute-start | bytes 98312 | tf_op jit(solution)/shard_map/ppermute | solution.py:20
  26.7 1.8 collective-permute-start.5
  29.1 3.4 %collective-permute-done.5 = bf16[2,128,64]{2,1,0:T(8,128)(2,1)S(1)} collective-permute-done((bf16[2,128,64]{2,1,0:T(8,128)(2,1)S(1)}, bf16[2,128,64]{2,1,0:T(8,128)(2,1)S(1)}, u32[]{:S(2)}, u32[]{:S(2)}) %collective-permute-start.5) | collective-permute-done | bytes 32800 | tf_op jit(solution)/shard_map/ppermute | solution.py:20
  33.2 6.5 %shard_map.76 = (bf16[4,64,2752]{2,1,0:T(8,128)(2,1)}, bf16[4,64,2752]{2,1,0:T(8,128)(2,1)}) custom-call(s32[4]{0:T(128)} %pad_add_fusion.where_ref._, bf16[128,64]{1,0:T(8,128)(2,1)} %get-tuple-element.48.proj_ref, bf16[2,128,22016]{2,1,0:T(8,128)(2,1)} %grads_ref.3, s32[4]{0:T(128)} %pad_add_fusion.where_ref._), custom_call_target="tpu_custom_call" | custom-call | flops 360710144 | bytes 8454144 | tf_op jit(solution)/shard_map/pallas_call | solution.py:96
  39.6 3.4 %collective-permute-done.6.other_ref.refs_1_ = bf16[4,64,2752]{2,1,0:T(8,128)(2,1)S(1)} collective-permute-done((bf16[4,64,2752]{2,1,0:T(8,128)(2,1)}, bf16[4,64,2752]{2,1,0:T(8,128)(2,1)S(1)}, u32[]{:S(2)}, u32[]{:S(2)}) %collective-permute-start.6) | collective-permute-done | bytes 1409056 | tf_op jit(solution)/shard_map/ppermute | solution.py:28
  43.1 1.1 copy-done.2
  44.2 3.0 %shard_map.77 = (bf16[64,2752]{1,0:T(8,128)(2,1)}, bf16[64,2752]{1,0:T(8,128)(2,1)}, f32[64,2752]{1,0:T(8,128)}) custom-call(bf16[4,64,2752]{2,1,0:T(8,128)(2,1)} %get-tuple-element.22.mine_ref.refs_0_, bf16[4,64,2752]{2,1,0:T(8,128)(2,1)} %copy-done.2), custom_call_target="tpu_custom_call" | custom-call | flops 528384 | bytes 3522560 | tf_op jit(solution)/shard_map/pallas_call | solution.py:124
  47.2 1.5 collective-permute-start.7
  48.6 1.7 collective-permute-start.12
  50.4 5.2 %shard_map.78 = (bf16[512,1024]{1,0:T(8,128)(2,1)}, bf16[512,1024]{1,0:T(8,128)(2,1)}) custom-call(s32[4]{0:T(128)} %pad_add_fusion.where_ref._, bf16[2,512,1024]{2,1,0:T(8,128)(2,1)} %bases_ref.3, bf16[64,2752]{1,0:T(8,128)(2,1)} %get-tuple-element.24._), custom_call_target="tpu_custom_call" | custom-call | flops 2147483648 | bytes 3145728 | tf_op jit(solution)/shard_map/pallas_call | solution.py:60
  55.6 3.4 %collective-permute-done.7.one_ref = bf16[64,2752]{1,0:T(8,128)(2,1)S(1)} collective-permute-done((bf16[64,2752]{1,0:T(8,128)(2,1)}, bf16[64,2752]{1,0:T(8,128)(2,1)S(1)}, u32[]{:S(2)}, u32[]{:S(2)}) %collective-permute-start.7) | collective-permute-done | bytes 352288 | tf_op jit(solution)/shard_map/ppermute | solution.py:20
  59.8 2.0 %shard_map.79._ = bf16[64,2752]{1,0:T(8,128)(2,1)} custom-call(bf16[64,2752]{1,0:T(8,128)(2,1)} %copy-done.11, f32[64,2752]{1,0:T(8,128)} %get-tuple-element.26.two_ref, bf16[512,1024]{1,0:T(8,128)(2,1)} %get-tuple-element.25._.columns_ref), custom_call_target="tpu_custom_call" | custom-call | flops 176128 | bytes 1409024 | tf_op jit(solution)/shard_map/pallas_call | solution.py:139
  62.1 6.5 %shard_map.80 = (bf16[4,64,2752]{2,1,0:T(8,128)(2,1)}, bf16[4,64,2752]{2,1,0:T(8,128)(2,1)}) custom-call(s32[4]{0:T(128)} %pad_add_fusion.where_ref._, bf16[128,64]{1,0:T(8,128)(2,1)} %get-tuple-element.47.proj_ref, bf16[2,128,22016]{2,1,0:T(8,128)(2,1)} %grads_ref.3, bf16[64,2752]{1,0:T(8,128)(2,1)} %shard_map.79._), custom_call_target="tpu_custom_call" | custom-call | flops 360710144 | bytes 8454144 | tf_op jit(solution)/shard_map/pallas_call | solution.py:96
  68.6 4.2 %collective-permute-done.13.refs_3_ = bf16[64,2752]{1,0:T(8,128)(2,1)S(1)} collective-permute-done((bf16[64,2752]{1,0:T(8,128)(2,1)}, bf16[64,2752]{1,0:T(8,128)(2,1)S(1)}, u32[]{:S(2)}, u32[]{:S(2)}) %collective-permute-start.13) | collective-permute-done | bytes 352288 | tf_op jit(solution)/shard_map/ppermute | solution.py:20
  73.6 4.2 %shard_map.83 = (f32[2,64,2752]{2,1,0:T(8,128)}, f32[2,64,2752]{2,1,0:T(8,128)}, bf16[64,2816]{1,0:T(8,128)(2,1)}) custom-call(bf16[4,64,2752]{2,1,0:T(8,128)(2,1)} %get-tuple-element.22.mine_ref.refs_0_, bf16[4,64,2752]{2,1,0:T(8,128)(2,1)} %copy-done.2, bf16[64,2752]{1,0:T(8,128)(2,1)} %copy-done.8, bf16[64,2752]{1,0:T(8,128)(2,1)} %copy-done.10, ...), custom_call_target="tpu_custom_call" | custom-call | flops 5283840 | bytes 4579328 | tf_op jit(solution)/shard_map/pallas_call | solution.py:185
  77.9 3.2 %collective-permute-done.8.other_ref.refs_1_ = bf16[4,64,2752]{2,1,0:T(8,128)(2,1)S(1)} collective-permute-done((bf16[4,64,2752]{2,1,0:T(8,128)(2,1)S(1)}, bf16[4,64,2752]{2,1,0:T(8,128)(2,1)S(1)}, u32[]{:S(2)}, u32[]{:S(2)}) %collective-permute-start.8) | collective-permute-done | bytes 1409056 | tf_op jit(solution)/shard_map/ppermute | solution.py:28
  82.2 3.1 %shard_map.81 = (bf16[64,2752]{1,0:T(8,128)(2,1)}, bf16[64,2752]{1,0:T(8,128)(2,1)}, f32[64,2752]{1,0:T(8,128)}) custom-call(bf16[4,64,2752]{2,1,0:T(8,128)(2,1)} %get-tuple-element.27.mine_ref.refs_6_.refs_0_, bf16[4,64,2752]{2,1,0:T(8,128)(2,1)} %copy-done.1), custom_call_target="tpu_custom_call" | custom-call | flops 528384 | bytes 3522560 | tf_op jit(solution)/shard_map/pallas_call | solution.py:124
  85.5 1.8 collective-permute-start.9
  87.3 8.7 %collective-permute-done.10.one_ref = bf16[64,2752]{1,0:T(8,128)(2,1)S(1)} collective-permute-done((bf16[64,2752]{1,0:T(8,128)(2,1)}, bf16[64,2752]{1,0:T(8,128)(2,1)S(1)}, u32[]{:S(2)}, u32[]{:S(2)}) %collective-permute-start.10) | collective-permute-done | bytes 352288 | tf_op jit(solution)/shard_map/ppermute | solution.py:20
  96.7 2.0 %shard_map.82 = bf16[64,2752]{1,0:T(8,128)(2,1)} custom-call(bf16[64,2752]{1,0:T(8,128)(2,1)} %copy-done.12, f32[64,2752]{1,0:T(8,128)} %get-tuple-element.31.two_ref, bf16[64,2752]{1,0:T(8,128)(2,1)} %get-tuple-element.30._), custom_call_target="tpu_custom_call" | custom-call | flops 176128 | bytes 1409024 | tf_op jit(solution)/shard_map/pallas_call | solution.py:139
  98.7 1.5 collective-permute-start.11
  100.2 8.4 %collective-permute-done.11.refs_3_.refs_8_ = bf16[64,2752]{1,0:T(8,128)(2,1)S(1)} collective-permute-done((bf16[64,2752]{1,0:T(8,128)(2,1)}, bf16[64,2752]{1,0:T(8,128)(2,1)S(1)}, u32[]{:S(2)}, u32[]{:S(2)}) %collective-permute-start.11) | collective-permute-done | bytes 352288 | tf_op jit(solution)/shard_map/ppermute | solution.py:20
  109.4 4.0 %shard_map.84 = (f32[2,64,2752]{2,1,0:T(8,128)}, f32[2,64,2752]{2,1,0:T(8,128)}, bf16[64,1408]{1,0:T(8,128)(2,1)}, bf16[64,1408]{1,0:T(8,128)(2,1)}) custom-call(bf16[4,64,2752]{2,1,0:T(8,128)(2,1)} %get-tuple-element.27.mine_ref.refs_6_.refs_0_, bf16[4,64,2752]{2,1,0:T(8,128)(2,1)} %copy-done.1, ...), custom_call_target="tpu_custom_call", output_to_operand_aliasing={{0}: (6, {}), {1}: (7, {})} | custom-call | flops 5283840 | bytes 4579328 | tf_op jit(solution)/shard_map/pallas_call | solution.py:185
  113.5 1.8 collective-permute-start.21
  115.3 1.4 collective-permute-start.22
  116.7 1.9 collective-permute-start.14
  118.7 6.3 %collective-permute-done.21.refs_1_ = bf16[64,1408]{1,0:T(8,128)(2,1)S(1)} collective-permute-done((bf16[64,1408]{1,0:T(8,128)(2,1)}, bf16[64,1408]{1,0:T(8,128)(2,1)S(1)}, u32[]{:S(2)}, u32[]{:S(2)}) %collective-permute-start.21) | collective-permute-done | bytes 180256 | tf_op jit(solution)/shard_map/ppermute | solution.py:20
  125.0 3.3 %collective-permute-done.22.refs_2_ = bf16[64,1408]{1,0:T(8,128)(2,1)S(1)} collective-permute-done((bf16[64,1408]{1,0:T(8,128)(2,1)}, bf16[64,1408]{1,0:T(8,128)(2,1)S(1)}, u32[]{:S(2)}, u32[]{:S(2)}) %collective-permute-start.22) | collective-permute-done | bytes 180256 | tf_op jit(solution)/shard_map/ppermute | solution.py:20
  128.3 4.3 %collective-permute-done.23.refs_3_ = bf16[64,1408]{1,0:T(8,128)(2,1)S(1)} collective-permute-done((bf16[64,1408]{1,0:T(8,128)(2,1)}, bf16[64,1408]{1,0:T(8,128)(2,1)S(1)}, u32[]{:S(2)}, u32[]{:S(2)}) %collective-permute-start.23) | collective-permute-done | bytes 180256 | tf_op jit(solution)/shard_map/ppermute | solution.py:20
  133.2 2.1 %shard_map.86.refs_0_ = bf16[256,1408]{1,0:T(8,128)(2,1)} custom-call(bf16[64,1408]{1,0:T(8,128)(2,1)} %get-tuple-element.37.refs_0_, bf16[64,1408]{1,0:T(8,128)(2,1)} %copy-done.16, bf16[64,1408]{1,0:T(8,128)(2,1)} %copy-done.17, bf16[64,1408]{1,0:T(8,128)(2,1)} %copy-done.18), custom_call_target="tpu_custom_call" | custom-call | bytes 1441792 | tf_op jit(solution)/shard_map/pallas_call | solution.py:205
  135.4 1.9 %collective-permute-start.24 = (bf16[256,1408]{1,0:T(8,128)(2,1)}, bf16[256,1408]{1,0:T(8,128)(2,1)S(1)}, u32[]{:S(2)}, u32[]{:S(2)}) collective-permute-start(bf16[256,1408]{1,0:T(8,128)(2,1)} %shard_map.86.refs_0_), channel_id=1, source_target_pairs={{1,0},{2,1},{3,2},{0,3},{5,4},{6,5},{7,6},{4,7},{9,8},{10,9},{11,1... | collective-permute-start | bytes 2162696 | tf_op jit(solution)/shard_map/ppermute | solution.py:20
  138.8 2.1 %shard_map.85.refs_0_ = bf16[256,1408]{1,0:T(8,128)(2,1)} custom-call(bf16[64,1408]{1,0:T(8,128)(2,1)} %get-tuple-element.35.refs_0_, bf16[64,1408]{1,0:T(8,128)(2,1)} %copy-done.13, bf16[64,1408]{1,0:T(8,128)(2,1)} %copy-done.14, bf16[64,1408]{1,0:T(8,128)(2,1)} %copy-done.15), custom_call_target="tpu_custom_call" | custom-call | bytes 1441792 | tf_op jit(solution)/shard_map/pallas_call | solution.py:205
  140.9 3.1 %collective-permute-start.17 = (bf16[256,1408]{1,0:T(8,128)(2,1)}, bf16[256,1408]{1,0:T(8,128)(2,1)S(1)}, u32[]{:S(2)}, u32[]{:S(2)}) collective-permute-start(bf16[256,1408]{1,0:T(8,128)(2,1)} %shard_map.85.refs_0_), channel_id=1, source_target_pairs={{4,0},{8,4},{12,8},{0,12},{5,1},{9,5},{13,9},{1,13},{6,2},{10,6},{... | collective-permute-start | bytes 2162696 | tf_op jit(solution)/shard_map/ppermute | solution.py:20
  144.0 10.7 %collective-permute-done.24.refs_1_ = bf16[256,1408]{1,0:T(8,128)(2,1)S(1)} collective-permute-done((bf16[256,1408]{1,0:T(8,128)(2,1)}, bf16[256,1408]{1,0:T(8,128)(2,1)S(1)}, u32[]{:S(2)}, u32[]{:S(2)}) %collective-permute-start.24) | collective-permute-done | bytes 720928 | tf_op jit(solution)/shard_map/ppermute | solution.py:20
  155.5 1.4 collective-permute-start.25
  160.1 2.7 %collective-permute-start.18 = (bf16[128,1408]{1,0:T(8,128)(2,1)}, bf16[128,1408]{1,0:T(8,128)(2,1)}, u32[]{:S(2)}, u32[]{:S(2)}) collective-permute-start(bf16[128,1408]{1,0:T(8,128)(2,1)} %slice.66), channel_id=1, source_target_pairs={{4,0},{8,4},{12,8},{0,12},{5,1},{9,5},{13,9},{1,13},{6,2},{10,6},{... | collective-permute-start | bytes 1081352 | tf_op jit(solution)/shard_map/ppermute | solution.py:20
  164.5 11.0 %shard_map.87.refs_5_ = bf16[2,2752,512]{2,1,0:T(8,128)(2,1)} custom-call(bf16[2,512,1024]{2,1,0:T(8,128)(2,1)} %bases_ref.3, bf16[1024,2816]{1,0:T(8,128)(2,1)} %all-gather.2.cloned.1.call-done.gathered_ref), custom_call_target="tpu_custom_call" | custom-call | flops 2885681152 | bytes 9502720 | tf_op jit(solution)/shard_map/pallas_call | solution.py:255
  175.6 5.4 %shard_map.88.refs_5_ = bf16[2,2752,512]{2,1,0:T(8,128)(2,1)} custom-call(bf16[512,1024]{1,0:T(8,128)(2,1)} %get-tuple-element.36.columns_ref, bf16[256,1408]{1,0:T(8,128)(2,1)} %shard_map.86.refs_0_, bf16[256,1408]{1,0:T(8,128)(2,1)} %copy-done.3, bf16[128,1408]{1,0:T(8,128)(2,1)} %collective-permute-done.25.refs_2_, ...), custom_call_target="tpu_custom_call", output_to_operand_aliasing={{}: (6, {})} | custom-call | flops 1476395008 | bytes 5373952 | tf_op jit(solution)/shard_map/pallas_call | solution.py:234
  181.0 5.4 %shard_map.89 = bf16[2,2752,512]{2,1,0:T(8,128)(2,1)} custom-call(bf16[512,1024]{1,0:T(8,128)(2,1)} %get-tuple-element.25._.columns_ref, bf16[256,1408]{1,0:T(8,128)(2,1)} %shard_map.85.refs_0_, bf16[256,1408]{1,0:T(8,128)(2,1)} %copy-done.5, bf16[128,1408]{1,0:T(8,128)(2,1)} %collective-permute-done.18.refs_2_, ...), custom_call_target="tpu_custom_call", output_to_operand_aliasing={{}: (6, {})} | custom-call | flops 1476395008 | bytes 5373952 | tf_op jit(solution)/shard_map/pallas_call | solution.py:234
  (77 shorter events, 14.3 us)
Async XLA Ops:
  7.2 1.6 copy-start
  7.2 157.4 %all-gather.2.cloned.1.call-start = ((), (), s32[]{:S(2)}) async-start(), calls=%async_computation | async-start | bytes 6127616 | tf_op jit(solution)/shard_map/all_gather | solution.py:314
  11.7 6.7 %collective-permute-start = (bf16[2,128,256]{2,1,0:T(8,128)(2,1)S(1)}, bf16[2,128,256]{2,1,0:T(8,128)(2,1)S(1)}, u32[]{:S(2)}, u32[]{:S(2)}) collective-permute-start(bf16[2,128,256]{2,1,0:T(8,128)(2,1)S(1)} %get-tuple-element.41), channel_id=1, source_target_pairs={{12,0},{0,4},{4,8},{8,12},{13,1},{1,5},{5,9},{9,13},{14,2},{2,6},{... | collective-permute-start | bytes 393224 | tf_op jit(solution)/shard_map/ppermute | solution.py:20
  13.4 7.1 %collective-permute-start.1 = (bf16[2,128,256]{2,1,0:T(8,128)(2,1)S(1)}, bf16[2,128,256]{2,1,0:T(8,128)(2,1)S(1)}, u32[]{:S(2)}, u32[]{:S(2)}) collective-permute-start(bf16[2,128,256]{2,1,0:T(8,128)(2,1)S(1)} %get-tuple-element.43), channel_id=1, source_target_pairs={{4,0},{8,4},{12,8},{0,12},{5,1},{9,5},{13,9},{1,13},{6,2},{10,6},{... | collective-permute-start | bytes 393224 | tf_op jit(solution)/shard_map/ppermute | solution.py:20
  15.0 7.3 %collective-permute-start.2 = (bf16[2,128,256]{2,1,0:T(8,128)(2,1)S(1)}, bf16[2,128,256]{2,1,0:T(8,128)(2,1)S(1)}, u32[]{:S(2)}, u32[]{:S(2)}) collective-permute-start(bf16[2,128,256]{2,1,0:T(8,128)(2,1)S(1)} %get-tuple-element.42), channel_id=1, source_target_pairs={{8,0},{12,4},{0,8},{4,12},{9,1},{13,5},{1,9},{5,13},{10,2},{14,6},... | collective-permute-start | bytes 393224 | tf_op jit(solution)/shard_map/ppermute | solution.py:20
  22.5 6.6 %collective-permute-start.3 = (bf16[2,128,64]{2,1,0:T(8,128)(2,1)S(1)}, bf16[2,128,64]{2,1,0:T(8,128)(2,1)S(1)}, u32[]{:S(2)}, u32[]{:S(2)}) collective-permute-start(bf16[2,128,64]{2,1,0:T(8,128)(2,1)S(1)} %get-tuple-element.44), channel_id=1, source_target_pairs={{3,0},{0,1},{1,2},{2,3},{7,4},{4,5},{5,6},{6,7},{11,8},{8,9},{9,10... | collective-permute-start | bytes 98312 | tf_op jit(solution)/shard_map/ppermute | solution.py:20
  24.5 4.6 %collective-permute-start.4 = (bf16[2,128,64]{2,1,0:T(8,128)(2,1)S(1)}, bf16[2,128,64]{2,1,0:T(8,128)(2,1)S(1)}, u32[]{:S(2)}, u32[]{:S(2)}) collective-permute-start(bf16[2,128,64]{2,1,0:T(8,128)(2,1)S(1)} %get-tuple-element.46), channel_id=1, source_target_pairs={{1,0},{2,1},{3,2},{0,3},{5,4},{6,5},{7,6},{4,7},{9,8},{10,9},{11,1... | collective-permute-start | bytes 98312 | tf_op jit(solution)/shard_map/ppermute | solution.py:20
  26.7 5.8 %collective-permute-start.5 = (bf16[2,128,64]{2,1,0:T(8,128)(2,1)S(1)}, bf16[2,128,64]{2,1,0:T(8,128)(2,1)S(1)}, u32[]{:S(2)}, u32[]{:S(2)}) collective-permute-start(bf16[2,128,64]{2,1,0:T(8,128)(2,1)S(1)} %get-tuple-element.45), channel_id=1, source_target_pairs={{2,0},{3,1},{0,2},{1,3},{6,4},{7,5},{4,6},{5,7},{10,8},{11,9},{8,1... | collective-permute-start | bytes 98312 | tf_op jit(solution)/shard_map/ppermute | solution.py:20
  39.6 3.4 %collective-permute-start.6 = (bf16[4,64,2752]{2,1,0:T(8,128)(2,1)}, bf16[4,64,2752]{2,1,0:T(8,128)(2,1)S(1)}, u32[]{:S(2)}, u32[]{:S(2)}) collective-permute-start(bf16[4,64,2752]{2,1,0:T(8,128)(2,1)} %get-tuple-element.23), channel_id=1, source_target_pairs={{0,16},{16,0},{1,17},{17,1},{2,18},{18,2},{3,19},{19,3},{4,20},{20... | collective-permute-start | bytes 4227080 | tf_op jit(solution)/shard_map/ppermute | solution.py:28
  43.1 1.1 copy-start.2
  47.2 11.9 %collective-permute-start.7 = (bf16[64,2752]{1,0:T(8,128)(2,1)}, bf16[64,2752]{1,0:T(8,128)(2,1)S(1)}, u32[]{:S(2)}, u32[]{:S(2)}) collective-permute-start(bf16[64,2752]{1,0:T(8,128)(2,1)} %get-tuple-element.24._), channel_id=1, source_target_pairs={{96,0},{0,32},{32,64},{64,96},{97,1},{1,33},{33,65},{65,97},{98,2}... | collective-permute-start | bytes 1056776 | tf_op jit(solution)/shard_map/ppermute | solution.py:20
  48.6 20.0 %collective-permute-start.12 = (bf16[64,2752]{1,0:T(8,128)(2,1)}, bf16[64,2752]{1,0:T(8,128)(2,1)S(1)}, u32[]{:S(2)}, u32[]{:S(2)}) collective-permute-start(bf16[64,2752]{1,0:T(8,128)(2,1)} %get-tuple-element.32), channel_id=1, source_target_pairs={{32,0},{64,32},{96,64},{0,96},{33,1},{65,33},{97,65},{1,97},{34,2}... | collective-permute-start | bytes 1056776 | tf_op jit(solution)/shard_map/ppermute | solution.py:20
  59.0 0.8 copy-start.11
  61.8 11.0 %collective-permute-start.13 = (bf16[64,2752]{1,0:T(8,128)(2,1)}, bf16[64,2752]{1,0:T(8,128)(2,1)S(1)}, u32[]{:S(2)}, u32[]{:S(2)}) collective-permute-start(bf16[64,2752]{1,0:T(8,128)(2,1)} %shard_map.79._), channel_id=1, source_target_pairs={{96,0},{0,32},{32,64},{64,96},{97,1},{1,33},{33,65},{65,97},{98,2}... | collective-permute-start | bytes 1056776 | tf_op jit(solution)/shard_map/ppermute | solution.py:20
  68.6 4.3 %copy-start.8 = (bf16[64,2752]{1,0:T(8,128)(2,1)}, bf16[64,2752]{1,0:T(8,128)(2,1)S(1)}, u32[]{:S(2)}) copy-start(bf16[64,2752]{1,0:T(8,128)(2,1)S(1)} %collective-permute-done.12.refs_2_) | copy-start | bytes 1056772
  72.9 0.7 copy-start.10
  73.6 4.2 %copy-start.19 = (bf16[4,64,2752]{2,1,0:T(8,128)(2,1)S(1)}, bf16[4,64,2752]{2,1,0:T(8,128)(2,1)}, u32[]{:S(2)}) copy-start(bf16[4,64,2752]{2,1,0:T(8,128)(2,1)} %get-tuple-element.28) | copy-start | bytes 4227076
  77.8 3.3 %collective-permute-start.8 = (bf16[4,64,2752]{2,1,0:T(8,128)(2,1)S(1)}, bf16[4,64,2752]{2,1,0:T(8,128)(2,1)S(1)}, u32[]{:S(2)}, u32[]{:S(2)}) collective-permute-start(bf16[4,64,2752]{2,1,0:T(8,128)(2,1)S(1)} %copy-done.19), channel_id=1, source_target_pairs={{0,16},{16,0},{1,17},{17,1},{2,18},{18,2},{3,19},{19,3},{4,20},{20... | collective-permute-start | bytes 4227080 | tf_op jit(solution)/shard_map/ppermute | solution.py:28
  81.1 1.1 copy-start.1
  85.3 10.7 %collective-permute-start.10 = (bf16[64,2752]{1,0:T(8,128)(2,1)}, bf16[64,2752]{1,0:T(8,128)(2,1)S(1)}, u32[]{:S(2)}, u32[]{:S(2)}) collective-permute-start(bf16[64,2752]{1,0:T(8,128)(2,1)} %get-tuple-element.30._), channel_id=1, source_target_pairs={{32,0},{64,32},{96,64},{0,96},{33,1},{65,33},{97,65},{1,97},{34,2}... | collective-permute-start | bytes 1056776 | tf_op jit(solution)/shard_map/ppermute | solution.py:20
  85.5 14.7 %collective-permute-start.9 = (bf16[64,2752]{1,0:T(8,128)(2,1)}, bf16[64,2752]{1,0:T(8,128)(2,1)S(1)}, u32[]{:S(2)}, u32[]{:S(2)}) collective-permute-start(bf16[64,2752]{1,0:T(8,128)(2,1)} %get-tuple-element.29), channel_id=1, source_target_pairs={{96,0},{0,32},{32,64},{64,96},{97,1},{1,33},{33,65},{65,97},{98,2}... | collective-permute-start | bytes 1056776 | tf_op jit(solution)/shard_map/ppermute | solution.py:20
  96.0 0.7 copy-start.12
  98.7 10.0 %collective-permute-start.11 = (bf16[64,2752]{1,0:T(8,128)(2,1)}, bf16[64,2752]{1,0:T(8,128)(2,1)S(1)}, u32[]{:S(2)}, u32[]{:S(2)}) collective-permute-start(bf16[64,2752]{1,0:T(8,128)(2,1)} %shard_map.82), channel_id=1, source_target_pairs={{32,0},{64,32},{96,64},{0,96},{33,1},{65,33},{97,65},{1,97},{34,2}... | collective-permute-start | bytes 1056776 | tf_op jit(solution)/shard_map/ppermute | solution.py:20
  100.2 8.4 %copy-start.9 = (bf16[64,2752]{1,0:T(8,128)(2,1)}, bf16[64,2752]{1,0:T(8,128)(2,1)S(1)}, u32[]{:S(2)}) copy-start(bf16[64,2752]{1,0:T(8,128)(2,1)S(1)} %collective-permute-done.9.refs_2_) | copy-start | bytes 1056772
  108.7 0.8 copy-start.7
  113.5 11.5 %collective-permute-start.21 = (bf16[64,1408]{1,0:T(8,128)(2,1)}, bf16[64,1408]{1,0:T(8,128)(2,1)S(1)}, u32[]{:S(2)}, u32[]{:S(2)}) collective-permute-start(bf16[64,1408]{1,0:T(8,128)(2,1)} %get-tuple-element.37.refs_0_), channel_id=1, source_target_pairs={{4,0},{8,4},{12,8},{0,12},{5,1},{9,5},{13,9},{1,13},{6,2},{10,6},{... | collective-permute-start | bytes 540680 | tf_op jit(solution)/shard_map/ppermute | solution.py:20
  115.3 13.0 %collective-permute-start.22 = (bf16[64,1408]{1,0:T(8,128)(2,1)}, bf16[64,1408]{1,0:T(8,128)(2,1)S(1)}, u32[]{:S(2)}, u32[]{:S(2)}) collective-permute-start(bf16[64,1408]{1,0:T(8,128)(2,1)} %get-tuple-element.37.refs_0_), channel_id=1, source_target_pairs={{8,0},{12,4},{0,8},{4,12},{9,1},{13,5},{1,9},{5,13},{10,2},{14,6},... | collective-permute-start | bytes 540680 | tf_op jit(solution)/shard_map/ppermute | solution.py:20
  116.7 15.9 %collective-permute-start.23 = (bf16[64,1408]{1,0:T(8,128)(2,1)}, bf16[64,1408]{1,0:T(8,128)(2,1)S(1)}, u32[]{:S(2)}, u32[]{:S(2)}) collective-permute-start(bf16[64,1408]{1,0:T(8,128)(2,1)} %get-tuple-element.37.refs_0_), channel_id=1, source_target_pairs={{12,0},{0,4},{4,8},{8,12},{13,1},{1,5},{5,9},{9,13},{14,2},{2,6},{... | collective-permute-start | bytes 540680 | tf_op jit(solution)/shard_map/ppermute | solution.py:20
  116.7 20.7 %collective-permute-start.14 = (bf16[64,1408]{1,0:T(8,128)(2,1)}, bf16[64,1408]{1,0:T(8,128)(2,1)S(1)}, u32[]{:S(2)}, u32[]{:S(2)}) collective-permute-start(bf16[64,1408]{1,0:T(8,128)(2,1)} %get-tuple-element.35.refs_0_), channel_id=1, source_target_pairs={{1,0},{2,1},{3,2},{0,3},{5,4},{6,5},{7,6},{4,7},{9,8},{10,9},{11,1... | collective-permute-start | bytes 540680 | tf_op jit(solution)/shard_map/ppermute | solution.py:20
  118.5 18.9 %collective-permute-start.15 = (bf16[64,1408]{1,0:T(8,128)(2,1)}, bf16[64,1408]{1,0:T(8,128)(2,1)S(1)}, u32[]{:S(2)}, u32[]{:S(2)}) collective-permute-start(bf16[64,1408]{1,0:T(8,128)(2,1)} %get-tuple-element.35.refs_0_), channel_id=1, source_target_pairs={{2,0},{3,1},{0,2},{1,3},{6,4},{7,5},{4,6},{5,7},{10,8},{11,9},{8,1... | collective-permute-start | bytes 540680 | tf_op jit(solution)/shard_map/ppermute | solution.py:20
  125.0 7.6 %copy-start.16 = (bf16[64,1408]{1,0:T(8,128)(2,1)}, bf16[64,1408]{1,0:T(8,128)(2,1)S(1)}, u32[]{:S(2)}) copy-start(bf16[64,1408]{1,0:T(8,128)(2,1)S(1)} %collective-permute-done.21.refs_1_) | copy-start | bytes 540676
  125.0 12.4 %collective-permute-start.16 = (bf16[64,1408]{1,0:T(8,128)(2,1)}, bf16[64,1408]{1,0:T(8,128)(2,1)S(1)}, u32[]{:S(2)}, u32[]{:S(2)}) collective-permute-start(bf16[64,1408]{1,0:T(8,128)(2,1)} %get-tuple-element.35.refs_0_), channel_id=1, source_target_pairs={{3,0},{0,1},{1,2},{2,3},{7,4},{4,5},{5,6},{6,7},{11,8},{8,9},{9,10... | collective-permute-start | bytes 540680 | tf_op jit(solution)/shard_map/ppermute | solution.py:20
  128.3 4.3 %copy-start.17 = (bf16[64,1408]{1,0:T(8,128)(2,1)}, bf16[64,1408]{1,0:T(8,128)(2,1)S(1)}, u32[]{:S(2)}) copy-start(bf16[64,1408]{1,0:T(8,128)(2,1)S(1)} %collective-permute-done.22.refs_2_) | copy-start | bytes 540676
  132.5 0.7 copy-start.18
  135.4 19.4 %collective-permute-start.24 = (bf16[256,1408]{1,0:T(8,128)(2,1)}, bf16[256,1408]{1,0:T(8,128)(2,1)S(1)}, u32[]{:S(2)}, u32[]{:S(2)}) collective-permute-start(bf16[256,1408]{1,0:T(8,128)(2,1)} %shard_map.86.refs_0_), channel_id=1, source_target_pairs={{1,0},{2,1},{3,2},{0,3},{5,4},{6,5},{7,6},{4,7},{9,8},{10,9},{11,1... | collective-permute-start | bytes 2162696 | tf_op jit(solution)/shard_map/ppermute | solution.py:20
  137.3 19.7 %collective-permute-start.26 = (bf16[256,1408]{1,0:T(8,128)(2,1)}, bf16[256,1408]{1,0:T(8,128)(2,1)S(1)}, u32[]{:S(2)}, u32[]{:S(2)}) collective-permute-start(bf16[256,1408]{1,0:T(8,128)(2,1)} %shard_map.86.refs_0_), channel_id=1, source_target_pairs={{3,0},{0,1},{1,2},{2,3},{7,4},{4,5},{5,6},{6,7},{11,8},{8,9},{9,10... | collective-permute-start | bytes 2162696 | tf_op jit(solution)/shard_map/ppermute | solution.py:20
  137.4 0.7 copy-start.13
  137.4 0.7 copy-start.14
  140.9 17.5 %collective-permute-start.17 = (bf16[256,1408]{1,0:T(8,128)(2,1)}, bf16[256,1408]{1,0:T(8,128)(2,1)S(1)}, u32[]{:S(2)}, u32[]{:S(2)}) collective-permute-start(bf16[256,1408]{1,0:T(8,128)(2,1)} %shard_map.85.refs_0_), channel_id=1, source_target_pairs={{4,0},{8,4},{12,8},{0,12},{5,1},{9,5},{13,9},{1,13},{6,2},{10,6},{... | collective-permute-start | bytes 2162696 | tf_op jit(solution)/shard_map/ppermute | solution.py:20
  144.0 18.8 %collective-permute-start.19 = (bf16[256,1408]{1,0:T(8,128)(2,1)}, bf16[256,1408]{1,0:T(8,128)(2,1)S(1)}, u32[]{:S(2)}, u32[]{:S(2)}) collective-permute-start(bf16[256,1408]{1,0:T(8,128)(2,1)} %shard_map.85.refs_0_), channel_id=1, source_target_pairs={{12,0},{0,4},{4,8},{8,12},{13,1},{1,5},{5,9},{9,13},{14,2},{2,6},{... | collective-permute-start | bytes 2162696 | tf_op jit(solution)/shard_map/ppermute | solution.py:20
  154.7 20.8 %copy-start.3 = (bf16[256,1408]{1,0:T(8,128)(2,1)}, bf16[256,1408]{1,0:T(8,128)(2,1)S(1)}, u32[]{:S(2)}) copy-start(bf16[256,1408]{1,0:T(8,128)(2,1)S(1)} %collective-permute-done.24.refs_1_) | copy-start | bytes 2162692
  155.5 20.0 %collective-permute-start.25 = (bf16[128,1408]{1,0:T(8,128)(2,1)}, bf16[128,1408]{1,0:T(8,128)(2,1)}, u32[]{:S(2)}, u32[]{:S(2)}) collective-permute-start(bf16[128,1408]{1,0:T(8,128)(2,1)} %slice.68), channel_id=1, source_target_pairs={{1,0},{2,1},{3,2},{0,3},{5,4},{6,5},{7,6},{4,7},{9,8},{10,9},{11,1... | collective-permute-start | bytes 1081352 | tf_op jit(solution)/shard_map/ppermute | solution.py:20
  157.0 18.6 %copy-start.4 = (bf16[256,1408]{1,0:T(8,128)(2,1)}, bf16[256,1408]{1,0:T(8,128)(2,1)S(1)}, u32[]{:S(2)}) copy-start(bf16[256,1408]{1,0:T(8,128)(2,1)S(1)} %collective-permute-done.26.refs_4_) | copy-start | bytes 2162692
  157.8 17.8 %collective-permute-start.27 = (bf16[128,1408]{1,0:T(8,128)(2,1)}, bf16[128,1408]{1,0:T(8,128)(2,1)}, u32[]{:S(2)}, u32[]{:S(2)}) collective-permute-start(bf16[128,1408]{1,0:T(8,128)(2,1)} %slice.69), channel_id=1, source_target_pairs={{3,0},{0,1},{1,2},{2,3},{7,4},{4,5},{5,6},{6,7},{11,8},{8,9},{9,10... | collective-permute-start | bytes 1081352 | tf_op jit(solution)/shard_map/ppermute | solution.py:20
  158.4 0.9 copy-start.5
  160.1 20.9 %collective-permute-start.18 = (bf16[128,1408]{1,0:T(8,128)(2,1)}, bf16[128,1408]{1,0:T(8,128)(2,1)}, u32[]{:S(2)}, u32[]{:S(2)}) collective-permute-start(bf16[128,1408]{1,0:T(8,128)(2,1)} %slice.66), channel_id=1, source_target_pairs={{4,0},{8,4},{12,8},{0,12},{5,1},{9,5},{13,9},{1,13},{6,2},{10,6},{... | collective-permute-start | bytes 1081352 | tf_op jit(solution)/shard_map/ppermute | solution.py:20
  162.8 0.9 copy-start.6
  164.5 16.5 %collective-permute-start.20 = (bf16[128,1408]{1,0:T(8,128)(2,1)}, bf16[128,1408]{1,0:T(8,128)(2,1)}, u32[]{:S(2)}, u32[]{:S(2)}) collective-permute-start(bf16[128,1408]{1,0:T(8,128)(2,1)} %slice.67), channel_id=1, source_target_pairs={{12,0},{0,4},{4,8},{8,12},{13,1},{1,5},{5,9},{9,13},{14,2},{2,6},{... | collective-permute-start | bytes 1081352 | tf_op jit(solution)/shard_map/ppermute | solution.py:20
  (1 other events, 0.7 us)
Sparse Core Ops, SparseCore 0:
  77.9 64.6 all-gather.1

commit v4 on v3

--- a/solution.py
+++ b/solution.py
@@ -71,93 +71,64 @@
     )(where, bases, after)
 
 
-def partial_kernel(where_ref, proj_ref, grads_ref, _, mine_ref, other_ref):
-    half = mine_ref.shape[2]
-    both = lax.dot_general(
-        proj_ref[...], grads_ref[0], (((0,), (0,)), ((), ())), preferred_element_type=F32
-    ).astype(BF16)
-    low, high = both[:, :half], both[:, half:]
-
-    @pl.when(where_ref[1] == 0)
-    def _():
-        mine_ref[0] = low
-        other_ref[0] = high
-
-    @pl.when(where_ref[1] == 1)
-    def _():
-        mine_ref[0] = high
-        other_ref[0] = low
-
-
-def partial_grads(where, proj, grads, which, after):
+def partial_kernel(where_ref, proj_ref, other_proj_ref, grads_ref, other_grads_ref, _, *outs):
+    step = pl.program_id(0)
+    proj = jnp.concatenate([proj_ref[...], other_proj_ref[...]], axis=0)
+    grads = jnp.concatenate([grads_ref[0], other_grads_ref[0]], axis=0)
+    total = lax.dot_general(proj, grads, (((0,), (0,)), ((), ())), preferred_element_type=F32)
+    span, width = total.shape[1], outs[0].shape[1]
+    later = pltpu.roll(total, width, 1)
+    total = jnp.where(where_ref[1] == 1, later, total)[:, :width]
+    for i, ref in enumerate(outs):
+
+        @pl.when(step == i)
+        def _(ref=ref):
+            ref[...] = total.astype(ref.dtype)
+
+
+def partial_grads(where, proj, other_proj, grads, other_grads, which, after):
     tokens, rank_part = proj.shape
     pair = grads.shape[2] // SIDE
-    out = held((SIDE, rank_part, pair // 2))
+    width = pair // 2
+    span = (width + LANES - 1) // LANES * LANES
+    skip = (pair - span) // LANES
+
+    def window(i, w):
+        block = (w[0] + i) & (SIDE - 1)
+        return which, 0, pl.multiple_of((block * (pair // LANES) + w[1] * skip) * LANES, LANES)
+
+    small = pl.BlockSpec((tokens, rank_part), lambda i, w: (0, 0))
+    large = pl.BlockSpec((pl.Element(1), pl.Element(tokens), pl.Element(span)), window)
     return pl.pallas_call(
         partial_kernel,
         grid_spec=pltpu.PrefetchScalarGridSpec(
             num_scalar_prefetch=1,
             grid=(SIDE,),
-            in_specs=[
-                pl.BlockSpec((tokens, rank_part), lambda i, w: (0, 0)),
-                pl.BlockSpec((1, tokens, pair), lambda i, w: (which, 0, (w[0] + i) % SIDE)),
-                ANYWHERE,
-            ],
-            out_specs=[pl.BlockSpec((1, rank_part, pair // 2), lambda i, w: (i, 0, 0))] * 2,
-        ),
-        out_shape=[out, out],
+            in_specs=[small, small, large, large, ANYWHERE],
+            out_specs=[pl.BlockSpec((rank_part, width), lambda i, w: (0, 0))] * SIDE,
+        ),
+        out_shape=[held((rank_part, width), F32)] + [held((rank_part, width))] * (SIDE - 1),
         compiler_params=PARAMS,
         cost_estimate=cost(
-            2 * tokens * rank_part * pair * SIDE, 2 * tokens * pair * SIDE + 2 * rank_part * pair * SIDE
-        ),
-    )(where, proj, grads, after)
-
-
-def sums_kernel(mine_ref, other_ref, near_ref, far_ref, via_ref, *, order):
-    for i, ref in zip(order, (near_ref, far_ref, via_ref)):
-        total = mine_ref[i].astype(F32) + other_ref[i].astype(F32)
-        ref[...] = total.astype(ref.dtype)
-
-
-def sums(mine, other, order):
-    _, rows, width = mine.shape
-    return pl.pallas_call(
-        functools.partial(sums_kernel, order=order),
-        out_shape=[held((rows, width)), held((rows, width)), held((rows, width), F32)],
-        compiler_params=PARAMS,
-        cost_estimate=cost(3 * rows * width, 20 * rows * width),
-    )(mine, other)
-
-
-def relay_kernel(one_ref, two_ref, _, out_ref):
-    out_ref[...] = (one_ref[...].astype(F32) + two_ref[...]).astype(BF16)
-
-
-def relay(one, two, after):
-    rows, width = one.shape
-    whole = pl.BlockSpec((rows, width), lambda: (0, 0))
-    return pl.pallas_call(
-        relay_kernel,
-        in_specs=[whole, whole, ANYWHERE],
-        out_specs=whole,
-        out_shape=held((rows, width)),
-        compiler_params=PARAMS,
-        cost_estimate=cost(rows * width, 8 * rows * width),
-    )(one, two, after)
+            4 * tokens * rank_part * width * SIDE, 4 * (tokens + rank_part) * width * SIDE
+        ),
+    )(where, proj, other_proj, grads, other_grads, after)
 
 
 def direction_kernel(*refs, pieces):
-    mine_ref, other_ref, one_ref, two_ref, first_ref, second_ref = refs[:6]
+    own_ref, first_ref, second_ref = refs[0], refs[4], refs[5]
     new_first_ref, new_second_ref = refs[-2 - pieces : -pieces]
-    gradient = mine_ref[0].astype(F32) + other_ref[0].astype(F32)
-    gradient = gradient + one_ref[...].astype(F32) + two_ref[...].astype(F32)
+    gradient = own_ref[...]
+    for ref in refs[1:4]:
+        gradient = gradient + ref[...].astype(F32)
     new_first = 0.9 * first_ref[0] + 0.1 * gradient
     new_second = 0.999 * second_ref[0] + 0.001 * gradient * gradient
     new_first_ref[0] = new_first
     new_second_ref[0] = new_second
     first_fix = 1.0 - 0.9**1000.0
     second_fix = 1.0 - 0.999**1000.0
-    direction = (new_first / first_fix / (jnp.sqrt(new_second / second_fix) + 1e-08)).astype(BF16)
+    root = jnp.sqrt(new_second * (1.0 / second_fix)) + 1e-08
+    direction = (new_first * (1.0 / first_fix) / root).astype(BF16)
     low = 0
     for ref in refs[-pieces:]:
         size = min(ref.shape[1], direction.shape[1] - low)
@@ -167,16 +138,15 @@
         low += size
 
 
-def directions(mine, other, one, two, first_moment, second_moment, which, pieces, before, after):
+def directions(own_sum, sums, first_moment, second_moment, which, pieces, before, after):
     _, rows, width = first_moment.shape
     cut = (width // pieces + LANES - 1) // LANES * LANES
-    tile = 16
-    zero = pl.BlockSpec((1, tile, width), lambda i: (0, i, 0))
+    tile = 32
     flat = pl.BlockSpec((tile, width), lambda i: (i, 0))
     own = pl.BlockSpec((1, tile, width), lambda i: (which, i, 0))
     half = pl.BlockSpec((tile, cut), lambda i: (i, 0))
-    in_specs = [zero, zero, flat, flat, own, own]
-    args = [mine, other, one, two, first_moment, second_moment]
+    in_specs = [flat] * SIDE + [own, own]
+    args = [own_sum, *sums, first_moment, second_moment]
     aliases = {len(args) + i: i for i in range(len(before))}
     args += [*before, after]
     in_specs += [ANYWHERE] * (len(before) + 1)
@@ -210,37 +180,67 @@
     )(*pieces)
 
 
-def expand_kernel(columns_ref, *refs, count):
-    pieces, out_ref = refs[:count], refs[-1]
-    width = pieces[0].shape[1]
-    for low in range(0, width, 256):
-        high = min(low + 256, width)
-        total, at = None, 0
-        for piece in pieces:
-            depth = piece.shape[0]
-            term = jnp.dot(
-                columns_ref[:, at : at + depth], piece[:, low:high], preferred_element_type=F32
+def expand_kernel(*refs, counts, which):
+    halves = len(counts)
+    out_ref, columns, pieces, outs, in_sems, out_sems = refs[-6:]
+    cut = pieces.shape[2]
+    loads, refs = [], list(refs)
+    for half, count in enumerate(counts):
+        loads.append([(refs.pop(0), columns.at[half])])
+        at = 0
+        for _ in range(count):
+            ref = refs.pop(0)
+            loads[half].append((ref, pieces.at[half, pl.ds(at, ref.shape[0])]))
+            at += ref.shape[0]
+    copies = [
+        [pltpu.make_async_copy(a, b, in_sems.at[half, i]) for i, (a, b) in enumerate(group)]
+        for half, group in enumerate(loads)
+    ]
+    for group in copies:
+        for copy in group:
+            copy.start()
+    stores = []
+    for half, group in enumerate(copies):
+        for copy in group:
+            copy.wait()
+        for low in range(0, cut, 256):
+            high = min(low + 256, cut)
+            total = jnp.dot(columns[half], pieces[half, :, low:high], preferred_element_type=F32)
+            outs[half, low:high, :] = total.T.astype(BF16)
+        size = min(cut, out_ref.shape[1] - half * cut)
+        stores.append(
+            pltpu.make_async_copy(
+                outs.at[half, pl.ds(0, size)],
+                out_ref.at[which, pl.ds(half * cut, size)],
+                out_sems.at[half],
             )
-            total = term if total is None else total + term
-            at += depth
-        out_ref[0, low:high, :] = total.T.astype(BF16)
-
-
-def expand_half(columns, pieces, which, place, update):
-    rows, ranks = columns.shape
-    cut = pieces[0].shape[1]
-    in_specs = [pl.BlockSpec((rows, ranks), lambda i: (0, 0))]
-    in_specs += [pl.BlockSpec(p.shape, lambda i: (0, 0)) for p in pieces]
-    return pl.pallas_call(
-        functools.partial(expand_kernel, count=len(pieces)),
-        grid=(1,),
-        in_specs=[*in_specs, ANYWHERE],
-        out_specs=pl.BlockSpec((1, cut, rows), lambda i: (which, place, 0)),
+        )
+        stores[-1].start()
+    for store in stores:
+        store.wait()
+
+
+def expand_halves(halves, which, update):
+    rows, ranks = halves[0][0].shape
+    cut = halves[0][1][0].shape[1]
+    counts = tuple(len(pieces) for _, pieces in halves)
+    args = [array for columns, pieces in halves for array in (columns, *pieces)]
+    return pl.pallas_call(
+        functools.partial(expand_kernel, counts=counts, which=which),
+        in_specs=[ANYWHERE] * (len(args) + 1),
+        out_specs=ANYWHERE,
         out_shape=jax.ShapeDtypeStruct(update.shape, BF16),
-        input_output_aliases={len(in_specs): 0},
-        compiler_params=PARAMS,
-        cost_estimate=cost(2 * rows * ranks * cut, 2 * (rows * ranks + ranks * cut + rows * cut)),
-    )(columns, *pieces, update)
+        scratch_shapes=[
+            pltpu.VMEM((len(halves), rows, ranks), BF16),
+            pltpu.VMEM((len(halves), ranks, cut), BF16),
+            pltpu.VMEM((len(halves), cut, rows), BF16),
+            pltpu.SemaphoreType.DMA((len(halves), max(counts) + 1)),
+            pltpu.SemaphoreType.DMA((len(halves),)),
+        ],
+        input_output_aliases={len(args): 0},
+        compiler_params=PARAMS,
+        cost_estimate=cost(4 * rows * ranks * cut, 4 * (rows * ranks + ranks * cut + rows * cut)),
+    )(*args, update)
 
 
 def expand_whole_kernel(bases_ref, gathered_ref, out_ref):
@@ -251,7 +251,7 @@
 
 def expand_whole(bases, gathered, which, width):
     count, rows, ranks = bases.shape
-    tile = 256
+    tile = gathered.shape[1] // 2
     return pl.pallas_call(
         expand_whole_kernel,
         grid=(gathered.shape[1] // tile,),
@@ -284,6 +284,8 @@
     features, ranks = bases.shape[1:]
     part = ranks // (SIDE * SIDE)
     width = first_moment.shape[2]
+
+    other_grads = swap_cores(out_grads)
 
     column = jnp.arange(ranks)
     slow, fast, inner = column // (SIDE * part), column // part % SIDE, column % part
@@ -300,31 +302,29 @@
             total = total + send(blocks[i], axis, i).astype(F32)
         partial = total.astype(BF16)
 
-    mine, other = partial_grads(where, partial[0], out_grads, 0, where)
-    other = swap_cores(other)
-    near, far, via = sums(mine, other, (3, 2, 1))
-    columns_y, columns_z = arrange(where, bases, 1, far)
-    near = send(near, "x", -1)
-    passed = relay(send(far, "x", 1), via, columns_y)
-    mine_1, other_1 = partial_grads(where, partial[1], out_grads, 1, passed)
-    passed = send(passed, "x", 1)
+    other_partial = swap_cores(partial)
+    own_sum, *sums = partial_grads(
+        where, partial[0], other_partial[0], out_grads, other_grads, 0, where
+    )
+    own_sum_1, *sums_1 = partial_grads(
+        where, partial[1], other_partial[1], out_grads, other_grads, 1, own_sum
+    )
+    columns_y, columns_z = arrange(where, bases, 1, own_sum_1)
+    sums = [send(value, "x", i + 1) for i, value in enumerate(sums)]
+    sums_1 = [send(value, "x", i + 1) for i, value in enumerate(sums_1)]
+
     *moments, whole = directions(
-        mine, other, near, passed, first_moment, second_moment, 0, 1, [], mine_1
+        own_sum, sums, first_moment, second_moment, 0, 1, [], columns_y
     )
     gathered = lax.all_gather(whole, ("y", "z"), axis=0, tiled=True)
 
-    other_1 = swap_cores(other_1)
-    near, far, via = sums(mine_1, other_1, (1, 2, 3))
-    near = send(near, "x", 1)
-    passed = send(relay(send(far, "x", -1), via, far), "x", -1)
     *moments, left, right = directions(
-        mine_1, other_1, near, passed, first_moment, second_moment, 1, 2, moments, passed
+        own_sum_1, sums_1, first_moment, second_moment, 1, 2, moments, columns_y
     )
     pieces_left = ring_gather(left, "y", "z")
     pieces_right = ring_gather(right, "z", "y")
     update = expand_whole(bases, gathered, 0, width)
-    update = expand_half(columns_z, pieces_left, 1, 0, update)
-    update = expand_half(columns_y, pieces_right, 1, 1, update)
+    update = expand_halves([(columns_z, pieces_left), (columns_y, pieces_right)], 1, update)
     return jnp.swapaxes(update, 1, 2), *moments
 
 

time: 194 us -> 175 us (0.902)
  Pallas kernels: 62.6 us -> 42.6 us
  starting transfers between devices: 33.6 us -> 46.3 us
  waiting for transfers between devices: 64.6 us -> 56.2 us
  local copies, waits for them, and re-layouts: 14.6 us -> 10.9 us
    pallas_call x6 -> x1, Pallas kernels: 20.9 us -> 7.09 us  [expand_halves(): pl.pallas_call(functools.partial(expand_kernel, counts=counts, which=whic...]
    ppermute x26, starting transfers between devices: 33.5 us -> 46.1 us  [receive(): lax.ppermute(value, axis, [((i + distance) % SIDE, i) for i in range(SIDE)])]
    ppermute x2, waiting for transfers between devices: 6.64 us -> 0.62 us  [swap_cores(): return lax.ppermute(value, 'c', [(0, 1), (1, 0)])]
    unnamed x40, local copies, waits for them, and re-layouts: 10.7 us -> 6.34 us
    pallas_call x1, Pallas kernels: 11 us -> 6.93 us  [expand_whole(): pl.pallas_call(expand_whole_kernel, grid=(gathered.shape[1] // tile,), in...]
    ppermute x26, waiting for transfers between devices: 58 us -> 55.6 us  [receive(): lax.ppermute(value, axis, [((i + distance) % SIDE, i) for i in range(SIDE)])]
    pallas_call x2, Pallas kernels: 8.18 us -> 6.21 us  [directions(): pl.pallas_call(functools.partial(direction_kernel, pieces=pieces), grid=(...]
  transfers between devices with their start and end apart: 29 -> 29, of which waited for: 14 -> 15; matrix products, arithmetic and copies ran while one was open for 2% -> 5% of each run, Pallas kernels for 23% -> 15%
where the time goes in v4:
time: 175 us; the launch traced here: 174 us
  waiting for transfers between devices  56.2 us (32%)
  starting transfers between devices  46.3 us (26%)
  Pallas kernels  42.6 us (24%)
  between operations  14.2 us (8%)
  local copies, waits for them, and re-layouts  10.9 us (6%)
  matrix products  2.9 us (2%)
    ppermute x26, waiting for transfers between devices, receive(): lax.ppermute(value, axis, [((i + distance) % SIDE, i) for i in range(SIDE)])  55.6 us
    ppermute x26, starting transfers between devices, receive(): lax.ppermute(value, axis, [((i + distance) % SIDE, i) for i in range(SIDE)])  46.1 us
    pallas_call x2, Pallas kernels, partial_grads(): pl.pallas_call(partial_kernel, grid_spec=pltpu.PrefetchScalarGridSpec(num...  12.7 us
    pallas_call x1, Pallas kernels, expand_halves(): pl.pallas_call(functools.partial(expand_kernel, counts=counts, which=whic...  7.09 us
    pallas_call x1, Pallas kernels, expand_whole(): pl.pallas_call(expand_whole_kernel, grid=(gathered.shape[1] // tile,), in...  6.93 us
    unnamed x40, local copies, waits for them, and re-layouts  6.34 us
    pallas_call x2, Pallas kernels, directions(): pl.pallas_call(functools.partial(direction_kernel, pieces=pieces), grid=(...  6.21 us
    pallas_call x1, Pallas kernels, arrange(): pl.pallas_call(arrange_kernel, grid_spec=pltpu.PrefetchScalarGridSpec(num...  5.31 us
  transfers between devices with their start and end apart: 29, of which 15 were waited for; matrix products, arithmetic and copies ran while one was open for 5% of the time, Pallas kernels for 15%

profile of v4, /device:TPU:0, one launch (start us, length us, event | category | flops | bytes accessed | tf_op | source)
XLA Modules:
  0.0 173.9 jit_solution(1547990459814960414)
XLA Ops:
  7.3 1.4 copy-done
  8.8 2.9 %fusion.4 = bf16[2,128,1024]{2,1,0:T(8,128)(2,1)S(1)} fusion(s32[1024]{0:T(1024)S(1)} %fusion.21, bf16[2,512,1024]{2,1,0:T(8,128)(2,1)} %bases_ref.3, bf16[128,8192]{1,0:T(8,128)(2,1)S(1)} %copy-done, s32[]{:T(128)S(6)} %select_n.54), kind=kOutput, calls=%fused_computation.4 | convolution fusion | flops 806879232 | bytes 2756612 | tf_op jit(solution)/shard_map/ktr,rs->kts/dot_general | solution.py:296
  11.7 1.7 collective-permute-start
  13.4 2.9 %collective-permute-start.2 = (bf16[2,128,256]{2,1,0:T(8,128)(2,1)S(1)}, bf16[2,128,256]{2,1,0:T(8,128)(2,1)S(1)}, u32[]{:S(2)}, u32[]{:S(2)}) collective-permute-start(bf16[2,128,256]{2,1,0:T(8,128)(2,1)S(1)} %get-tuple-element.38), channel_id=1, source_target_pairs={{8,0},{12,4},{0,8},{4,12},{9,1},{13,5},{1,9},{5,13},{10,2},{14,6},... | collective-permute-start | bytes 393224 | tf_op jit(solution)/shard_map/ppermute | solution.py:20
  16.3 1.3 collective-permute-start.1
  18.4 4.0 %collective-permute-done.2 = bf16[2,128,256]{2,1,0:T(8,128)(2,1)S(1)} collective-permute-done((bf16[2,128,256]{2,1,0:T(8,128)(2,1)S(1)}, bf16[2,128,256]{2,1,0:T(8,128)(2,1)S(1)}, u32[]{:S(2)}, u32[]{:S(2)}) %collective-permute-start.2) | collective-permute-done | bytes 131104 | tf_op jit(solution)/shard_map/ppermute | solution.py:20
  22.5 2.0 %collective-permute-start.3 = (bf16[2,128,64]{2,1,0:T(8,128)(2,1)S(1)}, bf16[2,128,64]{2,1,0:T(8,128)(2,1)S(1)}, u32[]{:S(2)}, u32[]{:S(2)}) collective-permute-start(bf16[2,128,64]{2,1,0:T(8,128)(2,1)S(1)} %get-tuple-element.40), channel_id=1, source_target_pairs={{3,0},{0,1},{1,2},{2,3},{7,4},{4,5},{5,6},{6,7},{11,8},{8,9},{9,10... | collective-permute-start | bytes 98312 | tf_op jit(solution)/shard_map/ppermute | solution.py:20
  24.5 3.6 %collective-permute-start.5 = (bf16[2,128,64]{2,1,0:T(8,128)(2,1)S(1)}, bf16[2,128,64]{2,1,0:T(8,128)(2,1)S(1)}, u32[]{:S(2)}, u32[]{:S(2)}) collective-permute-start(bf16[2,128,64]{2,1,0:T(8,128)(2,1)S(1)} %get-tuple-element.41), channel_id=1, source_target_pairs={{2,0},{3,1},{0,2},{1,3},{6,4},{7,5},{4,6},{5,7},{10,8},{11,9},{8,1... | collective-permute-start | bytes 98312 | tf_op jit(solution)/shard_map/ppermute | solution.py:20
  28.1 1.0 collective-permute-start.4
  29.8 1.3 collective-permute-done.5
  31.1 1.3 collective-permute-done.4
  34.4 6.4 %shard_map.76 = (f32[64,2752]{1,0:T(8,128)}, bf16[64,2752]{1,0:T(8,128)(2,1)}, bf16[64,2752]{1,0:T(8,128)(2,1)}, bf16[64,2752]{1,0:T(8,128)(2,1)}) custom-call(s32[4]{0:T(128)} %pad_add_fusion.where_ref._, bf16[128,64]{1,0:T(8,128)(2,1)} %get-tuple-element.45.proj_ref, bf16[128,64]{1,0:T(8,128)(2,1)} %get-tuple-element.43.other_proj_ref, ...), custom_call_target="tpu_custom_call" | custom-call | flops 360710144 | bytes 8454144 | tf_op jit(solution)/shard_map/pallas_call | solution.py:102
  40.7 1.5 collective-permute-start.11
  42.2 2.7 %collective-permute-start.12 = (bf16[64,2752]{1,0:T(8,128)(2,1)}, bf16[64,2752]{1,0:T(8,128)(2,1)S(1)}, u32[]{:S(2)}, u32[]{:S(2)}) collective-permute-start(bf16[64,2752]{1,0:T(8,128)(2,1)} %get-tuple-element.27), channel_id=1, source_target_pairs={{64,0},{96,32},{0,64},{32,96},{65,1},{97,33},{1,65},{33,97},{66,2}... | collective-permute-start | bytes 1056776 | tf_op jit(solution)/shard_map/ppermute | solution.py:20
  45.0 1.4 collective-permute-start.13
  46.4 6.4 %shard_map.77 = (f32[64,2752]{1,0:T(8,128)}, bf16[64,2752]{1,0:T(8,128)(2,1)}, bf16[64,2752]{1,0:T(8,128)(2,1)}, bf16[64,2752]{1,0:T(8,128)(2,1)}) custom-call(s32[4]{0:T(128)} %pad_add_fusion.where_ref._, bf16[128,64]{1,0:T(8,128)(2,1)} %get-tuple-element.46.proj_ref, bf16[128,64]{1,0:T(8,128)(2,1)} %get-tuple-element.44.other_proj_ref, ...), custom_call_target="tpu_custom_call" | custom-call | flops 360710144 | bytes 8454144 | tf_op jit(solution)/shard_map/pallas_call | solution.py:102
  52.8 5.3 %shard_map.78 = (bf16[512,1024]{1,0:T(8,128)(2,1)}, bf16[512,1024]{1,0:T(8,128)(2,1)}) custom-call(s32[4]{0:T(128)} %pad_add_fusion.where_ref._, bf16[2,512,1024]{2,1,0:T(8,128)(2,1)} %bases_ref.3, f32[64,2752]{1,0:T(8,128)} %get-tuple-element.21._.refs_0_), custom_call_target="tpu_custom_call" | custom-call | flops 2147483648 | bytes 3145728 | tf_op jit(solution)/shard_map/pallas_call | solution.py:60
  58.1 3.3 %collective-permute-done.12.refs_2_ = bf16[64,2752]{1,0:T(8,128)(2,1)S(1)} collective-permute-done((bf16[64,2752]{1,0:T(8,128)(2,1)}, bf16[64,2752]{1,0:T(8,128)(2,1)S(1)}, u32[]{:S(2)}, u32[]{:S(2)}) %collective-permute-start.12) | collective-permute-done | bytes 352288 | tf_op jit(solution)/shard_map/ppermute | solution.py:20
  62.2 3.1 %shard_map.79 = (f32[2,64,2752]{2,1,0:T(8,128)}, f32[2,64,2752]{2,1,0:T(8,128)}, bf16[64,2816]{1,0:T(8,128)(2,1)}) custom-call(f32[64,2752]{1,0:T(8,128)} %get-tuple-element.20._.refs_0_, bf16[64,2752]{1,0:T(8,128)(2,1)} %copy-done.8, bf16[64,2752]{1,0:T(8,128)(2,1)} %copy-done.9, bf16[64,2752]{1,0:T(8,128)(2,1)} %copy-done.10, f32[2,64,2752]{2,1,0:T(8,128)} %refs_4_.3, ...), custom_call_target="tpu_custom_call" | custom-call | flops 5283840 | bytes 4579328 | tf_op jit(solution)/shard_map/pallas_call | solution.py:155
  65.4 1.3 collective-permute-start.8
  66.7 2.4 %collective-permute-start.9 = (bf16[64,2752]{1,0:T(8,128)(2,1)S(1)}, bf16[64,2752]{1,0:T(8,128)(2,1)S(1)}, u32[]{:S(2)}, u32[]{:S(2)}) collective-permute-start(bf16[64,2752]{1,0:T(8,128)(2,1)S(1)} %copy-done.18), channel_id=1, source_target_pairs={{64,0},{96,32},{0,64},{32,96},{65,1},{97,33},{1,65},{33,97},{66,2}... | collective-permute-start | bytes 1056776 | tf_op jit(solution)/shard_map/ppermute | solution.py:20
  69.1 1.6 collective-permute-start.10
  70.6 5.7 %collective-permute-done.8.refs_1_ = bf16[64,2752]{1,0:T(8,128)(2,1)S(1)} collective-permute-done((bf16[64,2752]{1,0:T(8,128)(2,1)S(1)}, bf16[64,2752]{1,0:T(8,128)(2,1)S(1)}, u32[]{:S(2)}, u32[]{:S(2)}) %collective-permute-start.8) | collective-permute-done | bytes 352288 | tf_op jit(solution)/shard_map/ppermute | solution.py:20
  76.3 8.8 %collective-permute-done.9.refs_2_ = bf16[64,2752]{1,0:T(8,128)(2,1)S(1)} collective-permute-done((bf16[64,2752]{1,0:T(8,128)(2,1)S(1)}, bf16[64,2752]{1,0:T(8,128)(2,1)S(1)}, u32[]{:S(2)}, u32[]{:S(2)}) %collective-permute-start.9) | collective-permute-done | bytes 352288 | tf_op jit(solution)/shard_map/ppermute | solution.py:20
  85.1 0.8 copy-done.6
  86.0 3.1 %shard_map.80 = (f32[2,64,2752]{2,1,0:T(8,128)}, f32[2,64,2752]{2,1,0:T(8,128)}, bf16[64,1408]{1,0:T(8,128)(2,1)}, bf16[64,1408]{1,0:T(8,128)(2,1)}) custom-call(f32[64,2752]{1,0:T(8,128)} %get-tuple-element.21._.refs_0_, bf16[64,2752]{1,0:T(8,128)(2,1)} %copy-done.5, bf16[64,2752]{1,0:T(8,128)(2,1)} %copy-done.6, ...), custom_call_target="tpu_custom_call", output_to_operand_aliasing={{0}: (6, {}), {1}: (7, {})} | custom-call | flops 5283840 | bytes 4579328 | tf_op jit(solution)/shard_map/pallas_call | solution.py:155
  89.3 3.4 %collective-permute-start.22 = (bf16[64,1408]{1,0:T(8,128)(2,1)}, bf16[64,1408]{1,0:T(8,128)(2,1)S(1)}, u32[]{:S(2)}, u32[]{:S(2)}) collective-permute-start(bf16[64,1408]{1,0:T(8,128)(2,1)} %get-tuple-element.33.refs_0_), channel_id=1, source_target_pairs={{2,0},{3,1},{0,2},{1,3},{6,4},{7,5},{4,6},{5,7},{10,8},{11,9},{8,1... | collective-permute-start | bytes 540680 | tf_op jit(solution)/shard_map/ppermute | solution.py:20
  93.3 1.2 collective-permute-start.16
  94.5 2.4 %collective-permute-start.15 = (bf16[64,1408]{1,0:T(8,128)(2,1)}, bf16[64,1408]{1,0:T(8,128)(2,1)S(1)}, u32[]{:S(2)}, u32[]{:S(2)}) collective-permute-start(bf16[64,1408]{1,0:T(8,128)(2,1)} %get-tuple-element.32.refs_0_), channel_id=1, source_target_pairs={{8,0},{12,4},{0,8},{4,12},{9,1},{13,5},{1,9},{5,13},{10,2},{14,6},... | collective-permute-start | bytes 540680 | tf_op jit(solution)/shard_map/ppermute | solution.py:20
  97.6 2.1 %collective-permute-start.14 = (bf16[64,1408]{1,0:T(8,128)(2,1)}, bf16[64,1408]{1,0:T(8,128)(2,1)S(1)}, u32[]{:S(2)}, u32[]{:S(2)}) collective-permute-start(bf16[64,1408]{1,0:T(8,128)(2,1)} %get-tuple-element.32.refs_0_), channel_id=1, source_target_pairs={{4,0},{8,4},{12,8},{0,12},{5,1},{9,5},{13,9},{1,13},{6,2},{10,6},{... | collective-permute-start | bytes 540680 | tf_op jit(solution)/shard_map/ppermute | solution.py:20
  100.5 3.5 %collective-permute-done.21.refs_1_ = bf16[64,1408]{1,0:T(8,128)(2,1)S(1)} collective-permute-done((bf16[64,1408]{1,0:T(8,128)(2,1)}, bf16[64,1408]{1,0:T(8,128)(2,1)S(1)}, u32[]{:S(2)}, u32[]{:S(2)}) %collective-permute-start.21) | collective-permute-done | bytes 180256 | tf_op jit(solution)/shard_map/ppermute | solution.py:20
  104.6 2.2 %shard_map.82.refs_7_ = bf16[256,1408]{1,0:T(8,128)(2,1)} custom-call(bf16[64,1408]{1,0:T(8,128)(2,1)} %get-tuple-element.33.refs_0_, bf16[64,1408]{1,0:T(8,128)(2,1)} %copy-done.16, bf16[64,1408]{1,0:T(8,128)(2,1)} %copy-done.15, bf16[64,1408]{1,0:T(8,128)(2,1)} %copy-done.14), custom_call_target="tpu_custom_call" | custom-call | bytes 1441792 | tf_op jit(solution)/shard_map/pallas_call | solution.py:175
  107.4 2.7 %collective-permute-start.24 = (bf16[256,1408]{1,0:T(8,128)(2,1)}, bf16[256,1408]{1,0:T(8,128)(2,1)S(1)}, u32[]{:S(2)}, u32[]{:S(2)}) collective-permute-start(bf16[256,1408]{1,0:T(8,128)(2,1)} %shard_map.82.refs_7_), channel_id=1, source_target_pairs={{4,0},{8,4},{12,8},{0,12},{5,1},{9,5},{13,9},{1,13},{6,2},{10,6},{... | collective-permute-start | bytes 2162696 | tf_op jit(solution)/shard_map/ppermute | solution.py:20
  110.4 2.8 %collective-permute-done.14.refs_1_ = bf16[64,1408]{1,0:T(8,128)(2,1)S(1)} collective-permute-done((bf16[64,1408]{1,0:T(8,128)(2,1)}, bf16[64,1408]{1,0:T(8,128)(2,1)S(1)}, u32[]{:S(2)}, u32[]{:S(2)}) %collective-permute-start.14) | collective-permute-done | bytes 180256 | tf_op jit(solution)/shard_map/ppermute | solution.py:20
  113.8 2.1 %shard_map.81.refs_1_ = bf16[256,1408]{1,0:T(8,128)(2,1)} custom-call(bf16[64,1408]{1,0:T(8,128)(2,1)} %get-tuple-element.32.refs_0_, bf16[64,1408]{1,0:T(8,128)(2,1)} %copy-done.13, bf16[64,1408]{1,0:T(8,128)(2,1)} %copy-done.12, bf16[64,1408]{1,0:T(8,128)(2,1)} %copy-done.11), custom_call_target="tpu_custom_call" | custom-call | bytes 1441792 | tf_op jit(solution)/shard_map/pallas_call | solution.py:175
  116.0 1.9 %collective-permute-start.19 = (bf16[256,1408]{1,0:T(8,128)(2,1)}, bf16[256,1408]{1,0:T(8,128)(2,1)S(1)}, u32[]{:S(2)}, u32[]{:S(2)}) collective-permute-start(bf16[256,1408]{1,0:T(8,128)(2,1)} %shard_map.81.refs_1_), channel_id=1, source_target_pairs={{3,0},{0,1},{1,2},{2,3},{7,4},{4,5},{5,6},{6,7},{11,8},{8,9},{9,10... | collective-permute-start | bytes 2162696 | tf_op jit(solution)/shard_map/ppermute | solution.py:20
  117.8 1.4 collective-permute-start.17
  119.2 22.4 %collective-permute-done.26.refs_11_ = bf16[256,1408]{1,0:T(8,128)(2,1)S(1)} collective-permute-done((bf16[256,1408]{1,0:T(8,128)(2,1)}, bf16[256,1408]{1,0:T(8,128)(2,1)S(1)}, u32[]{:S(2)}, u32[]{:S(2)}) %collective-permute-start.26) | collective-permute-done | bytes 720928 | tf_op jit(solution)/shard_map/ppermute | solution.py:20
  141.5 0.8 slice.79
  142.5 0.8 slice.78
  143.4 3.1 %collective-permute-start.25 = (bf16[128,1408]{1,0:T(8,128)(2,1)}, bf16[128,1408]{1,0:T(8,128)(2,1)}, u32[]{:S(2)}, u32[]{:S(2)}) collective-permute-start(bf16[128,1408]{1,0:T(8,128)(2,1)} %slice.78), channel_id=1, source_target_pairs={{4,0},{8,4},{12,8},{0,12},{5,1},{9,5},{13,9},{1,13},{6,2},{10,6},{... | collective-permute-start | bytes 1081352 | tf_op jit(solution)/shard_map/ppermute | solution.py:20
  146.4 0.9 copy-done.3
  147.3 0.8 slice.77
  148.1 0.9 copy-done.4
  149.0 0.8 slice.76
  149.7 3.2 %collective-permute-start.18 = (bf16[128,1408]{1,0:T(8,128)(2,1)}, bf16[128,1408]{1,0:T(8,128)(2,1)}, u32[]{:S(2)}, u32[]{:S(2)}) collective-permute-start(bf16[128,1408]{1,0:T(8,128)(2,1)} %slice.76), channel_id=1, source_target_pairs={{1,0},{2,1},{3,2},{0,3},{5,4},{6,5},{7,6},{4,7},{9,8},{10,9},{11,1... | collective-permute-start | bytes 1081352 | tf_op jit(solution)/shard_map/ppermute | solution.py:20
  152.9 6.9 %shard_map.83.refs_12_ = bf16[2,2752,512]{2,1,0:T(8,128)(2,1)} custom-call(bf16[2,512,1024]{2,1,0:T(8,128)(2,1)} %bases_ref.3, bf16[1024,2816]{1,0:T(8,128)(2,1)} %all-gather.2.cloned.1.call-done.gathered_ref), custom_call_target="tpu_custom_call" | custom-call | flops 2885681152 | bytes 9502720 | tf_op jit(solution)/shard_map/pallas_call | solution.py:255
  159.9 7.1 %shard_map.84 = bf16[2,2752,512]{2,1,0:T(8,128)(2,1)} custom-call(bf16[512,1024]{1,0:T(8,128)(2,1)} %get-tuple-element.22.refs_0_, bf16[256,1408]{1,0:T(8,128)(2,1)} %shard_map.81.refs_1_, bf16[256,1408]{1,0:T(8,128)(2,1)} %copy-done.4, bf16[128,1408]{1,0:T(8,128)(2,1)} %collective-permute-done.18.refs_3_, ...), custom_call_target="tpu_custom_call", output_to_operand_aliasing={{}: (12, {})} | custom-call | flops 2952790016 | bytes 10747904 | tf_op jit(solution)/shard_map/pallas_call | solution.py:228
  (73 shorter events, 9.5 us)
Async XLA Ops:
  7.2 1.6 copy-start
  7.2 145.8 %all-gather.2.cloned.1.call-start = ((), (), s32[]{:S(2)}) async-start(), calls=%async_computation | async-start | bytes 6127616 | tf_op jit(solution)/shard_map/all_gather | solution.py:319
  7.2 27.2 %collective-permute-start.7 = (bf16[2,128,22016]{2,1,0:T(8,128)(2,1)}, bf16[2,128,22016]{2,1,0:T(8,128)(2,1)}, u32[]{:S(2)}, u32[]{:S(2)}) collective-permute-start(bf16[2,128,22016]{2,1,0:T(8,128)(2,1)} %grads_ref.3), channel_id=1, source_target_pairs={{0,16},{16,0},{1,17},{17,1},{2,18},{18,2},{3,19},{19,3},{4,20},{20... | collective-permute-start | bytes 33816584 | tf_op jit(solution)/shard_map/ppermute | solution.py:28
  11.7 6.7 %collective-permute-start = (bf16[2,128,256]{2,1,0:T(8,128)(2,1)S(1)}, bf16[2,128,256]{2,1,0:T(8,128)(2,1)S(1)}, u32[]{:S(2)}, u32[]{:S(2)}) collective-permute-start(bf16[2,128,256]{2,1,0:T(8,128)(2,1)S(1)} %get-tuple-element.37), channel_id=1, source_target_pairs={{12,0},{0,4},{4,8},{8,12},{13,1},{1,5},{5,9},{9,13},{14,2},{2,6},{... | collective-permute-start | bytes 393224 | tf_op jit(solution)/shard_map/ppermute | solution.py:20
  13.4 8.9 %collective-permute-start.2 = (bf16[2,128,256]{2,1,0:T(8,128)(2,1)S(1)}, bf16[2,128,256]{2,1,0:T(8,128)(2,1)S(1)}, u32[]{:S(2)}, u32[]{:S(2)}) collective-permute-start(bf16[2,128,256]{2,1,0:T(8,128)(2,1)S(1)} %get-tuple-element.38), channel_id=1, source_target_pairs={{8,0},{12,4},{0,8},{4,12},{9,1},{13,5},{1,9},{5,13},{10,2},{14,6},... | collective-permute-start | bytes 393224 | tf_op jit(solution)/shard_map/ppermute | solution.py:20
  16.3 6.0 %collective-permute-start.1 = (bf16[2,128,256]{2,1,0:T(8,128)(2,1)S(1)}, bf16[2,128,256]{2,1,0:T(8,128)(2,1)S(1)}, u32[]{:S(2)}, u32[]{:S(2)}) collective-permute-start(bf16[2,128,256]{2,1,0:T(8,128)(2,1)S(1)} %get-tuple-element.39), channel_id=1, source_target_pairs={{4,0},{8,4},{12,8},{0,12},{5,1},{9,5},{13,9},{1,13},{6,2},{10,6},{... | collective-permute-start | bytes 393224 | tf_op jit(solution)/shard_map/ppermute | solution.py:20
  22.5 7.2 %collective-permute-start.3 = (bf16[2,128,64]{2,1,0:T(8,128)(2,1)S(1)}, bf16[2,128,64]{2,1,0:T(8,128)(2,1)S(1)}, u32[]{:S(2)}, u32[]{:S(2)}) collective-permute-start(bf16[2,128,64]{2,1,0:T(8,128)(2,1)S(1)} %get-tuple-element.40), channel_id=1, source_target_pairs={{3,0},{0,1},{1,2},{2,3},{7,4},{4,5},{5,6},{6,7},{11,8},{8,9},{9,10... | collective-permute-start | bytes 98312 | tf_op jit(solution)/shard_map/ppermute | solution.py:20
  24.5 6.5 %collective-permute-start.5 = (bf16[2,128,64]{2,1,0:T(8,128)(2,1)S(1)}, bf16[2,128,64]{2,1,0:T(8,128)(2,1)S(1)}, u32[]{:S(2)}, u32[]{:S(2)}) collective-permute-start(bf16[2,128,64]{2,1,0:T(8,128)(2,1)S(1)} %get-tuple-element.41), channel_id=1, source_target_pairs={{2,0},{3,1},{0,2},{1,3},{6,4},{7,5},{4,6},{5,7},{10,8},{11,9},{8,1... | collective-permute-start | bytes 98312 | tf_op jit(solution)/shard_map/ppermute | solution.py:20
  28.1 4.3 %collective-permute-start.4 = (bf16[2,128,64]{2,1,0:T(8,128)(2,1)S(1)}, bf16[2,128,64]{2,1,0:T(8,128)(2,1)S(1)}, u32[]{:S(2)}, u32[]{:S(2)}) collective-permute-start(bf16[2,128,64]{2,1,0:T(8,128)(2,1)S(1)} %get-tuple-element.42), channel_id=1, source_target_pairs={{1,0},{2,1},{3,2},{0,3},{5,4},{6,5},{7,6},{4,7},{9,8},{10,9},{11,1... | collective-permute-start | bytes 98312 | tf_op jit(solution)/shard_map/ppermute | solution.py:20
  32.4 1.3 collective-permute-start.6
  40.7 17.3 %collective-permute-start.11 = (bf16[64,2752]{1,0:T(8,128)(2,1)}, bf16[64,2752]{1,0:T(8,128)(2,1)S(1)}, u32[]{:S(2)}, u32[]{:S(2)}) collective-permute-start(bf16[64,2752]{1,0:T(8,128)(2,1)} %get-tuple-element.26), channel_id=1, source_target_pairs={{96,0},{0,32},{32,64},{64,96},{97,1},{1,33},{33,65},{65,97},{98,2}... | collective-permute-start | bytes 1056776 | tf_op jit(solution)/shard_map/ppermute | solution.py:20
  42.2 19.1 %collective-permute-start.12 = (bf16[64,2752]{1,0:T(8,128)(2,1)}, bf16[64,2752]{1,0:T(8,128)(2,1)S(1)}, u32[]{:S(2)}, u32[]{:S(2)}) collective-permute-start(bf16[64,2752]{1,0:T(8,128)(2,1)} %get-tuple-element.27), channel_id=1, source_target_pairs={{64,0},{96,32},{0,64},{32,96},{65,1},{97,33},{1,65},{33,97},{66,2}... | collective-permute-start | bytes 1056776 | tf_op jit(solution)/shard_map/ppermute | solution.py:20
  45.0 16.4 %collective-permute-start.13 = (bf16[64,2752]{1,0:T(8,128)(2,1)}, bf16[64,2752]{1,0:T(8,128)(2,1)S(1)}, u32[]{:S(2)}, u32[]{:S(2)}) collective-permute-start(bf16[64,2752]{1,0:T(8,128)(2,1)} %get-tuple-element.28), channel_id=1, source_target_pairs={{32,0},{64,32},{96,64},{0,96},{33,1},{65,33},{97,65},{1,97},{34,2}... | collective-permute-start | bytes 1056776 | tf_op jit(solution)/shard_map/ppermute | solution.py:20
  58.1 3.3 %copy-start.8 = (bf16[64,2752]{1,0:T(8,128)(2,1)}, bf16[64,2752]{1,0:T(8,128)(2,1)S(1)}, u32[]{:S(2)}) copy-start(bf16[64,2752]{1,0:T(8,128)(2,1)S(1)} %collective-permute-done.11.refs_1_) | copy-start | bytes 1056772
  61.3 0.8 copy-start.9
  61.3 0.9 copy-start.10
  62.2 3.2 %copy-start.19 = (bf16[64,2752]{1,0:T(8,128)(2,1)S(1)}, bf16[64,2752]{1,0:T(8,128)(2,1)}, u32[]{:S(2)}) copy-start(bf16[64,2752]{1,0:T(8,128)(2,1)} %get-tuple-element.23) | copy-start | bytes 1056772
  62.2 4.4 %copy-start.18 = (bf16[64,2752]{1,0:T(8,128)(2,1)S(1)}, bf16[64,2752]{1,0:T(8,128)(2,1)}, u32[]{:S(2)}) copy-start(bf16[64,2752]{1,0:T(8,128)(2,1)} %get-tuple-element.24) | copy-start | bytes 1056772
  62.2 6.8 %copy-start.17 = (bf16[64,2752]{1,0:T(8,128)(2,1)S(1)}, bf16[64,2752]{1,0:T(8,128)(2,1)}, u32[]{:S(2)}) copy-start(bf16[64,2752]{1,0:T(8,128)(2,1)} %get-tuple-element.25) | copy-start | bytes 1056772
  65.4 10.9 %collective-permute-start.8 = (bf16[64,2752]{1,0:T(8,128)(2,1)S(1)}, bf16[64,2752]{1,0:T(8,128)(2,1)S(1)}, u32[]{:S(2)}, u32[]{:S(2)}) collective-permute-start(bf16[64,2752]{1,0:T(8,128)(2,1)S(1)} %copy-done.19), channel_id=1, source_target_pairs={{96,0},{0,32},{32,64},{64,96},{97,1},{1,33},{33,65},{65,97},{98,2}... | collective-permute-start | bytes 1056776 | tf_op jit(solution)/shard_map/ppermute | solution.py:20
  66.7 18.4 %collective-permute-start.9 = (bf16[64,2752]{1,0:T(8,128)(2,1)S(1)}, bf16[64,2752]{1,0:T(8,128)(2,1)S(1)}, u32[]{:S(2)}, u32[]{:S(2)}) collective-permute-start(bf16[64,2752]{1,0:T(8,128)(2,1)S(1)} %copy-done.18), channel_id=1, source_target_pairs={{64,0},{96,32},{0,64},{32,96},{65,1},{97,33},{1,65},{33,97},{66,2}... | collective-permute-start | bytes 1056776 | tf_op jit(solution)/shard_map/ppermute | solution.py:20
  69.1 16.0 %collective-permute-start.10 = (bf16[64,2752]{1,0:T(8,128)(2,1)S(1)}, bf16[64,2752]{1,0:T(8,128)(2,1)S(1)}, u32[]{:S(2)}, u32[]{:S(2)}) collective-permute-start(bf16[64,2752]{1,0:T(8,128)(2,1)S(1)} %copy-done.17), channel_id=1, source_target_pairs={{32,0},{64,32},{96,64},{0,96},{33,1},{65,33},{97,65},{1,97},{34,2}... | collective-permute-start | bytes 1056776 | tf_op jit(solution)/shard_map/ppermute | solution.py:20
  76.3 8.8 %copy-start.5 = (bf16[64,2752]{1,0:T(8,128)(2,1)}, bf16[64,2752]{1,0:T(8,128)(2,1)S(1)}, u32[]{:S(2)}) copy-start(bf16[64,2752]{1,0:T(8,128)(2,1)S(1)} %collective-permute-done.8.refs_1_) | copy-start | bytes 1056772
  85.1 0.8 copy-start.6
  85.1 0.9 copy-start.7
  89.1 8.5 %collective-permute-start.23 = (bf16[64,1408]{1,0:T(8,128)(2,1)}, bf16[64,1408]{1,0:T(8,128)(2,1)S(1)}, u32[]{:S(2)}, u32[]{:S(2)}) collective-permute-start(bf16[64,1408]{1,0:T(8,128)(2,1)} %get-tuple-element.33.refs_0_), channel_id=1, source_target_pairs={{3,0},{0,1},{1,2},{2,3},{7,4},{4,5},{5,6},{6,7},{11,8},{8,9},{9,10... | collective-permute-start | bytes 540680 | tf_op jit(solution)/shard_map/ppermute | solution.py:20
  89.3 11.1 %collective-permute-start.22 = (bf16[64,1408]{1,0:T(8,128)(2,1)}, bf16[64,1408]{1,0:T(8,128)(2,1)S(1)}, u32[]{:S(2)}, u32[]{:S(2)}) collective-permute-start(bf16[64,1408]{1,0:T(8,128)(2,1)} %get-tuple-element.33.refs_0_), channel_id=1, source_target_pairs={{2,0},{3,1},{0,2},{1,3},{6,4},{7,5},{4,6},{5,7},{10,8},{11,9},{8,1... | collective-permute-start | bytes 540680 | tf_op jit(solution)/shard_map/ppermute | solution.py:20
  92.8 11.2 %collective-permute-start.21 = (bf16[64,1408]{1,0:T(8,128)(2,1)}, bf16[64,1408]{1,0:T(8,128)(2,1)S(1)}, u32[]{:S(2)}, u32[]{:S(2)}) collective-permute-start(bf16[64,1408]{1,0:T(8,128)(2,1)} %get-tuple-element.33.refs_0_), channel_id=1, source_target_pairs={{1,0},{2,1},{3,2},{0,3},{5,4},{6,5},{7,6},{4,7},{9,8},{10,9},{11,1... | collective-permute-start | bytes 540680 | tf_op jit(solution)/shard_map/ppermute | solution.py:20
  93.3 16.8 %collective-permute-start.16 = (bf16[64,1408]{1,0:T(8,128)(2,1)}, bf16[64,1408]{1,0:T(8,128)(2,1)S(1)}, u32[]{:S(2)}, u32[]{:S(2)}) collective-permute-start(bf16[64,1408]{1,0:T(8,128)(2,1)} %get-tuple-element.32.refs_0_), channel_id=1, source_target_pairs={{12,0},{0,4},{4,8},{8,12},{13,1},{1,5},{5,9},{9,13},{14,2},{2,6},{... | collective-permute-start | bytes 540680 | tf_op jit(solution)/shard_map/ppermute | solution.py:20
  94.5 15.9 %collective-permute-start.15 = (bf16[64,1408]{1,0:T(8,128)(2,1)}, bf16[64,1408]{1,0:T(8,128)(2,1)S(1)}, u32[]{:S(2)}, u32[]{:S(2)}) collective-permute-start(bf16[64,1408]{1,0:T(8,128)(2,1)} %get-tuple-element.32.refs_0_), channel_id=1, source_target_pairs={{8,0},{12,4},{0,8},{4,12},{9,1},{13,5},{1,9},{5,13},{10,2},{14,6},... | collective-permute-start | bytes 540680 | tf_op jit(solution)/shard_map/ppermute | solution.py:20
  97.6 6.3 %copy-start.14 = (bf16[64,1408]{1,0:T(8,128)(2,1)}, bf16[64,1408]{1,0:T(8,128)(2,1)S(1)}, u32[]{:S(2)}) copy-start(bf16[64,1408]{1,0:T(8,128)(2,1)S(1)} %collective-permute-done.23.refs_3_) | copy-start | bytes 540676
  97.6 15.5 %collective-permute-start.14 = (bf16[64,1408]{1,0:T(8,128)(2,1)}, bf16[64,1408]{1,0:T(8,128)(2,1)S(1)}, u32[]{:S(2)}, u32[]{:S(2)}) collective-permute-start(bf16[64,1408]{1,0:T(8,128)(2,1)} %get-tuple-element.32.refs_0_), channel_id=1, source_target_pairs={{4,0},{8,4},{12,8},{0,12},{5,1},{9,5},{13,9},{1,13},{6,2},{10,6},{... | collective-permute-start | bytes 540680 | tf_op jit(solution)/shard_map/ppermute | solution.py:20
  100.5 3.5 %copy-start.15 = (bf16[64,1408]{1,0:T(8,128)(2,1)}, bf16[64,1408]{1,0:T(8,128)(2,1)S(1)}, u32[]{:S(2)}) copy-start(bf16[64,1408]{1,0:T(8,128)(2,1)S(1)} %collective-permute-done.22.refs_2_) | copy-start | bytes 540676
  106.8 34.7 %collective-permute-start.26 = (bf16[256,1408]{1,0:T(8,128)(2,1)}, bf16[256,1408]{1,0:T(8,128)(2,1)S(1)}, u32[]{:S(2)}, u32[]{:S(2)}) collective-permute-start(bf16[256,1408]{1,0:T(8,128)(2,1)} %shard_map.82.refs_7_), channel_id=1, source_target_pairs={{12,0},{0,4},{4,8},{8,12},{13,1},{1,5},{5,9},{9,13},{14,2},{2,6},{... | collective-permute-start | bytes 2162696 | tf_op jit(solution)/shard_map/ppermute | solution.py:20
  107.4 35.1 %collective-permute-start.24 = (bf16[256,1408]{1,0:T(8,128)(2,1)}, bf16[256,1408]{1,0:T(8,128)(2,1)S(1)}, u32[]{:S(2)}, u32[]{:S(2)}) collective-permute-start(bf16[256,1408]{1,0:T(8,128)(2,1)} %shard_map.82.refs_7_), channel_id=1, source_target_pairs={{4,0},{8,4},{12,8},{0,12},{5,1},{9,5},{13,9},{1,13},{6,2},{10,6},{... | collective-permute-start | bytes 2162696 | tf_op jit(solution)/shard_map/ppermute | solution.py:20
  110.1 3.1 %copy-start.11 = (bf16[64,1408]{1,0:T(8,128)(2,1)}, bf16[64,1408]{1,0:T(8,128)(2,1)S(1)}, u32[]{:S(2)}) copy-start(bf16[64,1408]{1,0:T(8,128)(2,1)S(1)} %collective-permute-done.16.refs_3_) | copy-start | bytes 540676
  110.4 2.8 %copy-start.12 = (bf16[64,1408]{1,0:T(8,128)(2,1)}, bf16[64,1408]{1,0:T(8,128)(2,1)S(1)}, u32[]{:S(2)}) copy-start(bf16[64,1408]{1,0:T(8,128)(2,1)S(1)} %collective-permute-done.15.refs_2_) | copy-start | bytes 540676
  113.1 0.7 copy-start.13
  116.0 30.5 %collective-permute-start.19 = (bf16[256,1408]{1,0:T(8,128)(2,1)}, bf16[256,1408]{1,0:T(8,128)(2,1)S(1)}, u32[]{:S(2)}, u32[]{:S(2)}) collective-permute-start(bf16[256,1408]{1,0:T(8,128)(2,1)} %shard_map.81.refs_1_), channel_id=1, source_target_pairs={{3,0},{0,1},{1,2},{2,3},{7,4},{4,5},{5,6},{6,7},{11,8},{8,9},{9,10... | collective-permute-start | bytes 2162696 | tf_op jit(solution)/shard_map/ppermute | solution.py:20
  117.8 30.3 %collective-permute-start.17 = (bf16[256,1408]{1,0:T(8,128)(2,1)}, bf16[256,1408]{1,0:T(8,128)(2,1)S(1)}, u32[]{:S(2)}, u32[]{:S(2)}) collective-permute-start(bf16[256,1408]{1,0:T(8,128)(2,1)} %shard_map.81.refs_1_), channel_id=1, source_target_pairs={{1,0},{2,1},{3,2},{0,3},{5,4},{6,5},{7,6},{4,7},{9,8},{10,9},{11,1... | collective-permute-start | bytes 2162696 | tf_op jit(solution)/shard_map/ppermute | solution.py:20
  141.5 18.3 %copy-start.1 = (bf16[256,1408]{1,0:T(8,128)(2,1)}, bf16[256,1408]{1,0:T(8,128)(2,1)S(1)}, u32[]{:S(2)}) copy-start(bf16[256,1408]{1,0:T(8,128)(2,1)S(1)} %collective-permute-done.26.refs_11_) | copy-start | bytes 2162692
  142.4 17.5 %collective-permute-start.27 = (bf16[128,1408]{1,0:T(8,128)(2,1)}, bf16[128,1408]{1,0:T(8,128)(2,1)}, u32[]{:S(2)}, u32[]{:S(2)}) collective-permute-start(bf16[128,1408]{1,0:T(8,128)(2,1)} %slice.79), channel_id=1, source_target_pairs={{12,0},{0,4},{4,8},{8,12},{13,1},{1,5},{5,9},{9,13},{14,2},{2,6},{... | collective-permute-start | bytes 1081352 | tf_op jit(solution)/shard_map/ppermute | solution.py:20
  142.5 17.3 %copy-start.2 = (bf16[256,1408]{1,0:T(8,128)(2,1)}, bf16[256,1408]{1,0:T(8,128)(2,1)S(1)}, u32[]{:S(2)}) copy-start(bf16[256,1408]{1,0:T(8,128)(2,1)S(1)} %collective-permute-done.24.refs_8_) | copy-start | bytes 2162692
  143.4 16.5 %collective-permute-start.25 = (bf16[128,1408]{1,0:T(8,128)(2,1)}, bf16[128,1408]{1,0:T(8,128)(2,1)}, u32[]{:S(2)}, u32[]{:S(2)}) collective-permute-start(bf16[128,1408]{1,0:T(8,128)(2,1)} %slice.78), channel_id=1, source_target_pairs={{4,0},{8,4},{12,8},{0,12},{5,1},{9,5},{13,9},{1,13},{6,2},{10,6},{... | collective-permute-start | bytes 1081352 | tf_op jit(solution)/shard_map/ppermute | solution.py:20
  146.4 0.9 copy-start.3
  148.0 11.8 %collective-permute-start.20 = (bf16[128,1408]{1,0:T(8,128)(2,1)}, bf16[128,1408]{1,0:T(8,128)(2,1)}, u32[]{:S(2)}, u32[]{:S(2)}) collective-permute-start(bf16[128,1408]{1,0:T(8,128)(2,1)} %slice.77), channel_id=1, source_target_pairs={{3,0},{0,1},{1,2},{2,3},{7,4},{4,5},{5,6},{6,7},{11,8},{8,9},{9,10... | collective-permute-start | bytes 1081352 | tf_op jit(solution)/shard_map/ppermute | solution.py:20
  148.1 0.9 copy-start.4
  149.7 10.2 %collective-permute-start.18 = (bf16[128,1408]{1,0:T(8,128)(2,1)}, bf16[128,1408]{1,0:T(8,128)(2,1)}, u32[]{:S(2)}, u32[]{:S(2)}) collective-permute-start(bf16[128,1408]{1,0:T(8,128)(2,1)} %slice.76), channel_id=1, source_target_pairs={{1,0},{2,1},{3,2},{0,3},{5,4},{6,5},{7,6},{4,7},{9,8},{10,9},{11,1... | collective-permute-start | bytes 1081352 | tf_op jit(solution)/shard_map/ppermute | solution.py:20
  (1 other events, 0.7 us)
Sparse Core Ops, SparseCore 0:
  65.5 77.4 all-gather.1

commit v5 on v4

--- a/solution.py
+++ b/solution.py
@@ -50,24 +50,22 @@
             wanted = (((y + dy) & (SIDE - 1)) * SIDE + ((z + dz) & (SIDE - 1))) * part
             wanted = wanted + (column & (part - 1))
             place = jnp.where(source == wanted, 1.0, 0.0).astype(BF16)
-            out_ref[:, low : low + block] = jnp.dot(
-                bases_ref[0], place, preferred_element_type=F32
-            ).astype(BF16)
-
-
-def arrange(where, bases, which, after):
-    _, rows, ranks = bases.shape
+            for k in range(bases_ref.shape[0]):
+                out_ref[k, :, low : low + block] = jnp.dot(
+                    bases_ref[k], place, preferred_element_type=F32
+                ).astype(BF16)
+
+
+def arrange(where, bases, after):
+    whole = pl.BlockSpec(bases.shape, lambda i, w: (0, 0, 0))
     return pl.pallas_call(
         arrange_kernel,
         grid_spec=pltpu.PrefetchScalarGridSpec(
-            num_scalar_prefetch=1,
-            grid=(1,),
-            in_specs=[pl.BlockSpec((1, rows, ranks), lambda i, w: (which, 0, 0)), ANYWHERE],
-            out_specs=[pl.BlockSpec((rows, ranks), lambda i, w: (0, 0))] * 2,
+            num_scalar_prefetch=1, grid=(1,), in_specs=[whole, ANYWHERE], out_specs=[whole] * 2
         ),
-        out_shape=[held((rows, ranks))] * 2,
-        compiler_params=PARAMS,
-        cost_estimate=cost(4 * rows * ranks * ranks, 6 * rows * ranks),
+        out_shape=[held(bases.shape)] * 2,
+        compiler_params=PARAMS,
+        cost_estimate=cost(4 * bases.size * bases.shape[2], 6 * bases.size),
     )(where, bases, after)
 
 
@@ -186,7 +184,7 @@
     cut = pieces.shape[2]
     loads, refs = [], list(refs)
     for half, count in enumerate(counts):
-        loads.append([(refs.pop(0), columns.at[half])])
+        loads.append([(refs.pop(0).at[which], columns.at[half])])
         at = 0
         for _ in range(count):
             ref = refs.pop(0)
@@ -220,16 +218,20 @@
         store.wait()
 
 
-def expand_halves(halves, which, update):
-    rows, ranks = halves[0][0].shape
+def expand_halves(halves, which, width, update):
+    count, rows, ranks = halves[0][0].shape
     cut = halves[0][1][0].shape[1]
     counts = tuple(len(pieces) for _, pieces in halves)
     args = [array for columns, pieces in halves for array in (columns, *pieces)]
+    aliases = {}
+    if update is not None:
+        aliases = {len(args): 0}
+        args.append(update)
     return pl.pallas_call(
         functools.partial(expand_kernel, counts=counts, which=which),
-        in_specs=[ANYWHERE] * (len(args) + 1),
+        in_specs=[ANYWHERE] * len(args),
         out_specs=ANYWHERE,
-        out_shape=jax.ShapeDtypeStruct(update.shape, BF16),
+        out_shape=jax.ShapeDtypeStruct((count, width, rows), BF16),
         scratch_shapes=[
             pltpu.VMEM((len(halves), rows, ranks), BF16),
             pltpu.VMEM((len(halves), ranks, cut), BF16),
@@ -237,42 +239,19 @@
             pltpu.SemaphoreType.DMA((len(halves), max(counts) + 1)),
             pltpu.SemaphoreType.DMA((len(halves),)),
         ],
-        input_output_aliases={len(args): 0},
+        input_output_aliases=aliases,
         compiler_params=PARAMS,
         cost_estimate=cost(4 * rows * ranks * cut, 4 * (rows * ranks + ranks * cut + rows * cut)),
-    )(*args, update)
-
-
-def expand_whole_kernel(bases_ref, gathered_ref, out_ref):
-    out_ref[0] = (
-        jnp.dot(bases_ref[0], gathered_ref[...], preferred_element_type=F32).T.astype(BF16)
-    )
-
-
-def expand_whole(bases, gathered, which, width):
-    count, rows, ranks = bases.shape
-    tile = gathered.shape[1] // 2
-    return pl.pallas_call(
-        expand_whole_kernel,
-        grid=(gathered.shape[1] // tile,),
-        in_specs=[
-            pl.BlockSpec((1, rows, ranks), lambda i: (which, 0, 0)),
-            pl.BlockSpec((ranks, tile), lambda i: (0, i)),
-        ],
-        out_specs=pl.BlockSpec((1, tile, rows), lambda i: (which, i, 0)),
-        out_shape=jax.ShapeDtypeStruct((count, width, rows), BF16),
-        compiler_params=PARAMS,
-        cost_estimate=cost(
-            2 * rows * ranks * width, 2 * (rows * ranks + ranks * width + rows * width)
-        ),
-    )(bases, gathered)
-
-
-def ring_gather(value, first, second):
+    )(*args)
+
+
+def ring_gather(value, first, second, split):
     row = stack([value] + [receive(value, first, d) for d in (1, 2, 3)])
-    half = row.shape[0] // 2
     after = receive(row, second, 1)
     before = receive(row, second, -1)
+    if not split:
+        return row, after, receive(after, second, 1), before
+    half = row.shape[0] // 2
     far_top = receive(after[:half], second, 1)
     far_bottom = receive(before[half:], second, -1)
     return row, after, far_top, far_bottom, before
@@ -309,22 +288,20 @@
     own_sum_1, *sums_1 = partial_grads(
         where, partial[1], other_partial[1], out_grads, other_grads, 1, own_sum
     )
-    columns_y, columns_z = arrange(where, bases, 1, own_sum_1)
+    columns_y, columns_z = arrange(where, bases, own_sum_1)
     sums = [send(value, "x", i + 1) for i, value in enumerate(sums)]
     sums_1 = [send(value, "x", i + 1) for i, value in enumerate(sums_1)]
 
-    *moments, whole = directions(
-        own_sum, sums, first_moment, second_moment, 0, 1, [], columns_y
-    )
-    gathered = lax.all_gather(whole, ("y", "z"), axis=0, tiled=True)
-
-    *moments, left, right = directions(
-        own_sum_1, sums_1, first_moment, second_moment, 1, 2, moments, columns_y
-    )
-    pieces_left = ring_gather(left, "y", "z")
-    pieces_right = ring_gather(right, "z", "y")
-    update = expand_whole(bases, gathered, 0, width)
-    update = expand_halves([(columns_z, pieces_left), (columns_y, pieces_right)], 1, update)
+    moments, update = [], None
+    for which, parts in enumerate(([own_sum, sums], [own_sum_1, sums_1])):
+        *moments, left, right = directions(
+            *parts, first_moment, second_moment, which, 2, moments, columns_y
+        )
+        halves = [
+            (columns_z, ring_gather(left, "y", "z", which == 1)),
+            (columns_y, ring_gather(right, "z", "y", which == 1)),
+        ]
+        update = expand_halves(halves, which, width, update)
     return jnp.swapaxes(update, 1, 2), *moments
 
 

time: 175 us -> 171 us (0.977)
  starting transfers between devices: 46.3 us -> 64.7 us
  waiting for transfers between devices: 56.2 us -> 40.1 us
  between operations: 14.2 us -> 1.13 us
  Pallas kernels: 42.6 us -> 49.6 us
    ppermute x26 -> x38, starting transfers between devices: 46.1 us -> 64.5 us  [receive(): lax.ppermute(value, axis, [((i + distance) % SIDE, i) for i in range(SIDE)])]
    ppermute x26 -> x38, waiting for transfers between devices: 55.6 us -> 39.5 us  [receive(): lax.ppermute(value, axis, [((i + distance) % SIDE, i) for i in range(SIDE)])]
    pallas_call x1 -> x2, Pallas kernels: 7.09 us -> 14.1 us  [expand_halves(): pl.pallas_call(functools.partial(expand_kernel, counts=counts, which=whic...]
    pallas_call x1 -> x0, Pallas kernels: 6.93 us -> none  [expand_whole(): pl.pallas_call(expand_whole_kernel, grid=(gathered.shape[1] // tile,), in...]
    pallas_call x2 -> x4, Pallas kernels: 4.34 us -> 8.53 us  [stack(): pl.pallas_call(stack_kernel, out_shape=held((rows * len(pieces), width)),...]
    pallas_call x1, Pallas kernels: 5.31 us -> 8.13 us  [arrange(): pl.pallas_call(arrange_kernel, grid_spec=pltpu.PrefetchScalarGridSpec(num...]
    unnamed x40 -> x72, local copies, waits for them, and re-layouts: 6.34 us -> 6.45 us
  transfers between devices with their start and end apart: 29 -> 40, of which waited for: 15 -> 14; matrix products, arithmetic and copies ran while one was open for 5% -> 4% of each run, Pallas kernels for 15% -> 20%
where the time goes in v5:
time: 171 us; the launch traced here: 169 us
  starting transfers between devices  64.7 us (38%)
  Pallas kernels  49.6 us (29%)
  waiting for transfers between devices  40.1 us (23%)
  local copies, waits for them, and re-layouts  10.2 us (6%)
  matrix products  2.91 us (2%)
    ppermute x38, starting transfers between devices, receive(): lax.ppermute(value, axis, [((i + distance) % SIDE, i) for i in range(SIDE)])  64.5 us
    ppermute x38, waiting for transfers between devices, receive(): lax.ppermute(value, axis, [((i + distance) % SIDE, i) for i in range(SIDE)])  39.5 us
    pallas_call x2, Pallas kernels, expand_halves(): pl.pallas_call(functools.partial(expand_kernel, counts=counts, which=whic...  14.1 us
    pallas_call x2, Pallas kernels, partial_grads(): pl.pallas_call(partial_kernel, grid_spec=pltpu.PrefetchScalarGridSpec(num...  12.7 us
    pallas_call x4, Pallas kernels, stack(): pl.pallas_call(stack_kernel, out_shape=held((rows * len(pieces), width)),...  8.53 us
    pallas_call x1, Pallas kernels, arrange(): pl.pallas_call(arrange_kernel, grid_spec=pltpu.PrefetchScalarGridSpec(num...  8.13 us
    unnamed x72, local copies, waits for them, and re-layouts  6.45 us
    pallas_call x2, Pallas kernels, directions(): pl.pallas_call(functools.partial(direction_kernel, pieces=pieces), grid=(...  6.1 us
  transfers between devices with their start and end apart: 40, of which 14 were waited for; matrix products, arithmetic and copies ran while one was open for 4% of the time, Pallas kernels for 20%

profile of v5, /device:TPU:0, one launch (start us, length us, event | category | flops | bytes accessed | tf_op | source)
XLA Modules:
  0.0 169.4 jit_solution(1094396648956625321)
XLA Ops:
  0.8 1.5 copy-done
  2.2 2.9 %fusion.4 = bf16[2,128,1024]{2,1,0:T(8,128)(2,1)S(1)} fusion(s32[1024]{0:T(1024)S(1)} %fusion.21, bf16[2,512,1024]{2,1,0:T(8,128)(2,1)} %bases_ref.1, bf16[128,8192]{1,0:T(8,128)(2,1)S(1)} %copy-done, s32[]{:T(128)S(6)} %select_n.54), kind=kOutput, calls=%fused_computation.4 | convolution fusion | flops 806879232 | bytes 2756612 | tf_op jit(solution)/shard_map/ktr,rs->kts/dot_general | solution.py:275
  5.2 1.7 %collective-permute-start = (bf16[2,128,256]{2,1,0:T(8,128)(2,1)S(1)}, bf16[2,128,256]{2,1,0:T(8,128)(2,1)S(1)}, u32[]{:S(2)}, u32[]{:S(2)}) collective-permute-start(bf16[2,128,256]{2,1,0:T(8,128)(2,1)S(1)} %get-tuple-element.39), channel_id=1, source_target_pairs={{12,0},{0,4},{4,8},{8,12},{13,1},{1,5},{5,9},{9,13},{14,2},{2,6},{... | collective-permute-start | bytes 393224 | tf_op jit(solution)/shard_map/ppermute | solution.py:20
  6.9 2.9 %collective-permute-start.2 = (bf16[2,128,256]{2,1,0:T(8,128)(2,1)S(1)}, bf16[2,128,256]{2,1,0:T(8,128)(2,1)S(1)}, u32[]{:S(2)}, u32[]{:S(2)}) collective-permute-start(bf16[2,128,256]{2,1,0:T(8,128)(2,1)S(1)} %get-tuple-element.40), channel_id=1, source_target_pairs={{8,0},{12,4},{0,8},{4,12},{9,1},{13,5},{1,9},{5,13},{10,2},{14,6},... | collective-permute-start | bytes 393224 | tf_op jit(solution)/shard_map/ppermute | solution.py:20
  9.8 1.3 collective-permute-start.1
  11.8 4.0 %collective-permute-done.2 = bf16[2,128,256]{2,1,0:T(8,128)(2,1)S(1)} collective-permute-done((bf16[2,128,256]{2,1,0:T(8,128)(2,1)S(1)}, bf16[2,128,256]{2,1,0:T(8,128)(2,1)S(1)}, u32[]{:S(2)}, u32[]{:S(2)}) %collective-permute-start.2) | collective-permute-done | bytes 131104 | tf_op jit(solution)/shard_map/ppermute | solution.py:20
  16.0 2.0 %collective-permute-start.3 = (bf16[2,128,64]{2,1,0:T(8,128)(2,1)S(1)}, bf16[2,128,64]{2,1,0:T(8,128)(2,1)S(1)}, u32[]{:S(2)}, u32[]{:S(2)}) collective-permute-start(bf16[2,128,64]{2,1,0:T(8,128)(2,1)S(1)} %get-tuple-element.42), channel_id=1, source_target_pairs={{3,0},{0,1},{1,2},{2,3},{7,4},{4,5},{5,6},{6,7},{11,8},{8,9},{9,10... | collective-permute-start | bytes 98312 | tf_op jit(solution)/shard_map/ppermute | solution.py:20
  18.0 3.6 %collective-permute-start.5 = (bf16[2,128,64]{2,1,0:T(8,128)(2,1)S(1)}, bf16[2,128,64]{2,1,0:T(8,128)(2,1)S(1)}, u32[]{:S(2)}, u32[]{:S(2)}) collective-permute-start(bf16[2,128,64]{2,1,0:T(8,128)(2,1)S(1)} %get-tuple-element.43), channel_id=1, source_target_pairs={{2,0},{3,1},{0,2},{1,3},{6,4},{7,5},{4,6},{5,7},{10,8},{11,9},{8,1... | collective-permute-start | bytes 98312 | tf_op jit(solution)/shard_map/ppermute | solution.py:20
  23.3 1.3 collective-permute-done.5
  24.5 1.3 collective-permute-done.4
  27.9 6.3 %shard_map.76 = (f32[64,2752]{1,0:T(8,128)}, bf16[64,2752]{1,0:T(8,128)(2,1)}, bf16[64,2752]{1,0:T(8,128)(2,1)}, bf16[64,2752]{1,0:T(8,128)(2,1)}) custom-call(s32[4]{0:T(128)} %pad_add_fusion.where_ref._, bf16[128,64]{1,0:T(8,128)(2,1)} %get-tuple-element.47.proj_ref, bf16[128,64]{1,0:T(8,128)(2,1)} %get-tuple-element.45.other_proj_ref, ...), custom_call_target="tpu_custom_call" | custom-call | flops 360710144 | bytes 8454144 | tf_op jit(solution)/shard_map/pallas_call | solution.py:100
  34.2 1.5 collective-permute-start.11
  35.7 2.7 %collective-permute-start.12 = (bf16[64,2752]{1,0:T(8,128)(2,1)}, bf16[64,2752]{1,0:T(8,128)(2,1)S(1)}, u32[]{:S(2)}, u32[]{:S(2)}) collective-permute-start(bf16[64,2752]{1,0:T(8,128)(2,1)} %get-tuple-element.28), channel_id=1, source_target_pairs={{64,0},{96,32},{0,64},{32,96},{65,1},{97,33},{1,65},{33,97},{66,2}... | collective-permute-start | bytes 1056776 | tf_op jit(solution)/shard_map/ppermute | solution.py:20
  38.4 1.4 collective-permute-start.13
  39.8 6.4 %shard_map.77 = (f32[64,2752]{1,0:T(8,128)}, bf16[64,2752]{1,0:T(8,128)(2,1)}, bf16[64,2752]{1,0:T(8,128)(2,1)}, bf16[64,2752]{1,0:T(8,128)(2,1)}) custom-call(s32[4]{0:T(128)} %pad_add_fusion.where_ref._, bf16[128,64]{1,0:T(8,128)(2,1)} %get-tuple-element.48.proj_ref, bf16[128,64]{1,0:T(8,128)(2,1)} %get-tuple-element.46.other_proj_ref, ...), custom_call_target="tpu_custom_call" | custom-call | flops 360710144 | bytes 8454144 | tf_op jit(solution)/shard_map/pallas_call | solution.py:100
  47.7 1.9 %collective-permute-start.10 = (bf16[64,2752]{1,0:T(8,128)(2,1)}, bf16[64,2752]{1,0:T(8,128)(2,1)S(1)}, u32[]{:S(2)}, u32[]{:S(2)}) collective-permute-start(bf16[64,2752]{1,0:T(8,128)(2,1)} %get-tuple-element.26), channel_id=1, source_target_pairs={{32,0},{64,32},{96,64},{0,96},{33,1},{65,33},{97,65},{1,97},{34,2}... | collective-permute-start | bytes 1056776 | tf_op jit(solution)/shard_map/ppermute | solution.py:20
  49.5 8.1 %shard_map.78 = (bf16[2,512,1024]{2,1,0:T(8,128)(2,1)}, bf16[2,512,1024]{2,1,0:T(8,128)(2,1)}) custom-call(s32[4]{0:T(128)} %pad_add_fusion.where_ref._, bf16[2,512,1024]{2,1,0:T(8,128)(2,1)} %bases_ref.1, f32[64,2752]{1,0:T(8,128)} %get-tuple-element.22._.refs_0_), custom_call_target="tpu_custom_call" | custom-call | flops 4294967296 | bytes 6291456 | tf_op jit(solution)/shard_map/pallas_call | solution.py:61
  58.5 3.0 %shard_map.79 = (f32[2,64,2752]{2,1,0:T(8,128)}, f32[2,64,2752]{2,1,0:T(8,128)}, bf16[64,1408]{1,0:T(8,128)(2,1)}, bf16[64,1408]{1,0:T(8,128)(2,1)}) custom-call(f32[64,2752]{1,0:T(8,128)} %get-tuple-element.21._.refs_0_, bf16[64,2752]{1,0:T(8,128)(2,1)} %copy-done.16, bf16[64,2752]{1,0:T(8,128)(2,1)} %copy-done.17, bf16[64,2752]{1,0:T(8,128)(2,1)} %copy-done.18, ...), custom_call_target="tpu_custom_call" | custom-call | flops 5283840 | bytes 4579328 | tf_op jit(solution)/shard_map/pallas_call | solution.py:153
  61.6 1.7 collective-permute-done.8.refs_1_
  63.2 7.0 %collective-permute-done.9.refs_2_ = bf16[64,2752]{1,0:T(8,128)(2,1)S(1)} collective-permute-done((bf16[64,2752]{1,0:T(8,128)(2,1)}, bf16[64,2752]{1,0:T(8,128)(2,1)S(1)}, u32[]{:S(2)}, u32[]{:S(2)}) %collective-permute-start.9) | collective-permute-done | bytes 352288 | tf_op jit(solution)/shard_map/ppermute | solution.py:20
  71.2 3.1 %shard_map.80 = (f32[2,64,2752]{2,1,0:T(8,128)}, f32[2,64,2752]{2,1,0:T(8,128)}, bf16[64,1408]{1,0:T(8,128)(2,1)}, bf16[64,1408]{1,0:T(8,128)(2,1)}) custom-call(f32[64,2752]{1,0:T(8,128)} %get-tuple-element.22._.refs_0_, bf16[64,2752]{1,0:T(8,128)(2,1)} %copy-done.13, bf16[64,2752]{1,0:T(8,128)(2,1)} %copy-done.14, ...), custom_call_target="tpu_custom_call", output_to_operand_aliasing={{0}: (6, {}), {1}: (7, {})} | custom-call | flops 5283840 | bytes 4579328 | tf_op jit(solution)/shard_map/pallas_call | solution.py:153
  74.6 1.2 collective-permute-start.30
  75.9 2.4 %collective-permute-start.29 = (bf16[64,1408]{1,0:T(8,128)(2,1)S(1)}, bf16[64,1408]{1,0:T(8,128)(2,1)S(1)}, u32[]{:S(2)}, u32[]{:S(2)}) collective-permute-start(bf16[64,1408]{1,0:T(8,128)(2,1)S(1)} %copy-done.23), channel_id=1, source_target_pairs={{8,0},{12,4},{0,8},{4,12},{9,1},{13,5},{1,9},{5,13},{10,2},{14,6},... | collective-permute-start | bytes 540680 | tf_op jit(solution)/shard_map/ppermute | solution.py:20
  78.3 1.6 collective-permute-start.28
  79.8 1.3 collective-permute-start.36
  81.7 2.7 %collective-permute-start.35 = (bf16[64,1408]{1,0:T(8,128)(2,1)S(1)}, bf16[64,1408]{1,0:T(8,128)(2,1)S(1)}, u32[]{:S(2)}, u32[]{:S(2)}) collective-permute-start(bf16[64,1408]{1,0:T(8,128)(2,1)S(1)} %copy-done.22), channel_id=1, source_target_pairs={{2,0},{3,1},{0,2},{1,3},{6,4},{7,5},{4,6},{5,7},{10,8},{11,9},{8,1... | collective-permute-start | bytes 540680 | tf_op jit(solution)/shard_map/ppermute | solution.py:20
  84.4 1.6 collective-permute-start.34
  86.0 3.1 %collective-permute-start.22 = (bf16[64,1408]{1,0:T(8,128)(2,1)}, bf16[64,1408]{1,0:T(8,128)(2,1)S(1)}, u32[]{:S(2)}, u32[]{:S(2)}) collective-permute-start(bf16[64,1408]{1,0:T(8,128)(2,1)} %get-tuple-element.34.refs_0_), channel_id=1, source_target_pairs={{2,0},{3,1},{0,2},{1,3},{6,4},{7,5},{4,6},{5,7},{10,8},{11,9},{8,1... | collective-permute-start | bytes 540680 | tf_op jit(solution)/shard_map/ppermute | solution.py:20
  90.6 2.2 %collective-permute-done.35.refs_2_ = bf16[64,1408]{1,0:T(8,128)(2,1)S(1)} collective-permute-done((bf16[64,1408]{1,0:T(8,128)(2,1)S(1)}, bf16[64,1408]{1,0:T(8,128)(2,1)S(1)}, u32[]{:S(2)}, u32[]{:S(2)}) %collective-permute-start.35) | collective-permute-done | bytes 180256 | tf_op jit(solution)/shard_map/ppermute | solution.py:20
  92.8 1.7 collective-permute-start.15
  94.6 1.3 collective-permute-start.14
  95.9 2.1 %shard_map.83.refs_1_ = bf16[256,1408]{1,0:T(8,128)(2,1)} custom-call(bf16[64,1408]{1,0:T(8,128)(2,1)} %get-tuple-element.35.refs_0_, bf16[64,1408]{1,0:T(8,128)(2,1)} %copy-done.28, bf16[64,1408]{1,0:T(8,128)(2,1)} %copy-done.27, bf16[64,1408]{1,0:T(8,128)(2,1)} %copy-done.25), custom_call_target="tpu_custom_call" | custom-call | bytes 1441792 | tf_op jit(solution)/shard_map/pallas_call | solution.py:173
  98.0 2.2 %shard_map.84.refs_6_ = bf16[256,1408]{1,0:T(8,128)(2,1)} custom-call(bf16[64,1408]{1,0:T(8,128)(2,1)} %get-tuple-element.36.refs_0_, bf16[64,1408]{1,0:T(8,128)(2,1)} %copy-done.35, bf16[64,1408]{1,0:T(8,128)(2,1)} %copy-done.32, bf16[64,1408]{1,0:T(8,128)(2,1)} %copy-done.29), custom_call_target="tpu_custom_call" | custom-call | bytes 1441792 | tf_op jit(solution)/shard_map/pallas_call | solution.py:173
  101.3 3.7 %collective-permute-start.31 = (bf16[256,1408]{1,0:T(8,128)(2,1)}, bf16[256,1408]{1,0:T(8,128)(2,1)S(1)}, u32[]{:S(2)}, u32[]{:S(2)}) collective-permute-start(bf16[256,1408]{1,0:T(8,128)(2,1)} %shard_map.83.refs_1_), channel_id=1, source_target_pairs={{1,0},{2,1},{3,2},{0,3},{5,4},{6,5},{7,6},{4,7},{9,8},{10,9},{11,1... | collective-permute-start | bytes 2162696 | tf_op jit(solution)/shard_map/ppermute | solution.py:20
  105.0 2.1 %shard_map.82.refs_7_ = bf16[256,1408]{1,0:T(8,128)(2,1)} custom-call(bf16[64,1408]{1,0:T(8,128)(2,1)} %get-tuple-element.34.refs_0_, bf16[64,1408]{1,0:T(8,128)(2,1)} %copy-done.34, bf16[64,1408]{1,0:T(8,128)(2,1)} %copy-done.31, bf16[64,1408]{1,0:T(8,128)(2,1)} %copy-done.24), custom_call_target="tpu_custom_call" | custom-call | bytes 1441792 | tf_op jit(solution)/shard_map/pallas_call | solution.py:173
  107.7 2.7 %collective-permute-start.24 = (bf16[256,1408]{1,0:T(8,128)(2,1)}, bf16[256,1408]{1,0:T(8,128)(2,1)S(1)}, u32[]{:S(2)}, u32[]{:S(2)}) collective-permute-start(bf16[256,1408]{1,0:T(8,128)(2,1)} %shard_map.82.refs_7_), channel_id=1, source_target_pairs={{4,0},{8,4},{12,8},{0,12},{5,1},{9,5},{13,9},{1,13},{6,2},{10,6},{... | collective-permute-start | bytes 2162696 | tf_op jit(solution)/shard_map/ppermute | solution.py:20
  111.1 2.1 %shard_map.81.refs_1_ = bf16[256,1408]{1,0:T(8,128)(2,1)} custom-call(bf16[64,1408]{1,0:T(8,128)(2,1)} %get-tuple-element.33.refs_0_, bf16[64,1408]{1,0:T(8,128)(2,1)} %copy-done.33, bf16[64,1408]{1,0:T(8,128)(2,1)} %copy-done.30, bf16[64,1408]{1,0:T(8,128)(2,1)} %copy-done.26), custom_call_target="tpu_custom_call" | custom-call | bytes 1441792 | tf_op jit(solution)/shard_map/pallas_call | solution.py:173
  113.2 6.4 %collective-permute-done.37.refs_7_ = bf16[256,1408]{1,0:T(8,128)(2,1)S(1)} collective-permute-done((bf16[256,1408]{1,0:T(8,128)(2,1)}, bf16[256,1408]{1,0:T(8,128)(2,1)S(1)}, u32[]{:S(2)}, u32[]{:S(2)}) %collective-permute-start.37) | collective-permute-done | bytes 720928 | tf_op jit(solution)/shard_map/ppermute | solution.py:20
  119.6 3.2 %collective-permute-start.17 = (bf16[256,1408]{1,0:T(8,128)(2,1)}, bf16[256,1408]{1,0:T(8,128)(2,1)S(1)}, u32[]{:S(2)}, u32[]{:S(2)}) collective-permute-start(bf16[256,1408]{1,0:T(8,128)(2,1)} %shard_map.81.refs_1_), channel_id=1, source_target_pairs={{1,0},{2,1},{3,2},{0,3},{5,4},{6,5},{7,6},{4,7},{9,8},{10,9},{11,1... | collective-permute-start | bytes 2162696 | tf_op jit(solution)/shard_map/ppermute | solution.py:20
  122.8 2.0 %collective-permute-start.39 = (bf16[256,1408]{1,0:T(8,128)(2,1)S(1)}, bf16[256,1408]{1,0:T(8,128)(2,1)S(1)}, u32[]{:S(2)}, u32[]{:S(2)}) collective-permute-start(bf16[256,1408]{1,0:T(8,128)(2,1)S(1)} %copy-done.2), channel_id=1, source_target_pairs={{12,0},{0,4},{4,8},{8,12},{13,1},{1,5},{5,9},{9,13},{14,2},{2,6},{... | collective-permute-start | bytes 2162696 | tf_op jit(solution)/shard_map/ppermute | solution.py:20
  124.9 6.4 %collective-permute-done.24.refs_8_ = bf16[256,1408]{1,0:T(8,128)(2,1)S(1)} collective-permute-done((bf16[256,1408]{1,0:T(8,128)(2,1)}, bf16[256,1408]{1,0:T(8,128)(2,1)S(1)}, u32[]{:S(2)}, u32[]{:S(2)}) %collective-permute-start.24) | collective-permute-done | bytes 720928 | tf_op jit(solution)/shard_map/ppermute | solution.py:20
  131.3 2.7 %collective-permute-start.38 = (bf16[256,1408]{1,0:T(8,128)(2,1)S(1)}, bf16[256,1408]{1,0:T(8,128)(2,1)S(1)}, u32[]{:S(2)}, u32[]{:S(2)}) collective-permute-start(bf16[256,1408]{1,0:T(8,128)(2,1)S(1)} %collective-permute-done.37.refs_7_), channel_id=1, source_target_pairs={{4,0},{8,4},{12,8},{0,12},{5,1},{9,5},{13,9},{1,13},{6,2},{10,6},{... | collective-permute-start | bytes 2162696 | tf_op jit(solution)/shard_map/ppermute | solution.py:20
  134.0 3.0 %collective-permute-start.32 = (bf16[256,1408]{1,0:T(8,128)(2,1)S(1)}, bf16[256,1408]{1,0:T(8,128)(2,1)S(1)}, u32[]{:S(2)}, u32[]{:S(2)}) collective-permute-start(bf16[256,1408]{1,0:T(8,128)(2,1)S(1)} %collective-permute-done.31.refs_2_), channel_id=1, source_target_pairs={{1,0},{2,1},{3,2},{0,3},{5,4},{6,5},{7,6},{4,7},{9,8},{10,9},{11,1... | collective-permute-start | bytes 2162696 | tf_op jit(solution)/shard_map/ppermute | solution.py:20
  139.9 2.7 %collective-permute-start.25 = (bf16[128,1408]{1,0:T(8,128)(2,1)}, bf16[128,1408]{1,0:T(8,128)(2,1)S(1)}, u32[]{:S(2)}, u32[]{:S(2)}) collective-permute-start(bf16[128,1408]{1,0:T(8,128)(2,1)} %slice.78), channel_id=1, source_target_pairs={{4,0},{8,4},{12,8},{0,12},{5,1},{9,5},{13,9},{1,13},{6,2},{10,6},{... | collective-permute-start | bytes 1081352 | tf_op jit(solution)/shard_map/ppermute | solution.py:20
  143.4 7.0 %collective-permute-done.38.refs_8_ = bf16[256,1408]{1,0:T(8,128)(2,1)S(1)} collective-permute-done((bf16[256,1408]{1,0:T(8,128)(2,1)S(1)}, bf16[256,1408]{1,0:T(8,128)(2,1)S(1)}, u32[]{:S(2)}, u32[]{:S(2)}) %collective-permute-start.38) | collective-permute-done | bytes 720928 | tf_op jit(solution)/shard_map/ppermute | solution.py:20
  150.3 2.0 %collective-permute-start.18 = (bf16[128,1408]{1,0:T(8,128)(2,1)}, bf16[128,1408]{1,0:T(8,128)(2,1)S(1)}, u32[]{:S(2)}, u32[]{:S(2)}) collective-permute-start(bf16[128,1408]{1,0:T(8,128)(2,1)} %slice.76), channel_id=1, source_target_pairs={{1,0},{2,1},{3,2},{0,3},{5,4},{6,5},{7,6},{4,7},{9,8},{10,9},{11,1... | collective-permute-start | bytes 1081352 | tf_op jit(solution)/shard_map/ppermute | solution.py:20
  153.3 7.1 %shard_map.85.refs_12_ = bf16[2,2752,512]{2,1,0:T(8,128)(2,1)} custom-call(bf16[2,512,1024]{2,1,0:T(8,128)(2,1)} %get-tuple-element.23.refs_0_, bf16[256,1408]{1,0:T(8,128)(2,1)} %shard_map.83.refs_1_, bf16[256,1408]{1,0:T(8,128)(2,1)} %copy-done.8, bf16[256,1408]{1,0:T(8,128)(2,1)} %copy-done.12, bf16[256,1408]{1,0:T(8,128)(2,1)} %copy-done.10, ...), custom_call_target="tpu_custom_call" | custom-call | flops 2952790016 | bytes 10747904 | tf_op jit(solution)/shard_map/pallas_call | solution.py:230
  162.1 7.1 %shard_map.86 = bf16[2,2752,512]{2,1,0:T(8,128)(2,1)} custom-call(bf16[2,512,1024]{2,1,0:T(8,128)(2,1)} %get-tuple-element.23.refs_0_, bf16[256,1408]{1,0:T(8,128)(2,1)} %shard_map.81.refs_1_, bf16[256,1408]{1,0:T(8,128)(2,1)} %copy-done.6, bf16[128,1408]{1,0:T(8,128)(2,1)} %copy-done.21, ...), custom_call_target="tpu_custom_call", output_to_operand_aliasing={{}: (12, {})} | custom-call | flops 2952790016 | bytes 10747904 | tf_op jit(solution)/shard_map/pallas_call | solution.py:230
  (128 shorter events, 19.2 us)
Async XLA Ops:
  0.6 27.2 %collective-permute-start.7 = (bf16[2,128,22016]{2,1,0:T(8,128)(2,1)}, bf16[2,128,22016]{2,1,0:T(8,128)(2,1)}, u32[]{:S(2)}, u32[]{:S(2)}) collective-permute-start(bf16[2,128,22016]{2,1,0:T(8,128)(2,1)} %grads_ref.3), channel_id=1, source_target_pairs={{0,16},{16,0},{1,17},{17,1},{2,18},{18,2},{3,19},{19,3},{4,20},{20... | collective-permute-start | bytes 33816584 | tf_op jit(solution)/shard_map/ppermute | solution.py:28
  5.2 6.7 %collective-permute-start = (bf16[2,128,256]{2,1,0:T(8,128)(2,1)S(1)}, bf16[2,128,256]{2,1,0:T(8,128)(2,1)S(1)}, u32[]{:S(2)}, u32[]{:S(2)}) collective-permute-start(bf16[2,128,256]{2,1,0:T(8,128)(2,1)S(1)} %get-tuple-element.39), channel_id=1, source_target_pairs={{12,0},{0,4},{4,8},{8,12},{13,1},{1,5},{5,9},{9,13},{14,2},{2,6},{... | collective-permute-start | bytes 393224 | tf_op jit(solution)/shard_map/ppermute | solution.py:20
  6.9 8.9 %collective-permute-start.2 = (bf16[2,128,256]{2,1,0:T(8,128)(2,1)S(1)}, bf16[2,128,256]{2,1,0:T(8,128)(2,1)S(1)}, u32[]{:S(2)}, u32[]{:S(2)}) collective-permute-start(bf16[2,128,256]{2,1,0:T(8,128)(2,1)S(1)} %get-tuple-element.40), channel_id=1, source_target_pairs={{8,0},{12,4},{0,8},{4,12},{9,1},{13,5},{1,9},{5,13},{10,2},{14,6},... | collective-permute-start | bytes 393224 | tf_op jit(solution)/shard_map/ppermute | solution.py:20
  9.8 6.0 %collective-permute-start.1 = (bf16[2,128,256]{2,1,0:T(8,128)(2,1)S(1)}, bf16[2,128,256]{2,1,0:T(8,128)(2,1)S(1)}, u32[]{:S(2)}, u32[]{:S(2)}) collective-permute-start(bf16[2,128,256]{2,1,0:T(8,128)(2,1)S(1)} %get-tuple-element.41), channel_id=1, source_target_pairs={{4,0},{8,4},{12,8},{0,12},{5,1},{9,5},{13,9},{1,13},{6,2},{10,6},{... | collective-permute-start | bytes 393224 | tf_op jit(solution)/shard_map/ppermute | solution.py:20
  16.0 7.2 %collective-permute-start.3 = (bf16[2,128,64]{2,1,0:T(8,128)(2,1)S(1)}, bf16[2,128,64]{2,1,0:T(8,128)(2,1)S(1)}, u32[]{:S(2)}, u32[]{:S(2)}) collective-permute-start(bf16[2,128,64]{2,1,0:T(8,128)(2,1)S(1)} %get-tuple-element.42), channel_id=1, source_target_pairs={{3,0},{0,1},{1,2},{2,3},{7,4},{4,5},{5,6},{6,7},{11,8},{8,9},{9,10... | collective-permute-start | bytes 98312 | tf_op jit(solution)/shard_map/ppermute | solution.py:20
  18.0 6.5 %collective-permute-start.5 = (bf16[2,128,64]{2,1,0:T(8,128)(2,1)S(1)}, bf16[2,128,64]{2,1,0:T(8,128)(2,1)S(1)}, u32[]{:S(2)}, u32[]{:S(2)}) collective-permute-start(bf16[2,128,64]{2,1,0:T(8,128)(2,1)S(1)} %get-tuple-element.43), channel_id=1, source_target_pairs={{2,0},{3,1},{0,2},{1,3},{6,4},{7,5},{4,6},{5,7},{10,8},{11,9},{8,1... | collective-permute-start | bytes 98312 | tf_op jit(solution)/shard_map/ppermute | solution.py:20
  21.6 4.3 %collective-permute-start.4 = (bf16[2,128,64]{2,1,0:T(8,128)(2,1)S(1)}, bf16[2,128,64]{2,1,0:T(8,128)(2,1)S(1)}, u32[]{:S(2)}, u32[]{:S(2)}) collective-permute-start(bf16[2,128,64]{2,1,0:T(8,128)(2,1)S(1)} %get-tuple-element.44), channel_id=1, source_target_pairs={{1,0},{2,1},{3,2},{0,3},{5,4},{6,5},{7,6},{4,7},{9,8},{10,9},{11,1... | collective-permute-start | bytes 98312 | tf_op jit(solution)/shard_map/ppermute | solution.py:20
  25.9 1.3 collective-permute-start.6
  34.2 13.5 %collective-permute-start.11 = (bf16[64,2752]{1,0:T(8,128)(2,1)}, bf16[64,2752]{1,0:T(8,128)(2,1)S(1)}, u32[]{:S(2)}, u32[]{:S(2)}) collective-permute-start(bf16[64,2752]{1,0:T(8,128)(2,1)} %get-tuple-element.27), channel_id=1, source_target_pairs={{96,0},{0,32},{32,64},{64,96},{97,1},{1,33},{33,65},{65,97},{98,2}... | collective-permute-start | bytes 1056776 | tf_op jit(solution)/shard_map/ppermute | solution.py:20
  35.7 22.0 %collective-permute-start.12 = (bf16[64,2752]{1,0:T(8,128)(2,1)}, bf16[64,2752]{1,0:T(8,128)(2,1)S(1)}, u32[]{:S(2)}, u32[]{:S(2)}) collective-permute-start(bf16[64,2752]{1,0:T(8,128)(2,1)} %get-tuple-element.28), channel_id=1, source_target_pairs={{64,0},{96,32},{0,64},{32,96},{65,1},{97,33},{1,65},{33,97},{66,2}... | collective-permute-start | bytes 1056776 | tf_op jit(solution)/shard_map/ppermute | solution.py:20
  38.4 19.3 %collective-permute-start.13 = (bf16[64,2752]{1,0:T(8,128)(2,1)}, bf16[64,2752]{1,0:T(8,128)(2,1)S(1)}, u32[]{:S(2)}, u32[]{:S(2)}) collective-permute-start(bf16[64,2752]{1,0:T(8,128)(2,1)} %get-tuple-element.29), channel_id=1, source_target_pairs={{32,0},{64,32},{96,64},{0,96},{33,1},{65,33},{97,65},{1,97},{34,2}... | collective-permute-start | bytes 1056776 | tf_op jit(solution)/shard_map/ppermute | solution.py:20
  46.2 17.0 %collective-permute-start.8 = (bf16[64,2752]{1,0:T(8,128)(2,1)}, bf16[64,2752]{1,0:T(8,128)(2,1)S(1)}, u32[]{:S(2)}, u32[]{:S(2)}) collective-permute-start(bf16[64,2752]{1,0:T(8,128)(2,1)} %get-tuple-element.24), channel_id=1, source_target_pairs={{96,0},{0,32},{32,64},{64,96},{97,1},{1,33},{33,65},{65,97},{98,2}... | collective-permute-start | bytes 1056776 | tf_op jit(solution)/shard_map/ppermute | solution.py:20
  46.8 23.5 %collective-permute-start.9 = (bf16[64,2752]{1,0:T(8,128)(2,1)}, bf16[64,2752]{1,0:T(8,128)(2,1)S(1)}, u32[]{:S(2)}, u32[]{:S(2)}) collective-permute-start(bf16[64,2752]{1,0:T(8,128)(2,1)} %get-tuple-element.25), channel_id=1, source_target_pairs={{64,0},{96,32},{0,64},{32,96},{65,1},{97,33},{1,65},{33,97},{66,2}... | collective-permute-start | bytes 1056776 | tf_op jit(solution)/shard_map/ppermute | solution.py:20
  47.7 22.6 %collective-permute-start.10 = (bf16[64,2752]{1,0:T(8,128)(2,1)}, bf16[64,2752]{1,0:T(8,128)(2,1)S(1)}, u32[]{:S(2)}, u32[]{:S(2)}) collective-permute-start(bf16[64,2752]{1,0:T(8,128)(2,1)} %get-tuple-element.26), channel_id=1, source_target_pairs={{32,0},{64,32},{96,64},{0,96},{33,1},{65,33},{97,65},{1,97},{34,2}... | collective-permute-start | bytes 1056776 | tf_op jit(solution)/shard_map/ppermute | solution.py:20
  74.2 7.4 %collective-permute-start.23 = (bf16[64,1408]{1,0:T(8,128)(2,1)}, bf16[64,1408]{1,0:T(8,128)(2,1)S(1)}, u32[]{:S(2)}, u32[]{:S(2)}) collective-permute-start(bf16[64,1408]{1,0:T(8,128)(2,1)} %get-tuple-element.34.refs_0_), channel_id=1, source_target_pairs={{3,0},{0,1},{1,2},{2,3},{7,4},{4,5},{5,6},{6,7},{11,8},{8,9},{9,10... | collective-permute-start | bytes 540680 | tf_op jit(solution)/shard_map/ppermute | solution.py:20
  74.6 9.7 %collective-permute-start.30 = (bf16[64,1408]{1,0:T(8,128)(2,1)S(1)}, bf16[64,1408]{1,0:T(8,128)(2,1)S(1)}, u32[]{:S(2)}, u32[]{:S(2)}) collective-permute-start(bf16[64,1408]{1,0:T(8,128)(2,1)S(1)} %copy-done.23), channel_id=1, source_target_pairs={{12,0},{0,4},{4,8},{8,12},{13,1},{1,5},{5,9},{9,13},{14,2},{2,6},{... | collective-permute-start | bytes 540680 | tf_op jit(solution)/shard_map/ppermute | solution.py:20
  75.9 10.1 %collective-permute-start.29 = (bf16[64,1408]{1,0:T(8,128)(2,1)S(1)}, bf16[64,1408]{1,0:T(8,128)(2,1)S(1)}, u32[]{:S(2)}, u32[]{:S(2)}) collective-permute-start(bf16[64,1408]{1,0:T(8,128)(2,1)S(1)} %copy-done.23), channel_id=1, source_target_pairs={{8,0},{12,4},{0,8},{4,12},{9,1},{13,5},{1,9},{5,13},{10,2},{14,6},... | collective-permute-start | bytes 540680 | tf_op jit(solution)/shard_map/ppermute | solution.py:20
  78.3 10.8 %collective-permute-start.28 = (bf16[64,1408]{1,0:T(8,128)(2,1)S(1)}, bf16[64,1408]{1,0:T(8,128)(2,1)S(1)}, u32[]{:S(2)}, u32[]{:S(2)}) collective-permute-start(bf16[64,1408]{1,0:T(8,128)(2,1)S(1)} %copy-done.23), channel_id=1, source_target_pairs={{4,0},{8,4},{12,8},{0,12},{5,1},{9,5},{13,9},{1,13},{6,2},{10,6},{... | collective-permute-start | bytes 540680 | tf_op jit(solution)/shard_map/ppermute | solution.py:20
  79.8 9.7 %collective-permute-start.36 = (bf16[64,1408]{1,0:T(8,128)(2,1)S(1)}, bf16[64,1408]{1,0:T(8,128)(2,1)S(1)}, u32[]{:S(2)}, u32[]{:S(2)}) collective-permute-start(bf16[64,1408]{1,0:T(8,128)(2,1)S(1)} %copy-done.22), channel_id=1, source_target_pairs={{3,0},{0,1},{1,2},{2,3},{7,4},{4,5},{5,6},{6,7},{11,8},{8,9},{9,10... | collective-permute-start | bytes 540680 | tf_op jit(solution)/shard_map/ppermute | solution.py:20
  81.7 23.3 %copy-start.24 = (bf16[64,1408]{1,0:T(8,128)(2,1)}, bf16[64,1408]{1,0:T(8,128)(2,1)S(1)}, u32[]{:S(2)}) copy-start(bf16[64,1408]{1,0:T(8,128)(2,1)S(1)} %collective-permute-done.23.refs_3_) | copy-start | bytes 540676
  81.7 11.1 %collective-permute-start.35 = (bf16[64,1408]{1,0:T(8,128)(2,1)S(1)}, bf16[64,1408]{1,0:T(8,128)(2,1)S(1)}, u32[]{:S(2)}, u32[]{:S(2)}) collective-permute-start(bf16[64,1408]{1,0:T(8,128)(2,1)S(1)} %copy-done.22), channel_id=1, source_target_pairs={{2,0},{3,1},{0,2},{1,3},{6,4},{7,5},{4,6},{5,7},{10,8},{11,9},{8,1... | collective-permute-start | bytes 540680 | tf_op jit(solution)/shard_map/ppermute | solution.py:20
  84.4 10.2 %collective-permute-start.34 = (bf16[64,1408]{1,0:T(8,128)(2,1)S(1)}, bf16[64,1408]{1,0:T(8,128)(2,1)S(1)}, u32[]{:S(2)}, u32[]{:S(2)}) collective-permute-start(bf16[64,1408]{1,0:T(8,128)(2,1)S(1)} %copy-done.22), channel_id=1, source_target_pairs={{1,0},{2,1},{3,2},{0,3},{5,4},{6,5},{7,6},{4,7},{9,8},{10,9},{11,1... | collective-permute-start | bytes 540680 | tf_op jit(solution)/shard_map/ppermute | solution.py:20
  86.0 14.2 %collective-permute-start.22 = (bf16[64,1408]{1,0:T(8,128)(2,1)}, bf16[64,1408]{1,0:T(8,128)(2,1)S(1)}, u32[]{:S(2)}, u32[]{:S(2)}) collective-permute-start(bf16[64,1408]{1,0:T(8,128)(2,1)} %get-tuple-element.34.refs_0_), channel_id=1, source_target_pairs={{2,0},{3,1},{0,2},{1,3},{6,4},{7,5},{4,6},{5,7},{10,8},{11,9},{8,1... | collective-permute-start | bytes 540680 | tf_op jit(solution)/shard_map/ppermute | solution.py:20
  89.1 12.2 %collective-permute-start.21 = (bf16[64,1408]{1,0:T(8,128)(2,1)}, bf16[64,1408]{1,0:T(8,128)(2,1)S(1)}, u32[]{:S(2)}, u32[]{:S(2)}) collective-permute-start(bf16[64,1408]{1,0:T(8,128)(2,1)} %get-tuple-element.34.refs_0_), channel_id=1, source_target_pairs={{1,0},{2,1},{3,2},{0,3},{5,4},{6,5},{7,6},{4,7},{9,8},{10,9},{11,1... | collective-permute-start | bytes 540680 | tf_op jit(solution)/shard_map/ppermute | solution.py:20
  89.6 17.6 %collective-permute-start.16 = (bf16[64,1408]{1,0:T(8,128)(2,1)}, bf16[64,1408]{1,0:T(8,128)(2,1)S(1)}, u32[]{:S(2)}, u32[]{:S(2)}) collective-permute-start(bf16[64,1408]{1,0:T(8,128)(2,1)} %get-tuple-element.33.refs_0_), channel_id=1, source_target_pairs={{12,0},{0,4},{4,8},{8,12},{13,1},{1,5},{5,9},{9,13},{14,2},{2,6},{... | collective-permute-start | bytes 540680 | tf_op jit(solution)/shard_map/ppermute | solution.py:20
  92.8 14.9 %collective-permute-start.15 = (bf16[64,1408]{1,0:T(8,128)(2,1)}, bf16[64,1408]{1,0:T(8,128)(2,1)S(1)}, u32[]{:S(2)}, u32[]{:S(2)}) collective-permute-start(bf16[64,1408]{1,0:T(8,128)(2,1)} %get-tuple-element.33.refs_0_), channel_id=1, source_target_pairs={{8,0},{12,4},{0,8},{4,12},{9,1},{13,5},{1,9},{5,13},{10,2},{14,6},... | collective-permute-start | bytes 540680 | tf_op jit(solution)/shard_map/ppermute | solution.py:20
  94.6 15.8 %collective-permute-start.14 = (bf16[64,1408]{1,0:T(8,128)(2,1)}, bf16[64,1408]{1,0:T(8,128)(2,1)S(1)}, u32[]{:S(2)}, u32[]{:S(2)}) collective-permute-start(bf16[64,1408]{1,0:T(8,128)(2,1)} %get-tuple-element.33.refs_0_), channel_id=1, source_target_pairs={{4,0},{8,4},{12,8},{0,12},{5,1},{9,5},{13,9},{1,13},{6,2},{10,6},{... | collective-permute-start | bytes 540680 | tf_op jit(solution)/shard_map/ppermute | solution.py:20
  98.0 26.8 %copy-start.1 = (bf16[256,1408]{1,0:T(8,128)(2,1)S(1)}, bf16[256,1408]{1,0:T(8,128)(2,1)}, u32[]{:S(2)}) copy-start(bf16[256,1408]{1,0:T(8,128)(2,1)} %shard_map.83.refs_1_) | copy-start | bytes 2162692
  100.2 22.6 %copy-start.2 = (bf16[256,1408]{1,0:T(8,128)(2,1)S(1)}, bf16[256,1408]{1,0:T(8,128)(2,1)}, u32[]{:S(2)}) copy-start(bf16[256,1408]{1,0:T(8,128)(2,1)} %shard_map.84.refs_6_) | copy-start | bytes 2162692
  100.2 19.4 %collective-permute-start.37 = (bf16[256,1408]{1,0:T(8,128)(2,1)}, bf16[256,1408]{1,0:T(8,128)(2,1)S(1)}, u32[]{:S(2)}, u32[]{:S(2)}) collective-permute-start(bf16[256,1408]{1,0:T(8,128)(2,1)} %shard_map.84.refs_6_), channel_id=1, source_target_pairs={{4,0},{8,4},{12,8},{0,12},{5,1},{9,5},{13,9},{1,13},{6,2},{10,6},{... | collective-permute-start | bytes 2162696 | tf_op jit(solution)/shard_map/ppermute | solution.py:20
  101.3 21.5 %collective-permute-start.31 = (bf16[256,1408]{1,0:T(8,128)(2,1)}, bf16[256,1408]{1,0:T(8,128)(2,1)S(1)}, u32[]{:S(2)}, u32[]{:S(2)}) collective-permute-start(bf16[256,1408]{1,0:T(8,128)(2,1)} %shard_map.83.refs_1_), channel_id=1, source_target_pairs={{1,0},{2,1},{3,2},{0,3},{5,4},{6,5},{7,6},{4,7},{9,8},{10,9},{11,1... | collective-permute-start | bytes 2162696 | tf_op jit(solution)/shard_map/ppermute | solution.py:20
  107.1 17.7 %collective-permute-start.26 = (bf16[256,1408]{1,0:T(8,128)(2,1)}, bf16[256,1408]{1,0:T(8,128)(2,1)S(1)}, u32[]{:S(2)}, u32[]{:S(2)}) collective-permute-start(bf16[256,1408]{1,0:T(8,128)(2,1)} %shard_map.82.refs_7_), channel_id=1, source_target_pairs={{12,0},{0,4},{4,8},{8,12},{13,1},{1,5},{5,9},{9,13},{14,2},{2,6},{... | collective-permute-start | bytes 2162696 | tf_op jit(solution)/shard_map/ppermute | solution.py:20
  107.7 23.6 %collective-permute-start.24 = (bf16[256,1408]{1,0:T(8,128)(2,1)}, bf16[256,1408]{1,0:T(8,128)(2,1)S(1)}, u32[]{:S(2)}, u32[]{:S(2)}) collective-permute-start(bf16[256,1408]{1,0:T(8,128)(2,1)} %shard_map.82.refs_7_), channel_id=1, source_target_pairs={{4,0},{8,4},{12,8},{0,12},{5,1},{9,5},{13,9},{1,13},{6,2},{10,6},{... | collective-permute-start | bytes 2162696 | tf_op jit(solution)/shard_map/ppermute | solution.py:20
  113.2 20.8 %collective-permute-start.19 = (bf16[256,1408]{1,0:T(8,128)(2,1)}, bf16[256,1408]{1,0:T(8,128)(2,1)S(1)}, u32[]{:S(2)}, u32[]{:S(2)}) collective-permute-start(bf16[256,1408]{1,0:T(8,128)(2,1)} %shard_map.81.refs_1_), channel_id=1, source_target_pairs={{3,0},{0,1},{1,2},{2,3},{7,4},{4,5},{5,6},{6,7},{11,8},{8,9},{9,10... | collective-permute-start | bytes 2162696 | tf_op jit(solution)/shard_map/ppermute | solution.py:20
  119.6 33.7 %copy-start.7 = (bf16[256,1408]{1,0:T(8,128)(2,1)}, bf16[256,1408]{1,0:T(8,128)(2,1)S(1)}, u32[]{:S(2)}) copy-start(bf16[256,1408]{1,0:T(8,128)(2,1)S(1)} %collective-permute-done.37.refs_7_) | copy-start | bytes 2162692
  119.6 18.9 %collective-permute-start.17 = (bf16[256,1408]{1,0:T(8,128)(2,1)}, bf16[256,1408]{1,0:T(8,128)(2,1)S(1)}, u32[]{:S(2)}, u32[]{:S(2)}) collective-permute-start(bf16[256,1408]{1,0:T(8,128)(2,1)} %shard_map.81.refs_1_), channel_id=1, source_target_pairs={{1,0},{2,1},{3,2},{0,3},{5,4},{6,5},{7,6},{4,7},{9,8},{10,9},{11,1... | collective-permute-start | bytes 2162696 | tf_op jit(solution)/shard_map/ppermute | solution.py:20
  122.8 30.5 %copy-start.8 = (bf16[256,1408]{1,0:T(8,128)(2,1)}, bf16[256,1408]{1,0:T(8,128)(2,1)S(1)}, u32[]{:S(2)}) copy-start(bf16[256,1408]{1,0:T(8,128)(2,1)S(1)} %collective-permute-done.31.refs_2_) | copy-start | bytes 2162692
  122.8 17.1 %collective-permute-start.39 = (bf16[256,1408]{1,0:T(8,128)(2,1)S(1)}, bf16[256,1408]{1,0:T(8,128)(2,1)S(1)}, u32[]{:S(2)}, u32[]{:S(2)}) collective-permute-start(bf16[256,1408]{1,0:T(8,128)(2,1)S(1)} %copy-done.2), channel_id=1, source_target_pairs={{12,0},{0,4},{4,8},{8,12},{13,1},{1,5},{5,9},{9,13},{14,2},{2,6},{... | collective-permute-start | bytes 2162696 | tf_op jit(solution)/shard_map/ppermute | solution.py:20
  124.8 35.6 %copy-start.3 = (bf16[256,1408]{1,0:T(8,128)(2,1)}, bf16[256,1408]{1,0:T(8,128)(2,1)S(1)}, u32[]{:S(2)}) copy-start(bf16[256,1408]{1,0:T(8,128)(2,1)S(1)} %collective-permute-done.26.refs_11_) | copy-start | bytes 2162692
  124.8 18.6 %collective-permute-start.33 = (bf16[256,1408]{1,0:T(8,128)(2,1)S(1)}, bf16[256,1408]{1,0:T(8,128)(2,1)S(1)}, u32[]{:S(2)}, u32[]{:S(2)}) collective-permute-start(bf16[256,1408]{1,0:T(8,128)(2,1)S(1)} %copy-done.1), channel_id=1, source_target_pairs={{3,0},{0,1},{1,2},{2,3},{7,4},{4,5},{5,6},{6,7},{11,8},{8,9},{9,10... | collective-permute-start | bytes 2162696 | tf_op jit(solution)/shard_map/ppermute | solution.py:20
  131.3 29.1 %copy-start.4 = (bf16[256,1408]{1,0:T(8,128)(2,1)}, bf16[256,1408]{1,0:T(8,128)(2,1)S(1)}, u32[]{:S(2)}) copy-start(bf16[256,1408]{1,0:T(8,128)(2,1)S(1)} %collective-permute-done.24.refs_8_) | copy-start | bytes 2162692
  131.3 19.1 %collective-permute-start.38 = (bf16[256,1408]{1,0:T(8,128)(2,1)S(1)}, bf16[256,1408]{1,0:T(8,128)(2,1)S(1)}, u32[]{:S(2)}, u32[]{:S(2)}) collective-permute-start(bf16[256,1408]{1,0:T(8,128)(2,1)S(1)} %collective-permute-done.37.refs_7_), channel_id=1, source_target_pairs={{4,0},{8,4},{12,8},{0,12},{5,1},{9,5},{13,9},{1,13},{6,2},{10,6},{... | collective-permute-start | bytes 2162696 | tf_op jit(solution)/shard_map/ppermute | solution.py:20
  134.0 26.5 %copy-start.5 = (bf16[256,1408]{1,0:T(8,128)(2,1)}, bf16[256,1408]{1,0:T(8,128)(2,1)S(1)}, u32[]{:S(2)}) copy-start(bf16[256,1408]{1,0:T(8,128)(2,1)S(1)} %collective-permute-done.19.refs_5_) | copy-start | bytes 2162692
  134.0 18.4 %collective-permute-start.32 = (bf16[256,1408]{1,0:T(8,128)(2,1)S(1)}, bf16[256,1408]{1,0:T(8,128)(2,1)S(1)}, u32[]{:S(2)}, u32[]{:S(2)}) collective-permute-start(bf16[256,1408]{1,0:T(8,128)(2,1)S(1)} %collective-permute-done.31.refs_2_), channel_id=1, source_target_pairs={{1,0},{2,1},{3,2},{0,3},{5,4},{6,5},{7,6},{4,7},{9,8},{10,9},{11,1... | collective-permute-start | bytes 2162696 | tf_op jit(solution)/shard_map/ppermute | solution.py:20
  138.5 21.9 %collective-permute-start.27 = (bf16[128,1408]{1,0:T(8,128)(2,1)}, bf16[128,1408]{1,0:T(8,128)(2,1)}, u32[]{:S(2)}, u32[]{:S(2)}) collective-permute-start(bf16[128,1408]{1,0:T(8,128)(2,1)} %slice.79), channel_id=1, source_target_pairs={{12,0},{0,4},{4,8},{8,12},{13,1},{1,5},{5,9},{9,13},{14,2},{2,6},{... | collective-permute-start | bytes 1081352 | tf_op jit(solution)/shard_map/ppermute | solution.py:20
  139.9 20.5 %collective-permute-start.25 = (bf16[128,1408]{1,0:T(8,128)(2,1)}, bf16[128,1408]{1,0:T(8,128)(2,1)S(1)}, u32[]{:S(2)}, u32[]{:S(2)}) collective-permute-start(bf16[128,1408]{1,0:T(8,128)(2,1)} %slice.78), channel_id=1, source_target_pairs={{4,0},{8,4},{12,8},{0,12},{5,1},{9,5},{13,9},{1,13},{6,2},{10,6},{... | collective-permute-start | bytes 1081352 | tf_op jit(solution)/shard_map/ppermute | solution.py:20
  143.3 17.1 %collective-permute-start.20 = (bf16[128,1408]{1,0:T(8,128)(2,1)S(1)}, bf16[128,1408]{1,0:T(8,128)(2,1)S(1)}, u32[]{:S(2)}, u32[]{:S(2)}) collective-permute-start(bf16[128,1408]{1,0:T(8,128)(2,1)S(1)} %slice.77), channel_id=1, source_target_pairs={{3,0},{0,1},{1,2},{2,3},{7,4},{4,5},{5,6},{6,7},{11,8},{8,9},{9,10... | collective-permute-start | bytes 1081352 | tf_op jit(solution)/shard_map/ppermute | solution.py:20
  150.3 10.1 %collective-permute-start.18 = (bf16[128,1408]{1,0:T(8,128)(2,1)}, bf16[128,1408]{1,0:T(8,128)(2,1)S(1)}, u32[]{:S(2)}, u32[]{:S(2)}) collective-permute-start(bf16[128,1408]{1,0:T(8,128)(2,1)} %slice.76), channel_id=1, source_target_pairs={{1,0},{2,1},{3,2},{0,3},{5,4},{6,5},{7,6},{4,7},{9,8},{10,9},{11,1... | collective-permute-start | bytes 1081352 | tf_op jit(solution)/shard_map/ppermute | solution.py:20
  (28 other events, 143.2 us)

commit v6 on v5

--- a/solution.py
+++ b/solution.py
@@ -292,15 +292,16 @@
     sums = [send(value, "x", i + 1) for i, value in enumerate(sums)]
     sums_1 = [send(value, "x", i + 1) for i, value in enumerate(sums_1)]
 
-    moments, update = [], None
+    moments, update, after = [], None, columns_y
     for which, parts in enumerate(([own_sum, sums], [own_sum_1, sums_1])):
         *moments, left, right = directions(
-            *parts, first_moment, second_moment, which, 2, moments, columns_y
+            *parts, first_moment, second_moment, which, 2, moments, after
         )
         halves = [
             (columns_z, ring_gather(left, "y", "z", which == 1)),
             (columns_y, ring_gather(right, "z", "y", which == 1)),
         ]
+        after = halves[0][1][0]
         update = expand_halves(halves, which, width, update)
     return jnp.swapaxes(update, 1, 2), *moments
 

time: 171 us -> 165 us (0.965)
  starting transfers between devices: 64.7 us -> 56.4 us
  waiting for transfers between devices: 40.1 us -> 43.7 us
    ppermute x38, starting transfers between devices: 64.5 us -> 56.2 us  [receive(): lax.ppermute(value, axis, [((i + distance) % SIDE, i) for i in range(SIDE)])]
    ppermute x38, waiting for transfers between devices: 39.5 us -> 43.1 us  [receive(): lax.ppermute(value, axis, [((i + distance) % SIDE, i) for i in range(SIDE)])]
    unnamed x72 -> x68, local copies, waits for them, and re-layouts: 6.45 us -> 6.46 us
  transfers between devices with their start and end apart: 40 -> 40, of which waited for: 14 -> 14; matrix products, arithmetic and copies ran while one was open for 4% -> 5% of each run, Pallas kernels for 20% -> 22%
where the time goes in v6:
time: 165 us
  starting transfers between devices  56.4 us (34%)
  Pallas kernels  49.6 us (30%)
  waiting for transfers between devices  43.7 us (26%)
  local copies, waits for them, and re-layouts  10.3 us (6%)
  matrix products  2.91 us (2%)
    ppermute x38, starting transfers between devices, receive(): lax.ppermute(value, axis, [((i + distance) % SIDE, i) for i in range(SIDE)])  56.2 us
    ppermute x38, waiting for transfers between devices, receive(): lax.ppermute(value, axis, [((i + distance) % SIDE, i) for i in range(SIDE)])  43.1 us
    pallas_call x2, Pallas kernels, expand_halves(): pl.pallas_call(functools.partial(expand_kernel, counts=counts, which=whic...  14.1 us
    pallas_call x2, Pallas kernels, partial_grads(): pl.pallas_call(partial_kernel, grid_spec=pltpu.PrefetchScalarGridSpec(num...  12.7 us
    pallas_call x4, Pallas kernels, stack(): pl.pallas_call(stack_kernel, out_shape=held((rows * len(pieces), width)),...  8.54 us
    pallas_call x1, Pallas kernels, arrange(): pl.pallas_call(arrange_kernel, grid_spec=pltpu.PrefetchScalarGridSpec(num...  8.13 us
    unnamed x68, local copies, waits for them, and re-layouts  6.46 us
    pallas_call x2, Pallas kernels, directions(): pl.pallas_call(functools.partial(direction_kernel, pieces=pieces), grid=(...  6.1 us
  transfers between devices with their start and end apart: 40, of which 14 were waited for; matrix products, arithmetic and copies ran while one was open for 5% of the time, Pallas kernels for 22%

profile of v6, /device:TPU:0, one launch (start us, length us, event | category | flops | bytes accessed | tf_op | source)
XLA Modules:
  0.0 164.7 jit_solution(12583353936823415858)
XLA Ops:
  0.8 1.5 copy-done
  2.2 2.9 %fusion.4 = bf16[2,128,1024]{2,1,0:T(8,128)(2,1)S(1)} fusion(s32[1024]{0:T(1024)S(1)} %fusion.21, bf16[2,512,1024]{2,1,0:T(8,128)(2,1)} %bases_ref.1, bf16[128,8192]{1,0:T(8,128)(2,1)S(1)} %copy-done, s32[]{:T(128)S(6)} %select_n.54), kind=kOutput, calls=%fused_computation.4 | convolution fusion | flops 806879232 | bytes 2756612 | tf_op jit(solution)/shard_map/ktr,rs->kts/dot_general | solution.py:275
  5.2 1.7 %collective-permute-start = (bf16[2,128,256]{2,1,0:T(8,128)(2,1)S(1)}, bf16[2,128,256]{2,1,0:T(8,128)(2,1)S(1)}, u32[]{:S(2)}, u32[]{:S(2)}) collective-permute-start(bf16[2,128,256]{2,1,0:T(8,128)(2,1)S(1)} %get-tuple-element.39), channel_id=1, source_target_pairs={{12,0},{0,4},{4,8},{8,12},{13,1},{1,5},{5,9},{9,13},{14,2},{2,6},{... | collective-permute-start | bytes 393224 | tf_op jit(solution)/shard_map/ppermute | solution.py:20
  6.9 1.6 collective-permute-start.1
  8.5 2.1 %collective-permute-start.2 = (bf16[2,128,256]{2,1,0:T(8,128)(2,1)S(1)}, bf16[2,128,256]{2,1,0:T(8,128)(2,1)S(1)}, u32[]{:S(2)}, u32[]{:S(2)}) collective-permute-start(bf16[2,128,256]{2,1,0:T(8,128)(2,1)S(1)} %get-tuple-element.40), channel_id=1, source_target_pairs={{8,0},{12,4},{0,8},{4,12},{9,1},{13,5},{1,9},{5,13},{10,2},{14,6},... | collective-permute-start | bytes 393224 | tf_op jit(solution)/shard_map/ppermute | solution.py:20
  11.8 2.2 %collective-permute-done.1 = bf16[2,128,256]{2,1,0:T(8,128)(2,1)S(1)} collective-permute-done((bf16[2,128,256]{2,1,0:T(8,128)(2,1)S(1)}, bf16[2,128,256]{2,1,0:T(8,128)(2,1)S(1)}, u32[]{:S(2)}, u32[]{:S(2)}) %collective-permute-start.1) | collective-permute-done | bytes 131104 | tf_op jit(solution)/shard_map/ppermute | solution.py:20
  14.0 1.8 %collective-permute-done.2 = bf16[2,128,256]{2,1,0:T(8,128)(2,1)S(1)} collective-permute-done((bf16[2,128,256]{2,1,0:T(8,128)(2,1)S(1)}, bf16[2,128,256]{2,1,0:T(8,128)(2,1)S(1)}, u32[]{:S(2)}, u32[]{:S(2)}) %collective-permute-start.2) | collective-permute-done | bytes 131104 | tf_op jit(solution)/shard_map/ppermute | solution.py:20
  16.0 2.0 %collective-permute-start.3 = (bf16[2,128,64]{2,1,0:T(8,128)(2,1)S(1)}, bf16[2,128,64]{2,1,0:T(8,128)(2,1)S(1)}, u32[]{:S(2)}, u32[]{:S(2)}) collective-permute-start(bf16[2,128,64]{2,1,0:T(8,128)(2,1)S(1)} %get-tuple-element.42), channel_id=1, source_target_pairs={{3,0},{0,1},{1,2},{2,3},{7,4},{4,5},{5,6},{6,7},{11,8},{8,9},{9,10... | collective-permute-start | bytes 98312 | tf_op jit(solution)/shard_map/ppermute | solution.py:20
  18.0 2.2 %collective-permute-start.4 = (bf16[2,128,64]{2,1,0:T(8,128)(2,1)S(1)}, bf16[2,128,64]{2,1,0:T(8,128)(2,1)S(1)}, u32[]{:S(2)}, u32[]{:S(2)}) collective-permute-start(bf16[2,128,64]{2,1,0:T(8,128)(2,1)S(1)} %get-tuple-element.44), channel_id=1, source_target_pairs={{1,0},{2,1},{3,2},{0,3},{5,4},{6,5},{7,6},{4,7},{9,8},{10,9},{11,1... | collective-permute-start | bytes 98312 | tf_op jit(solution)/shard_map/ppermute | solution.py:20
  20.2 1.8 %collective-permute-start.5 = (bf16[2,128,64]{2,1,0:T(8,128)(2,1)S(1)}, bf16[2,128,64]{2,1,0:T(8,128)(2,1)S(1)}, u32[]{:S(2)}, u32[]{:S(2)}) collective-permute-start(bf16[2,128,64]{2,1,0:T(8,128)(2,1)S(1)} %get-tuple-element.43), channel_id=1, source_target_pairs={{2,0},{3,1},{0,2},{1,3},{6,4},{7,5},{4,6},{5,7},{10,8},{11,9},{8,1... | collective-permute-start | bytes 98312 | tf_op jit(solution)/shard_map/ppermute | solution.py:20
  22.6 3.4 %collective-permute-done.5 = bf16[2,128,64]{2,1,0:T(8,128)(2,1)S(1)} collective-permute-done((bf16[2,128,64]{2,1,0:T(8,128)(2,1)S(1)}, bf16[2,128,64]{2,1,0:T(8,128)(2,1)S(1)}, u32[]{:S(2)}, u32[]{:S(2)}) %collective-permute-start.5) | collective-permute-done | bytes 32800 | tf_op jit(solution)/shard_map/ppermute | solution.py:20
  28.0 6.3 %shard_map.76 = (f32[64,2752]{1,0:T(8,128)}, bf16[64,2752]{1,0:T(8,128)(2,1)}, bf16[64,2752]{1,0:T(8,128)(2,1)}, bf16[64,2752]{1,0:T(8,128)(2,1)}) custom-call(s32[4]{0:T(128)} %pad_add_fusion.where_ref._, bf16[128,64]{1,0:T(8,128)(2,1)} %get-tuple-element.47.proj_ref, bf16[128,64]{1,0:T(8,128)(2,1)} %get-tuple-element.45.other_proj_ref, ...), custom_call_target="tpu_custom_call" | custom-call | flops 360710144 | bytes 8454144 | tf_op jit(solution)/shard_map/pallas_call | solution.py:100
  34.3 1.5 collective-permute-start.11
  35.8 2.7 %collective-permute-start.12 = (bf16[64,2752]{1,0:T(8,128)(2,1)}, bf16[64,2752]{1,0:T(8,128)(2,1)S(1)}, u32[]{:S(2)}, u32[]{:S(2)}) collective-permute-start(bf16[64,2752]{1,0:T(8,128)(2,1)} %get-tuple-element.28), channel_id=1, source_target_pairs={{64,0},{96,32},{0,64},{32,96},{65,1},{97,33},{1,65},{33,97},{66,2}... | collective-permute-start | bytes 1056776 | tf_op jit(solution)/shard_map/ppermute | solution.py:20
  38.5 1.4 collective-permute-start.13
  40.0 6.4 %shard_map.77 = (f32[64,2752]{1,0:T(8,128)}, bf16[64,2752]{1,0:T(8,128)(2,1)}, bf16[64,2752]{1,0:T(8,128)(2,1)}, bf16[64,2752]{1,0:T(8,128)(2,1)}) custom-call(s32[4]{0:T(128)} %pad_add_fusion.where_ref._, bf16[128,64]{1,0:T(8,128)(2,1)} %get-tuple-element.48.proj_ref, bf16[128,64]{1,0:T(8,128)(2,1)} %get-tuple-element.46.other_proj_ref, ...), custom_call_target="tpu_custom_call" | custom-call | flops 360710144 | bytes 8454144 | tf_op jit(solution)/shard_map/pallas_call | solution.py:100
  46.3 2.0 %collective-permute-start.8 = (bf16[64,2752]{1,0:T(8,128)(2,1)}, bf16[64,2752]{1,0:T(8,128)(2,1)S(1)}, u32[]{:S(2)}, u32[]{:S(2)}) collective-permute-start(bf16[64,2752]{1,0:T(8,128)(2,1)} %get-tuple-element.24), channel_id=1, source_target_pairs={{96,0},{0,32},{32,64},{64,96},{97,1},{1,33},{33,65},{65,97},{98,2}... | collective-permute-start | bytes 1056776 | tf_op jit(solution)/shard_map/ppermute | solution.py:20
  49.1 8.1 %shard_map.78 = (bf16[2,512,1024]{2,1,0:T(8,128)(2,1)}, bf16[2,512,1024]{2,1,0:T(8,128)(2,1)}) custom-call(s32[4]{0:T(128)} %pad_add_fusion.where_ref._, bf16[2,512,1024]{2,1,0:T(8,128)(2,1)} %bases_ref.1, f32[64,2752]{1,0:T(8,128)} %get-tuple-element.22._.refs_0_), custom_call_target="tpu_custom_call" | custom-call | flops 4294967296 | bytes 6291456 | tf_op jit(solution)/shard_map/pallas_call | solution.py:61
  58.1 3.0 %shard_map.79 = (f32[2,64,2752]{2,1,0:T(8,128)}, f32[2,64,2752]{2,1,0:T(8,128)}, bf16[64,1408]{1,0:T(8,128)(2,1)}, bf16[64,1408]{1,0:T(8,128)(2,1)}) custom-call(f32[64,2752]{1,0:T(8,128)} %get-tuple-element.21._.refs_0_, bf16[64,2752]{1,0:T(8,128)(2,1)} %copy-done.16, bf16[64,2752]{1,0:T(8,128)(2,1)} %copy-done.17, bf16[64,2752]{1,0:T(8,128)(2,1)} %copy-done.18, ...), custom_call_target="tpu_custom_call" | custom-call | flops 5283840 | bytes 4579328 | tf_op jit(solution)/shard_map/pallas_call | solution.py:153
  61.1 1.9 %collective-permute-start.14 = (bf16[64,1408]{1,0:T(8,128)(2,1)}, bf16[64,1408]{1,0:T(8,128)(2,1)S(1)}, u32[]{:S(2)}, u32[]{:S(2)}) collective-permute-start(bf16[64,1408]{1,0:T(8,128)(2,1)} %get-tuple-element.33.refs_0_), channel_id=1, source_target_pairs={{4,0},{8,4},{12,8},{0,12},{5,1},{9,5},{13,9},{1,13},{6,2},{10,6},{... | collective-permute-start | bytes 540680 | tf_op jit(solution)/shard_map/ppermute | solution.py:20
  63.1 1.3 collective-permute-start.15
  64.5 5.5 %collective-permute-done.14.refs_1_ = bf16[64,1408]{1,0:T(8,128)(2,1)S(1)} collective-permute-done((bf16[64,1408]{1,0:T(8,128)(2,1)}, bf16[64,1408]{1,0:T(8,128)(2,1)S(1)}, u32[]{:S(2)}, u32[]{:S(2)}) %collective-permute-start.14) | collective-permute-done | bytes 180256 | tf_op jit(solution)/shard_map/ppermute | solution.py:20
  70.0 1.9 %collective-permute-start.34 = (bf16[64,1408]{1,0:T(8,128)(2,1)}, bf16[64,1408]{1,0:T(8,128)(2,1)S(1)}, u32[]{:S(2)}, u32[]{:S(2)}) collective-permute-start(bf16[64,1408]{1,0:T(8,128)(2,1)} %get-tuple-element.36.refs_0_), channel_id=1, source_target_pairs={{1,0},{2,1},{3,2},{0,3},{5,4},{6,5},{7,6},{4,7},{9,8},{10,9},{11,1... | collective-permute-start | bytes 540680 | tf_op jit(solution)/shard_map/ppermute | solution.py:20
  71.9 1.5 collective-permute-start.35
  74.5 2.1 %shard_map.80.refs_8_.refs_1_ = bf16[256,1408]{1,0:T(8,128)(2,1)} custom-call(bf16[64,1408]{1,0:T(8,128)(2,1)} %get-tuple-element.33.refs_0_, bf16[64,1408]{1,0:T(8,128)(2,1)} %copy-done.31, bf16[64,1408]{1,0:T(8,128)(2,1)} %copy-done.32, bf16[64,1408]{1,0:T(8,128)(2,1)} %copy-done.33), custom_call_target="tpu_custom_call" | custom-call | bytes 1441792 | tf_op jit(solution)/shard_map/pallas_call | solution.py:173
  77.5 3.1 %shard_map.81 = (f32[2,64,2752]{2,1,0:T(8,128)}, f32[2,64,2752]{2,1,0:T(8,128)}, bf16[64,1408]{1,0:T(8,128)(2,1)}, bf16[64,1408]{1,0:T(8,128)(2,1)}) custom-call(f32[64,2752]{1,0:T(8,128)} %get-tuple-element.22._.refs_0_, bf16[64,2752]{1,0:T(8,128)(2,1)} %copy-done.14, bf16[64,2752]{1,0:T(8,128)(2,1)} %copy-done.15, ...), custom_call_target="tpu_custom_call", output_to_operand_aliasing={{0}: (6, {}), {1}: (7, {})} | custom-call | flops 5283840 | bytes 4579328 | tf_op jit(solution)/shard_map/pallas_call | solution.py:153
  80.6 2.3 %collective-permute-start.24 = (bf16[64,1408]{1,0:T(8,128)(2,1)}, bf16[64,1408]{1,0:T(8,128)(2,1)S(1)}, u32[]{:S(2)}, u32[]{:S(2)}) collective-permute-start(bf16[64,1408]{1,0:T(8,128)(2,1)} %get-tuple-element.35.refs_0_), channel_id=1, source_target_pairs={{1,0},{2,1},{3,2},{0,3},{5,4},{6,5},{7,6},{4,7},{9,8},{10,9},{11,1... | collective-permute-start | bytes 540680 | tf_op jit(solution)/shard_map/ppermute | solution.py:20
  84.6 2.8 %collective-permute-start.17 = (bf16[64,1408]{1,0:T(8,128)(2,1)}, bf16[64,1408]{1,0:T(8,128)(2,1)S(1)}, u32[]{:S(2)}, u32[]{:S(2)}) collective-permute-start(bf16[64,1408]{1,0:T(8,128)(2,1)} %get-tuple-element.34.refs_0_), channel_id=1, source_target_pairs={{4,0},{8,4},{12,8},{0,12},{5,1},{9,5},{13,9},{1,13},{6,2},{10,6},{... | collective-permute-start | bytes 540680 | tf_op jit(solution)/shard_map/ppermute | solution.py:20
  87.7 2.1 %collective-permute-done.24.refs_1_ = bf16[64,1408]{1,0:T(8,128)(2,1)S(1)} collective-permute-done((bf16[64,1408]{1,0:T(8,128)(2,1)}, bf16[64,1408]{1,0:T(8,128)(2,1)S(1)}, u32[]{:S(2)}, u32[]{:S(2)}) %collective-permute-start.24) | collective-permute-done | bytes 180256 | tf_op jit(solution)/shard_map/ppermute | solution.py:20
  89.8 2.2 %shard_map.84.refs_6_ = bf16[256,1408]{1,0:T(8,128)(2,1)} custom-call(bf16[64,1408]{1,0:T(8,128)(2,1)} %get-tuple-element.36.refs_0_, bf16[64,1408]{1,0:T(8,128)(2,1)} %copy-done.22, bf16[64,1408]{1,0:T(8,128)(2,1)} %copy-done.23, bf16[64,1408]{1,0:T(8,128)(2,1)} %copy-done.24), custom_call_target="tpu_custom_call" | custom-call | bytes 1441792 | tf_op jit(solution)/shard_map/pallas_call | solution.py:173
  92.0 3.2 %collective-permute-start.37 = (bf16[256,1408]{1,0:T(8,128)(2,1)}, bf16[256,1408]{1,0:T(8,128)(2,1)S(1)}, u32[]{:S(2)}, u32[]{:S(2)}) collective-permute-start(bf16[256,1408]{1,0:T(8,128)(2,1)} %shard_map.84.refs_6_), channel_id=1, source_target_pairs={{4,0},{8,4},{12,8},{0,12},{5,1},{9,5},{13,9},{1,13},{6,2},{10,6},{... | collective-permute-start | bytes 2162696 | tf_op jit(solution)/shard_map/ppermute | solution.py:20
  95.3 3.6 %collective-permute-start.31 = (bf16[256,1408]{1,0:T(8,128)(2,1)S(1)}, bf16[256,1408]{1,0:T(8,128)(2,1)S(1)}, u32[]{:S(2)}, u32[]{:S(2)}) collective-permute-start(bf16[256,1408]{1,0:T(8,128)(2,1)S(1)} %copy-done.1), channel_id=1, source_target_pairs={{1,0},{2,1},{3,2},{0,3},{5,4},{6,5},{7,6},{4,7},{9,8},{10,9},{11,1... | collective-permute-start | bytes 2162696 | tf_op jit(solution)/shard_map/ppermute | solution.py:20
  98.9 2.1 %shard_map.83.refs_7_ = bf16[256,1408]{1,0:T(8,128)(2,1)} custom-call(bf16[64,1408]{1,0:T(8,128)(2,1)} %get-tuple-element.35.refs_0_, bf16[64,1408]{1,0:T(8,128)(2,1)} %copy-done.26, bf16[64,1408]{1,0:T(8,128)(2,1)} %copy-done.28, bf16[64,1408]{1,0:T(8,128)(2,1)} %copy-done.30), custom_call_target="tpu_custom_call" | custom-call | bytes 1441792 | tf_op jit(solution)/shard_map/pallas_call | solution.py:173
  101.0 2.0 %collective-permute-start.29 = (bf16[256,1408]{1,0:T(8,128)(2,1)}, bf16[256,1408]{1,0:T(8,128)(2,1)S(1)}, u32[]{:S(2)}, u32[]{:S(2)}) collective-permute-start(bf16[256,1408]{1,0:T(8,128)(2,1)} %shard_map.83.refs_7_), channel_id=1, source_target_pairs={{12,0},{0,4},{4,8},{8,12},{13,1},{1,5},{5,9},{9,13},{14,2},{2,6},{... | collective-permute-start | bytes 2162696 | tf_op jit(solution)/shard_map/ppermute | solution.py:20
  103.7 2.1 %shard_map.82.refs_1_ = bf16[256,1408]{1,0:T(8,128)(2,1)} custom-call(bf16[64,1408]{1,0:T(8,128)(2,1)} %get-tuple-element.34.refs_0_, bf16[64,1408]{1,0:T(8,128)(2,1)} %copy-done.25, bf16[64,1408]{1,0:T(8,128)(2,1)} %copy-done.27, bf16[64,1408]{1,0:T(8,128)(2,1)} %copy-done.29), custom_call_target="tpu_custom_call" | custom-call | bytes 1441792 | tf_op jit(solution)/shard_map/pallas_call | solution.py:173
  106.4 5.7 %collective-permute-done.37.refs_7_ = bf16[256,1408]{1,0:T(8,128)(2,1)S(1)} collective-permute-done((bf16[256,1408]{1,0:T(8,128)(2,1)}, bf16[256,1408]{1,0:T(8,128)(2,1)S(1)}, u32[]{:S(2)}, u32[]{:S(2)}) %collective-permute-start.37) | collective-permute-done | bytes 720928 | tf_op jit(solution)/shard_map/ppermute | solution.py:20
  113.0 2.4 %collective-permute-done.31.refs_2_ = bf16[256,1408]{1,0:T(8,128)(2,1)S(1)} collective-permute-done((bf16[256,1408]{1,0:T(8,128)(2,1)S(1)}, bf16[256,1408]{1,0:T(8,128)(2,1)S(1)}, u32[]{:S(2)}, u32[]{:S(2)}) %collective-permute-start.31) | collective-permute-done | bytes 720928 | tf_op jit(solution)/shard_map/ppermute | solution.py:20
  115.5 8.3 %collective-permute-done.27.refs_8_ = bf16[256,1408]{1,0:T(8,128)(2,1)S(1)} collective-permute-done((bf16[256,1408]{1,0:T(8,128)(2,1)}, bf16[256,1408]{1,0:T(8,128)(2,1)S(1)}, u32[]{:S(2)}, u32[]{:S(2)}) %collective-permute-start.27) | collective-permute-done | bytes 720928 | tf_op jit(solution)/shard_map/ppermute | solution.py:20
  123.8 1.9 %collective-permute-start.33 = (bf16[256,1408]{1,0:T(8,128)(2,1)S(1)}, bf16[256,1408]{1,0:T(8,128)(2,1)S(1)}, u32[]{:S(2)}, u32[]{:S(2)}) collective-permute-start(bf16[256,1408]{1,0:T(8,128)(2,1)S(1)} %copy-done.1), channel_id=1, source_target_pairs={{3,0},{0,1},{1,2},{2,3},{7,4},{4,5},{5,6},{6,7},{11,8},{8,9},{9,10... | collective-permute-start | bytes 2162696 | tf_op jit(solution)/shard_map/ppermute | solution.py:20
  125.7 3.0 %collective-permute-start.38 = (bf16[256,1408]{1,0:T(8,128)(2,1)S(1)}, bf16[256,1408]{1,0:T(8,128)(2,1)S(1)}, u32[]{:S(2)}, u32[]{:S(2)}) collective-permute-start(bf16[256,1408]{1,0:T(8,128)(2,1)S(1)} %collective-permute-done.37.refs_7_), channel_id=1, source_target_pairs={{4,0},{8,4},{12,8},{0,12},{5,1},{9,5},{13,9},{1,13},{6,2},{10,6},{... | collective-permute-start | bytes 2162696 | tf_op jit(solution)/shard_map/ppermute | solution.py:20
  128.7 1.8 %collective-permute-start.32 = (bf16[256,1408]{1,0:T(8,128)(2,1)S(1)}, bf16[256,1408]{1,0:T(8,128)(2,1)S(1)}, u32[]{:S(2)}, u32[]{:S(2)}) collective-permute-start(bf16[256,1408]{1,0:T(8,128)(2,1)S(1)} %collective-permute-done.31.refs_2_), channel_id=1, source_target_pairs={{1,0},{2,1},{3,2},{0,3},{5,4},{6,5},{7,6},{4,7},{9,8},{10,9},{11,1... | collective-permute-start | bytes 2162696 | tf_op jit(solution)/shard_map/ppermute | solution.py:20
  133.1 1.9 %collective-permute-start.30 = (bf16[128,1408]{1,0:T(8,128)(2,1)}, bf16[128,1408]{1,0:T(8,128)(2,1)S(1)}, u32[]{:S(2)}, u32[]{:S(2)}) collective-permute-start(bf16[128,1408]{1,0:T(8,128)(2,1)} %slice.79), channel_id=1, source_target_pairs={{12,0},{0,4},{4,8},{8,12},{13,1},{1,5},{5,9},{9,13},{14,2},{2,6},{... | collective-permute-start | bytes 1081352 | tf_op jit(solution)/shard_map/ppermute | solution.py:20
  134.9 5.7 %collective-permute-done.33.refs_4_ = bf16[256,1408]{1,0:T(8,128)(2,1)S(1)} collective-permute-done((bf16[256,1408]{1,0:T(8,128)(2,1)S(1)}, bf16[256,1408]{1,0:T(8,128)(2,1)S(1)}, u32[]{:S(2)}, u32[]{:S(2)}) %collective-permute-start.33) | collective-permute-done | bytes 720928 | tf_op jit(solution)/shard_map/ppermute | solution.py:20
  140.6 2.0 %collective-permute-start.21 = (bf16[128,1408]{1,0:T(8,128)(2,1)S(1)}, bf16[128,1408]{1,0:T(8,128)(2,1)S(1)}, u32[]{:S(2)}, u32[]{:S(2)}) collective-permute-start(bf16[128,1408]{1,0:T(8,128)(2,1)S(1)} %slice.76), channel_id=1, source_target_pairs={{1,0},{2,1},{3,2},{0,3},{5,4},{6,5},{7,6},{4,7},{9,8},{10,9},{11,1... | collective-permute-start | bytes 1081352 | tf_op jit(solution)/shard_map/ppermute | solution.py:20
  142.7 2.6 %collective-permute-done.38.refs_8_ = bf16[256,1408]{1,0:T(8,128)(2,1)S(1)} collective-permute-done((bf16[256,1408]{1,0:T(8,128)(2,1)S(1)}, bf16[256,1408]{1,0:T(8,128)(2,1)S(1)}, u32[]{:S(2)}, u32[]{:S(2)}) %collective-permute-start.38) | collective-permute-done | bytes 720928 | tf_op jit(solution)/shard_map/ppermute | solution.py:20
  145.9 1.9 %collective-permute-done.32.refs_3_ = bf16[256,1408]{1,0:T(8,128)(2,1)S(1)} collective-permute-done((bf16[256,1408]{1,0:T(8,128)(2,1)S(1)}, bf16[256,1408]{1,0:T(8,128)(2,1)S(1)}, u32[]{:S(2)}, u32[]{:S(2)}) %collective-permute-start.32) | collective-permute-done | bytes 720928 | tf_op jit(solution)/shard_map/ppermute | solution.py:20
  148.7 7.1 %shard_map.85.refs_12_ = bf16[2,2752,512]{2,1,0:T(8,128)(2,1)} custom-call(bf16[2,512,1024]{2,1,0:T(8,128)(2,1)} %get-tuple-element.23.refs_0_, bf16[256,1408]{1,0:T(8,128)(2,1)} %shard_map.80.refs_8_.refs_1_, bf16[256,1408]{1,0:T(8,128)(2,1)} %copy-done.8, bf16[256,1408]{1,0:T(8,128)(2,1)} %copy-done.12, bf16[256,1408]{1,0:T(8,128)(2,1)} %copy-done.10, ...), custom_call_target="tpu_custom_call" | custom-call | flops 2952790016 | bytes 10747904 | tf_op jit(solution)/shard_map/pallas_call | solution.py:230
  157.5 7.1 %shard_map.86 = bf16[2,2752,512]{2,1,0:T(8,128)(2,1)} custom-call(bf16[2,512,1024]{2,1,0:T(8,128)(2,1)} %get-tuple-element.23.refs_0_, bf16[256,1408]{1,0:T(8,128)(2,1)} %shard_map.82.refs_1_, bf16[256,1408]{1,0:T(8,128)(2,1)} %copy-done.5, bf16[128,1408]{1,0:T(8,128)(2,1)} %copy-done.20, ...), custom_call_target="tpu_custom_call", output_to_operand_aliasing={{}: (12, {})} | custom-call | flops 2952790016 | bytes 10747904 | tf_op jit(solution)/shard_map/pallas_call | solution.py:230
  (124 shorter events, 17.8 us)
Async XLA Ops:
  0.6 27.3 %collective-permute-start.7 = (bf16[2,128,22016]{2,1,0:T(8,128)(2,1)}, bf16[2,128,22016]{2,1,0:T(8,128)(2,1)}, u32[]{:S(2)}, u32[]{:S(2)}) collective-permute-start(bf16[2,128,22016]{2,1,0:T(8,128)(2,1)} %grads_ref.3), channel_id=1, source_target_pairs={{0,16},{16,0},{1,17},{17,1},{2,18},{18,2},{3,19},{19,3},{4,20},{20... | collective-permute-start | bytes 33816584 | tf_op jit(solution)/shard_map/ppermute | solution.py:28
  5.2 6.7 %collective-permute-start = (bf16[2,128,256]{2,1,0:T(8,128)(2,1)S(1)}, bf16[2,128,256]{2,1,0:T(8,128)(2,1)S(1)}, u32[]{:S(2)}, u32[]{:S(2)}) collective-permute-start(bf16[2,128,256]{2,1,0:T(8,128)(2,1)S(1)} %get-tuple-element.39), channel_id=1, source_target_pairs={{12,0},{0,4},{4,8},{8,12},{13,1},{1,5},{5,9},{9,13},{14,2},{2,6},{... | collective-permute-start | bytes 393224 | tf_op jit(solution)/shard_map/ppermute | solution.py:20
  6.9 7.1 %collective-permute-start.1 = (bf16[2,128,256]{2,1,0:T(8,128)(2,1)S(1)}, bf16[2,128,256]{2,1,0:T(8,128)(2,1)S(1)}, u32[]{:S(2)}, u32[]{:S(2)}) collective-permute-start(bf16[2,128,256]{2,1,0:T(8,128)(2,1)S(1)} %get-tuple-element.41), channel_id=1, source_target_pairs={{4,0},{8,4},{12,8},{0,12},{5,1},{9,5},{13,9},{1,13},{6,2},{10,6},{... | collective-permute-start | bytes 393224 | tf_op jit(solution)/shard_map/ppermute | solution.py:20
  8.5 7.3 %collective-permute-start.2 = (bf16[2,128,256]{2,1,0:T(8,128)(2,1)S(1)}, bf16[2,128,256]{2,1,0:T(8,128)(2,1)S(1)}, u32[]{:S(2)}, u32[]{:S(2)}) collective-permute-start(bf16[2,128,256]{2,1,0:T(8,128)(2,1)S(1)} %get-tuple-element.40), channel_id=1, source_target_pairs={{8,0},{12,4},{0,8},{4,12},{9,1},{13,5},{1,9},{5,13},{10,2},{14,6},... | collective-permute-start | bytes 393224 | tf_op jit(solution)/shard_map/ppermute | solution.py:20
  16.0 6.5 %collective-permute-start.3 = (bf16[2,128,64]{2,1,0:T(8,128)(2,1)S(1)}, bf16[2,128,64]{2,1,0:T(8,128)(2,1)S(1)}, u32[]{:S(2)}, u32[]{:S(2)}) collective-permute-start(bf16[2,128,64]{2,1,0:T(8,128)(2,1)S(1)} %get-tuple-element.42), channel_id=1, source_target_pairs={{3,0},{0,1},{1,2},{2,3},{7,4},{4,5},{5,6},{6,7},{11,8},{8,9},{9,10... | collective-permute-start | bytes 98312 | tf_op jit(solution)/shard_map/ppermute | solution.py:20
  18.0 4.6 %collective-permute-start.4 = (bf16[2,128,64]{2,1,0:T(8,128)(2,1)S(1)}, bf16[2,128,64]{2,1,0:T(8,128)(2,1)S(1)}, u32[]{:S(2)}, u32[]{:S(2)}) collective-permute-start(bf16[2,128,64]{2,1,0:T(8,128)(2,1)S(1)} %get-tuple-element.44), channel_id=1, source_target_pairs={{1,0},{2,1},{3,2},{0,3},{5,4},{6,5},{7,6},{4,7},{9,8},{10,9},{11,1... | collective-permute-start | bytes 98312 | tf_op jit(solution)/shard_map/ppermute | solution.py:20
  20.2 5.8 %collective-permute-start.5 = (bf16[2,128,64]{2,1,0:T(8,128)(2,1)S(1)}, bf16[2,128,64]{2,1,0:T(8,128)(2,1)S(1)}, u32[]{:S(2)}, u32[]{:S(2)}) collective-permute-start(bf16[2,128,64]{2,1,0:T(8,128)(2,1)S(1)} %get-tuple-element.43), channel_id=1, source_target_pairs={{2,0},{3,1},{0,2},{1,3},{6,4},{7,5},{4,6},{5,7},{10,8},{11,9},{8,1... | collective-permute-start | bytes 98312 | tf_op jit(solution)/shard_map/ppermute | solution.py:20
  26.0 1.3 collective-permute-start.6
  34.3 14.1 %collective-permute-start.11 = (bf16[64,2752]{1,0:T(8,128)(2,1)}, bf16[64,2752]{1,0:T(8,128)(2,1)S(1)}, u32[]{:S(2)}, u32[]{:S(2)}) collective-permute-start(bf16[64,2752]{1,0:T(8,128)(2,1)} %get-tuple-element.27), channel_id=1, source_target_pairs={{96,0},{0,32},{32,64},{64,96},{97,1},{1,33},{33,65},{65,97},{98,2}... | collective-permute-start | bytes 1056776 | tf_op jit(solution)/shard_map/ppermute | solution.py:20
  35.8 21.4 %collective-permute-start.12 = (bf16[64,2752]{1,0:T(8,128)(2,1)}, bf16[64,2752]{1,0:T(8,128)(2,1)S(1)}, u32[]{:S(2)}, u32[]{:S(2)}) collective-permute-start(bf16[64,2752]{1,0:T(8,128)(2,1)} %get-tuple-element.28), channel_id=1, source_target_pairs={{64,0},{96,32},{0,64},{32,96},{65,1},{97,33},{1,65},{33,97},{66,2}... | collective-permute-start | bytes 1056776 | tf_op jit(solution)/shard_map/ppermute | solution.py:20
  38.5 18.7 %collective-permute-start.13 = (bf16[64,2752]{1,0:T(8,128)(2,1)}, bf16[64,2752]{1,0:T(8,128)(2,1)S(1)}, u32[]{:S(2)}, u32[]{:S(2)}) collective-permute-start(bf16[64,2752]{1,0:T(8,128)(2,1)} %get-tuple-element.29), channel_id=1, source_target_pairs={{32,0},{64,32},{96,64},{0,96},{33,1},{65,33},{97,65},{1,97},{34,2}... | collective-permute-start | bytes 1056776 | tf_op jit(solution)/shard_map/ppermute | solution.py:20
  46.3 18.1 %collective-permute-start.10 = (bf16[64,2752]{1,0:T(8,128)(2,1)}, bf16[64,2752]{1,0:T(8,128)(2,1)S(1)}, u32[]{:S(2)}, u32[]{:S(2)}) collective-permute-start(bf16[64,2752]{1,0:T(8,128)(2,1)} %get-tuple-element.26), channel_id=1, source_target_pairs={{32,0},{64,32},{96,64},{0,96},{33,1},{65,33},{97,65},{1,97},{34,2}... | collective-permute-start | bytes 1056776 | tf_op jit(solution)/shard_map/ppermute | solution.py:20
  46.3 30.3 %collective-permute-start.8 = (bf16[64,2752]{1,0:T(8,128)(2,1)}, bf16[64,2752]{1,0:T(8,128)(2,1)S(1)}, u32[]{:S(2)}, u32[]{:S(2)}) collective-permute-start(bf16[64,2752]{1,0:T(8,128)(2,1)} %get-tuple-element.24), channel_id=1, source_target_pairs={{96,0},{0,32},{32,64},{64,96},{97,1},{1,33},{33,65},{65,97},{98,2}... | collective-permute-start | bytes 1056776 | tf_op jit(solution)/shard_map/ppermute | solution.py:20
  48.4 28.3 %collective-permute-start.9 = (bf16[64,2752]{1,0:T(8,128)(2,1)}, bf16[64,2752]{1,0:T(8,128)(2,1)S(1)}, u32[]{:S(2)}, u32[]{:S(2)}) collective-permute-start(bf16[64,2752]{1,0:T(8,128)(2,1)} %get-tuple-element.25), channel_id=1, source_target_pairs={{64,0},{96,32},{0,64},{32,96},{65,1},{97,33},{1,65},{33,97},{66,2}... | collective-permute-start | bytes 1056776 | tf_op jit(solution)/shard_map/ppermute | solution.py:20
  61.1 8.9 %collective-permute-start.14 = (bf16[64,1408]{1,0:T(8,128)(2,1)}, bf16[64,1408]{1,0:T(8,128)(2,1)S(1)}, u32[]{:S(2)}, u32[]{:S(2)}) collective-permute-start(bf16[64,1408]{1,0:T(8,128)(2,1)} %get-tuple-element.33.refs_0_), channel_id=1, source_target_pairs={{4,0},{8,4},{12,8},{0,12},{5,1},{9,5},{13,9},{1,13},{6,2},{10,6},{... | collective-permute-start | bytes 540680 | tf_op jit(solution)/shard_map/ppermute | solution.py:20
  63.1 8.9 %collective-permute-start.15 = (bf16[64,1408]{1,0:T(8,128)(2,1)}, bf16[64,1408]{1,0:T(8,128)(2,1)S(1)}, u32[]{:S(2)}, u32[]{:S(2)}) collective-permute-start(bf16[64,1408]{1,0:T(8,128)(2,1)} %get-tuple-element.33.refs_0_), channel_id=1, source_target_pairs={{8,0},{12,4},{0,8},{4,12},{9,1},{13,5},{1,9},{5,13},{10,2},{14,6},... | collective-permute-start | bytes 540680 | tf_op jit(solution)/shard_map/ppermute | solution.py:20
  64.4 9.2 %collective-permute-start.16 = (bf16[64,1408]{1,0:T(8,128)(2,1)}, bf16[64,1408]{1,0:T(8,128)(2,1)S(1)}, u32[]{:S(2)}, u32[]{:S(2)}) collective-permute-start(bf16[64,1408]{1,0:T(8,128)(2,1)} %get-tuple-element.33.refs_0_), channel_id=1, source_target_pairs={{12,0},{0,4},{4,8},{8,12},{13,1},{1,5},{5,9},{9,13},{14,2},{2,6},{... | collective-permute-start | bytes 540680 | tf_op jit(solution)/shard_map/ppermute | solution.py:20
  70.0 13.7 %collective-permute-start.34 = (bf16[64,1408]{1,0:T(8,128)(2,1)}, bf16[64,1408]{1,0:T(8,128)(2,1)S(1)}, u32[]{:S(2)}, u32[]{:S(2)}) collective-permute-start(bf16[64,1408]{1,0:T(8,128)(2,1)} %get-tuple-element.36.refs_0_), channel_id=1, source_target_pairs={{1,0},{2,1},{3,2},{0,3},{5,4},{6,5},{7,6},{4,7},{9,8},{10,9},{11,1... | collective-permute-start | bytes 540680 | tf_op jit(solution)/shard_map/ppermute | solution.py:20
  71.9 12.6 %collective-permute-start.35 = (bf16[64,1408]{1,0:T(8,128)(2,1)}, bf16[64,1408]{1,0:T(8,128)(2,1)S(1)}, u32[]{:S(2)}, u32[]{:S(2)}) collective-permute-start(bf16[64,1408]{1,0:T(8,128)(2,1)} %get-tuple-element.36.refs_0_), channel_id=1, source_target_pairs={{2,0},{3,1},{0,2},{1,3},{6,4},{7,5},{4,6},{5,7},{10,8},{11,9},{8,1... | collective-permute-start | bytes 540680 | tf_op jit(solution)/shard_map/ppermute | solution.py:20
  73.6 13.8 %collective-permute-start.36 = (bf16[64,1408]{1,0:T(8,128)(2,1)}, bf16[64,1408]{1,0:T(8,128)(2,1)S(1)}, u32[]{:S(2)}, u32[]{:S(2)}) collective-permute-start(bf16[64,1408]{1,0:T(8,128)(2,1)} %get-tuple-element.36.refs_0_), channel_id=1, source_target_pairs={{3,0},{0,1},{1,2},{2,3},{7,4},{4,5},{5,6},{6,7},{11,8},{8,9},{9,10... | collective-permute-start | bytes 540680 | tf_op jit(solution)/shard_map/ppermute | solution.py:20
  77.5 17.7 %copy-start.1 = (bf16[256,1408]{1,0:T(8,128)(2,1)S(1)}, bf16[256,1408]{1,0:T(8,128)(2,1)}, u32[]{:S(2)}) copy-start(bf16[256,1408]{1,0:T(8,128)(2,1)} %shard_map.80.refs_8_.refs_1_) | copy-start | bytes 2162692
  80.6 9.2 %collective-permute-start.24 = (bf16[64,1408]{1,0:T(8,128)(2,1)}, bf16[64,1408]{1,0:T(8,128)(2,1)S(1)}, u32[]{:S(2)}, u32[]{:S(2)}) collective-permute-start(bf16[64,1408]{1,0:T(8,128)(2,1)} %get-tuple-element.35.refs_0_), channel_id=1, source_target_pairs={{1,0},{2,1},{3,2},{0,3},{5,4},{6,5},{7,6},{4,7},{9,8},{10,9},{11,1... | collective-permute-start | bytes 540680 | tf_op jit(solution)/shard_map/ppermute | solution.py:20
  83.0 9.0 %collective-permute-start.25 = (bf16[64,1408]{1,0:T(8,128)(2,1)}, bf16[64,1408]{1,0:T(8,128)(2,1)S(1)}, u32[]{:S(2)}, u32[]{:S(2)}) collective-permute-start(bf16[64,1408]{1,0:T(8,128)(2,1)} %get-tuple-element.35.refs_0_), channel_id=1, source_target_pairs={{2,0},{3,1},{0,2},{1,3},{6,4},{7,5},{4,6},{5,7},{10,8},{11,9},{8,1... | collective-permute-start | bytes 540680 | tf_op jit(solution)/shard_map/ppermute | solution.py:20
  83.7 11.6 %collective-permute-start.26 = (bf16[64,1408]{1,0:T(8,128)(2,1)}, bf16[64,1408]{1,0:T(8,128)(2,1)S(1)}, u32[]{:S(2)}, u32[]{:S(2)}) collective-permute-start(bf16[64,1408]{1,0:T(8,128)(2,1)} %get-tuple-element.35.refs_0_), channel_id=1, source_target_pairs={{3,0},{0,1},{1,2},{2,3},{7,4},{4,5},{5,6},{6,7},{11,8},{8,9},{9,10... | collective-permute-start | bytes 540680 | tf_op jit(solution)/shard_map/ppermute | solution.py:20
  84.6 16.4 %collective-permute-start.17 = (bf16[64,1408]{1,0:T(8,128)(2,1)}, bf16[64,1408]{1,0:T(8,128)(2,1)S(1)}, u32[]{:S(2)}, u32[]{:S(2)}) collective-permute-start(bf16[64,1408]{1,0:T(8,128)(2,1)} %get-tuple-element.34.refs_0_), channel_id=1, source_target_pairs={{4,0},{8,4},{12,8},{0,12},{5,1},{9,5},{13,9},{1,13},{6,2},{10,6},{... | collective-permute-start | bytes 540680 | tf_op jit(solution)/shard_map/ppermute | solution.py:20
  87.3 13.7 %collective-permute-start.18 = (bf16[64,1408]{1,0:T(8,128)(2,1)}, bf16[64,1408]{1,0:T(8,128)(2,1)S(1)}, u32[]{:S(2)}, u32[]{:S(2)}) collective-permute-start(bf16[64,1408]{1,0:T(8,128)(2,1)} %get-tuple-element.34.refs_0_), channel_id=1, source_target_pairs={{8,0},{12,4},{0,8},{4,12},{9,1},{13,5},{1,9},{5,13},{10,2},{14,6},... | collective-permute-start | bytes 540680 | tf_op jit(solution)/shard_map/ppermute | solution.py:20
  89.8 13.2 %collective-permute-start.19 = (bf16[64,1408]{1,0:T(8,128)(2,1)}, bf16[64,1408]{1,0:T(8,128)(2,1)S(1)}, u32[]{:S(2)}, u32[]{:S(2)}) collective-permute-start(bf16[64,1408]{1,0:T(8,128)(2,1)} %get-tuple-element.34.refs_0_), channel_id=1, source_target_pairs={{12,0},{0,4},{4,8},{8,12},{13,1},{1,5},{5,9},{9,13},{14,2},{2,6},{... | collective-permute-start | bytes 540680 | tf_op jit(solution)/shard_map/ppermute | solution.py:20
  92.0 23.5 %copy-start.2 = (bf16[256,1408]{1,0:T(8,128)(2,1)S(1)}, bf16[256,1408]{1,0:T(8,128)(2,1)}, u32[]{:S(2)}) copy-start(bf16[256,1408]{1,0:T(8,128)(2,1)} %shard_map.84.refs_6_) | copy-start | bytes 2162692
  92.0 20.2 %collective-permute-start.37 = (bf16[256,1408]{1,0:T(8,128)(2,1)}, bf16[256,1408]{1,0:T(8,128)(2,1)S(1)}, u32[]{:S(2)}, u32[]{:S(2)}) collective-permute-start(bf16[256,1408]{1,0:T(8,128)(2,1)} %shard_map.84.refs_6_), channel_id=1, source_target_pairs={{4,0},{8,4},{12,8},{0,12},{5,1},{9,5},{13,9},{1,13},{6,2},{10,6},{... | collective-permute-start | bytes 2162696 | tf_op jit(solution)/shard_map/ppermute | solution.py:20
  95.3 20.2 %collective-permute-start.31 = (bf16[256,1408]{1,0:T(8,128)(2,1)S(1)}, bf16[256,1408]{1,0:T(8,128)(2,1)S(1)}, u32[]{:S(2)}, u32[]{:S(2)}) collective-permute-start(bf16[256,1408]{1,0:T(8,128)(2,1)S(1)} %copy-done.1), channel_id=1, source_target_pairs={{1,0},{2,1},{3,2},{0,3},{5,4},{6,5},{7,6},{4,7},{9,8},{10,9},{11,1... | collective-permute-start | bytes 2162696 | tf_op jit(solution)/shard_map/ppermute | solution.py:20
  101.0 22.8 %collective-permute-start.27 = (bf16[256,1408]{1,0:T(8,128)(2,1)}, bf16[256,1408]{1,0:T(8,128)(2,1)S(1)}, u32[]{:S(2)}, u32[]{:S(2)}) collective-permute-start(bf16[256,1408]{1,0:T(8,128)(2,1)} %shard_map.83.refs_7_), channel_id=1, source_target_pairs={{4,0},{8,4},{12,8},{0,12},{5,1},{9,5},{13,9},{1,13},{6,2},{10,6},{... | collective-permute-start | bytes 2162696 | tf_op jit(solution)/shard_map/ppermute | solution.py:20
  101.0 24.6 %collective-permute-start.29 = (bf16[256,1408]{1,0:T(8,128)(2,1)}, bf16[256,1408]{1,0:T(8,128)(2,1)S(1)}, u32[]{:S(2)}, u32[]{:S(2)}) collective-permute-start(bf16[256,1408]{1,0:T(8,128)(2,1)} %shard_map.83.refs_7_), channel_id=1, source_target_pairs={{12,0},{0,4},{4,8},{8,12},{13,1},{1,5},{5,9},{9,13},{14,2},{2,6},{... | collective-permute-start | bytes 2162696 | tf_op jit(solution)/shard_map/ppermute | solution.py:20
  105.8 22.9 %collective-permute-start.20 = (bf16[256,1408]{1,0:T(8,128)(2,1)}, bf16[256,1408]{1,0:T(8,128)(2,1)S(1)}, u32[]{:S(2)}, u32[]{:S(2)}) collective-permute-start(bf16[256,1408]{1,0:T(8,128)(2,1)} %shard_map.82.refs_1_), channel_id=1, source_target_pairs={{1,0},{2,1},{3,2},{0,3},{5,4},{6,5},{7,6},{4,7},{9,8},{10,9},{11,1... | collective-permute-start | bytes 2162696 | tf_op jit(solution)/shard_map/ppermute | solution.py:20
  112.2 36.5 %copy-start.7 = (bf16[256,1408]{1,0:T(8,128)(2,1)}, bf16[256,1408]{1,0:T(8,128)(2,1)S(1)}, u32[]{:S(2)}) copy-start(bf16[256,1408]{1,0:T(8,128)(2,1)S(1)} %collective-permute-done.37.refs_7_) | copy-start | bytes 2162692
  112.2 19.9 %collective-permute-start.22 = (bf16[256,1408]{1,0:T(8,128)(2,1)}, bf16[256,1408]{1,0:T(8,128)(2,1)S(1)}, u32[]{:S(2)}, u32[]{:S(2)}) collective-permute-start(bf16[256,1408]{1,0:T(8,128)(2,1)} %shard_map.82.refs_1_), channel_id=1, source_target_pairs={{3,0},{0,1},{1,2},{2,3},{7,4},{4,5},{5,6},{6,7},{11,8},{8,9},{9,10... | collective-permute-start | bytes 2162696 | tf_op jit(solution)/shard_map/ppermute | solution.py:20
  115.5 33.2 %copy-start.8 = (bf16[256,1408]{1,0:T(8,128)(2,1)}, bf16[256,1408]{1,0:T(8,128)(2,1)S(1)}, u32[]{:S(2)}) copy-start(bf16[256,1408]{1,0:T(8,128)(2,1)S(1)} %collective-permute-done.31.refs_2_) | copy-start | bytes 2162692
  115.5 17.6 %collective-permute-start.39 = (bf16[256,1408]{1,0:T(8,128)(2,1)S(1)}, bf16[256,1408]{1,0:T(8,128)(2,1)S(1)}, u32[]{:S(2)}, u32[]{:S(2)}) collective-permute-start(bf16[256,1408]{1,0:T(8,128)(2,1)S(1)} %copy-done.2), channel_id=1, source_target_pairs={{12,0},{0,4},{4,8},{8,12},{13,1},{1,5},{5,9},{9,13},{14,2},{2,6},{... | collective-permute-start | bytes 2162696 | tf_op jit(solution)/shard_map/ppermute | solution.py:20
  123.8 32.0 %copy-start.3 = (bf16[256,1408]{1,0:T(8,128)(2,1)}, bf16[256,1408]{1,0:T(8,128)(2,1)S(1)}, u32[]{:S(2)}) copy-start(bf16[256,1408]{1,0:T(8,128)(2,1)S(1)} %collective-permute-done.27.refs_8_) | copy-start | bytes 2162692
  123.8 16.8 %collective-permute-start.33 = (bf16[256,1408]{1,0:T(8,128)(2,1)S(1)}, bf16[256,1408]{1,0:T(8,128)(2,1)S(1)}, u32[]{:S(2)}, u32[]{:S(2)}) collective-permute-start(bf16[256,1408]{1,0:T(8,128)(2,1)S(1)} %copy-done.1), channel_id=1, source_target_pairs={{3,0},{0,1},{1,2},{2,3},{7,4},{4,5},{5,6},{6,7},{11,8},{8,9},{9,10... | collective-permute-start | bytes 2162696 | tf_op jit(solution)/shard_map/ppermute | solution.py:20
  125.7 30.1 %copy-start.4 = (bf16[256,1408]{1,0:T(8,128)(2,1)}, bf16[256,1408]{1,0:T(8,128)(2,1)S(1)}, u32[]{:S(2)}) copy-start(bf16[256,1408]{1,0:T(8,128)(2,1)S(1)} %collective-permute-done.29.refs_11_) | copy-start | bytes 2162692
  125.7 19.6 %collective-permute-start.38 = (bf16[256,1408]{1,0:T(8,128)(2,1)S(1)}, bf16[256,1408]{1,0:T(8,128)(2,1)S(1)}, u32[]{:S(2)}, u32[]{:S(2)}) collective-permute-start(bf16[256,1408]{1,0:T(8,128)(2,1)S(1)} %collective-permute-done.37.refs_7_), channel_id=1, source_target_pairs={{4,0},{8,4},{12,8},{0,12},{5,1},{9,5},{13,9},{1,13},{6,2},{10,6},{... | collective-permute-start | bytes 2162696 | tf_op jit(solution)/shard_map/ppermute | solution.py:20
  128.7 27.1 %copy-start.5 = (bf16[256,1408]{1,0:T(8,128)(2,1)}, bf16[256,1408]{1,0:T(8,128)(2,1)S(1)}, u32[]{:S(2)}) copy-start(bf16[256,1408]{1,0:T(8,128)(2,1)S(1)} %collective-permute-done.20.refs_2_) | copy-start | bytes 2162692
  128.7 19.1 %collective-permute-start.32 = (bf16[256,1408]{1,0:T(8,128)(2,1)S(1)}, bf16[256,1408]{1,0:T(8,128)(2,1)S(1)}, u32[]{:S(2)}, u32[]{:S(2)}) collective-permute-start(bf16[256,1408]{1,0:T(8,128)(2,1)S(1)} %collective-permute-done.31.refs_2_), channel_id=1, source_target_pairs={{1,0},{2,1},{3,2},{0,3},{5,4},{6,5},{7,6},{4,7},{9,8},{10,9},{11,1... | collective-permute-start | bytes 2162696 | tf_op jit(solution)/shard_map/ppermute | solution.py:20
  132.1 23.7 %copy-start.6 = (bf16[256,1408]{1,0:T(8,128)(2,1)}, bf16[256,1408]{1,0:T(8,128)(2,1)S(1)}, u32[]{:S(2)}) copy-start(bf16[256,1408]{1,0:T(8,128)(2,1)S(1)} %collective-permute-done.22.refs_5_) | copy-start | bytes 2162692
  132.1 23.7 %collective-permute-start.28 = (bf16[128,1408]{1,0:T(8,128)(2,1)}, bf16[128,1408]{1,0:T(8,128)(2,1)}, u32[]{:S(2)}, u32[]{:S(2)}) collective-permute-start(bf16[128,1408]{1,0:T(8,128)(2,1)} %slice.78), channel_id=1, source_target_pairs={{4,0},{8,4},{12,8},{0,12},{5,1},{9,5},{13,9},{1,13},{6,2},{10,6},{... | collective-permute-start | bytes 1081352 | tf_op jit(solution)/shard_map/ppermute | solution.py:20
  133.1 22.7 %collective-permute-start.30 = (bf16[128,1408]{1,0:T(8,128)(2,1)}, bf16[128,1408]{1,0:T(8,128)(2,1)S(1)}, u32[]{:S(2)}, u32[]{:S(2)}) collective-permute-start(bf16[128,1408]{1,0:T(8,128)(2,1)} %slice.79), channel_id=1, source_target_pairs={{12,0},{0,4},{4,8},{8,12},{13,1},{1,5},{5,9},{9,13},{14,2},{2,6},{... | collective-permute-start | bytes 1081352 | tf_op jit(solution)/shard_map/ppermute | solution.py:20
  140.6 15.2 %collective-permute-start.21 = (bf16[128,1408]{1,0:T(8,128)(2,1)S(1)}, bf16[128,1408]{1,0:T(8,128)(2,1)S(1)}, u32[]{:S(2)}, u32[]{:S(2)}) collective-permute-start(bf16[128,1408]{1,0:T(8,128)(2,1)S(1)} %slice.76), channel_id=1, source_target_pairs={{1,0},{2,1},{3,2},{0,3},{5,4},{6,5},{7,6},{4,7},{9,8},{10,9},{11,1... | collective-permute-start | bytes 1081352 | tf_op jit(solution)/shard_map/ppermute | solution.py:20
  145.3 10.6 %collective-permute-start.23 = (bf16[128,1408]{1,0:T(8,128)(2,1)}, bf16[128,1408]{1,0:T(8,128)(2,1)S(1)}, u32[]{:S(2)}, u32[]{:S(2)}) collective-permute-start(bf16[128,1408]{1,0:T(8,128)(2,1)} %slice.77), channel_id=1, source_target_pairs={{3,0},{0,1},{1,2},{2,3},{7,4},{4,5},{5,6},{6,7},{11,8},{8,9},{9,10... | collective-permute-start | bytes 1081352 | tf_op jit(solution)/shard_map/ppermute | solution.py:20
  (26 other events, 99.7 us)

commit v7 on v6

--- a/solution.py
+++ b/solution.py
@@ -71,7 +71,7 @@
 
 def partial_kernel(where_ref, proj_ref, other_proj_ref, grads_ref, other_grads_ref, _, *outs):
     step = pl.program_id(0)
-    proj = jnp.concatenate([proj_ref[...], other_proj_ref[...]], axis=0)
+    proj = jnp.concatenate([proj_ref[0], other_proj_ref[0]], axis=0)
     grads = jnp.concatenate([grads_ref[0], other_grads_ref[0]], axis=0)
     total = lax.dot_general(proj, grads, (((0,), (0,)), ((), ())), preferred_element_type=F32)
     span, width = total.shape[1], outs[0].shape[1]
@@ -85,7 +85,7 @@
 
 
 def partial_grads(where, proj, other_proj, grads, other_grads, which, after):
-    tokens, rank_part = proj.shape
+    _, tokens, rank_part = proj.shape
     pair = grads.shape[2] // SIDE
     width = pair // 2
     span = (width + LANES - 1) // LANES * LANES
@@ -95,7 +95,7 @@
         block = (w[0] + i) & (SIDE - 1)
         return which, 0, pl.multiple_of((block * (pair // LANES) + w[1] * skip) * LANES, LANES)
 
-    small = pl.BlockSpec((tokens, rank_part), lambda i, w: (0, 0))
+    small = pl.BlockSpec((1, tokens, rank_part), lambda i, w: (which, 0, 0))
     large = pl.BlockSpec((pl.Element(1), pl.Element(tokens), pl.Element(span)), window)
     return pl.pallas_call(
         partial_kernel,
@@ -201,10 +201,9 @@
     for half, group in enumerate(copies):
         for copy in group:
             copy.wait()
-        for low in range(0, cut, 256):
-            high = min(low + 256, cut)
-            total = jnp.dot(columns[half], pieces[half, :, low:high], preferred_element_type=F32)
-            outs[half, low:high, :] = total.T.astype(BF16)
+        outs[half] = lax.dot_general(
+            pieces[half], columns[half], (((0,), (1,)), ((), ())), preferred_element_type=F32
+        ).astype(BF16)
         size = min(cut, out_ref.shape[1] - half * cut)
         stores.append(
             pltpu.make_async_copy(
@@ -283,10 +282,10 @@
 
     other_partial = swap_cores(partial)
     own_sum, *sums = partial_grads(
-        where, partial[0], other_partial[0], out_grads, other_grads, 0, where
+        where, partial, other_partial, out_grads, other_grads, 0, where
     )
     own_sum_1, *sums_1 = partial_grads(
-        where, partial[1], other_partial[1], out_grads, other_grads, 1, own_sum
+        where, partial, other_partial, out_grads, other_grads, 1, own_sum
     )
     columns_y, columns_z = arrange(where, bases, own_sum_1)
     sums = [send(value, "x", i + 1) for i, value in enumerate(sums)]

time: 165 us -> 164 us (level)
    unnamed x68 -> x72, local copies, waits for them, and re-layouts: 6.46 us -> 7.09 us
  transfers between devices with their start and end apart: 40 -> 40, of which waited for: 14 -> 16; matrix products, arithmetic and copies ran while one was open for 5% -> 4% of each run, Pallas kernels for 22% -> 22%
where the time goes in v7:
time: 164 us
  starting transfers between devices  56.4 us (34%)
  Pallas kernels  48.8 us (30%)
  waiting for transfers between devices  44.2 us (27%)
  local copies, waits for them, and re-layouts  9.63 us (6%)
  matrix products  2.91 us (2%)
    ppermute x38, starting transfers between devices, receive(): lax.ppermute(value, axis, [((i + distance) % SIDE, i) for i in range(SIDE)])  56.2 us
    ppermute x38, waiting for transfers between devices, receive(): lax.ppermute(value, axis, [((i + distance) % SIDE, i) for i in range(SIDE)])  43.7 us
    pallas_call x2, Pallas kernels, expand_halves(): pl.pallas_call(functools.partial(expand_kernel, counts=counts, which=whic...  13.4 us
    pallas_call x2, Pallas kernels, partial_grads(): pl.pallas_call(partial_kernel, grid_spec=pltpu.PrefetchScalarGridSpec(num...  12.7 us
    pallas_call x4, Pallas kernels, stack(): pl.pallas_call(stack_kernel, out_shape=held((rows * len(pieces), width)),...  8.54 us
    pallas_call x1, Pallas kernels, arrange(): pl.pallas_call(arrange_kernel, grid_spec=pltpu.PrefetchScalarGridSpec(num...  8.13 us
    unnamed x72, local copies, waits for them, and re-layouts  7.09 us
    pallas_call x2, Pallas kernels, directions(): pl.pallas_call(functools.partial(direction_kernel, pieces=pieces), grid=(...  6.1 us
  transfers between devices with their start and end apart: 40, of which 16 were waited for; matrix products, arithmetic and copies ran while one was open for 4% of the time, Pallas kernels for 22%

profile of v7, /device:TPU:0, one launch (start us, length us, event | category | flops | bytes accessed | tf_op | source)
XLA Modules:
  0.0 164.0 jit_solution(8635733913094533346)
XLA Ops:
  0.8 1.5 copy-done
  2.2 2.9 %fusion.4 = bf16[2,128,1024]{2,1,0:T(8,128)(2,1)S(1)} fusion(s32[1024]{0:T(1024)S(1)} %fusion.21, bf16[2,512,1024]{2,1,0:T(8,128)(2,1)} %bases_ref.1, bf16[128,8192]{1,0:T(8,128)(2,1)S(1)} %copy-done, s32[]{:T(128)S(6)} %select_n.54), kind=kOutput, calls=%fused_computation.4 | convolution fusion | flops 806879232 | bytes 2756612 | tf_op jit(solution)/shard_map/ktr,rs->kts/dot_general | solution.py:274
  5.2 1.7 %collective-permute-start = (bf16[2,128,256]{2,1,0:T(8,128)(2,1)S(1)}, bf16[2,128,256]{2,1,0:T(8,128)(2,1)S(1)}, u32[]{:S(2)}, u32[]{:S(2)}) collective-permute-start(bf16[2,128,256]{2,1,0:T(8,128)(2,1)S(1)} %get-tuple-element.39), channel_id=1, source_target_pairs={{12,0},{0,4},{4,8},{8,12},{13,1},{1,5},{5,9},{9,13},{14,2},{2,6},{... | collective-permute-start | bytes 393224 | tf_op jit(solution)/shard_map/ppermute | solution.py:20
  6.9 1.6 collective-permute-start.1
  8.5 2.1 %collective-permute-start.2 = (bf16[2,128,256]{2,1,0:T(8,128)(2,1)S(1)}, bf16[2,128,256]{2,1,0:T(8,128)(2,1)S(1)}, u32[]{:S(2)}, u32[]{:S(2)}) collective-permute-start(bf16[2,128,256]{2,1,0:T(8,128)(2,1)S(1)} %get-tuple-element.40), channel_id=1, source_target_pairs={{8,0},{12,4},{0,8},{4,12},{9,1},{13,5},{1,9},{5,13},{10,2},{14,6},... | collective-permute-start | bytes 393224 | tf_op jit(solution)/shard_map/ppermute | solution.py:20
  11.8 2.2 %collective-permute-done.1 = bf16[2,128,256]{2,1,0:T(8,128)(2,1)S(1)} collective-permute-done((bf16[2,128,256]{2,1,0:T(8,128)(2,1)S(1)}, bf16[2,128,256]{2,1,0:T(8,128)(2,1)S(1)}, u32[]{:S(2)}, u32[]{:S(2)}) %collective-permute-start.1) | collective-permute-done | bytes 131104 | tf_op jit(solution)/shard_map/ppermute | solution.py:20
  14.0 1.8 %collective-permute-done.2 = bf16[2,128,256]{2,1,0:T(8,128)(2,1)S(1)} collective-permute-done((bf16[2,128,256]{2,1,0:T(8,128)(2,1)S(1)}, bf16[2,128,256]{2,1,0:T(8,128)(2,1)S(1)}, u32[]{:S(2)}, u32[]{:S(2)}) %collective-permute-start.2) | collective-permute-done | bytes 131104 | tf_op jit(solution)/shard_map/ppermute | solution.py:20
  16.0 2.0 %collective-permute-start.3 = (bf16[2,128,64]{2,1,0:T(8,128)(2,1)S(1)}, bf16[2,128,64]{2,1,0:T(8,128)(2,1)S(1)}, u32[]{:S(2)}, u32[]{:S(2)}) collective-permute-start(bf16[2,128,64]{2,1,0:T(8,128)(2,1)S(1)} %get-tuple-element.42), channel_id=1, source_target_pairs={{3,0},{0,1},{1,2},{2,3},{7,4},{4,5},{5,6},{6,7},{11,8},{8,9},{9,10... | collective-permute-start | bytes 98312 | tf_op jit(solution)/shard_map/ppermute | solution.py:20
  18.0 2.2 %collective-permute-start.4 = (bf16[2,128,64]{2,1,0:T(8,128)(2,1)S(1)}, bf16[2,128,64]{2,1,0:T(8,128)(2,1)S(1)}, u32[]{:S(2)}, u32[]{:S(2)}) collective-permute-start(bf16[2,128,64]{2,1,0:T(8,128)(2,1)S(1)} %get-tuple-element.44), channel_id=1, source_target_pairs={{1,0},{2,1},{3,2},{0,3},{5,4},{6,5},{7,6},{4,7},{9,8},{10,9},{11,1... | collective-permute-start | bytes 98312 | tf_op jit(solution)/shard_map/ppermute | solution.py:20
  20.2 1.8 %collective-permute-start.5 = (bf16[2,128,64]{2,1,0:T(8,128)(2,1)S(1)}, bf16[2,128,64]{2,1,0:T(8,128)(2,1)S(1)}, u32[]{:S(2)}, u32[]{:S(2)}) collective-permute-start(bf16[2,128,64]{2,1,0:T(8,128)(2,1)S(1)} %get-tuple-element.43), channel_id=1, source_target_pairs={{2,0},{3,1},{0,2},{1,3},{6,4},{7,5},{4,6},{5,7},{10,8},{11,9},{8,1... | collective-permute-start | bytes 98312 | tf_op jit(solution)/shard_map/ppermute | solution.py:20
  22.6 3.4 %collective-permute-done.5 = bf16[2,128,64]{2,1,0:T(8,128)(2,1)S(1)} collective-permute-done((bf16[2,128,64]{2,1,0:T(8,128)(2,1)S(1)}, bf16[2,128,64]{2,1,0:T(8,128)(2,1)S(1)}, u32[]{:S(2)}, u32[]{:S(2)}) %collective-permute-start.5) | collective-permute-done | bytes 32800 | tf_op jit(solution)/shard_map/ppermute | solution.py:20
  28.0 6.3 %shard_map.76 = (f32[64,2752]{1,0:T(8,128)}, bf16[64,2752]{1,0:T(8,128)(2,1)}, bf16[64,2752]{1,0:T(8,128)(2,1)}, bf16[64,2752]{1,0:T(8,128)(2,1)}) custom-call(s32[4]{0:T(128)} %pad_add_fusion.where_ref._, bf16[2,128,64]{2,1,0:T(8,128)(2,1)} %copy-done.13, bf16[2,128,64]{2,1,0:T(8,128)(2,1)} %copy-done.23, bf16[2,128,22016]{2,1,0:T(8,128)(2,1)} %grads_ref.3, ...), custom_call_target="tpu_custom_call" | custom-call | flops 360710144 | bytes 8454144 | tf_op jit(solution)/shard_map/pallas_call | solution.py:100
  34.3 1.5 collective-permute-start.11
  35.8 2.7 %collective-permute-start.12 = (bf16[64,2752]{1,0:T(8,128)(2,1)}, bf16[64,2752]{1,0:T(8,128)(2,1)S(1)}, u32[]{:S(2)}, u32[]{:S(2)}) collective-permute-start(bf16[64,2752]{1,0:T(8,128)(2,1)} %get-tuple-element.28), channel_id=1, source_target_pairs={{64,0},{96,32},{0,64},{32,96},{65,1},{97,33},{1,65},{33,97},{66,2}... | collective-permute-start | bytes 1056776 | tf_op jit(solution)/shard_map/ppermute | solution.py:20
  38.5 1.4 collective-permute-start.13
  40.0 6.4 %shard_map.77 = (f32[64,2752]{1,0:T(8,128)}, bf16[64,2752]{1,0:T(8,128)(2,1)}, bf16[64,2752]{1,0:T(8,128)(2,1)}, bf16[64,2752]{1,0:T(8,128)(2,1)}) custom-call(s32[4]{0:T(128)} %pad_add_fusion.where_ref._, bf16[2,128,64]{2,1,0:T(8,128)(2,1)} %copy-done.13, bf16[2,128,64]{2,1,0:T(8,128)(2,1)} %copy-done.23, bf16[2,128,22016]{2,1,0:T(8,128)(2,1)} %grads_ref.3, ...), custom_call_target="tpu_custom_call" | custom-call | flops 360710144 | bytes 8454144 | tf_op jit(solution)/shard_map/pallas_call | solution.py:100
  46.4 2.0 %collective-permute-start.8 = (bf16[64,2752]{1,0:T(8,128)(2,1)}, bf16[64,2752]{1,0:T(8,128)(2,1)S(1)}, u32[]{:S(2)}, u32[]{:S(2)}) collective-permute-start(bf16[64,2752]{1,0:T(8,128)(2,1)} %get-tuple-element.24), channel_id=1, source_target_pairs={{96,0},{0,32},{32,64},{64,96},{97,1},{1,33},{33,65},{65,97},{98,2}... | collective-permute-start | bytes 1056776 | tf_op jit(solution)/shard_map/ppermute | solution.py:20
  49.1 8.1 %shard_map.78 = (bf16[2,512,1024]{2,1,0:T(8,128)(2,1)}, bf16[2,512,1024]{2,1,0:T(8,128)(2,1)}) custom-call(s32[4]{0:T(128)} %pad_add_fusion.where_ref._, bf16[2,512,1024]{2,1,0:T(8,128)(2,1)} %bases_ref.1, f32[64,2752]{1,0:T(8,128)} %get-tuple-element.22._.refs_0_), custom_call_target="tpu_custom_call" | custom-call | flops 4294967296 | bytes 6291456 | tf_op jit(solution)/shard_map/pallas_call | solution.py:61
  58.1 3.0 %shard_map.79 = (f32[2,64,2752]{2,1,0:T(8,128)}, f32[2,64,2752]{2,1,0:T(8,128)}, bf16[64,1408]{1,0:T(8,128)(2,1)}, bf16[64,1408]{1,0:T(8,128)(2,1)}) custom-call(f32[64,2752]{1,0:T(8,128)} %get-tuple-element.21._.refs_0_, bf16[64,2752]{1,0:T(8,128)(2,1)} %copy-done.17, bf16[64,2752]{1,0:T(8,128)(2,1)} %copy-done.18, bf16[64,2752]{1,0:T(8,128)(2,1)} %copy-done.19, ...), custom_call_target="tpu_custom_call" | custom-call | flops 5283840 | bytes 4579328 | tf_op jit(solution)/shard_map/pallas_call | solution.py:153
  61.2 1.9 %collective-permute-start.14 = (bf16[64,1408]{1,0:T(8,128)(2,1)}, bf16[64,1408]{1,0:T(8,128)(2,1)S(1)}, u32[]{:S(2)}, u32[]{:S(2)}) collective-permute-start(bf16[64,1408]{1,0:T(8,128)(2,1)} %get-tuple-element.33.refs_0_), channel_id=1, source_target_pairs={{4,0},{8,4},{12,8},{0,12},{5,1},{9,5},{13,9},{1,13},{6,2},{10,6},{... | collective-permute-start | bytes 540680 | tf_op jit(solution)/shard_map/ppermute | solution.py:20
  63.1 1.4 collective-permute-start.15
  64.5 5.5 %collective-permute-done.14.refs_1_ = bf16[64,1408]{1,0:T(8,128)(2,1)S(1)} collective-permute-done((bf16[64,1408]{1,0:T(8,128)(2,1)}, bf16[64,1408]{1,0:T(8,128)(2,1)S(1)}, u32[]{:S(2)}, u32[]{:S(2)}) %collective-permute-start.14) | collective-permute-done | bytes 180256 | tf_op jit(solution)/shard_map/ppermute | solution.py:20
  70.0 1.9 %collective-permute-start.34 = (bf16[64,1408]{1,0:T(8,128)(2,1)}, bf16[64,1408]{1,0:T(8,128)(2,1)S(1)}, u32[]{:S(2)}, u32[]{:S(2)}) collective-permute-start(bf16[64,1408]{1,0:T(8,128)(2,1)} %get-tuple-element.36.refs_0_), channel_id=1, source_target_pairs={{1,0},{2,1},{3,2},{0,3},{5,4},{6,5},{7,6},{4,7},{9,8},{10,9},{11,1... | collective-permute-start | bytes 540680 | tf_op jit(solution)/shard_map/ppermute | solution.py:20
  72.0 1.5 collective-permute-start.35
  74.5 2.1 %shard_map.80.refs_8_.refs_1_ = bf16[256,1408]{1,0:T(8,128)(2,1)} custom-call(bf16[64,1408]{1,0:T(8,128)(2,1)} %get-tuple-element.33.refs_0_, bf16[64,1408]{1,0:T(8,128)(2,1)} %copy-done.33, bf16[64,1408]{1,0:T(8,128)(2,1)} %copy-done.34, bf16[64,1408]{1,0:T(8,128)(2,1)} %copy-done.35), custom_call_target="tpu_custom_call" | custom-call | bytes 1441792 | tf_op jit(solution)/shard_map/pallas_call | solution.py:173
  77.6 3.1 %shard_map.81 = (f32[2,64,2752]{2,1,0:T(8,128)}, f32[2,64,2752]{2,1,0:T(8,128)}, bf16[64,1408]{1,0:T(8,128)(2,1)}, bf16[64,1408]{1,0:T(8,128)(2,1)}) custom-call(f32[64,2752]{1,0:T(8,128)} %get-tuple-element.22._.refs_0_, bf16[64,2752]{1,0:T(8,128)(2,1)} %copy-done.15, bf16[64,2752]{1,0:T(8,128)(2,1)} %copy-done.16, ...), custom_call_target="tpu_custom_call", output_to_operand_aliasing={{0}: (6, {}), {1}: (7, {})} | custom-call | flops 5283840 | bytes 4579328 | tf_op jit(solution)/shard_map/pallas_call | solution.py:153
  80.6 2.3 %collective-permute-start.24 = (bf16[64,1408]{1,0:T(8,128)(2,1)}, bf16[64,1408]{1,0:T(8,128)(2,1)S(1)}, u32[]{:S(2)}, u32[]{:S(2)}) collective-permute-start(bf16[64,1408]{1,0:T(8,128)(2,1)} %get-tuple-element.35.refs_0_), channel_id=1, source_target_pairs={{1,0},{2,1},{3,2},{0,3},{5,4},{6,5},{7,6},{4,7},{9,8},{10,9},{11,1... | collective-permute-start | bytes 540680 | tf_op jit(solution)/shard_map/ppermute | solution.py:20
  84.6 2.8 %collective-permute-start.17 = (bf16[64,1408]{1,0:T(8,128)(2,1)}, bf16[64,1408]{1,0:T(8,128)(2,1)S(1)}, u32[]{:S(2)}, u32[]{:S(2)}) collective-permute-start(bf16[64,1408]{1,0:T(8,128)(2,1)} %get-tuple-element.34.refs_0_), channel_id=1, source_target_pairs={{4,0},{8,4},{12,8},{0,12},{5,1},{9,5},{13,9},{1,13},{6,2},{10,6},{... | collective-permute-start | bytes 540680 | tf_op jit(solution)/shard_map/ppermute | solution.py:20
  87.7 2.1 %collective-permute-done.24.refs_1_ = bf16[64,1408]{1,0:T(8,128)(2,1)S(1)} collective-permute-done((bf16[64,1408]{1,0:T(8,128)(2,1)}, bf16[64,1408]{1,0:T(8,128)(2,1)S(1)}, u32[]{:S(2)}, u32[]{:S(2)}) %collective-permute-start.24) | collective-permute-done | bytes 180256 | tf_op jit(solution)/shard_map/ppermute | solution.py:20
  89.8 2.2 %shard_map.84.refs_6_ = bf16[256,1408]{1,0:T(8,128)(2,1)} custom-call(bf16[64,1408]{1,0:T(8,128)(2,1)} %get-tuple-element.36.refs_0_, bf16[64,1408]{1,0:T(8,128)(2,1)} %copy-done.24, bf16[64,1408]{1,0:T(8,128)(2,1)} %copy-done.25, bf16[64,1408]{1,0:T(8,128)(2,1)} %copy-done.26), custom_call_target="tpu_custom_call" | custom-call | bytes 1441792 | tf_op jit(solution)/shard_map/pallas_call | solution.py:173
  92.0 3.2 %collective-permute-start.37 = (bf16[256,1408]{1,0:T(8,128)(2,1)}, bf16[256,1408]{1,0:T(8,128)(2,1)S(1)}, u32[]{:S(2)}, u32[]{:S(2)}) collective-permute-start(bf16[256,1408]{1,0:T(8,128)(2,1)} %shard_map.84.refs_6_), channel_id=1, source_target_pairs={{4,0},{8,4},{12,8},{0,12},{5,1},{9,5},{13,9},{1,13},{6,2},{10,6},{... | collective-permute-start | bytes 2162696 | tf_op jit(solution)/shard_map/ppermute | solution.py:20
  95.3 3.6 %collective-permute-start.31 = (bf16[256,1408]{1,0:T(8,128)(2,1)S(1)}, bf16[256,1408]{1,0:T(8,128)(2,1)S(1)}, u32[]{:S(2)}, u32[]{:S(2)}) collective-permute-start(bf16[256,1408]{1,0:T(8,128)(2,1)S(1)} %copy-done.1), channel_id=1, source_target_pairs={{1,0},{2,1},{3,2},{0,3},{5,4},{6,5},{7,6},{4,7},{9,8},{10,9},{11,1... | collective-permute-start | bytes 2162696 | tf_op jit(solution)/shard_map/ppermute | solution.py:20
  98.9 2.1 %shard_map.83.refs_7_ = bf16[256,1408]{1,0:T(8,128)(2,1)} custom-call(bf16[64,1408]{1,0:T(8,128)(2,1)} %get-tuple-element.35.refs_0_, bf16[64,1408]{1,0:T(8,128)(2,1)} %copy-done.28, bf16[64,1408]{1,0:T(8,128)(2,1)} %copy-done.30, bf16[64,1408]{1,0:T(8,128)(2,1)} %copy-done.32), custom_call_target="tpu_custom_call" | custom-call | bytes 1441792 | tf_op jit(solution)/shard_map/pallas_call | solution.py:173
  101.1 2.0 %collective-permute-start.29 = (bf16[256,1408]{1,0:T(8,128)(2,1)}, bf16[256,1408]{1,0:T(8,128)(2,1)S(1)}, u32[]{:S(2)}, u32[]{:S(2)}) collective-permute-start(bf16[256,1408]{1,0:T(8,128)(2,1)} %shard_map.83.refs_7_), channel_id=1, source_target_pairs={{12,0},{0,4},{4,8},{8,12},{13,1},{1,5},{5,9},{9,13},{14,2},{2,6},{... | collective-permute-start | bytes 2162696 | tf_op jit(solution)/shard_map/ppermute | solution.py:20
  103.7 2.1 %shard_map.82.refs_1_ = bf16[256,1408]{1,0:T(8,128)(2,1)} custom-call(bf16[64,1408]{1,0:T(8,128)(2,1)} %get-tuple-element.34.refs_0_, bf16[64,1408]{1,0:T(8,128)(2,1)} %copy-done.27, bf16[64,1408]{1,0:T(8,128)(2,1)} %copy-done.29, bf16[64,1408]{1,0:T(8,128)(2,1)} %copy-done.31), custom_call_target="tpu_custom_call" | custom-call | bytes 1441792 | tf_op jit(solution)/shard_map/pallas_call | solution.py:173
  106.4 5.7 %collective-permute-done.37.refs_7_ = bf16[256,1408]{1,0:T(8,128)(2,1)S(1)} collective-permute-done((bf16[256,1408]{1,0:T(8,128)(2,1)}, bf16[256,1408]{1,0:T(8,128)(2,1)S(1)}, u32[]{:S(2)}, u32[]{:S(2)}) %collective-permute-start.37) | collective-permute-done | bytes 720928 | tf_op jit(solution)/shard_map/ppermute | solution.py:20
  113.0 2.4 %collective-permute-done.31.refs_2_ = bf16[256,1408]{1,0:T(8,128)(2,1)S(1)} collective-permute-done((bf16[256,1408]{1,0:T(8,128)(2,1)S(1)}, bf16[256,1408]{1,0:T(8,128)(2,1)S(1)}, u32[]{:S(2)}, u32[]{:S(2)}) %collective-permute-start.31) | collective-permute-done | bytes 720928 | tf_op jit(solution)/shard_map/ppermute | solution.py:20
  115.5 8.3 %collective-permute-done.27.refs_8_ = bf16[256,1408]{1,0:T(8,128)(2,1)S(1)} collective-permute-done((bf16[256,1408]{1,0:T(8,128)(2,1)}, bf16[256,1408]{1,0:T(8,128)(2,1)S(1)}, u32[]{:S(2)}, u32[]{:S(2)}) %collective-permute-start.27) | collective-permute-done | bytes 720928 | tf_op jit(solution)/shard_map/ppermute | solution.py:20
  123.8 1.9 %collective-permute-start.33 = (bf16[256,1408]{1,0:T(8,128)(2,1)S(1)}, bf16[256,1408]{1,0:T(8,128)(2,1)S(1)}, u32[]{:S(2)}, u32[]{:S(2)}) collective-permute-start(bf16[256,1408]{1,0:T(8,128)(2,1)S(1)} %copy-done.1), channel_id=1, source_target_pairs={{3,0},{0,1},{1,2},{2,3},{7,4},{4,5},{5,6},{6,7},{11,8},{8,9},{9,10... | collective-permute-start | bytes 2162696 | tf_op jit(solution)/shard_map/ppermute | solution.py:20
  125.7 3.0 %collective-permute-start.38 = (bf16[256,1408]{1,0:T(8,128)(2,1)S(1)}, bf16[256,1408]{1,0:T(8,128)(2,1)S(1)}, u32[]{:S(2)}, u32[]{:S(2)}) collective-permute-start(bf16[256,1408]{1,0:T(8,128)(2,1)S(1)} %collective-permute-done.37.refs_7_), channel_id=1, source_target_pairs={{4,0},{8,4},{12,8},{0,12},{5,1},{9,5},{13,9},{1,13},{6,2},{10,6},{... | collective-permute-start | bytes 2162696 | tf_op jit(solution)/shard_map/ppermute | solution.py:20
  128.7 1.8 %collective-permute-start.32 = (bf16[256,1408]{1,0:T(8,128)(2,1)S(1)}, bf16[256,1408]{1,0:T(8,128)(2,1)S(1)}, u32[]{:S(2)}, u32[]{:S(2)}) collective-permute-start(bf16[256,1408]{1,0:T(8,128)(2,1)S(1)} %collective-permute-done.31.refs_2_), channel_id=1, source_target_pairs={{1,0},{2,1},{3,2},{0,3},{5,4},{6,5},{7,6},{4,7},{9,8},{10,9},{11,1... | collective-permute-start | bytes 2162696 | tf_op jit(solution)/shard_map/ppermute | solution.py:20
  133.1 1.9 %collective-permute-start.30 = (bf16[128,1408]{1,0:T(8,128)(2,1)}, bf16[128,1408]{1,0:T(8,128)(2,1)S(1)}, u32[]{:S(2)}, u32[]{:S(2)}) collective-permute-start(bf16[128,1408]{1,0:T(8,128)(2,1)} %slice.59), channel_id=1, source_target_pairs={{12,0},{0,4},{4,8},{8,12},{13,1},{1,5},{5,9},{9,13},{14,2},{2,6},{... | collective-permute-start | bytes 1081352 | tf_op jit(solution)/shard_map/ppermute | solution.py:20
  134.9 5.7 %collective-permute-done.33.refs_4_ = bf16[256,1408]{1,0:T(8,128)(2,1)S(1)} collective-permute-done((bf16[256,1408]{1,0:T(8,128)(2,1)S(1)}, bf16[256,1408]{1,0:T(8,128)(2,1)S(1)}, u32[]{:S(2)}, u32[]{:S(2)}) %collective-permute-start.33) | collective-permute-done | bytes 720928 | tf_op jit(solution)/shard_map/ppermute | solution.py:20
  140.6 2.0 %collective-permute-start.21 = (bf16[128,1408]{1,0:T(8,128)(2,1)S(1)}, bf16[128,1408]{1,0:T(8,128)(2,1)S(1)}, u32[]{:S(2)}, u32[]{:S(2)}) collective-permute-start(bf16[128,1408]{1,0:T(8,128)(2,1)S(1)} %slice.56), channel_id=1, source_target_pairs={{1,0},{2,1},{3,2},{0,3},{5,4},{6,5},{7,6},{4,7},{9,8},{10,9},{11,1... | collective-permute-start | bytes 1081352 | tf_op jit(solution)/shard_map/ppermute | solution.py:20
  142.7 2.6 %collective-permute-done.38.refs_8_ = bf16[256,1408]{1,0:T(8,128)(2,1)S(1)} collective-permute-done((bf16[256,1408]{1,0:T(8,128)(2,1)S(1)}, bf16[256,1408]{1,0:T(8,128)(2,1)S(1)}, u32[]{:S(2)}, u32[]{:S(2)}) %collective-permute-start.38) | collective-permute-done | bytes 720928 | tf_op jit(solution)/shard_map/ppermute | solution.py:20
  145.9 1.9 %collective-permute-done.32.refs_3_ = bf16[256,1408]{1,0:T(8,128)(2,1)S(1)} collective-permute-done((bf16[256,1408]{1,0:T(8,128)(2,1)S(1)}, bf16[256,1408]{1,0:T(8,128)(2,1)S(1)}, u32[]{:S(2)}, u32[]{:S(2)}) %collective-permute-start.32) | collective-permute-done | bytes 720928 | tf_op jit(solution)/shard_map/ppermute | solution.py:20
  148.7 6.7 %shard_map.85.refs_12_ = bf16[2,2752,512]{2,1,0:T(8,128)(2,1)} custom-call(bf16[2,512,1024]{2,1,0:T(8,128)(2,1)} %get-tuple-element.23.refs_0_, bf16[256,1408]{1,0:T(8,128)(2,1)} %shard_map.80.refs_8_.refs_1_, bf16[256,1408]{1,0:T(8,128)(2,1)} %copy-done.8, bf16[256,1408]{1,0:T(8,128)(2,1)} %copy-done.12, bf16[256,1408]{1,0:T(8,128)(2,1)} %copy-done.10, ...), custom_call_target="tpu_custom_call" | custom-call | flops 2952790016 | bytes 10747904 | tf_op jit(solution)/shard_map/pallas_call | solution.py:229
  157.1 6.7 %shard_map.86 = bf16[2,2752,512]{2,1,0:T(8,128)(2,1)} custom-call(bf16[2,512,1024]{2,1,0:T(8,128)(2,1)} %get-tuple-element.23.refs_0_, bf16[256,1408]{1,0:T(8,128)(2,1)} %shard_map.82.refs_1_, bf16[256,1408]{1,0:T(8,128)(2,1)} %copy-done.5, bf16[128,1408]{1,0:T(8,128)(2,1)} %copy-done.21, ...), custom_call_target="tpu_custom_call", output_to_operand_aliasing={{}: (12, {})} | custom-call | flops 2952790016 | bytes 10747904 | tf_op jit(solution)/shard_map/pallas_call | solution.py:229
  (126 shorter events, 17.8 us)
Async XLA Ops:
  0.6 26.7 %collective-permute-start.7 = (bf16[2,128,22016]{2,1,0:T(8,128)(2,1)}, bf16[2,128,22016]{2,1,0:T(8,128)(2,1)}, u32[]{:S(2)}, u32[]{:S(2)}) collective-permute-start(bf16[2,128,22016]{2,1,0:T(8,128)(2,1)} %grads_ref.3), channel_id=1, source_target_pairs={{0,16},{16,0},{1,17},{17,1},{2,18},{18,2},{3,19},{19,3},{4,20},{20... | collective-permute-start | bytes 33816584 | tf_op jit(solution)/shard_map/ppermute | solution.py:28
  5.2 6.7 %collective-permute-start = (bf16[2,128,256]{2,1,0:T(8,128)(2,1)S(1)}, bf16[2,128,256]{2,1,0:T(8,128)(2,1)S(1)}, u32[]{:S(2)}, u32[]{:S(2)}) collective-permute-start(bf16[2,128,256]{2,1,0:T(8,128)(2,1)S(1)} %get-tuple-element.39), channel_id=1, source_target_pairs={{12,0},{0,4},{4,8},{8,12},{13,1},{1,5},{5,9},{9,13},{14,2},{2,6},{... | collective-permute-start | bytes 393224 | tf_op jit(solution)/shard_map/ppermute | solution.py:20
  6.9 7.1 %collective-permute-start.1 = (bf16[2,128,256]{2,1,0:T(8,128)(2,1)S(1)}, bf16[2,128,256]{2,1,0:T(8,128)(2,1)S(1)}, u32[]{:S(2)}, u32[]{:S(2)}) collective-permute-start(bf16[2,128,256]{2,1,0:T(8,128)(2,1)S(1)} %get-tuple-element.41), channel_id=1, source_target_pairs={{4,0},{8,4},{12,8},{0,12},{5,1},{9,5},{13,9},{1,13},{6,2},{10,6},{... | collective-permute-start | bytes 393224 | tf_op jit(solution)/shard_map/ppermute | solution.py:20
  8.5 7.3 %collective-permute-start.2 = (bf16[2,128,256]{2,1,0:T(8,128)(2,1)S(1)}, bf16[2,128,256]{2,1,0:T(8,128)(2,1)S(1)}, u32[]{:S(2)}, u32[]{:S(2)}) collective-permute-start(bf16[2,128,256]{2,1,0:T(8,128)(2,1)S(1)} %get-tuple-element.40), channel_id=1, source_target_pairs={{8,0},{12,4},{0,8},{4,12},{9,1},{13,5},{1,9},{5,13},{10,2},{14,6},... | collective-permute-start | bytes 393224 | tf_op jit(solution)/shard_map/ppermute | solution.py:20
  16.0 6.3 %collective-permute-start.3 = (bf16[2,128,64]{2,1,0:T(8,128)(2,1)S(1)}, bf16[2,128,64]{2,1,0:T(8,128)(2,1)S(1)}, u32[]{:S(2)}, u32[]{:S(2)}) collective-permute-start(bf16[2,128,64]{2,1,0:T(8,128)(2,1)S(1)} %get-tuple-element.42), channel_id=1, source_target_pairs={{3,0},{0,1},{1,2},{2,3},{7,4},{4,5},{5,6},{6,7},{11,8},{8,9},{9,10... | collective-permute-start | bytes 98312 | tf_op jit(solution)/shard_map/ppermute | solution.py:20
  18.0 4.6 %collective-permute-start.4 = (bf16[2,128,64]{2,1,0:T(8,128)(2,1)S(1)}, bf16[2,128,64]{2,1,0:T(8,128)(2,1)S(1)}, u32[]{:S(2)}, u32[]{:S(2)}) collective-permute-start(bf16[2,128,64]{2,1,0:T(8,128)(2,1)S(1)} %get-tuple-element.44), channel_id=1, source_target_pairs={{1,0},{2,1},{3,2},{0,3},{5,4},{6,5},{7,6},{4,7},{9,8},{10,9},{11,1... | collective-permute-start | bytes 98312 | tf_op jit(solution)/shard_map/ppermute | solution.py:20
  20.2 5.8 %collective-permute-start.5 = (bf16[2,128,64]{2,1,0:T(8,128)(2,1)S(1)}, bf16[2,128,64]{2,1,0:T(8,128)(2,1)S(1)}, u32[]{:S(2)}, u32[]{:S(2)}) collective-permute-start(bf16[2,128,64]{2,1,0:T(8,128)(2,1)S(1)} %get-tuple-element.43), channel_id=1, source_target_pairs={{2,0},{3,1},{0,2},{1,3},{6,4},{7,5},{4,6},{5,7},{10,8},{11,9},{8,1... | collective-permute-start | bytes 98312 | tf_op jit(solution)/shard_map/ppermute | solution.py:20
  26.0 1.3 collective-permute-start.6
  34.3 14.1 %collective-permute-start.11 = (bf16[64,2752]{1,0:T(8,128)(2,1)}, bf16[64,2752]{1,0:T(8,128)(2,1)S(1)}, u32[]{:S(2)}, u32[]{:S(2)}) collective-permute-start(bf16[64,2752]{1,0:T(8,128)(2,1)} %get-tuple-element.27), channel_id=1, source_target_pairs={{96,0},{0,32},{32,64},{64,96},{97,1},{1,33},{33,65},{65,97},{98,2}... | collective-permute-start | bytes 1056776 | tf_op jit(solution)/shard_map/ppermute | solution.py:20
  35.8 21.4 %collective-permute-start.12 = (bf16[64,2752]{1,0:T(8,128)(2,1)}, bf16[64,2752]{1,0:T(8,128)(2,1)S(1)}, u32[]{:S(2)}, u32[]{:S(2)}) collective-permute-start(bf16[64,2752]{1,0:T(8,128)(2,1)} %get-tuple-element.28), channel_id=1, source_target_pairs={{64,0},{96,32},{0,64},{32,96},{65,1},{97,33},{1,65},{33,97},{66,2}... | collective-permute-start | bytes 1056776 | tf_op jit(solution)/shard_map/ppermute | solution.py:20
  38.5 18.7 %collective-permute-start.13 = (bf16[64,2752]{1,0:T(8,128)(2,1)}, bf16[64,2752]{1,0:T(8,128)(2,1)S(1)}, u32[]{:S(2)}, u32[]{:S(2)}) collective-permute-start(bf16[64,2752]{1,0:T(8,128)(2,1)} %get-tuple-element.29), channel_id=1, source_target_pairs={{32,0},{64,32},{96,64},{0,96},{33,1},{65,33},{97,65},{1,97},{34,2}... | collective-permute-start | bytes 1056776 | tf_op jit(solution)/shard_map/ppermute | solution.py:20
  46.4 18.1 %collective-permute-start.10 = (bf16[64,2752]{1,0:T(8,128)(2,1)}, bf16[64,2752]{1,0:T(8,128)(2,1)S(1)}, u32[]{:S(2)}, u32[]{:S(2)}) collective-permute-start(bf16[64,2752]{1,0:T(8,128)(2,1)} %get-tuple-element.26), channel_id=1, source_target_pairs={{32,0},{64,32},{96,64},{0,96},{33,1},{65,33},{97,65},{1,97},{34,2}... | collective-permute-start | bytes 1056776 | tf_op jit(solution)/shard_map/ppermute | solution.py:20
  46.4 30.3 %collective-permute-start.8 = (bf16[64,2752]{1,0:T(8,128)(2,1)}, bf16[64,2752]{1,0:T(8,128)(2,1)S(1)}, u32[]{:S(2)}, u32[]{:S(2)}) collective-permute-start(bf16[64,2752]{1,0:T(8,128)(2,1)} %get-tuple-element.24), channel_id=1, source_target_pairs={{96,0},{0,32},{32,64},{64,96},{97,1},{1,33},{33,65},{65,97},{98,2}... | collective-permute-start | bytes 1056776 | tf_op jit(solution)/shard_map/ppermute | solution.py:20
  48.4 28.3 %collective-permute-start.9 = (bf16[64,2752]{1,0:T(8,128)(2,1)}, bf16[64,2752]{1,0:T(8,128)(2,1)S(1)}, u32[]{:S(2)}, u32[]{:S(2)}) collective-permute-start(bf16[64,2752]{1,0:T(8,128)(2,1)} %get-tuple-element.25), channel_id=1, source_target_pairs={{64,0},{96,32},{0,64},{32,96},{65,1},{97,33},{1,65},{33,97},{66,2}... | collective-permute-start | bytes 1056776 | tf_op jit(solution)/shard_map/ppermute | solution.py:20
  61.2 8.9 %collective-permute-start.14 = (bf16[64,1408]{1,0:T(8,128)(2,1)}, bf16[64,1408]{1,0:T(8,128)(2,1)S(1)}, u32[]{:S(2)}, u32[]{:S(2)}) collective-permute-start(bf16[64,1408]{1,0:T(8,128)(2,1)} %get-tuple-element.33.refs_0_), channel_id=1, source_target_pairs={{4,0},{8,4},{12,8},{0,12},{5,1},{9,5},{13,9},{1,13},{6,2},{10,6},{... | collective-permute-start | bytes 540680 | tf_op jit(solution)/shard_map/ppermute | solution.py:20
  63.1 8.9 %collective-permute-start.15 = (bf16[64,1408]{1,0:T(8,128)(2,1)}, bf16[64,1408]{1,0:T(8,128)(2,1)S(1)}, u32[]{:S(2)}, u32[]{:S(2)}) collective-permute-start(bf16[64,1408]{1,0:T(8,128)(2,1)} %get-tuple-element.33.refs_0_), channel_id=1, source_target_pairs={{8,0},{12,4},{0,8},{4,12},{9,1},{13,5},{1,9},{5,13},{10,2},{14,6},... | collective-permute-start | bytes 540680 | tf_op jit(solution)/shard_map/ppermute | solution.py:20
  64.4 9.2 %collective-permute-start.16 = (bf16[64,1408]{1,0:T(8,128)(2,1)}, bf16[64,1408]{1,0:T(8,128)(2,1)S(1)}, u32[]{:S(2)}, u32[]{:S(2)}) collective-permute-start(bf16[64,1408]{1,0:T(8,128)(2,1)} %get-tuple-element.33.refs_0_), channel_id=1, source_target_pairs={{12,0},{0,4},{4,8},{8,12},{13,1},{1,5},{5,9},{9,13},{14,2},{2,6},{... | collective-permute-start | bytes 540680 | tf_op jit(solution)/shard_map/ppermute | solution.py:20
  70.0 13.7 %collective-permute-start.34 = (bf16[64,1408]{1,0:T(8,128)(2,1)}, bf16[64,1408]{1,0:T(8,128)(2,1)S(1)}, u32[]{:S(2)}, u32[]{:S(2)}) collective-permute-start(bf16[64,1408]{1,0:T(8,128)(2,1)} %get-tuple-element.36.refs_0_), channel_id=1, source_target_pairs={{1,0},{2,1},{3,2},{0,3},{5,4},{6,5},{7,6},{4,7},{9,8},{10,9},{11,1... | collective-permute-start | bytes 540680 | tf_op jit(solution)/shard_map/ppermute | solution.py:20
  72.0 12.6 %collective-permute-start.35 = (bf16[64,1408]{1,0:T(8,128)(2,1)}, bf16[64,1408]{1,0:T(8,128)(2,1)S(1)}, u32[]{:S(2)}, u32[]{:S(2)}) collective-permute-start(bf16[64,1408]{1,0:T(8,128)(2,1)} %get-tuple-element.36.refs_0_), channel_id=1, source_target_pairs={{2,0},{3,1},{0,2},{1,3},{6,4},{7,5},{4,6},{5,7},{10,8},{11,9},{8,1... | collective-permute-start | bytes 540680 | tf_op jit(solution)/shard_map/ppermute | solution.py:20
  73.6 13.8 %collective-permute-start.36 = (bf16[64,1408]{1,0:T(8,128)(2,1)}, bf16[64,1408]{1,0:T(8,128)(2,1)S(1)}, u32[]{:S(2)}, u32[]{:S(2)}) collective-permute-start(bf16[64,1408]{1,0:T(8,128)(2,1)} %get-tuple-element.36.refs_0_), channel_id=1, source_target_pairs={{3,0},{0,1},{1,2},{2,3},{7,4},{4,5},{5,6},{6,7},{11,8},{8,9},{9,10... | collective-permute-start | bytes 540680 | tf_op jit(solution)/shard_map/ppermute | solution.py:20
  77.6 17.7 %copy-start.1 = (bf16[256,1408]{1,0:T(8,128)(2,1)S(1)}, bf16[256,1408]{1,0:T(8,128)(2,1)}, u32[]{:S(2)}) copy-start(bf16[256,1408]{1,0:T(8,128)(2,1)} %shard_map.80.refs_8_.refs_1_) | copy-start | bytes 2162692
  80.6 9.2 %collective-permute-start.24 = (bf16[64,1408]{1,0:T(8,128)(2,1)}, bf16[64,1408]{1,0:T(8,128)(2,1)S(1)}, u32[]{:S(2)}, u32[]{:S(2)}) collective-permute-start(bf16[64,1408]{1,0:T(8,128)(2,1)} %get-tuple-element.35.refs_0_), channel_id=1, source_target_pairs={{1,0},{2,1},{3,2},{0,3},{5,4},{6,5},{7,6},{4,7},{9,8},{10,9},{11,1... | collective-permute-start | bytes 540680 | tf_op jit(solution)/shard_map/ppermute | solution.py:20
  83.0 9.0 %collective-permute-start.25 = (bf16[64,1408]{1,0:T(8,128)(2,1)}, bf16[64,1408]{1,0:T(8,128)(2,1)S(1)}, u32[]{:S(2)}, u32[]{:S(2)}) collective-permute-start(bf16[64,1408]{1,0:T(8,128)(2,1)} %get-tuple-element.35.refs_0_), channel_id=1, source_target_pairs={{2,0},{3,1},{0,2},{1,3},{6,4},{7,5},{4,6},{5,7},{10,8},{11,9},{8,1... | collective-permute-start | bytes 540680 | tf_op jit(solution)/shard_map/ppermute | solution.py:20
  83.7 11.6 %collective-permute-start.26 = (bf16[64,1408]{1,0:T(8,128)(2,1)}, bf16[64,1408]{1,0:T(8,128)(2,1)S(1)}, u32[]{:S(2)}, u32[]{:S(2)}) collective-permute-start(bf16[64,1408]{1,0:T(8,128)(2,1)} %get-tuple-element.35.refs_0_), channel_id=1, source_target_pairs={{3,0},{0,1},{1,2},{2,3},{7,4},{4,5},{5,6},{6,7},{11,8},{8,9},{9,10... | collective-permute-start | bytes 540680 | tf_op jit(solution)/shard_map/ppermute | solution.py:20
  84.6 16.4 %collective-permute-start.17 = (bf16[64,1408]{1,0:T(8,128)(2,1)}, bf16[64,1408]{1,0:T(8,128)(2,1)S(1)}, u32[]{:S(2)}, u32[]{:S(2)}) collective-permute-start(bf16[64,1408]{1,0:T(8,128)(2,1)} %get-tuple-element.34.refs_0_), channel_id=1, source_target_pairs={{4,0},{8,4},{12,8},{0,12},{5,1},{9,5},{13,9},{1,13},{6,2},{10,6},{... | collective-permute-start | bytes 540680 | tf_op jit(solution)/shard_map/ppermute | solution.py:20
  87.3 13.7 %collective-permute-start.18 = (bf16[64,1408]{1,0:T(8,128)(2,1)}, bf16[64,1408]{1,0:T(8,128)(2,1)S(1)}, u32[]{:S(2)}, u32[]{:S(2)}) collective-permute-start(bf16[64,1408]{1,0:T(8,128)(2,1)} %get-tuple-element.34.refs_0_), channel_id=1, source_target_pairs={{8,0},{12,4},{0,8},{4,12},{9,1},{13,5},{1,9},{5,13},{10,2},{14,6},... | collective-permute-start | bytes 540680 | tf_op jit(solution)/shard_map/ppermute | solution.py:20
  89.8 13.2 %collective-permute-start.19 = (bf16[64,1408]{1,0:T(8,128)(2,1)}, bf16[64,1408]{1,0:T(8,128)(2,1)S(1)}, u32[]{:S(2)}, u32[]{:S(2)}) collective-permute-start(bf16[64,1408]{1,0:T(8,128)(2,1)} %get-tuple-element.34.refs_0_), channel_id=1, source_target_pairs={{12,0},{0,4},{4,8},{8,12},{13,1},{1,5},{5,9},{9,13},{14,2},{2,6},{... | collective-permute-start | bytes 540680 | tf_op jit(solution)/shard_map/ppermute | solution.py:20
  92.0 23.5 %copy-start.2 = (bf16[256,1408]{1,0:T(8,128)(2,1)S(1)}, bf16[256,1408]{1,0:T(8,128)(2,1)}, u32[]{:S(2)}) copy-start(bf16[256,1408]{1,0:T(8,128)(2,1)} %shard_map.84.refs_6_) | copy-start | bytes 2162692
  92.0 20.2 %collective-permute-start.37 = (bf16[256,1408]{1,0:T(8,128)(2,1)}, bf16[256,1408]{1,0:T(8,128)(2,1)S(1)}, u32[]{:S(2)}, u32[]{:S(2)}) collective-permute-start(bf16[256,1408]{1,0:T(8,128)(2,1)} %shard_map.84.refs_6_), channel_id=1, source_target_pairs={{4,0},{8,4},{12,8},{0,12},{5,1},{9,5},{13,9},{1,13},{6,2},{10,6},{... | collective-permute-start | bytes 2162696 | tf_op jit(solution)/shard_map/ppermute | solution.py:20
  95.3 20.2 %collective-permute-start.31 = (bf16[256,1408]{1,0:T(8,128)(2,1)S(1)}, bf16[256,1408]{1,0:T(8,128)(2,1)S(1)}, u32[]{:S(2)}, u32[]{:S(2)}) collective-permute-start(bf16[256,1408]{1,0:T(8,128)(2,1)S(1)} %copy-done.1), channel_id=1, source_target_pairs={{1,0},{2,1},{3,2},{0,3},{5,4},{6,5},{7,6},{4,7},{9,8},{10,9},{11,1... | collective-permute-start | bytes 2162696 | tf_op jit(solution)/shard_map/ppermute | solution.py:20
  101.0 22.8 %collective-permute-start.27 = (bf16[256,1408]{1,0:T(8,128)(2,1)}, bf16[256,1408]{1,0:T(8,128)(2,1)S(1)}, u32[]{:S(2)}, u32[]{:S(2)}) collective-permute-start(bf16[256,1408]{1,0:T(8,128)(2,1)} %shard_map.83.refs_7_), channel_id=1, source_target_pairs={{4,0},{8,4},{12,8},{0,12},{5,1},{9,5},{13,9},{1,13},{6,2},{10,6},{... | collective-permute-start | bytes 2162696 | tf_op jit(solution)/shard_map/ppermute | solution.py:20
  101.1 24.6 %collective-permute-start.29 = (bf16[256,1408]{1,0:T(8,128)(2,1)}, bf16[256,1408]{1,0:T(8,128)(2,1)S(1)}, u32[]{:S(2)}, u32[]{:S(2)}) collective-permute-start(bf16[256,1408]{1,0:T(8,128)(2,1)} %shard_map.83.refs_7_), channel_id=1, source_target_pairs={{12,0},{0,4},{4,8},{8,12},{13,1},{1,5},{5,9},{9,13},{14,2},{2,6},{... | collective-permute-start | bytes 2162696 | tf_op jit(solution)/shard_map/ppermute | solution.py:20
  105.8 22.9 %collective-permute-start.20 = (bf16[256,1408]{1,0:T(8,128)(2,1)}, bf16[256,1408]{1,0:T(8,128)(2,1)S(1)}, u32[]{:S(2)}, u32[]{:S(2)}) collective-permute-start(bf16[256,1408]{1,0:T(8,128)(2,1)} %shard_map.82.refs_1_), channel_id=1, source_target_pairs={{1,0},{2,1},{3,2},{0,3},{5,4},{6,5},{7,6},{4,7},{9,8},{10,9},{11,1... | collective-permute-start | bytes 2162696 | tf_op jit(solution)/shard_map/ppermute | solution.py:20
  112.2 36.5 %copy-start.7 = (bf16[256,1408]{1,0:T(8,128)(2,1)}, bf16[256,1408]{1,0:T(8,128)(2,1)S(1)}, u32[]{:S(2)}) copy-start(bf16[256,1408]{1,0:T(8,128)(2,1)S(1)} %collective-permute-done.37.refs_7_) | copy-start | bytes 2162692
  112.2 19.9 %collective-permute-start.22 = (bf16[256,1408]{1,0:T(8,128)(2,1)}, bf16[256,1408]{1,0:T(8,128)(2,1)S(1)}, u32[]{:S(2)}, u32[]{:S(2)}) collective-permute-start(bf16[256,1408]{1,0:T(8,128)(2,1)} %shard_map.82.refs_1_), channel_id=1, source_target_pairs={{3,0},{0,1},{1,2},{2,3},{7,4},{4,5},{5,6},{6,7},{11,8},{8,9},{9,10... | collective-permute-start | bytes 2162696 | tf_op jit(solution)/shard_map/ppermute | solution.py:20
  115.5 33.2 %copy-start.8 = (bf16[256,1408]{1,0:T(8,128)(2,1)}, bf16[256,1408]{1,0:T(8,128)(2,1)S(1)}, u32[]{:S(2)}) copy-start(bf16[256,1408]{1,0:T(8,128)(2,1)S(1)} %collective-permute-done.31.refs_2_) | copy-start | bytes 2162692
  115.5 17.6 %collective-permute-start.39 = (bf16[256,1408]{1,0:T(8,128)(2,1)S(1)}, bf16[256,1408]{1,0:T(8,128)(2,1)S(1)}, u32[]{:S(2)}, u32[]{:S(2)}) collective-permute-start(bf16[256,1408]{1,0:T(8,128)(2,1)S(1)} %copy-done.2), channel_id=1, source_target_pairs={{12,0},{0,4},{4,8},{8,12},{13,1},{1,5},{5,9},{9,13},{14,2},{2,6},{... | collective-permute-start | bytes 2162696 | tf_op jit(solution)/shard_map/ppermute | solution.py:20
  123.8 31.6 %copy-start.3 = (bf16[256,1408]{1,0:T(8,128)(2,1)}, bf16[256,1408]{1,0:T(8,128)(2,1)S(1)}, u32[]{:S(2)}) copy-start(bf16[256,1408]{1,0:T(8,128)(2,1)S(1)} %collective-permute-done.27.refs_8_) | copy-start | bytes 2162692
  123.8 16.8 %collective-permute-start.33 = (bf16[256,1408]{1,0:T(8,128)(2,1)S(1)}, bf16[256,1408]{1,0:T(8,128)(2,1)S(1)}, u32[]{:S(2)}, u32[]{:S(2)}) collective-permute-start(bf16[256,1408]{1,0:T(8,128)(2,1)S(1)} %copy-done.1), channel_id=1, source_target_pairs={{3,0},{0,1},{1,2},{2,3},{7,4},{4,5},{5,6},{6,7},{11,8},{8,9},{9,10... | collective-permute-start | bytes 2162696 | tf_op jit(solution)/shard_map/ppermute | solution.py:20
  125.7 29.7 %copy-start.4 = (bf16[256,1408]{1,0:T(8,128)(2,1)}, bf16[256,1408]{1,0:T(8,128)(2,1)S(1)}, u32[]{:S(2)}) copy-start(bf16[256,1408]{1,0:T(8,128)(2,1)S(1)} %collective-permute-done.29.refs_11_) | copy-start | bytes 2162692
  125.7 19.6 %collective-permute-start.38 = (bf16[256,1408]{1,0:T(8,128)(2,1)S(1)}, bf16[256,1408]{1,0:T(8,128)(2,1)S(1)}, u32[]{:S(2)}, u32[]{:S(2)}) collective-permute-start(bf16[256,1408]{1,0:T(8,128)(2,1)S(1)} %collective-permute-done.37.refs_7_), channel_id=1, source_target_pairs={{4,0},{8,4},{12,8},{0,12},{5,1},{9,5},{13,9},{1,13},{6,2},{10,6},{... | collective-permute-start | bytes 2162696 | tf_op jit(solution)/shard_map/ppermute | solution.py:20
  128.7 26.7 %copy-start.5 = (bf16[256,1408]{1,0:T(8,128)(2,1)}, bf16[256,1408]{1,0:T(8,128)(2,1)S(1)}, u32[]{:S(2)}) copy-start(bf16[256,1408]{1,0:T(8,128)(2,1)S(1)} %collective-permute-done.20.refs_2_) | copy-start | bytes 2162692
  128.7 19.1 %collective-permute-start.32 = (bf16[256,1408]{1,0:T(8,128)(2,1)S(1)}, bf16[256,1408]{1,0:T(8,128)(2,1)S(1)}, u32[]{:S(2)}, u32[]{:S(2)}) collective-permute-start(bf16[256,1408]{1,0:T(8,128)(2,1)S(1)} %collective-permute-done.31.refs_2_), channel_id=1, source_target_pairs={{1,0},{2,1},{3,2},{0,3},{5,4},{6,5},{7,6},{4,7},{9,8},{10,9},{11,1... | collective-permute-start | bytes 2162696 | tf_op jit(solution)/shard_map/ppermute | solution.py:20
  132.1 23.4 %copy-start.6 = (bf16[256,1408]{1,0:T(8,128)(2,1)}, bf16[256,1408]{1,0:T(8,128)(2,1)S(1)}, u32[]{:S(2)}) copy-start(bf16[256,1408]{1,0:T(8,128)(2,1)S(1)} %collective-permute-done.22.refs_5_) | copy-start | bytes 2162692
  132.1 23.4 %collective-permute-start.28 = (bf16[128,1408]{1,0:T(8,128)(2,1)}, bf16[128,1408]{1,0:T(8,128)(2,1)}, u32[]{:S(2)}, u32[]{:S(2)}) collective-permute-start(bf16[128,1408]{1,0:T(8,128)(2,1)} %slice.58), channel_id=1, source_target_pairs={{4,0},{8,4},{12,8},{0,12},{5,1},{9,5},{13,9},{1,13},{6,2},{10,6},{... | collective-permute-start | bytes 1081352 | tf_op jit(solution)/shard_map/ppermute | solution.py:20
  133.1 22.3 %collective-permute-start.30 = (bf16[128,1408]{1,0:T(8,128)(2,1)}, bf16[128,1408]{1,0:T(8,128)(2,1)S(1)}, u32[]{:S(2)}, u32[]{:S(2)}) collective-permute-start(bf16[128,1408]{1,0:T(8,128)(2,1)} %slice.59), channel_id=1, source_target_pairs={{12,0},{0,4},{4,8},{8,12},{13,1},{1,5},{5,9},{9,13},{14,2},{2,6},{... | collective-permute-start | bytes 1081352 | tf_op jit(solution)/shard_map/ppermute | solution.py:20
  140.6 14.8 %collective-permute-start.21 = (bf16[128,1408]{1,0:T(8,128)(2,1)S(1)}, bf16[128,1408]{1,0:T(8,128)(2,1)S(1)}, u32[]{:S(2)}, u32[]{:S(2)}) collective-permute-start(bf16[128,1408]{1,0:T(8,128)(2,1)S(1)} %slice.56), channel_id=1, source_target_pairs={{1,0},{2,1},{3,2},{0,3},{5,4},{6,5},{7,6},{4,7},{9,8},{10,9},{11,1... | collective-permute-start | bytes 1081352 | tf_op jit(solution)/shard_map/ppermute | solution.py:20
  145.3 10.2 %collective-permute-start.23 = (bf16[128,1408]{1,0:T(8,128)(2,1)}, bf16[128,1408]{1,0:T(8,128)(2,1)S(1)}, u32[]{:S(2)}, u32[]{:S(2)}) collective-permute-start(bf16[128,1408]{1,0:T(8,128)(2,1)} %slice.57), channel_id=1, source_target_pairs={{3,0},{0,1},{1,2},{2,3},{7,4},{4,5},{5,6},{6,7},{11,8},{8,9},{9,10... | collective-permute-start | bytes 1081352 | tf_op jit(solution)/shard_map/ppermute | solution.py:20
  (28 other events, 101.7 us)

commit v8 on v7

--- a/solution.py
+++ b/solution.py
@@ -41,19 +41,25 @@
     ranks = bases_ref.shape[2]
     part = ranks // (SIDE * SIDE)
     block = ranks // SIDE
-    for out_ref, y_outer in ((by_y_ref, True), (by_z_ref, False)):
-        for low in range(0, ranks, block):
-            source = lax.broadcasted_iota(jnp.int32, (ranks, block), 0)
-            column = lax.broadcasted_iota(jnp.int32, (ranks, block), 1) + low
-            outer, inner = column // (SIDE * part), (column // part) & (SIDE - 1)
-            dy, dz = (outer, inner) if y_outer else (inner, outer)
-            wanted = (((y + dy) & (SIDE - 1)) * SIDE + ((z + dz) & (SIDE - 1))) * part
-            wanted = wanted + (column & (part - 1))
-            place = jnp.where(source == wanted, 1.0, 0.0).astype(BF16)
-            for k in range(bases_ref.shape[0]):
-                out_ref[k, :, low : low + block] = jnp.dot(
-                    bases_ref[k], place, preferred_element_type=F32
-                ).astype(BF16)
+    source = lax.broadcasted_iota(jnp.int32, (block, block), 0)
+    column = lax.broadcasted_iota(jnp.int32, (block, block), 1)
+    wanted = ((z + column // part) & (SIDE - 1)) * part + (column & (part - 1))
+    place = jnp.where(source == wanted, 1.0, 0.0).astype(BF16)
+    for dy in range(SIDE):
+        start = pl.multiple_of(((y + dy) & (SIDE - 1)) * block, block)
+        for k in range(bases_ref.shape[0]):
+            by_y_ref[k, :, dy * block : (dy + 1) * block] = jnp.dot(
+                bases_ref[k, :, pl.ds(start, block)], place, preferred_element_type=F32
+            ).astype(BF16)
+    source = lax.broadcasted_iota(jnp.int32, (ranks, block), 0)
+    column = lax.broadcasted_iota(jnp.int32, (ranks, block), 1)
+    for dz in range(SIDE):
+        wanted = (((column // part) & (SIDE - 1)) * SIDE + dz) * part + (column & (part - 1))
+        place = jnp.where(source == wanted, 1.0, 0.0).astype(BF16)
+        for k in range(bases_ref.shape[0]):
+            by_z_ref[k, :, dz * block : (dz + 1) * block] = jnp.dot(
+                by_y_ref[k], place, preferred_element_type=F32
+            ).astype(BF16)
 
 
 def arrange(where, bases, after):

time: 164 us -> 164 us (level); the launches traced: 164 us -> 162 us
  waiting for transfers between devices: 44.2 us -> 42.1 us
  starting transfers between devices: 56.4 us -> 58.2 us
    ppermute x38, waiting for transfers between devices: 43.7 us -> 41.5 us  [receive(): lax.ppermute(value, axis, [((i + distance) % SIDE, i) for i in range(SIDE)])]
    ppermute x38, starting transfers between devices: 56.2 us -> 58 us  [receive(): lax.ppermute(value, axis, [((i + distance) % SIDE, i) for i in range(SIDE)])]
  transfers between devices with their start and end apart: 40 -> 40, of which waited for: 16 -> 18; matrix products, arithmetic and copies ran while one was open for 4% -> 4% of each run, Pallas kernels for 22% -> 21%
where the time goes in v8:
time: 164 us; the launch traced here: 162 us
  starting transfers between devices  58.2 us (35%)
  Pallas kernels  47.2 us (29%)
  waiting for transfers between devices  42.1 us (26%)
  local copies, waits for them, and re-layouts  9.66 us (6%)
  matrix products  2.91 us (2%)
    ppermute x38, starting transfers between devices, receive(): lax.ppermute(value, axis, [((i + distance) % SIDE, i) for i in range(SIDE)])  58 us
    ppermute x38, waiting for transfers between devices, receive(): lax.ppermute(value, axis, [((i + distance) % SIDE, i) for i in range(SIDE)])  41.5 us
    pallas_call x2, Pallas kernels, expand_halves(): pl.pallas_call(functools.partial(expand_kernel, counts=counts, which=whic...  13.4 us
    pallas_call x2, Pallas kernels, partial_grads(): pl.pallas_call(partial_kernel, grid_spec=pltpu.PrefetchScalarGridSpec(num...  12.7 us
    pallas_call x4, Pallas kernels, stack(): pl.pallas_call(stack_kernel, out_shape=held((rows * len(pieces), width)),...  8.54 us
    unnamed x72, local copies, waits for them, and re-layouts  7.1 us
    pallas_call x1, Pallas kernels, arrange(): pl.pallas_call(arrange_kernel, grid_spec=pltpu.PrefetchScalarGridSpec(num...  6.51 us
    pallas_call x2, Pallas kernels, directions(): pl.pallas_call(functools.partial(direction_kernel, pieces=pieces), grid=(...  6.1 us
  transfers between devices with their start and end apart: 40, of which 18 were waited for; matrix products, arithmetic and copies ran while one was open for 4% of the time, Pallas kernels for 21%

profile of v8, /device:TPU:0, one launch (start us, length us, event | category | flops | bytes accessed | tf_op | source)
XLA Modules:
  0.0 162.0 jit_solution(18179303020199444886)
XLA Ops:
  0.8 1.5 copy-done
  2.2 2.9 %fusion.4 = bf16[2,128,1024]{2,1,0:T(8,128)(2,1)S(1)} fusion(s32[1024]{0:T(1024)S(1)} %fusion.21, bf16[2,512,1024]{2,1,0:T(8,128)(2,1)} %bases_ref.1, bf16[128,8192]{1,0:T(8,128)(2,1)S(1)} %copy-done, s32[]{:T(128)S(6)} %select_n.54), kind=kOutput, calls=%fused_computation.4 | convolution fusion | flops 806879232 | bytes 2756612 | tf_op jit(solution)/shard_map/ktr,rs->kts/dot_general | solution.py:280
  5.2 1.7 %collective-permute-start = (bf16[2,128,256]{2,1,0:T(8,128)(2,1)S(1)}, bf16[2,128,256]{2,1,0:T(8,128)(2,1)S(1)}, u32[]{:S(2)}, u32[]{:S(2)}) collective-permute-start(bf16[2,128,256]{2,1,0:T(8,128)(2,1)S(1)} %get-tuple-element.39), channel_id=1, source_target_pairs={{12,0},{0,4},{4,8},{8,12},{13,1},{1,5},{5,9},{9,13},{14,2},{2,6},{... | collective-permute-start | bytes 393224 | tf_op jit(solution)/shard_map/ppermute | solution.py:20
  6.9 1.6 collective-permute-start.1
  8.5 2.1 %collective-permute-start.2 = (bf16[2,128,256]{2,1,0:T(8,128)(2,1)S(1)}, bf16[2,128,256]{2,1,0:T(8,128)(2,1)S(1)}, u32[]{:S(2)}, u32[]{:S(2)}) collective-permute-start(bf16[2,128,256]{2,1,0:T(8,128)(2,1)S(1)} %get-tuple-element.40), channel_id=1, source_target_pairs={{8,0},{12,4},{0,8},{4,12},{9,1},{13,5},{1,9},{5,13},{10,2},{14,6},... | collective-permute-start | bytes 393224 | tf_op jit(solution)/shard_map/ppermute | solution.py:20
  11.8 2.2 %collective-permute-done.1 = bf16[2,128,256]{2,1,0:T(8,128)(2,1)S(1)} collective-permute-done((bf16[2,128,256]{2,1,0:T(8,128)(2,1)S(1)}, bf16[2,128,256]{2,1,0:T(8,128)(2,1)S(1)}, u32[]{:S(2)}, u32[]{:S(2)}) %collective-permute-start.1) | collective-permute-done | bytes 131104 | tf_op jit(solution)/shard_map/ppermute | solution.py:20
  14.0 1.8 %collective-permute-done.2 = bf16[2,128,256]{2,1,0:T(8,128)(2,1)S(1)} collective-permute-done((bf16[2,128,256]{2,1,0:T(8,128)(2,1)S(1)}, bf16[2,128,256]{2,1,0:T(8,128)(2,1)S(1)}, u32[]{:S(2)}, u32[]{:S(2)}) %collective-permute-start.2) | collective-permute-done | bytes 131104 | tf_op jit(solution)/shard_map/ppermute | solution.py:20
  16.0 2.0 %collective-permute-start.3 = (bf16[2,128,64]{2,1,0:T(8,128)(2,1)S(1)}, bf16[2,128,64]{2,1,0:T(8,128)(2,1)S(1)}, u32[]{:S(2)}, u32[]{:S(2)}) collective-permute-start(bf16[2,128,64]{2,1,0:T(8,128)(2,1)S(1)} %get-tuple-element.42), channel_id=1, source_target_pairs={{3,0},{0,1},{1,2},{2,3},{7,4},{4,5},{5,6},{6,7},{11,8},{8,9},{9,10... | collective-permute-start | bytes 98312 | tf_op jit(solution)/shard_map/ppermute | solution.py:20
  18.0 2.2 %collective-permute-start.4 = (bf16[2,128,64]{2,1,0:T(8,128)(2,1)S(1)}, bf16[2,128,64]{2,1,0:T(8,128)(2,1)S(1)}, u32[]{:S(2)}, u32[]{:S(2)}) collective-permute-start(bf16[2,128,64]{2,1,0:T(8,128)(2,1)S(1)} %get-tuple-element.44), channel_id=1, source_target_pairs={{1,0},{2,1},{3,2},{0,3},{5,4},{6,5},{7,6},{4,7},{9,8},{10,9},{11,1... | collective-permute-start | bytes 98312 | tf_op jit(solution)/shard_map/ppermute | solution.py:20
  20.2 1.8 %collective-permute-start.5 = (bf16[2,128,64]{2,1,0:T(8,128)(2,1)S(1)}, bf16[2,128,64]{2,1,0:T(8,128)(2,1)S(1)}, u32[]{:S(2)}, u32[]{:S(2)}) collective-permute-start(bf16[2,128,64]{2,1,0:T(8,128)(2,1)S(1)} %get-tuple-element.43), channel_id=1, source_target_pairs={{2,0},{3,1},{0,2},{1,3},{6,4},{7,5},{4,6},{5,7},{10,8},{11,9},{8,1... | collective-permute-start | bytes 98312 | tf_op jit(solution)/shard_map/ppermute | solution.py:20
  22.6 3.4 %collective-permute-done.5 = bf16[2,128,64]{2,1,0:T(8,128)(2,1)S(1)} collective-permute-done((bf16[2,128,64]{2,1,0:T(8,128)(2,1)S(1)}, bf16[2,128,64]{2,1,0:T(8,128)(2,1)S(1)}, u32[]{:S(2)}, u32[]{:S(2)}) %collective-permute-start.5) | collective-permute-done | bytes 32800 | tf_op jit(solution)/shard_map/ppermute | solution.py:20
  28.0 6.3 %shard_map.76 = (f32[64,2752]{1,0:T(8,128)}, bf16[64,2752]{1,0:T(8,128)(2,1)}, bf16[64,2752]{1,0:T(8,128)(2,1)}, bf16[64,2752]{1,0:T(8,128)(2,1)}) custom-call(s32[4]{0:T(128)} %pad_add_fusion.where_ref._, bf16[2,128,64]{2,1,0:T(8,128)(2,1)} %copy-done.13, bf16[2,128,64]{2,1,0:T(8,128)(2,1)} %copy-done.23, bf16[2,128,22016]{2,1,0:T(8,128)(2,1)} %grads_ref.3, ...), custom_call_target="tpu_custom_call" | custom-call | flops 360710144 | bytes 8454144 | tf_op jit(solution)/shard_map/pallas_call | solution.py:106
  34.3 1.5 collective-permute-start.11
  35.8 2.7 %collective-permute-start.12 = (bf16[64,2752]{1,0:T(8,128)(2,1)}, bf16[64,2752]{1,0:T(8,128)(2,1)S(1)}, u32[]{:S(2)}, u32[]{:S(2)}) collective-permute-start(bf16[64,2752]{1,0:T(8,128)(2,1)} %get-tuple-element.28), channel_id=1, source_target_pairs={{64,0},{96,32},{0,64},{32,96},{65,1},{97,33},{1,65},{33,97},{66,2}... | collective-permute-start | bytes 1056776 | tf_op jit(solution)/shard_map/ppermute | solution.py:20
  38.5 1.4 collective-permute-start.13
  40.0 6.4 %shard_map.77 = (f32[64,2752]{1,0:T(8,128)}, bf16[64,2752]{1,0:T(8,128)(2,1)}, bf16[64,2752]{1,0:T(8,128)(2,1)}, bf16[64,2752]{1,0:T(8,128)(2,1)}) custom-call(s32[4]{0:T(128)} %pad_add_fusion.where_ref._, bf16[2,128,64]{2,1,0:T(8,128)(2,1)} %copy-done.13, bf16[2,128,64]{2,1,0:T(8,128)(2,1)} %copy-done.23, bf16[2,128,22016]{2,1,0:T(8,128)(2,1)} %grads_ref.3, ...), custom_call_target="tpu_custom_call" | custom-call | flops 360710144 | bytes 8454144 | tf_op jit(solution)/shard_map/pallas_call | solution.py:106
  46.4 2.0 %collective-permute-start.8 = (bf16[64,2752]{1,0:T(8,128)(2,1)}, bf16[64,2752]{1,0:T(8,128)(2,1)S(1)}, u32[]{:S(2)}, u32[]{:S(2)}) collective-permute-start(bf16[64,2752]{1,0:T(8,128)(2,1)} %get-tuple-element.24), channel_id=1, source_target_pairs={{96,0},{0,32},{32,64},{64,96},{97,1},{1,33},{33,65},{65,97},{98,2}... | collective-permute-start | bytes 1056776 | tf_op jit(solution)/shard_map/ppermute | solution.py:20
  49.1 6.5 %shard_map.78 = (bf16[2,512,1024]{2,1,0:T(8,128)(2,1)}, bf16[2,512,1024]{2,1,0:T(8,128)(2,1)}) custom-call(s32[4]{0:T(128)} %pad_add_fusion.where_ref._, bf16[2,512,1024]{2,1,0:T(8,128)(2,1)} %bases_ref.1, f32[64,2752]{1,0:T(8,128)} %get-tuple-element.22._.refs_0_), custom_call_target="tpu_custom_call" | custom-call | flops 4294967296 | bytes 6291456 | tf_op jit(solution)/shard_map/pallas_call | solution.py:67
  56.6 3.0 %shard_map.79 = (f32[2,64,2752]{2,1,0:T(8,128)}, f32[2,64,2752]{2,1,0:T(8,128)}, bf16[64,1408]{1,0:T(8,128)(2,1)}, bf16[64,1408]{1,0:T(8,128)(2,1)}) custom-call(f32[64,2752]{1,0:T(8,128)} %get-tuple-element.21._.refs_0_, bf16[64,2752]{1,0:T(8,128)(2,1)} %copy-done.17, bf16[64,2752]{1,0:T(8,128)(2,1)} %copy-done.18, bf16[64,2752]{1,0:T(8,128)(2,1)} %copy-done.19, ...), custom_call_target="tpu_custom_call" | custom-call | flops 5283840 | bytes 4579328 | tf_op jit(solution)/shard_map/pallas_call | solution.py:159
  59.7 1.9 %collective-permute-start.14 = (bf16[64,1408]{1,0:T(8,128)(2,1)}, bf16[64,1408]{1,0:T(8,128)(2,1)S(1)}, u32[]{:S(2)}, u32[]{:S(2)}) collective-permute-start(bf16[64,1408]{1,0:T(8,128)(2,1)} %get-tuple-element.33.refs_0_), channel_id=1, source_target_pairs={{4,0},{8,4},{12,8},{0,12},{5,1},{9,5},{13,9},{1,13},{6,2},{10,6},{... | collective-permute-start | bytes 540680 | tf_op jit(solution)/shard_map/ppermute | solution.py:20
  61.6 1.4 collective-permute-start.15
  64.5 3.9 %collective-permute-done.14.refs_1_ = bf16[64,1408]{1,0:T(8,128)(2,1)S(1)} collective-permute-done((bf16[64,1408]{1,0:T(8,128)(2,1)}, bf16[64,1408]{1,0:T(8,128)(2,1)S(1)}, u32[]{:S(2)}, u32[]{:S(2)}) %collective-permute-start.14) | collective-permute-done | bytes 180256 | tf_op jit(solution)/shard_map/ppermute | solution.py:20
  68.4 1.9 %collective-permute-start.34 = (bf16[64,1408]{1,0:T(8,128)(2,1)}, bf16[64,1408]{1,0:T(8,128)(2,1)S(1)}, u32[]{:S(2)}, u32[]{:S(2)}) collective-permute-start(bf16[64,1408]{1,0:T(8,128)(2,1)} %get-tuple-element.36.refs_0_), channel_id=1, source_target_pairs={{1,0},{2,1},{3,2},{0,3},{5,4},{6,5},{7,6},{4,7},{9,8},{10,9},{11,1... | collective-permute-start | bytes 540680 | tf_op jit(solution)/shard_map/ppermute | solution.py:20
  70.3 1.5 collective-permute-start.35
  72.9 2.1 %shard_map.80.refs_8_.refs_1_ = bf16[256,1408]{1,0:T(8,128)(2,1)} custom-call(bf16[64,1408]{1,0:T(8,128)(2,1)} %get-tuple-element.33.refs_0_, bf16[64,1408]{1,0:T(8,128)(2,1)} %copy-done.33, bf16[64,1408]{1,0:T(8,128)(2,1)} %copy-done.34, bf16[64,1408]{1,0:T(8,128)(2,1)} %copy-done.35), custom_call_target="tpu_custom_call" | custom-call | bytes 1441792 | tf_op jit(solution)/shard_map/pallas_call | solution.py:179
  75.9 3.1 %shard_map.81 = (f32[2,64,2752]{2,1,0:T(8,128)}, f32[2,64,2752]{2,1,0:T(8,128)}, bf16[64,1408]{1,0:T(8,128)(2,1)}, bf16[64,1408]{1,0:T(8,128)(2,1)}) custom-call(f32[64,2752]{1,0:T(8,128)} %get-tuple-element.22._.refs_0_, bf16[64,2752]{1,0:T(8,128)(2,1)} %copy-done.15, bf16[64,2752]{1,0:T(8,128)(2,1)} %copy-done.16, ...), custom_call_target="tpu_custom_call", output_to_operand_aliasing={{0}: (6, {}), {1}: (7, {})} | custom-call | flops 5283840 | bytes 4579328 | tf_op jit(solution)/shard_map/pallas_call | solution.py:159
  79.0 2.3 %collective-permute-start.24 = (bf16[64,1408]{1,0:T(8,128)(2,1)}, bf16[64,1408]{1,0:T(8,128)(2,1)S(1)}, u32[]{:S(2)}, u32[]{:S(2)}) collective-permute-start(bf16[64,1408]{1,0:T(8,128)(2,1)} %get-tuple-element.35.refs_0_), channel_id=1, source_target_pairs={{1,0},{2,1},{3,2},{0,3},{5,4},{6,5},{7,6},{4,7},{9,8},{10,9},{11,1... | collective-permute-start | bytes 540680 | tf_op jit(solution)/shard_map/ppermute | solution.py:20
  83.0 2.8 %collective-permute-start.17 = (bf16[64,1408]{1,0:T(8,128)(2,1)}, bf16[64,1408]{1,0:T(8,128)(2,1)S(1)}, u32[]{:S(2)}, u32[]{:S(2)}) collective-permute-start(bf16[64,1408]{1,0:T(8,128)(2,1)} %get-tuple-element.34.refs_0_), channel_id=1, source_target_pairs={{4,0},{8,4},{12,8},{0,12},{5,1},{9,5},{13,9},{1,13},{6,2},{10,6},{... | collective-permute-start | bytes 540680 | tf_op jit(solution)/shard_map/ppermute | solution.py:20
  86.1 1.7 %collective-permute-done.24.refs_1_ = bf16[64,1408]{1,0:T(8,128)(2,1)S(1)} collective-permute-done((bf16[64,1408]{1,0:T(8,128)(2,1)}, bf16[64,1408]{1,0:T(8,128)(2,1)S(1)}, u32[]{:S(2)}, u32[]{:S(2)}) %collective-permute-start.24) | collective-permute-done | bytes 180256 | tf_op jit(solution)/shard_map/ppermute | solution.py:20
  87.8 2.2 %shard_map.84.refs_6_ = bf16[256,1408]{1,0:T(8,128)(2,1)} custom-call(bf16[64,1408]{1,0:T(8,128)(2,1)} %get-tuple-element.36.refs_0_, bf16[64,1408]{1,0:T(8,128)(2,1)} %copy-done.24, bf16[64,1408]{1,0:T(8,128)(2,1)} %copy-done.25, bf16[64,1408]{1,0:T(8,128)(2,1)} %copy-done.26), custom_call_target="tpu_custom_call" | custom-call | bytes 1441792 | tf_op jit(solution)/shard_map/pallas_call | solution.py:179
  90.0 3.2 %collective-permute-start.37 = (bf16[256,1408]{1,0:T(8,128)(2,1)}, bf16[256,1408]{1,0:T(8,128)(2,1)S(1)}, u32[]{:S(2)}, u32[]{:S(2)}) collective-permute-start(bf16[256,1408]{1,0:T(8,128)(2,1)} %shard_map.84.refs_6_), channel_id=1, source_target_pairs={{4,0},{8,4},{12,8},{0,12},{5,1},{9,5},{13,9},{1,13},{6,2},{10,6},{... | collective-permute-start | bytes 2162696 | tf_op jit(solution)/shard_map/ppermute | solution.py:20
  93.3 3.6 %collective-permute-start.31 = (bf16[256,1408]{1,0:T(8,128)(2,1)S(1)}, bf16[256,1408]{1,0:T(8,128)(2,1)S(1)}, u32[]{:S(2)}, u32[]{:S(2)}) collective-permute-start(bf16[256,1408]{1,0:T(8,128)(2,1)S(1)} %copy-done.1), channel_id=1, source_target_pairs={{1,0},{2,1},{3,2},{0,3},{5,4},{6,5},{7,6},{4,7},{9,8},{10,9},{11,1... | collective-permute-start | bytes 2162696 | tf_op jit(solution)/shard_map/ppermute | solution.py:20
  96.9 2.1 %shard_map.83.refs_7_ = bf16[256,1408]{1,0:T(8,128)(2,1)} custom-call(bf16[64,1408]{1,0:T(8,128)(2,1)} %get-tuple-element.35.refs_0_, bf16[64,1408]{1,0:T(8,128)(2,1)} %copy-done.28, bf16[64,1408]{1,0:T(8,128)(2,1)} %copy-done.30, bf16[64,1408]{1,0:T(8,128)(2,1)} %copy-done.32), custom_call_target="tpu_custom_call" | custom-call | bytes 1441792 | tf_op jit(solution)/shard_map/pallas_call | solution.py:179
  99.1 2.0 %collective-permute-start.29 = (bf16[256,1408]{1,0:T(8,128)(2,1)}, bf16[256,1408]{1,0:T(8,128)(2,1)S(1)}, u32[]{:S(2)}, u32[]{:S(2)}) collective-permute-start(bf16[256,1408]{1,0:T(8,128)(2,1)} %shard_map.83.refs_7_), channel_id=1, source_target_pairs={{12,0},{0,4},{4,8},{8,12},{13,1},{1,5},{5,9},{9,13},{14,2},{2,6},{... | collective-permute-start | bytes 2162696 | tf_op jit(solution)/shard_map/ppermute | solution.py:20
  101.7 2.1 %shard_map.82.refs_1_ = bf16[256,1408]{1,0:T(8,128)(2,1)} custom-call(bf16[64,1408]{1,0:T(8,128)(2,1)} %get-tuple-element.34.refs_0_, bf16[64,1408]{1,0:T(8,128)(2,1)} %copy-done.27, bf16[64,1408]{1,0:T(8,128)(2,1)} %copy-done.29, bf16[64,1408]{1,0:T(8,128)(2,1)} %copy-done.31), custom_call_target="tpu_custom_call" | custom-call | bytes 1441792 | tf_op jit(solution)/shard_map/pallas_call | solution.py:179
  104.4 5.7 %collective-permute-done.37.refs_7_ = bf16[256,1408]{1,0:T(8,128)(2,1)S(1)} collective-permute-done((bf16[256,1408]{1,0:T(8,128)(2,1)}, bf16[256,1408]{1,0:T(8,128)(2,1)S(1)}, u32[]{:S(2)}, u32[]{:S(2)}) %collective-permute-start.37) | collective-permute-done | bytes 720928 | tf_op jit(solution)/shard_map/ppermute | solution.py:20
  111.4 2.1 %collective-permute-done.31.refs_2_ = bf16[256,1408]{1,0:T(8,128)(2,1)S(1)} collective-permute-done((bf16[256,1408]{1,0:T(8,128)(2,1)S(1)}, bf16[256,1408]{1,0:T(8,128)(2,1)S(1)}, u32[]{:S(2)}, u32[]{:S(2)}) %collective-permute-start.31) | collective-permute-done | bytes 720928 | tf_op jit(solution)/shard_map/ppermute | solution.py:20
  113.5 8.4 %collective-permute-done.27.refs_8_ = bf16[256,1408]{1,0:T(8,128)(2,1)S(1)} collective-permute-done((bf16[256,1408]{1,0:T(8,128)(2,1)}, bf16[256,1408]{1,0:T(8,128)(2,1)S(1)}, u32[]{:S(2)}, u32[]{:S(2)}) %collective-permute-start.27) | collective-permute-done | bytes 720928 | tf_op jit(solution)/shard_map/ppermute | solution.py:20
  121.9 1.9 %collective-permute-start.33 = (bf16[256,1408]{1,0:T(8,128)(2,1)S(1)}, bf16[256,1408]{1,0:T(8,128)(2,1)S(1)}, u32[]{:S(2)}, u32[]{:S(2)}) collective-permute-start(bf16[256,1408]{1,0:T(8,128)(2,1)S(1)} %copy-done.1), channel_id=1, source_target_pairs={{3,0},{0,1},{1,2},{2,3},{7,4},{4,5},{5,6},{6,7},{11,8},{8,9},{9,10... | collective-permute-start | bytes 2162696 | tf_op jit(solution)/shard_map/ppermute | solution.py:20
  123.7 3.1 %collective-permute-start.38 = (bf16[256,1408]{1,0:T(8,128)(2,1)S(1)}, bf16[256,1408]{1,0:T(8,128)(2,1)S(1)}, u32[]{:S(2)}, u32[]{:S(2)}) collective-permute-start(bf16[256,1408]{1,0:T(8,128)(2,1)S(1)} %collective-permute-done.37.refs_7_), channel_id=1, source_target_pairs={{4,0},{8,4},{12,8},{0,12},{5,1},{9,5},{13,9},{1,13},{6,2},{10,6},{... | collective-permute-start | bytes 2162696 | tf_op jit(solution)/shard_map/ppermute | solution.py:20
  126.8 1.9 %collective-permute-start.32 = (bf16[256,1408]{1,0:T(8,128)(2,1)S(1)}, bf16[256,1408]{1,0:T(8,128)(2,1)S(1)}, u32[]{:S(2)}, u32[]{:S(2)}) collective-permute-start(bf16[256,1408]{1,0:T(8,128)(2,1)S(1)} %collective-permute-done.31.refs_2_), channel_id=1, source_target_pairs={{1,0},{2,1},{3,2},{0,3},{5,4},{6,5},{7,6},{4,7},{9,8},{10,9},{11,1... | collective-permute-start | bytes 2162696 | tf_op jit(solution)/shard_map/ppermute | solution.py:20
  131.3 1.9 %collective-permute-start.30 = (bf16[128,1408]{1,0:T(8,128)(2,1)}, bf16[128,1408]{1,0:T(8,128)(2,1)S(1)}, u32[]{:S(2)}, u32[]{:S(2)}) collective-permute-start(bf16[128,1408]{1,0:T(8,128)(2,1)} %slice.59), channel_id=1, source_target_pairs={{12,0},{0,4},{4,8},{8,12},{13,1},{1,5},{5,9},{9,13},{14,2},{2,6},{... | collective-permute-start | bytes 1081352 | tf_op jit(solution)/shard_map/ppermute | solution.py:20
  133.2 5.5 %collective-permute-done.33.refs_4_ = bf16[256,1408]{1,0:T(8,128)(2,1)S(1)} collective-permute-done((bf16[256,1408]{1,0:T(8,128)(2,1)S(1)}, bf16[256,1408]{1,0:T(8,128)(2,1)S(1)}, u32[]{:S(2)}, u32[]{:S(2)}) %collective-permute-start.33) | collective-permute-done | bytes 720928 | tf_op jit(solution)/shard_map/ppermute | solution.py:20
  138.7 2.1 %collective-permute-start.21 = (bf16[128,1408]{1,0:T(8,128)(2,1)S(1)}, bf16[128,1408]{1,0:T(8,128)(2,1)S(1)}, u32[]{:S(2)}, u32[]{:S(2)}) collective-permute-start(bf16[128,1408]{1,0:T(8,128)(2,1)S(1)} %slice.56), channel_id=1, source_target_pairs={{1,0},{2,1},{3,2},{0,3},{5,4},{6,5},{7,6},{4,7},{9,8},{10,9},{11,1... | collective-permute-start | bytes 1081352 | tf_op jit(solution)/shard_map/ppermute | solution.py:20
  140.8 2.6 %collective-permute-done.38.refs_8_ = bf16[256,1408]{1,0:T(8,128)(2,1)S(1)} collective-permute-done((bf16[256,1408]{1,0:T(8,128)(2,1)S(1)}, bf16[256,1408]{1,0:T(8,128)(2,1)S(1)}, u32[]{:S(2)}, u32[]{:S(2)}) %collective-permute-start.38) | collective-permute-done | bytes 720928 | tf_op jit(solution)/shard_map/ppermute | solution.py:20
  144.1 1.7 %collective-permute-done.32.refs_3_ = bf16[256,1408]{1,0:T(8,128)(2,1)S(1)} collective-permute-done((bf16[256,1408]{1,0:T(8,128)(2,1)S(1)}, bf16[256,1408]{1,0:T(8,128)(2,1)S(1)}, u32[]{:S(2)}, u32[]{:S(2)}) %collective-permute-start.32) | collective-permute-done | bytes 720928 | tf_op jit(solution)/shard_map/ppermute | solution.py:20
  146.7 6.7 %shard_map.85.refs_12_ = bf16[2,2752,512]{2,1,0:T(8,128)(2,1)} custom-call(bf16[2,512,1024]{2,1,0:T(8,128)(2,1)} %get-tuple-element.23.refs_0_, bf16[256,1408]{1,0:T(8,128)(2,1)} %shard_map.80.refs_8_.refs_1_, bf16[256,1408]{1,0:T(8,128)(2,1)} %copy-done.8, bf16[256,1408]{1,0:T(8,128)(2,1)} %copy-done.12, bf16[256,1408]{1,0:T(8,128)(2,1)} %copy-done.10, ...), custom_call_target="tpu_custom_call" | custom-call | flops 2952790016 | bytes 10747904 | tf_op jit(solution)/shard_map/pallas_call | solution.py:235
  155.1 6.7 %shard_map.86 = bf16[2,2752,512]{2,1,0:T(8,128)(2,1)} custom-call(bf16[2,512,1024]{2,1,0:T(8,128)(2,1)} %get-tuple-element.23.refs_0_, bf16[256,1408]{1,0:T(8,128)(2,1)} %shard_map.82.refs_1_, bf16[256,1408]{1,0:T(8,128)(2,1)} %copy-done.5, bf16[128,1408]{1,0:T(8,128)(2,1)} %copy-done.21, ...), custom_call_target="tpu_custom_call", output_to_operand_aliasing={{}: (12, {})} | custom-call | flops 2952790016 | bytes 10747904 | tf_op jit(solution)/shard_map/pallas_call | solution.py:235
  (126 shorter events, 19.9 us)
Async XLA Ops:
  0.6 26.7 %collective-permute-start.7 = (bf16[2,128,22016]{2,1,0:T(8,128)(2,1)}, bf16[2,128,22016]{2,1,0:T(8,128)(2,1)}, u32[]{:S(2)}, u32[]{:S(2)}) collective-permute-start(bf16[2,128,22016]{2,1,0:T(8,128)(2,1)} %grads_ref.3), channel_id=1, source_target_pairs={{0,16},{16,0},{1,17},{17,1},{2,18},{18,2},{3,19},{19,3},{4,20},{20... | collective-permute-start | bytes 33816584 | tf_op jit(solution)/shard_map/ppermute | solution.py:28
  5.2 6.7 %collective-permute-start = (bf16[2,128,256]{2,1,0:T(8,128)(2,1)S(1)}, bf16[2,128,256]{2,1,0:T(8,128)(2,1)S(1)}, u32[]{:S(2)}, u32[]{:S(2)}) collective-permute-start(bf16[2,128,256]{2,1,0:T(8,128)(2,1)S(1)} %get-tuple-element.39), channel_id=1, source_target_pairs={{12,0},{0,4},{4,8},{8,12},{13,1},{1,5},{5,9},{9,13},{14,2},{2,6},{... | collective-permute-start | bytes 393224 | tf_op jit(solution)/shard_map/ppermute | solution.py:20
  6.9 7.1 %collective-permute-start.1 = (bf16[2,128,256]{2,1,0:T(8,128)(2,1)S(1)}, bf16[2,128,256]{2,1,0:T(8,128)(2,1)S(1)}, u32[]{:S(2)}, u32[]{:S(2)}) collective-permute-start(bf16[2,128,256]{2,1,0:T(8,128)(2,1)S(1)} %get-tuple-element.41), channel_id=1, source_target_pairs={{4,0},{8,4},{12,8},{0,12},{5,1},{9,5},{13,9},{1,13},{6,2},{10,6},{... | collective-permute-start | bytes 393224 | tf_op jit(solution)/shard_map/ppermute | solution.py:20
  8.5 7.3 %collective-permute-start.2 = (bf16[2,128,256]{2,1,0:T(8,128)(2,1)S(1)}, bf16[2,128,256]{2,1,0:T(8,128)(2,1)S(1)}, u32[]{:S(2)}, u32[]{:S(2)}) collective-permute-start(bf16[2,128,256]{2,1,0:T(8,128)(2,1)S(1)} %get-tuple-element.40), channel_id=1, source_target_pairs={{8,0},{12,4},{0,8},{4,12},{9,1},{13,5},{1,9},{5,13},{10,2},{14,6},... | collective-permute-start | bytes 393224 | tf_op jit(solution)/shard_map/ppermute | solution.py:20
  16.0 6.3 %collective-permute-start.3 = (bf16[2,128,64]{2,1,0:T(8,128)(2,1)S(1)}, bf16[2,128,64]{2,1,0:T(8,128)(2,1)S(1)}, u32[]{:S(2)}, u32[]{:S(2)}) collective-permute-start(bf16[2,128,64]{2,1,0:T(8,128)(2,1)S(1)} %get-tuple-element.42), channel_id=1, source_target_pairs={{3,0},{0,1},{1,2},{2,3},{7,4},{4,5},{5,6},{6,7},{11,8},{8,9},{9,10... | collective-permute-start | bytes 98312 | tf_op jit(solution)/shard_map/ppermute | solution.py:20
  18.0 4.6 %collective-permute-start.4 = (bf16[2,128,64]{2,1,0:T(8,128)(2,1)S(1)}, bf16[2,128,64]{2,1,0:T(8,128)(2,1)S(1)}, u32[]{:S(2)}, u32[]{:S(2)}) collective-permute-start(bf16[2,128,64]{2,1,0:T(8,128)(2,1)S(1)} %get-tuple-element.44), channel_id=1, source_target_pairs={{1,0},{2,1},{3,2},{0,3},{5,4},{6,5},{7,6},{4,7},{9,8},{10,9},{11,1... | collective-permute-start | bytes 98312 | tf_op jit(solution)/shard_map/ppermute | solution.py:20
  20.2 5.8 %collective-permute-start.5 = (bf16[2,128,64]{2,1,0:T(8,128)(2,1)S(1)}, bf16[2,128,64]{2,1,0:T(8,128)(2,1)S(1)}, u32[]{:S(2)}, u32[]{:S(2)}) collective-permute-start(bf16[2,128,64]{2,1,0:T(8,128)(2,1)S(1)} %get-tuple-element.43), channel_id=1, source_target_pairs={{2,0},{3,1},{0,2},{1,3},{6,4},{7,5},{4,6},{5,7},{10,8},{11,9},{8,1... | collective-permute-start | bytes 98312 | tf_op jit(solution)/shard_map/ppermute | solution.py:20
  26.0 1.3 collective-permute-start.6
  34.3 14.1 %collective-permute-start.11 = (bf16[64,2752]{1,0:T(8,128)(2,1)}, bf16[64,2752]{1,0:T(8,128)(2,1)S(1)}, u32[]{:S(2)}, u32[]{:S(2)}) collective-permute-start(bf16[64,2752]{1,0:T(8,128)(2,1)} %get-tuple-element.27), channel_id=1, source_target_pairs={{96,0},{0,32},{32,64},{64,96},{97,1},{1,33},{33,65},{65,97},{98,2}... | collective-permute-start | bytes 1056776 | tf_op jit(solution)/shard_map/ppermute | solution.py:20
  35.8 19.9 %collective-permute-start.12 = (bf16[64,2752]{1,0:T(8,128)(2,1)}, bf16[64,2752]{1,0:T(8,128)(2,1)S(1)}, u32[]{:S(2)}, u32[]{:S(2)}) collective-permute-start(bf16[64,2752]{1,0:T(8,128)(2,1)} %get-tuple-element.28), channel_id=1, source_target_pairs={{64,0},{96,32},{0,64},{32,96},{65,1},{97,33},{1,65},{33,97},{66,2}... | collective-permute-start | bytes 1056776 | tf_op jit(solution)/shard_map/ppermute | solution.py:20
  38.5 17.2 %collective-permute-start.13 = (bf16[64,2752]{1,0:T(8,128)(2,1)}, bf16[64,2752]{1,0:T(8,128)(2,1)S(1)}, u32[]{:S(2)}, u32[]{:S(2)}) collective-permute-start(bf16[64,2752]{1,0:T(8,128)(2,1)} %get-tuple-element.29), channel_id=1, source_target_pairs={{32,0},{64,32},{96,64},{0,96},{33,1},{65,33},{97,65},{1,97},{34,2}... | collective-permute-start | bytes 1056776 | tf_op jit(solution)/shard_map/ppermute | solution.py:20
  46.4 17.0 %collective-permute-start.10 = (bf16[64,2752]{1,0:T(8,128)(2,1)}, bf16[64,2752]{1,0:T(8,128)(2,1)S(1)}, u32[]{:S(2)}, u32[]{:S(2)}) collective-permute-start(bf16[64,2752]{1,0:T(8,128)(2,1)} %get-tuple-element.26), channel_id=1, source_target_pairs={{32,0},{64,32},{96,64},{0,96},{33,1},{65,33},{97,65},{1,97},{34,2}... | collective-permute-start | bytes 1056776 | tf_op jit(solution)/shard_map/ppermute | solution.py:20
  46.4 28.7 %collective-permute-start.8 = (bf16[64,2752]{1,0:T(8,128)(2,1)}, bf16[64,2752]{1,0:T(8,128)(2,1)S(1)}, u32[]{:S(2)}, u32[]{:S(2)}) collective-permute-start(bf16[64,2752]{1,0:T(8,128)(2,1)} %get-tuple-element.24), channel_id=1, source_target_pairs={{96,0},{0,32},{32,64},{64,96},{97,1},{1,33},{33,65},{65,97},{98,2}... | collective-permute-start | bytes 1056776 | tf_op jit(solution)/shard_map/ppermute | solution.py:20
  48.4 26.7 %collective-permute-start.9 = (bf16[64,2752]{1,0:T(8,128)(2,1)}, bf16[64,2752]{1,0:T(8,128)(2,1)S(1)}, u32[]{:S(2)}, u32[]{:S(2)}) collective-permute-start(bf16[64,2752]{1,0:T(8,128)(2,1)} %get-tuple-element.25), channel_id=1, source_target_pairs={{64,0},{96,32},{0,64},{32,96},{65,1},{97,33},{1,65},{33,97},{66,2}... | collective-permute-start | bytes 1056776 | tf_op jit(solution)/shard_map/ppermute | solution.py:20
  59.7 8.7 %collective-permute-start.14 = (bf16[64,1408]{1,0:T(8,128)(2,1)}, bf16[64,1408]{1,0:T(8,128)(2,1)S(1)}, u32[]{:S(2)}, u32[]{:S(2)}) collective-permute-start(bf16[64,1408]{1,0:T(8,128)(2,1)} %get-tuple-element.33.refs_0_), channel_id=1, source_target_pairs={{4,0},{8,4},{12,8},{0,12},{5,1},{9,5},{13,9},{1,13},{6,2},{10,6},{... | collective-permute-start | bytes 540680 | tf_op jit(solution)/shard_map/ppermute | solution.py:20
  61.6 8.8 %collective-permute-start.15 = (bf16[64,1408]{1,0:T(8,128)(2,1)}, bf16[64,1408]{1,0:T(8,128)(2,1)S(1)}, u32[]{:S(2)}, u32[]{:S(2)}) collective-permute-start(bf16[64,1408]{1,0:T(8,128)(2,1)} %get-tuple-element.33.refs_0_), channel_id=1, source_target_pairs={{8,0},{12,4},{0,8},{4,12},{9,1},{13,5},{1,9},{5,13},{10,2},{14,6},... | collective-permute-start | bytes 540680 | tf_op jit(solution)/shard_map/ppermute | solution.py:20
  63.4 8.6 %collective-permute-start.16 = (bf16[64,1408]{1,0:T(8,128)(2,1)}, bf16[64,1408]{1,0:T(8,128)(2,1)S(1)}, u32[]{:S(2)}, u32[]{:S(2)}) collective-permute-start(bf16[64,1408]{1,0:T(8,128)(2,1)} %get-tuple-element.33.refs_0_), channel_id=1, source_target_pairs={{12,0},{0,4},{4,8},{8,12},{13,1},{1,5},{5,9},{9,13},{14,2},{2,6},{... | collective-permute-start | bytes 540680 | tf_op jit(solution)/shard_map/ppermute | solution.py:20
  68.4 13.7 %collective-permute-start.34 = (bf16[64,1408]{1,0:T(8,128)(2,1)}, bf16[64,1408]{1,0:T(8,128)(2,1)S(1)}, u32[]{:S(2)}, u32[]{:S(2)}) collective-permute-start(bf16[64,1408]{1,0:T(8,128)(2,1)} %get-tuple-element.36.refs_0_), channel_id=1, source_target_pairs={{1,0},{2,1},{3,2},{0,3},{5,4},{6,5},{7,6},{4,7},{9,8},{10,9},{11,1... | collective-permute-start | bytes 540680 | tf_op jit(solution)/shard_map/ppermute | solution.py:20
  70.3 12.6 %collective-permute-start.35 = (bf16[64,1408]{1,0:T(8,128)(2,1)}, bf16[64,1408]{1,0:T(8,128)(2,1)S(1)}, u32[]{:S(2)}, u32[]{:S(2)}) collective-permute-start(bf16[64,1408]{1,0:T(8,128)(2,1)} %get-tuple-element.36.refs_0_), channel_id=1, source_target_pairs={{2,0},{3,1},{0,2},{1,3},{6,4},{7,5},{4,6},{5,7},{10,8},{11,9},{8,1... | collective-permute-start | bytes 540680 | tf_op jit(solution)/shard_map/ppermute | solution.py:20
  72.0 13.8 %collective-permute-start.36 = (bf16[64,1408]{1,0:T(8,128)(2,1)}, bf16[64,1408]{1,0:T(8,128)(2,1)S(1)}, u32[]{:S(2)}, u32[]{:S(2)}) collective-permute-start(bf16[64,1408]{1,0:T(8,128)(2,1)} %get-tuple-element.36.refs_0_), channel_id=1, source_target_pairs={{3,0},{0,1},{1,2},{2,3},{7,4},{4,5},{5,6},{6,7},{11,8},{8,9},{9,10... | collective-permute-start | bytes 540680 | tf_op jit(solution)/shard_map/ppermute | solution.py:20
  75.9 17.4 %copy-start.1 = (bf16[256,1408]{1,0:T(8,128)(2,1)S(1)}, bf16[256,1408]{1,0:T(8,128)(2,1)}, u32[]{:S(2)}) copy-start(bf16[256,1408]{1,0:T(8,128)(2,1)} %shard_map.80.refs_8_.refs_1_) | copy-start | bytes 2162692
  79.0 8.8 %collective-permute-start.24 = (bf16[64,1408]{1,0:T(8,128)(2,1)}, bf16[64,1408]{1,0:T(8,128)(2,1)S(1)}, u32[]{:S(2)}, u32[]{:S(2)}) collective-permute-start(bf16[64,1408]{1,0:T(8,128)(2,1)} %get-tuple-element.35.refs_0_), channel_id=1, source_target_pairs={{1,0},{2,1},{3,2},{0,3},{5,4},{6,5},{7,6},{4,7},{9,8},{10,9},{11,1... | collective-permute-start | bytes 540680 | tf_op jit(solution)/shard_map/ppermute | solution.py:20
  81.3 8.7 %collective-permute-start.25 = (bf16[64,1408]{1,0:T(8,128)(2,1)}, bf16[64,1408]{1,0:T(8,128)(2,1)S(1)}, u32[]{:S(2)}, u32[]{:S(2)}) collective-permute-start(bf16[64,1408]{1,0:T(8,128)(2,1)} %get-tuple-element.35.refs_0_), channel_id=1, source_target_pairs={{2,0},{3,1},{0,2},{1,3},{6,4},{7,5},{4,6},{5,7},{10,8},{11,9},{8,1... | collective-permute-start | bytes 540680 | tf_op jit(solution)/shard_map/ppermute | solution.py:20
  82.1 11.2 %collective-permute-start.26 = (bf16[64,1408]{1,0:T(8,128)(2,1)}, bf16[64,1408]{1,0:T(8,128)(2,1)S(1)}, u32[]{:S(2)}, u32[]{:S(2)}) collective-permute-start(bf16[64,1408]{1,0:T(8,128)(2,1)} %get-tuple-element.35.refs_0_), channel_id=1, source_target_pairs={{3,0},{0,1},{1,2},{2,3},{7,4},{4,5},{5,6},{6,7},{11,8},{8,9},{9,10... | collective-permute-start | bytes 540680 | tf_op jit(solution)/shard_map/ppermute | solution.py:20
  83.0 16.1 %collective-permute-start.17 = (bf16[64,1408]{1,0:T(8,128)(2,1)}, bf16[64,1408]{1,0:T(8,128)(2,1)S(1)}, u32[]{:S(2)}, u32[]{:S(2)}) collective-permute-start(bf16[64,1408]{1,0:T(8,128)(2,1)} %get-tuple-element.34.refs_0_), channel_id=1, source_target_pairs={{4,0},{8,4},{12,8},{0,12},{5,1},{9,5},{13,9},{1,13},{6,2},{10,6},{... | collective-permute-start | bytes 540680 | tf_op jit(solution)/shard_map/ppermute | solution.py:20
  85.7 13.4 %collective-permute-start.18 = (bf16[64,1408]{1,0:T(8,128)(2,1)}, bf16[64,1408]{1,0:T(8,128)(2,1)S(1)}, u32[]{:S(2)}, u32[]{:S(2)}) collective-permute-start(bf16[64,1408]{1,0:T(8,128)(2,1)} %get-tuple-element.34.refs_0_), channel_id=1, source_target_pairs={{8,0},{12,4},{0,8},{4,12},{9,1},{13,5},{1,9},{5,13},{10,2},{14,6},... | collective-permute-start | bytes 540680 | tf_op jit(solution)/shard_map/ppermute | solution.py:20
  87.8 13.2 %collective-permute-start.19 = (bf16[64,1408]{1,0:T(8,128)(2,1)}, bf16[64,1408]{1,0:T(8,128)(2,1)S(1)}, u32[]{:S(2)}, u32[]{:S(2)}) collective-permute-start(bf16[64,1408]{1,0:T(8,128)(2,1)} %get-tuple-element.34.refs_0_), channel_id=1, source_target_pairs={{12,0},{0,4},{4,8},{8,12},{13,1},{1,5},{5,9},{9,13},{14,2},{2,6},{... | collective-permute-start | bytes 540680 | tf_op jit(solution)/shard_map/ppermute | solution.py:20
  90.0 23.5 %copy-start.2 = (bf16[256,1408]{1,0:T(8,128)(2,1)S(1)}, bf16[256,1408]{1,0:T(8,128)(2,1)}, u32[]{:S(2)}) copy-start(bf16[256,1408]{1,0:T(8,128)(2,1)} %shard_map.84.refs_6_) | copy-start | bytes 2162692
  90.0 20.2 %collective-permute-start.37 = (bf16[256,1408]{1,0:T(8,128)(2,1)}, bf16[256,1408]{1,0:T(8,128)(2,1)S(1)}, u32[]{:S(2)}, u32[]{:S(2)}) collective-permute-start(bf16[256,1408]{1,0:T(8,128)(2,1)} %shard_map.84.refs_6_), channel_id=1, source_target_pairs={{4,0},{8,4},{12,8},{0,12},{5,1},{9,5},{13,9},{1,13},{6,2},{10,6},{... | collective-permute-start | bytes 2162696 | tf_op jit(solution)/shard_map/ppermute | solution.py:20
  93.3 20.2 %collective-permute-start.31 = (bf16[256,1408]{1,0:T(8,128)(2,1)S(1)}, bf16[256,1408]{1,0:T(8,128)(2,1)S(1)}, u32[]{:S(2)}, u32[]{:S(2)}) collective-permute-start(bf16[256,1408]{1,0:T(8,128)(2,1)S(1)} %copy-done.1), channel_id=1, source_target_pairs={{1,0},{2,1},{3,2},{0,3},{5,4},{6,5},{7,6},{4,7},{9,8},{10,9},{11,1... | collective-permute-start | bytes 2162696 | tf_op jit(solution)/shard_map/ppermute | solution.py:20
  99.0 22.8 %collective-permute-start.27 = (bf16[256,1408]{1,0:T(8,128)(2,1)}, bf16[256,1408]{1,0:T(8,128)(2,1)S(1)}, u32[]{:S(2)}, u32[]{:S(2)}) collective-permute-start(bf16[256,1408]{1,0:T(8,128)(2,1)} %shard_map.83.refs_7_), channel_id=1, source_target_pairs={{4,0},{8,4},{12,8},{0,12},{5,1},{9,5},{13,9},{1,13},{6,2},{10,6},{... | collective-permute-start | bytes 2162696 | tf_op jit(solution)/shard_map/ppermute | solution.py:20
  99.1 24.6 %collective-permute-start.29 = (bf16[256,1408]{1,0:T(8,128)(2,1)}, bf16[256,1408]{1,0:T(8,128)(2,1)S(1)}, u32[]{:S(2)}, u32[]{:S(2)}) collective-permute-start(bf16[256,1408]{1,0:T(8,128)(2,1)} %shard_map.83.refs_7_), channel_id=1, source_target_pairs={{12,0},{0,4},{4,8},{8,12},{13,1},{1,5},{5,9},{9,13},{14,2},{2,6},{... | collective-permute-start | bytes 2162696 | tf_op jit(solution)/shard_map/ppermute | solution.py:20
  103.8 23.0 %collective-permute-start.20 = (bf16[256,1408]{1,0:T(8,128)(2,1)}, bf16[256,1408]{1,0:T(8,128)(2,1)S(1)}, u32[]{:S(2)}, u32[]{:S(2)}) collective-permute-start(bf16[256,1408]{1,0:T(8,128)(2,1)} %shard_map.82.refs_1_), channel_id=1, source_target_pairs={{1,0},{2,1},{3,2},{0,3},{5,4},{6,5},{7,6},{4,7},{9,8},{10,9},{11,1... | collective-permute-start | bytes 2162696 | tf_op jit(solution)/shard_map/ppermute | solution.py:20
  110.2 36.5 %copy-start.7 = (bf16[256,1408]{1,0:T(8,128)(2,1)}, bf16[256,1408]{1,0:T(8,128)(2,1)S(1)}, u32[]{:S(2)}) copy-start(bf16[256,1408]{1,0:T(8,128)(2,1)S(1)} %collective-permute-done.37.refs_7_) | copy-start | bytes 2162692
  110.2 20.1 %collective-permute-start.22 = (bf16[256,1408]{1,0:T(8,128)(2,1)}, bf16[256,1408]{1,0:T(8,128)(2,1)S(1)}, u32[]{:S(2)}, u32[]{:S(2)}) collective-permute-start(bf16[256,1408]{1,0:T(8,128)(2,1)} %shard_map.82.refs_1_), channel_id=1, source_target_pairs={{3,0},{0,1},{1,2},{2,3},{7,4},{4,5},{5,6},{6,7},{11,8},{8,9},{9,10... | collective-permute-start | bytes 2162696 | tf_op jit(solution)/shard_map/ppermute | solution.py:20
  113.5 33.2 %copy-start.8 = (bf16[256,1408]{1,0:T(8,128)(2,1)}, bf16[256,1408]{1,0:T(8,128)(2,1)S(1)}, u32[]{:S(2)}) copy-start(bf16[256,1408]{1,0:T(8,128)(2,1)S(1)} %collective-permute-done.31.refs_2_) | copy-start | bytes 2162692
  113.5 17.8 %collective-permute-start.39 = (bf16[256,1408]{1,0:T(8,128)(2,1)S(1)}, bf16[256,1408]{1,0:T(8,128)(2,1)S(1)}, u32[]{:S(2)}, u32[]{:S(2)}) collective-permute-start(bf16[256,1408]{1,0:T(8,128)(2,1)S(1)} %copy-done.2), channel_id=1, source_target_pairs={{12,0},{0,4},{4,8},{8,12},{13,1},{1,5},{5,9},{9,13},{14,2},{2,6},{... | collective-permute-start | bytes 2162696 | tf_op jit(solution)/shard_map/ppermute | solution.py:20
  121.9 31.5 %copy-start.3 = (bf16[256,1408]{1,0:T(8,128)(2,1)}, bf16[256,1408]{1,0:T(8,128)(2,1)S(1)}, u32[]{:S(2)}) copy-start(bf16[256,1408]{1,0:T(8,128)(2,1)S(1)} %collective-permute-done.27.refs_8_) | copy-start | bytes 2162692
  121.9 16.8 %collective-permute-start.33 = (bf16[256,1408]{1,0:T(8,128)(2,1)S(1)}, bf16[256,1408]{1,0:T(8,128)(2,1)S(1)}, u32[]{:S(2)}, u32[]{:S(2)}) collective-permute-start(bf16[256,1408]{1,0:T(8,128)(2,1)S(1)} %copy-done.1), channel_id=1, source_target_pairs={{3,0},{0,1},{1,2},{2,3},{7,4},{4,5},{5,6},{6,7},{11,8},{8,9},{9,10... | collective-permute-start | bytes 2162696 | tf_op jit(solution)/shard_map/ppermute | solution.py:20
  123.7 29.7 %copy-start.4 = (bf16[256,1408]{1,0:T(8,128)(2,1)}, bf16[256,1408]{1,0:T(8,128)(2,1)S(1)}, u32[]{:S(2)}) copy-start(bf16[256,1408]{1,0:T(8,128)(2,1)S(1)} %collective-permute-done.29.refs_11_) | copy-start | bytes 2162692
  123.7 19.7 %collective-permute-start.38 = (bf16[256,1408]{1,0:T(8,128)(2,1)S(1)}, bf16[256,1408]{1,0:T(8,128)(2,1)S(1)}, u32[]{:S(2)}, u32[]{:S(2)}) collective-permute-start(bf16[256,1408]{1,0:T(8,128)(2,1)S(1)} %collective-permute-done.37.refs_7_), channel_id=1, source_target_pairs={{4,0},{8,4},{12,8},{0,12},{5,1},{9,5},{13,9},{1,13},{6,2},{10,6},{... | collective-permute-start | bytes 2162696 | tf_op jit(solution)/shard_map/ppermute | solution.py:20
  126.8 26.6 %copy-start.5 = (bf16[256,1408]{1,0:T(8,128)(2,1)}, bf16[256,1408]{1,0:T(8,128)(2,1)S(1)}, u32[]{:S(2)}) copy-start(bf16[256,1408]{1,0:T(8,128)(2,1)S(1)} %collective-permute-done.20.refs_2_) | copy-start | bytes 2162692
  126.8 18.9 %collective-permute-start.32 = (bf16[256,1408]{1,0:T(8,128)(2,1)S(1)}, bf16[256,1408]{1,0:T(8,128)(2,1)S(1)}, u32[]{:S(2)}, u32[]{:S(2)}) collective-permute-start(bf16[256,1408]{1,0:T(8,128)(2,1)S(1)} %collective-permute-done.31.refs_2_), channel_id=1, source_target_pairs={{1,0},{2,1},{3,2},{0,3},{5,4},{6,5},{7,6},{4,7},{9,8},{10,9},{11,1... | collective-permute-start | bytes 2162696 | tf_op jit(solution)/shard_map/ppermute | solution.py:20
  130.3 23.1 %copy-start.6 = (bf16[256,1408]{1,0:T(8,128)(2,1)}, bf16[256,1408]{1,0:T(8,128)(2,1)S(1)}, u32[]{:S(2)}) copy-start(bf16[256,1408]{1,0:T(8,128)(2,1)S(1)} %collective-permute-done.22.refs_5_) | copy-start | bytes 2162692
  130.3 23.1 %collective-permute-start.28 = (bf16[128,1408]{1,0:T(8,128)(2,1)}, bf16[128,1408]{1,0:T(8,128)(2,1)}, u32[]{:S(2)}, u32[]{:S(2)}) collective-permute-start(bf16[128,1408]{1,0:T(8,128)(2,1)} %slice.58), channel_id=1, source_target_pairs={{4,0},{8,4},{12,8},{0,12},{5,1},{9,5},{13,9},{1,13},{6,2},{10,6},{... | collective-permute-start | bytes 1081352 | tf_op jit(solution)/shard_map/ppermute | solution.py:20
  131.3 22.1 %collective-permute-start.30 = (bf16[128,1408]{1,0:T(8,128)(2,1)}, bf16[128,1408]{1,0:T(8,128)(2,1)S(1)}, u32[]{:S(2)}, u32[]{:S(2)}) collective-permute-start(bf16[128,1408]{1,0:T(8,128)(2,1)} %slice.59), channel_id=1, source_target_pairs={{12,0},{0,4},{4,8},{8,12},{13,1},{1,5},{5,9},{9,13},{14,2},{2,6},{... | collective-permute-start | bytes 1081352 | tf_op jit(solution)/shard_map/ppermute | solution.py:20
  138.7 14.8 %collective-permute-start.21 = (bf16[128,1408]{1,0:T(8,128)(2,1)S(1)}, bf16[128,1408]{1,0:T(8,128)(2,1)S(1)}, u32[]{:S(2)}, u32[]{:S(2)}) collective-permute-start(bf16[128,1408]{1,0:T(8,128)(2,1)S(1)} %slice.56), channel_id=1, source_target_pairs={{1,0},{2,1},{3,2},{0,3},{5,4},{6,5},{7,6},{4,7},{9,8},{10,9},{11,1... | collective-permute-start | bytes 1081352 | tf_op jit(solution)/shard_map/ppermute | solution.py:20
  143.4 10.1 %collective-permute-start.23 = (bf16[128,1408]{1,0:T(8,128)(2,1)}, bf16[128,1408]{1,0:T(8,128)(2,1)S(1)}, u32[]{:S(2)}, u32[]{:S(2)}) collective-permute-start(bf16[128,1408]{1,0:T(8,128)(2,1)} %slice.57), channel_id=1, source_target_pairs={{3,0},{0,1},{1,2},{2,3},{7,4},{4,5},{5,6},{6,7},{11,8},{8,9},{9,10... | collective-permute-start | bytes 1081352 | tf_op jit(solution)/shard_map/ppermute | solution.py:20
  (28 other events, 98.0 us)

commit v9 on v8

--- a/solution.py
+++ b/solution.py
@@ -282,7 +282,7 @@
         size = partial.shape[2] // SIDE
         blocks = [partial[:, :, i * size : (i + 1) * size] for i in range(SIDE)]
         total = blocks[0].astype(F32)
-        for i in (1, 3, 2):
+        for i in (2, 1, 3):
             total = total + send(blocks[i], axis, i).astype(F32)
         partial = total.astype(BF16)
 

time: 164 us -> 165 us (level)
  transfers between devices with their start and end apart: 40 -> 40, of which waited for: 18 -> 15; matrix products, arithmetic and copies ran while one was open for 4% -> 4% of each run, Pallas kernels for 21% -> 21%
where the time goes in v9:
time: 165 us; the launch traced here: 164 us
  starting transfers between devices  59.8 us (36%)
  Pallas kernels  47.2 us (29%)
  waiting for transfers between devices  42.5 us (26%)
  local copies, waits for them, and re-layouts  9.66 us (6%)
  matrix products  2.91 us (2%)
    ppermute x38, starting transfers between devices, receive(): lax.ppermute(value, axis, [((i + distance) % SIDE, i) for i in range(SIDE)])  59.6 us
    ppermute x38, waiting for transfers between devices, receive(): lax.ppermute(value, axis, [((i + distance) % SIDE, i) for i in range(SIDE)])  42 us
    pallas_call x2, Pallas kernels, expand_halves(): pl.pallas_call(functools.partial(expand_kernel, counts=counts, which=whic...  13.4 us
    pallas_call x2, Pallas kernels, partial_grads(): pl.pallas_call(partial_kernel, grid_spec=pltpu.PrefetchScalarGridSpec(num...  12.7 us
    pallas_call x4, Pallas kernels, stack(): pl.pallas_call(stack_kernel, out_shape=held((rows * len(pieces), width)),...  8.54 us
    unnamed x72, local copies, waits for them, and re-layouts  7.1 us
    pallas_call x1, Pallas kernels, arrange(): pl.pallas_call(arrange_kernel, grid_spec=pltpu.PrefetchScalarGridSpec(num...  6.51 us
    pallas_call x2, Pallas kernels, directions(): pl.pallas_call(functools.partial(direction_kernel, pieces=pieces), grid=(...  6.1 us
  transfers between devices with their start and end apart: 40, of which 15 were waited for; matrix products, arithmetic and copies ran while one was open for 4% of the time, Pallas kernels for 21%

profile of v9, /device:TPU:0, one launch (start us, length us, event | category | flops | bytes accessed | tf_op | source)
XLA Modules:
  0.0 164.1 jit_solution(13792092232578895113)
XLA Ops:
  0.8 1.5 copy-done
  2.2 2.9 %fusion.4 = bf16[2,128,1024]{2,1,0:T(8,128)(2,1)S(1)} fusion(s32[1024]{0:T(1024)S(1)} %fusion.21, bf16[2,512,1024]{2,1,0:T(8,128)(2,1)} %bases_ref.1, bf16[128,8192]{1,0:T(8,128)(2,1)S(1)} %copy-done, s32[]{:T(128)S(6)} %select_n.54), kind=kOutput, calls=%fused_computation.4 | convolution fusion | flops 806879232 | bytes 2756612 | tf_op jit(solution)/shard_map/ktr,rs->kts/dot_general | solution.py:280
  5.2 3.4 %collective-permute-start = (bf16[2,128,256]{2,1,0:T(8,128)(2,1)S(1)}, bf16[2,128,256]{2,1,0:T(8,128)(2,1)S(1)}, u32[]{:S(2)}, u32[]{:S(2)}) collective-permute-start(bf16[2,128,256]{2,1,0:T(8,128)(2,1)S(1)} %get-tuple-element.39), channel_id=1, source_target_pairs={{8,0},{12,4},{0,8},{4,12},{9,1},{13,5},{1,9},{5,13},{10,2},{14,6},... | collective-permute-start | bytes 393224 | tf_op jit(solution)/shard_map/ppermute | solution.py:20
  9.2 2.6 %collective-permute-start.2 = (bf16[2,128,256]{2,1,0:T(8,128)(2,1)S(1)}, bf16[2,128,256]{2,1,0:T(8,128)(2,1)S(1)}, u32[]{:S(2)}, u32[]{:S(2)}) collective-permute-start(bf16[2,128,256]{2,1,0:T(8,128)(2,1)S(1)} %get-tuple-element.40), channel_id=1, source_target_pairs={{4,0},{8,4},{12,8},{0,12},{5,1},{9,5},{13,9},{1,13},{6,2},{10,6},{... | collective-permute-start | bytes 393224 | tf_op jit(solution)/shard_map/ppermute | solution.py:20
  11.8 1.1 collective-permute-done
  12.9 2.3 %collective-permute-done.1 = bf16[2,128,256]{2,1,0:T(8,128)(2,1)S(1)} collective-permute-done((bf16[2,128,256]{2,1,0:T(8,128)(2,1)S(1)}, bf16[2,128,256]{2,1,0:T(8,128)(2,1)S(1)}, u32[]{:S(2)}, u32[]{:S(2)}) %collective-permute-start.1) | collective-permute-done | bytes 131104 | tf_op jit(solution)/shard_map/ppermute | solution.py:20
  15.4 4.0 %collective-permute-start.3 = (bf16[2,128,64]{2,1,0:T(8,128)(2,1)S(1)}, bf16[2,128,64]{2,1,0:T(8,128)(2,1)S(1)}, u32[]{:S(2)}, u32[]{:S(2)}) collective-permute-start(bf16[2,128,64]{2,1,0:T(8,128)(2,1)S(1)} %get-tuple-element.42), channel_id=1, source_target_pairs={{2,0},{3,1},{0,2},{1,3},{6,4},{7,5},{4,6},{5,7},{10,8},{11,9},{8,1... | collective-permute-start | bytes 98312 | tf_op jit(solution)/shard_map/ppermute | solution.py:20
  19.4 1.0 collective-permute-start.4
  20.4 2.2 %collective-permute-start.5 = (bf16[2,128,64]{2,1,0:T(8,128)(2,1)S(1)}, bf16[2,128,64]{2,1,0:T(8,128)(2,1)S(1)}, u32[]{:S(2)}, u32[]{:S(2)}) collective-permute-start(bf16[2,128,64]{2,1,0:T(8,128)(2,1)S(1)} %get-tuple-element.43), channel_id=1, source_target_pairs={{1,0},{2,1},{3,2},{0,3},{5,4},{6,5},{7,6},{4,7},{9,8},{10,9},{11,1... | collective-permute-start | bytes 98312 | tf_op jit(solution)/shard_map/ppermute | solution.py:20
  22.7 2.2 %collective-permute-done.4 = bf16[2,128,64]{2,1,0:T(8,128)(2,1)S(1)} collective-permute-done((bf16[2,128,64]{2,1,0:T(8,128)(2,1)S(1)}, bf16[2,128,64]{2,1,0:T(8,128)(2,1)S(1)}, u32[]{:S(2)}, u32[]{:S(2)}) %collective-permute-start.4) | collective-permute-done | bytes 32800 | tf_op jit(solution)/shard_map/ppermute | solution.py:20
  26.9 6.3 %shard_map.76 = (f32[64,2752]{1,0:T(8,128)}, bf16[64,2752]{1,0:T(8,128)(2,1)}, bf16[64,2752]{1,0:T(8,128)(2,1)}, bf16[64,2752]{1,0:T(8,128)(2,1)}) custom-call(s32[4]{0:T(128)} %pad_add_fusion.where_ref._, bf16[2,128,64]{2,1,0:T(8,128)(2,1)} %copy-done.13, bf16[2,128,64]{2,1,0:T(8,128)(2,1)} %copy-done.23, bf16[2,128,22016]{2,1,0:T(8,128)(2,1)} %grads_ref.3, ...), custom_call_target="tpu_custom_call" | custom-call | flops 360710144 | bytes 8454144 | tf_op jit(solution)/shard_map/pallas_call | solution.py:106
  33.2 1.5 collective-permute-start.11
  34.7 2.7 %collective-permute-start.12 = (bf16[64,2752]{1,0:T(8,128)(2,1)}, bf16[64,2752]{1,0:T(8,128)(2,1)S(1)}, u32[]{:S(2)}, u32[]{:S(2)}) collective-permute-start(bf16[64,2752]{1,0:T(8,128)(2,1)} %get-tuple-element.28), channel_id=1, source_target_pairs={{64,0},{96,32},{0,64},{32,96},{65,1},{97,33},{1,65},{33,97},{66,2}... | collective-permute-start | bytes 1056776 | tf_op jit(solution)/shard_map/ppermute | solution.py:20
  37.5 1.4 collective-permute-start.13
  38.9 6.4 %shard_map.77 = (f32[64,2752]{1,0:T(8,128)}, bf16[64,2752]{1,0:T(8,128)(2,1)}, bf16[64,2752]{1,0:T(8,128)(2,1)}, bf16[64,2752]{1,0:T(8,128)(2,1)}) custom-call(s32[4]{0:T(128)} %pad_add_fusion.where_ref._, bf16[2,128,64]{2,1,0:T(8,128)(2,1)} %copy-done.13, bf16[2,128,64]{2,1,0:T(8,128)(2,1)} %copy-done.23, bf16[2,128,22016]{2,1,0:T(8,128)(2,1)} %grads_ref.3, ...), custom_call_target="tpu_custom_call" | custom-call | flops 360710144 | bytes 8454144 | tf_op jit(solution)/shard_map/pallas_call | solution.py:106
  45.3 2.0 %collective-permute-start.8 = (bf16[64,2752]{1,0:T(8,128)(2,1)}, bf16[64,2752]{1,0:T(8,128)(2,1)S(1)}, u32[]{:S(2)}, u32[]{:S(2)}) collective-permute-start(bf16[64,2752]{1,0:T(8,128)(2,1)} %get-tuple-element.24), channel_id=1, source_target_pairs={{96,0},{0,32},{32,64},{64,96},{97,1},{1,33},{33,65},{65,97},{98,2}... | collective-permute-start | bytes 1056776 | tf_op jit(solution)/shard_map/ppermute | solution.py:20
  48.0 6.5 %shard_map.78 = (bf16[2,512,1024]{2,1,0:T(8,128)(2,1)}, bf16[2,512,1024]{2,1,0:T(8,128)(2,1)}) custom-call(s32[4]{0:T(128)} %pad_add_fusion.where_ref._, bf16[2,512,1024]{2,1,0:T(8,128)(2,1)} %bases_ref.1, f32[64,2752]{1,0:T(8,128)} %get-tuple-element.22._.refs_0_), custom_call_target="tpu_custom_call" | custom-call | flops 4294967296 | bytes 6291456 | tf_op jit(solution)/shard_map/pallas_call | solution.py:67
  55.6 3.0 %shard_map.79 = (f32[2,64,2752]{2,1,0:T(8,128)}, f32[2,64,2752]{2,1,0:T(8,128)}, bf16[64,1408]{1,0:T(8,128)(2,1)}, bf16[64,1408]{1,0:T(8,128)(2,1)}) custom-call(f32[64,2752]{1,0:T(8,128)} %get-tuple-element.21._.refs_0_, bf16[64,2752]{1,0:T(8,128)(2,1)} %copy-done.17, bf16[64,2752]{1,0:T(8,128)(2,1)} %copy-done.18, bf16[64,2752]{1,0:T(8,128)(2,1)} %copy-done.19, ...), custom_call_target="tpu_custom_call" | custom-call | flops 5283840 | bytes 4579328 | tf_op jit(solution)/shard_map/pallas_call | solution.py:159
  58.6 3.1 %collective-permute-start.14 = (bf16[64,1408]{1,0:T(8,128)(2,1)}, bf16[64,1408]{1,0:T(8,128)(2,1)S(1)}, u32[]{:S(2)}, u32[]{:S(2)}) collective-permute-start(bf16[64,1408]{1,0:T(8,128)(2,1)} %get-tuple-element.33.refs_0_), channel_id=1, source_target_pairs={{4,0},{8,4},{12,8},{0,12},{5,1},{9,5},{13,9},{1,13},{6,2},{10,6},{... | collective-permute-start | bytes 540680 | tf_op jit(solution)/shard_map/ppermute | solution.py:20
  62.3 1.4 collective-permute-start.16
  63.7 4.8 %collective-permute-done.14.refs_1_ = bf16[64,1408]{1,0:T(8,128)(2,1)S(1)} collective-permute-done((bf16[64,1408]{1,0:T(8,128)(2,1)}, bf16[64,1408]{1,0:T(8,128)(2,1)S(1)}, u32[]{:S(2)}, u32[]{:S(2)}) %collective-permute-start.14) | collective-permute-done | bytes 180256 | tf_op jit(solution)/shard_map/ppermute | solution.py:20
  68.5 3.2 %collective-permute-start.34 = (bf16[64,1408]{1,0:T(8,128)(2,1)}, bf16[64,1408]{1,0:T(8,128)(2,1)S(1)}, u32[]{:S(2)}, u32[]{:S(2)}) collective-permute-start(bf16[64,1408]{1,0:T(8,128)(2,1)} %get-tuple-element.36.refs_0_), channel_id=1, source_target_pairs={{1,0},{2,1},{3,2},{0,3},{5,4},{6,5},{7,6},{4,7},{9,8},{10,9},{11,1... | collective-permute-start | bytes 540680 | tf_op jit(solution)/shard_map/ppermute | solution.py:20
  72.1 2.2 %collective-permute-start.36 = (bf16[64,1408]{1,0:T(8,128)(2,1)}, bf16[64,1408]{1,0:T(8,128)(2,1)S(1)}, u32[]{:S(2)}, u32[]{:S(2)}) collective-permute-start(bf16[64,1408]{1,0:T(8,128)(2,1)} %get-tuple-element.36.refs_0_), channel_id=1, source_target_pairs={{3,0},{0,1},{1,2},{2,3},{7,4},{4,5},{5,6},{6,7},{11,8},{8,9},{9,10... | collective-permute-start | bytes 540680 | tf_op jit(solution)/shard_map/ppermute | solution.py:20
  74.3 2.1 %shard_map.80.refs_8_.refs_1_ = bf16[256,1408]{1,0:T(8,128)(2,1)} custom-call(bf16[64,1408]{1,0:T(8,128)(2,1)} %get-tuple-element.33.refs_0_, bf16[64,1408]{1,0:T(8,128)(2,1)} %copy-done.33, bf16[64,1408]{1,0:T(8,128)(2,1)} %copy-done.34, bf16[64,1408]{1,0:T(8,128)(2,1)} %copy-done.35), custom_call_target="tpu_custom_call" | custom-call | bytes 1441792 | tf_op jit(solution)/shard_map/pallas_call | solution.py:179
  77.4 3.1 %shard_map.81 = (f32[2,64,2752]{2,1,0:T(8,128)}, f32[2,64,2752]{2,1,0:T(8,128)}, bf16[64,1408]{1,0:T(8,128)(2,1)}, bf16[64,1408]{1,0:T(8,128)(2,1)}) custom-call(f32[64,2752]{1,0:T(8,128)} %get-tuple-element.22._.refs_0_, bf16[64,2752]{1,0:T(8,128)(2,1)} %copy-done.15, bf16[64,2752]{1,0:T(8,128)(2,1)} %copy-done.16, ...), custom_call_target="tpu_custom_call", output_to_operand_aliasing={{0}: (6, {}), {1}: (7, {})} | custom-call | flops 5283840 | bytes 4579328 | tf_op jit(solution)/shard_map/pallas_call | solution.py:159
  80.4 1.7 %collective-permute-start.24 = (bf16[64,1408]{1,0:T(8,128)(2,1)}, bf16[64,1408]{1,0:T(8,128)(2,1)S(1)}, u32[]{:S(2)}, u32[]{:S(2)}) collective-permute-start(bf16[64,1408]{1,0:T(8,128)(2,1)} %get-tuple-element.35.refs_0_), channel_id=1, source_target_pairs={{1,0},{2,1},{3,2},{0,3},{5,4},{6,5},{7,6},{4,7},{9,8},{10,9},{11,1... | collective-permute-start | bytes 540680 | tf_op jit(solution)/shard_map/ppermute | solution.py:20
  82.2 1.3 collective-permute-start.25
  84.4 2.8 %collective-permute-start.17 = (bf16[64,1408]{1,0:T(8,128)(2,1)}, bf16[64,1408]{1,0:T(8,128)(2,1)S(1)}, u32[]{:S(2)}, u32[]{:S(2)}) collective-permute-start(bf16[64,1408]{1,0:T(8,128)(2,1)} %get-tuple-element.34.refs_0_), channel_id=1, source_target_pairs={{4,0},{8,4},{12,8},{0,12},{5,1},{9,5},{13,9},{1,13},{6,2},{10,6},{... | collective-permute-start | bytes 540680 | tf_op jit(solution)/shard_map/ppermute | solution.py:20
  87.2 2.4 %collective-permute-done.24.refs_1_ = bf16[64,1408]{1,0:T(8,128)(2,1)S(1)} collective-permute-done((bf16[64,1408]{1,0:T(8,128)(2,1)}, bf16[64,1408]{1,0:T(8,128)(2,1)S(1)}, u32[]{:S(2)}, u32[]{:S(2)}) %collective-permute-start.24) | collective-permute-done | bytes 180256 | tf_op jit(solution)/shard_map/ppermute | solution.py:20
  89.6 2.2 %shard_map.84.refs_6_ = bf16[256,1408]{1,0:T(8,128)(2,1)} custom-call(bf16[64,1408]{1,0:T(8,128)(2,1)} %get-tuple-element.36.refs_0_, bf16[64,1408]{1,0:T(8,128)(2,1)} %copy-done.24, bf16[64,1408]{1,0:T(8,128)(2,1)} %copy-done.25, bf16[64,1408]{1,0:T(8,128)(2,1)} %copy-done.26), custom_call_target="tpu_custom_call" | custom-call | bytes 1441792 | tf_op jit(solution)/shard_map/pallas_call | solution.py:179
  91.7 3.2 %collective-permute-start.37 = (bf16[256,1408]{1,0:T(8,128)(2,1)}, bf16[256,1408]{1,0:T(8,128)(2,1)S(1)}, u32[]{:S(2)}, u32[]{:S(2)}) collective-permute-start(bf16[256,1408]{1,0:T(8,128)(2,1)} %shard_map.84.refs_6_), channel_id=1, source_target_pairs={{4,0},{8,4},{12,8},{0,12},{5,1},{9,5},{13,9},{1,13},{6,2},{10,6},{... | collective-permute-start | bytes 2162696 | tf_op jit(solution)/shard_map/ppermute | solution.py:20
  95.0 3.6 %collective-permute-start.31 = (bf16[256,1408]{1,0:T(8,128)(2,1)S(1)}, bf16[256,1408]{1,0:T(8,128)(2,1)S(1)}, u32[]{:S(2)}, u32[]{:S(2)}) collective-permute-start(bf16[256,1408]{1,0:T(8,128)(2,1)S(1)} %copy-done.1), channel_id=1, source_target_pairs={{1,0},{2,1},{3,2},{0,3},{5,4},{6,5},{7,6},{4,7},{9,8},{10,9},{11,1... | collective-permute-start | bytes 2162696 | tf_op jit(solution)/shard_map/ppermute | solution.py:20
  98.6 2.1 %shard_map.83.refs_7_ = bf16[256,1408]{1,0:T(8,128)(2,1)} custom-call(bf16[64,1408]{1,0:T(8,128)(2,1)} %get-tuple-element.35.refs_0_, bf16[64,1408]{1,0:T(8,128)(2,1)} %copy-done.28, bf16[64,1408]{1,0:T(8,128)(2,1)} %copy-done.30, bf16[64,1408]{1,0:T(8,128)(2,1)} %copy-done.32), custom_call_target="tpu_custom_call" | custom-call | bytes 1441792 | tf_op jit(solution)/shard_map/pallas_call | solution.py:179
  101.5 1.3 collective-permute-start.29
  103.5 2.1 %shard_map.82.refs_1_ = bf16[256,1408]{1,0:T(8,128)(2,1)} custom-call(bf16[64,1408]{1,0:T(8,128)(2,1)} %get-tuple-element.34.refs_0_, bf16[64,1408]{1,0:T(8,128)(2,1)} %copy-done.27, bf16[64,1408]{1,0:T(8,128)(2,1)} %copy-done.29, bf16[64,1408]{1,0:T(8,128)(2,1)} %copy-done.31), custom_call_target="tpu_custom_call" | custom-call | bytes 1441792 | tf_op jit(solution)/shard_map/pallas_call | solution.py:179
  106.2 5.7 %collective-permute-done.37.refs_7_ = bf16[256,1408]{1,0:T(8,128)(2,1)S(1)} collective-permute-done((bf16[256,1408]{1,0:T(8,128)(2,1)}, bf16[256,1408]{1,0:T(8,128)(2,1)S(1)}, u32[]{:S(2)}, u32[]{:S(2)}) %collective-permute-start.37) | collective-permute-done | bytes 720928 | tf_op jit(solution)/shard_map/ppermute | solution.py:20
  112.2 3.0 %collective-permute-done.31.refs_2_ = bf16[256,1408]{1,0:T(8,128)(2,1)S(1)} collective-permute-done((bf16[256,1408]{1,0:T(8,128)(2,1)S(1)}, bf16[256,1408]{1,0:T(8,128)(2,1)S(1)}, u32[]{:S(2)}, u32[]{:S(2)}) %collective-permute-start.31) | collective-permute-done | bytes 720928 | tf_op jit(solution)/shard_map/ppermute | solution.py:20
  115.2 8.7 %collective-permute-done.27.refs_8_ = bf16[256,1408]{1,0:T(8,128)(2,1)S(1)} collective-permute-done((bf16[256,1408]{1,0:T(8,128)(2,1)}, bf16[256,1408]{1,0:T(8,128)(2,1)S(1)}, u32[]{:S(2)}, u32[]{:S(2)}) %collective-permute-start.27) | collective-permute-done | bytes 720928 | tf_op jit(solution)/shard_map/ppermute | solution.py:20
  123.9 1.5 collective-permute-start.33
  125.4 3.3 %collective-permute-start.38 = (bf16[256,1408]{1,0:T(8,128)(2,1)S(1)}, bf16[256,1408]{1,0:T(8,128)(2,1)S(1)}, u32[]{:S(2)}, u32[]{:S(2)}) collective-permute-start(bf16[256,1408]{1,0:T(8,128)(2,1)S(1)} %collective-permute-done.37.refs_7_), channel_id=1, source_target_pairs={{4,0},{8,4},{12,8},{0,12},{5,1},{9,5},{13,9},{1,13},{6,2},{10,6},{... | collective-permute-start | bytes 2162696 | tf_op jit(solution)/shard_map/ppermute | solution.py:20
  128.8 1.8 %collective-permute-start.32 = (bf16[256,1408]{1,0:T(8,128)(2,1)S(1)}, bf16[256,1408]{1,0:T(8,128)(2,1)S(1)}, u32[]{:S(2)}, u32[]{:S(2)}) collective-permute-start(bf16[256,1408]{1,0:T(8,128)(2,1)S(1)} %collective-permute-done.31.refs_2_), channel_id=1, source_target_pairs={{1,0},{2,1},{3,2},{0,3},{5,4},{6,5},{7,6},{4,7},{9,8},{10,9},{11,1... | collective-permute-start | bytes 2162696 | tf_op jit(solution)/shard_map/ppermute | solution.py:20
  133.1 1.9 %collective-permute-start.30 = (bf16[128,1408]{1,0:T(8,128)(2,1)}, bf16[128,1408]{1,0:T(8,128)(2,1)S(1)}, u32[]{:S(2)}, u32[]{:S(2)}) collective-permute-start(bf16[128,1408]{1,0:T(8,128)(2,1)} %slice.59), channel_id=1, source_target_pairs={{12,0},{0,4},{4,8},{8,12},{13,1},{1,5},{5,9},{9,13},{14,2},{2,6},{... | collective-permute-start | bytes 1081352 | tf_op jit(solution)/shard_map/ppermute | solution.py:20
  135.0 5.9 %collective-permute-done.33.refs_4_ = bf16[256,1408]{1,0:T(8,128)(2,1)S(1)} collective-permute-done((bf16[256,1408]{1,0:T(8,128)(2,1)S(1)}, bf16[256,1408]{1,0:T(8,128)(2,1)S(1)}, u32[]{:S(2)}, u32[]{:S(2)}) %collective-permute-start.33) | collective-permute-done | bytes 720928 | tf_op jit(solution)/shard_map/ppermute | solution.py:20
  140.9 1.5 collective-permute-start.21
  142.4 3.0 %collective-permute-done.38.refs_8_ = bf16[256,1408]{1,0:T(8,128)(2,1)S(1)} collective-permute-done((bf16[256,1408]{1,0:T(8,128)(2,1)S(1)}, bf16[256,1408]{1,0:T(8,128)(2,1)S(1)}, u32[]{:S(2)}, u32[]{:S(2)}) %collective-permute-start.38) | collective-permute-done | bytes 720928 | tf_op jit(solution)/shard_map/ppermute | solution.py:20
  145.9 2.0 %collective-permute-done.32.refs_3_ = bf16[256,1408]{1,0:T(8,128)(2,1)S(1)} collective-permute-done((bf16[256,1408]{1,0:T(8,128)(2,1)S(1)}, bf16[256,1408]{1,0:T(8,128)(2,1)S(1)}, u32[]{:S(2)}, u32[]{:S(2)}) %collective-permute-start.32) | collective-permute-done | bytes 720928 | tf_op jit(solution)/shard_map/ppermute | solution.py:20
  148.8 6.7 %shard_map.85.refs_12_ = bf16[2,2752,512]{2,1,0:T(8,128)(2,1)} custom-call(bf16[2,512,1024]{2,1,0:T(8,128)(2,1)} %get-tuple-element.23.refs_0_, bf16[256,1408]{1,0:T(8,128)(2,1)} %shard_map.80.refs_8_.refs_1_, bf16[256,1408]{1,0:T(8,128)(2,1)} %copy-done.8, bf16[256,1408]{1,0:T(8,128)(2,1)} %copy-done.12, bf16[256,1408]{1,0:T(8,128)(2,1)} %copy-done.10, ...), custom_call_target="tpu_custom_call" | custom-call | flops 2952790016 | bytes 10747904 | tf_op jit(solution)/shard_map/pallas_call | solution.py:235
  157.2 6.7 %shard_map.86 = bf16[2,2752,512]{2,1,0:T(8,128)(2,1)} custom-call(bf16[2,512,1024]{2,1,0:T(8,128)(2,1)} %get-tuple-element.23.refs_0_, bf16[256,1408]{1,0:T(8,128)(2,1)} %shard_map.82.refs_1_, bf16[256,1408]{1,0:T(8,128)(2,1)} %copy-done.5, bf16[128,1408]{1,0:T(8,128)(2,1)} %copy-done.21, ...), custom_call_target="tpu_custom_call", output_to_operand_aliasing={{}: (12, {})} | custom-call | flops 2952790016 | bytes 10747904 | tf_op jit(solution)/shard_map/pallas_call | solution.py:235
  (126 shorter events, 15.5 us)
Async XLA Ops:
  0.6 25.6 %collective-permute-start.7 = (bf16[2,128,22016]{2,1,0:T(8,128)(2,1)}, bf16[2,128,22016]{2,1,0:T(8,128)(2,1)}, u32[]{:S(2)}, u32[]{:S(2)}) collective-permute-start(bf16[2,128,22016]{2,1,0:T(8,128)(2,1)} %grads_ref.3), channel_id=1, source_target_pairs={{0,16},{16,0},{1,17},{17,1},{2,18},{18,2},{3,19},{19,3},{4,20},{20... | collective-permute-start | bytes 33816584 | tf_op jit(solution)/shard_map/ppermute | solution.py:28
  5.2 7.7 %collective-permute-start = (bf16[2,128,256]{2,1,0:T(8,128)(2,1)S(1)}, bf16[2,128,256]{2,1,0:T(8,128)(2,1)S(1)}, u32[]{:S(2)}, u32[]{:S(2)}) collective-permute-start(bf16[2,128,256]{2,1,0:T(8,128)(2,1)S(1)} %get-tuple-element.39), channel_id=1, source_target_pairs={{8,0},{12,4},{0,8},{4,12},{9,1},{13,5},{1,9},{5,13},{10,2},{14,6},... | collective-permute-start | bytes 393224 | tf_op jit(solution)/shard_map/ppermute | solution.py:20
  8.5 6.7 %collective-permute-start.1 = (bf16[2,128,256]{2,1,0:T(8,128)(2,1)S(1)}, bf16[2,128,256]{2,1,0:T(8,128)(2,1)S(1)}, u32[]{:S(2)}, u32[]{:S(2)}) collective-permute-start(bf16[2,128,256]{2,1,0:T(8,128)(2,1)S(1)} %get-tuple-element.41), channel_id=1, source_target_pairs={{12,0},{0,4},{4,8},{8,12},{13,1},{1,5},{5,9},{9,13},{14,2},{2,6},{... | collective-permute-start | bytes 393224 | tf_op jit(solution)/shard_map/ppermute | solution.py:20
  9.2 6.0 %collective-permute-start.2 = (bf16[2,128,256]{2,1,0:T(8,128)(2,1)S(1)}, bf16[2,128,256]{2,1,0:T(8,128)(2,1)S(1)}, u32[]{:S(2)}, u32[]{:S(2)}) collective-permute-start(bf16[2,128,256]{2,1,0:T(8,128)(2,1)S(1)} %get-tuple-element.40), channel_id=1, source_target_pairs={{4,0},{8,4},{12,8},{0,12},{5,1},{9,5},{13,9},{1,13},{6,2},{10,6},{... | collective-permute-start | bytes 393224 | tf_op jit(solution)/shard_map/ppermute | solution.py:20
  15.4 7.2 %collective-permute-start.3 = (bf16[2,128,64]{2,1,0:T(8,128)(2,1)S(1)}, bf16[2,128,64]{2,1,0:T(8,128)(2,1)S(1)}, u32[]{:S(2)}, u32[]{:S(2)}) collective-permute-start(bf16[2,128,64]{2,1,0:T(8,128)(2,1)S(1)} %get-tuple-element.42), channel_id=1, source_target_pairs={{2,0},{3,1},{0,2},{1,3},{6,4},{7,5},{4,6},{5,7},{10,8},{11,9},{8,1... | collective-permute-start | bytes 98312 | tf_op jit(solution)/shard_map/ppermute | solution.py:20
  19.4 5.5 %collective-permute-start.4 = (bf16[2,128,64]{2,1,0:T(8,128)(2,1)S(1)}, bf16[2,128,64]{2,1,0:T(8,128)(2,1)S(1)}, u32[]{:S(2)}, u32[]{:S(2)}) collective-permute-start(bf16[2,128,64]{2,1,0:T(8,128)(2,1)S(1)} %get-tuple-element.44), channel_id=1, source_target_pairs={{3,0},{0,1},{1,2},{2,3},{7,4},{4,5},{5,6},{6,7},{11,8},{8,9},{9,10... | collective-permute-start | bytes 98312 | tf_op jit(solution)/shard_map/ppermute | solution.py:20
  20.4 4.5 %collective-permute-start.5 = (bf16[2,128,64]{2,1,0:T(8,128)(2,1)S(1)}, bf16[2,128,64]{2,1,0:T(8,128)(2,1)S(1)}, u32[]{:S(2)}, u32[]{:S(2)}) collective-permute-start(bf16[2,128,64]{2,1,0:T(8,128)(2,1)S(1)} %get-tuple-element.43), channel_id=1, source_target_pairs={{1,0},{2,1},{3,2},{0,3},{5,4},{6,5},{7,6},{4,7},{9,8},{10,9},{11,1... | collective-permute-start | bytes 98312 | tf_op jit(solution)/shard_map/ppermute | solution.py:20
  24.9 1.3 collective-permute-start.6
  33.2 14.1 %collective-permute-start.11 = (bf16[64,2752]{1,0:T(8,128)(2,1)}, bf16[64,2752]{1,0:T(8,128)(2,1)S(1)}, u32[]{:S(2)}, u32[]{:S(2)}) collective-permute-start(bf16[64,2752]{1,0:T(8,128)(2,1)} %get-tuple-element.27), channel_id=1, source_target_pairs={{96,0},{0,32},{32,64},{64,96},{97,1},{1,33},{33,65},{65,97},{98,2}... | collective-permute-start | bytes 1056776 | tf_op jit(solution)/shard_map/ppermute | solution.py:20
  34.7 19.9 %collective-permute-start.12 = (bf16[64,2752]{1,0:T(8,128)(2,1)}, bf16[64,2752]{1,0:T(8,128)(2,1)S(1)}, u32[]{:S(2)}, u32[]{:S(2)}) collective-permute-start(bf16[64,2752]{1,0:T(8,128)(2,1)} %get-tuple-element.28), channel_id=1, source_target_pairs={{64,0},{96,32},{0,64},{32,96},{65,1},{97,33},{1,65},{33,97},{66,2}... | collective-permute-start | bytes 1056776 | tf_op jit(solution)/shard_map/ppermute | solution.py:20
  37.5 17.2 %collective-permute-start.13 = (bf16[64,2752]{1,0:T(8,128)(2,1)}, bf16[64,2752]{1,0:T(8,128)(2,1)S(1)}, u32[]{:S(2)}, u32[]{:S(2)}) collective-permute-start(bf16[64,2752]{1,0:T(8,128)(2,1)} %get-tuple-element.29), channel_id=1, source_target_pairs={{32,0},{64,32},{96,64},{0,96},{33,1},{65,33},{97,65},{1,97},{34,2}... | collective-permute-start | bytes 1056776 | tf_op jit(solution)/shard_map/ppermute | solution.py:20
  45.3 17.0 %collective-permute-start.10 = (bf16[64,2752]{1,0:T(8,128)(2,1)}, bf16[64,2752]{1,0:T(8,128)(2,1)S(1)}, u32[]{:S(2)}, u32[]{:S(2)}) collective-permute-start(bf16[64,2752]{1,0:T(8,128)(2,1)} %get-tuple-element.26), channel_id=1, source_target_pairs={{32,0},{64,32},{96,64},{0,96},{33,1},{65,33},{97,65},{1,97},{34,2}... | collective-permute-start | bytes 1056776 | tf_op jit(solution)/shard_map/ppermute | solution.py:20
  45.3 31.2 %collective-permute-start.8 = (bf16[64,2752]{1,0:T(8,128)(2,1)}, bf16[64,2752]{1,0:T(8,128)(2,1)S(1)}, u32[]{:S(2)}, u32[]{:S(2)}) collective-permute-start(bf16[64,2752]{1,0:T(8,128)(2,1)} %get-tuple-element.24), channel_id=1, source_target_pairs={{96,0},{0,32},{32,64},{64,96},{97,1},{1,33},{33,65},{65,97},{98,2}... | collective-permute-start | bytes 1056776 | tf_op jit(solution)/shard_map/ppermute | solution.py:20
  47.3 29.2 %collective-permute-start.9 = (bf16[64,2752]{1,0:T(8,128)(2,1)}, bf16[64,2752]{1,0:T(8,128)(2,1)S(1)}, u32[]{:S(2)}, u32[]{:S(2)}) collective-permute-start(bf16[64,2752]{1,0:T(8,128)(2,1)} %get-tuple-element.25), channel_id=1, source_target_pairs={{64,0},{96,32},{0,64},{32,96},{65,1},{97,33},{1,65},{33,97},{66,2}... | collective-permute-start | bytes 1056776 | tf_op jit(solution)/shard_map/ppermute | solution.py:20
  58.6 9.9 %collective-permute-start.14 = (bf16[64,1408]{1,0:T(8,128)(2,1)}, bf16[64,1408]{1,0:T(8,128)(2,1)S(1)}, u32[]{:S(2)}, u32[]{:S(2)}) collective-permute-start(bf16[64,1408]{1,0:T(8,128)(2,1)} %get-tuple-element.33.refs_0_), channel_id=1, source_target_pairs={{4,0},{8,4},{12,8},{0,12},{5,1},{9,5},{13,9},{1,13},{6,2},{10,6},{... | collective-permute-start | bytes 540680 | tf_op jit(solution)/shard_map/ppermute | solution.py:20
  61.7 10.0 %collective-permute-start.15 = (bf16[64,1408]{1,0:T(8,128)(2,1)}, bf16[64,1408]{1,0:T(8,128)(2,1)S(1)}, u32[]{:S(2)}, u32[]{:S(2)}) collective-permute-start(bf16[64,1408]{1,0:T(8,128)(2,1)} %get-tuple-element.33.refs_0_), channel_id=1, source_target_pairs={{8,0},{12,4},{0,8},{4,12},{9,1},{13,5},{1,9},{5,13},{10,2},{14,6},... | collective-permute-start | bytes 540680 | tf_op jit(solution)/shard_map/ppermute | solution.py:20
  62.3 9.8 %collective-permute-start.16 = (bf16[64,1408]{1,0:T(8,128)(2,1)}, bf16[64,1408]{1,0:T(8,128)(2,1)S(1)}, u32[]{:S(2)}, u32[]{:S(2)}) collective-permute-start(bf16[64,1408]{1,0:T(8,128)(2,1)} %get-tuple-element.33.refs_0_), channel_id=1, source_target_pairs={{12,0},{0,4},{4,8},{8,12},{13,1},{1,5},{5,9},{9,13},{14,2},{2,6},{... | collective-permute-start | bytes 540680 | tf_op jit(solution)/shard_map/ppermute | solution.py:20
  68.5 15.0 %collective-permute-start.34 = (bf16[64,1408]{1,0:T(8,128)(2,1)}, bf16[64,1408]{1,0:T(8,128)(2,1)S(1)}, u32[]{:S(2)}, u32[]{:S(2)}) collective-permute-start(bf16[64,1408]{1,0:T(8,128)(2,1)} %get-tuple-element.36.refs_0_), channel_id=1, source_target_pairs={{1,0},{2,1},{3,2},{0,3},{5,4},{6,5},{7,6},{4,7},{9,8},{10,9},{11,1... | collective-permute-start | bytes 540680 | tf_op jit(solution)/shard_map/ppermute | solution.py:20
  71.7 12.6 %collective-permute-start.35 = (bf16[64,1408]{1,0:T(8,128)(2,1)}, bf16[64,1408]{1,0:T(8,128)(2,1)S(1)}, u32[]{:S(2)}, u32[]{:S(2)}) collective-permute-start(bf16[64,1408]{1,0:T(8,128)(2,1)} %get-tuple-element.36.refs_0_), channel_id=1, source_target_pairs={{2,0},{3,1},{0,2},{1,3},{6,4},{7,5},{4,6},{5,7},{10,8},{11,9},{8,1... | collective-permute-start | bytes 540680 | tf_op jit(solution)/shard_map/ppermute | solution.py:20
  72.1 15.0 %collective-permute-start.36 = (bf16[64,1408]{1,0:T(8,128)(2,1)}, bf16[64,1408]{1,0:T(8,128)(2,1)S(1)}, u32[]{:S(2)}, u32[]{:S(2)}) collective-permute-start(bf16[64,1408]{1,0:T(8,128)(2,1)} %get-tuple-element.36.refs_0_), channel_id=1, source_target_pairs={{3,0},{0,1},{1,2},{2,3},{7,4},{4,5},{5,6},{6,7},{11,8},{8,9},{9,10... | collective-permute-start | bytes 540680 | tf_op jit(solution)/shard_map/ppermute | solution.py:20
  77.4 17.6 %copy-start.1 = (bf16[256,1408]{1,0:T(8,128)(2,1)S(1)}, bf16[256,1408]{1,0:T(8,128)(2,1)}, u32[]{:S(2)}) copy-start(bf16[256,1408]{1,0:T(8,128)(2,1)} %shard_map.80.refs_8_.refs_1_) | copy-start | bytes 2162692
  80.4 9.1 %collective-permute-start.24 = (bf16[64,1408]{1,0:T(8,128)(2,1)}, bf16[64,1408]{1,0:T(8,128)(2,1)S(1)}, u32[]{:S(2)}, u32[]{:S(2)}) collective-permute-start(bf16[64,1408]{1,0:T(8,128)(2,1)} %get-tuple-element.35.refs_0_), channel_id=1, source_target_pairs={{1,0},{2,1},{3,2},{0,3},{5,4},{6,5},{7,6},{4,7},{9,8},{10,9},{11,1... | collective-permute-start | bytes 540680 | tf_op jit(solution)/shard_map/ppermute | solution.py:20
  82.2 9.6 %collective-permute-start.25 = (bf16[64,1408]{1,0:T(8,128)(2,1)}, bf16[64,1408]{1,0:T(8,128)(2,1)S(1)}, u32[]{:S(2)}, u32[]{:S(2)}) collective-permute-start(bf16[64,1408]{1,0:T(8,128)(2,1)} %get-tuple-element.35.refs_0_), channel_id=1, source_target_pairs={{2,0},{3,1},{0,2},{1,3},{6,4},{7,5},{4,6},{5,7},{10,8},{11,9},{8,1... | collective-permute-start | bytes 540680 | tf_op jit(solution)/shard_map/ppermute | solution.py:20
  83.5 11.5 %collective-permute-start.26 = (bf16[64,1408]{1,0:T(8,128)(2,1)}, bf16[64,1408]{1,0:T(8,128)(2,1)S(1)}, u32[]{:S(2)}, u32[]{:S(2)}) collective-permute-start(bf16[64,1408]{1,0:T(8,128)(2,1)} %get-tuple-element.35.refs_0_), channel_id=1, source_target_pairs={{3,0},{0,1},{1,2},{2,3},{7,4},{4,5},{5,6},{6,7},{11,8},{8,9},{9,10... | collective-permute-start | bytes 540680 | tf_op jit(solution)/shard_map/ppermute | solution.py:20
  84.4 16.4 %collective-permute-start.17 = (bf16[64,1408]{1,0:T(8,128)(2,1)}, bf16[64,1408]{1,0:T(8,128)(2,1)S(1)}, u32[]{:S(2)}, u32[]{:S(2)}) collective-permute-start(bf16[64,1408]{1,0:T(8,128)(2,1)} %get-tuple-element.34.refs_0_), channel_id=1, source_target_pairs={{4,0},{8,4},{12,8},{0,12},{5,1},{9,5},{13,9},{1,13},{6,2},{10,6},{... | collective-permute-start | bytes 540680 | tf_op jit(solution)/shard_map/ppermute | solution.py:20
  87.2 14.3 %collective-permute-start.18 = (bf16[64,1408]{1,0:T(8,128)(2,1)}, bf16[64,1408]{1,0:T(8,128)(2,1)S(1)}, u32[]{:S(2)}, u32[]{:S(2)}) collective-permute-start(bf16[64,1408]{1,0:T(8,128)(2,1)} %get-tuple-element.34.refs_0_), channel_id=1, source_target_pairs={{8,0},{12,4},{0,8},{4,12},{9,1},{13,5},{1,9},{5,13},{10,2},{14,6},... | collective-permute-start | bytes 540680 | tf_op jit(solution)/shard_map/ppermute | solution.py:20
  89.5 13.2 %collective-permute-start.19 = (bf16[64,1408]{1,0:T(8,128)(2,1)}, bf16[64,1408]{1,0:T(8,128)(2,1)S(1)}, u32[]{:S(2)}, u32[]{:S(2)}) collective-permute-start(bf16[64,1408]{1,0:T(8,128)(2,1)} %get-tuple-element.34.refs_0_), channel_id=1, source_target_pairs={{12,0},{0,4},{4,8},{8,12},{13,1},{1,5},{5,9},{9,13},{14,2},{2,6},{... | collective-permute-start | bytes 540680 | tf_op jit(solution)/shard_map/ppermute | solution.py:20
  91.7 23.5 %copy-start.2 = (bf16[256,1408]{1,0:T(8,128)(2,1)S(1)}, bf16[256,1408]{1,0:T(8,128)(2,1)}, u32[]{:S(2)}) copy-start(bf16[256,1408]{1,0:T(8,128)(2,1)} %shard_map.84.refs_6_) | copy-start | bytes 2162692
  91.7 20.2 %collective-permute-start.37 = (bf16[256,1408]{1,0:T(8,128)(2,1)}, bf16[256,1408]{1,0:T(8,128)(2,1)S(1)}, u32[]{:S(2)}, u32[]{:S(2)}) collective-permute-start(bf16[256,1408]{1,0:T(8,128)(2,1)} %shard_map.84.refs_6_), channel_id=1, source_target_pairs={{4,0},{8,4},{12,8},{0,12},{5,1},{9,5},{13,9},{1,13},{6,2},{10,6},{... | collective-permute-start | bytes 2162696 | tf_op jit(solution)/shard_map/ppermute | solution.py:20
  95.0 20.2 %collective-permute-start.31 = (bf16[256,1408]{1,0:T(8,128)(2,1)S(1)}, bf16[256,1408]{1,0:T(8,128)(2,1)S(1)}, u32[]{:S(2)}, u32[]{:S(2)}) collective-permute-start(bf16[256,1408]{1,0:T(8,128)(2,1)S(1)} %copy-done.1), channel_id=1, source_target_pairs={{1,0},{2,1},{3,2},{0,3},{5,4},{6,5},{7,6},{4,7},{9,8},{10,9},{11,1... | collective-permute-start | bytes 2162696 | tf_op jit(solution)/shard_map/ppermute | solution.py:20
  100.7 23.2 %collective-permute-start.27 = (bf16[256,1408]{1,0:T(8,128)(2,1)}, bf16[256,1408]{1,0:T(8,128)(2,1)S(1)}, u32[]{:S(2)}, u32[]{:S(2)}) collective-permute-start(bf16[256,1408]{1,0:T(8,128)(2,1)} %shard_map.83.refs_7_), channel_id=1, source_target_pairs={{4,0},{8,4},{12,8},{0,12},{5,1},{9,5},{13,9},{1,13},{6,2},{10,6},{... | collective-permute-start | bytes 2162696 | tf_op jit(solution)/shard_map/ppermute | solution.py:20
  101.5 24.0 %collective-permute-start.29 = (bf16[256,1408]{1,0:T(8,128)(2,1)}, bf16[256,1408]{1,0:T(8,128)(2,1)S(1)}, u32[]{:S(2)}, u32[]{:S(2)}) collective-permute-start(bf16[256,1408]{1,0:T(8,128)(2,1)} %shard_map.83.refs_7_), channel_id=1, source_target_pairs={{12,0},{0,4},{4,8},{8,12},{13,1},{1,5},{5,9},{9,13},{14,2},{2,6},{... | collective-permute-start | bytes 2162696 | tf_op jit(solution)/shard_map/ppermute | solution.py:20
  105.6 23.2 %collective-permute-start.20 = (bf16[256,1408]{1,0:T(8,128)(2,1)}, bf16[256,1408]{1,0:T(8,128)(2,1)S(1)}, u32[]{:S(2)}, u32[]{:S(2)}) collective-permute-start(bf16[256,1408]{1,0:T(8,128)(2,1)} %shard_map.82.refs_1_), channel_id=1, source_target_pairs={{1,0},{2,1},{3,2},{0,3},{5,4},{6,5},{7,6},{4,7},{9,8},{10,9},{11,1... | collective-permute-start | bytes 2162696 | tf_op jit(solution)/shard_map/ppermute | solution.py:20
  111.9 36.9 %copy-start.7 = (bf16[256,1408]{1,0:T(8,128)(2,1)}, bf16[256,1408]{1,0:T(8,128)(2,1)S(1)}, u32[]{:S(2)}) copy-start(bf16[256,1408]{1,0:T(8,128)(2,1)S(1)} %collective-permute-done.37.refs_7_) | copy-start | bytes 2162692
  111.9 20.2 %collective-permute-start.22 = (bf16[256,1408]{1,0:T(8,128)(2,1)}, bf16[256,1408]{1,0:T(8,128)(2,1)S(1)}, u32[]{:S(2)}, u32[]{:S(2)}) collective-permute-start(bf16[256,1408]{1,0:T(8,128)(2,1)} %shard_map.82.refs_1_), channel_id=1, source_target_pairs={{3,0},{0,1},{1,2},{2,3},{7,4},{4,5},{5,6},{6,7},{11,8},{8,9},{9,10... | collective-permute-start | bytes 2162696 | tf_op jit(solution)/shard_map/ppermute | solution.py:20
  115.2 33.6 %copy-start.8 = (bf16[256,1408]{1,0:T(8,128)(2,1)}, bf16[256,1408]{1,0:T(8,128)(2,1)S(1)}, u32[]{:S(2)}) copy-start(bf16[256,1408]{1,0:T(8,128)(2,1)S(1)} %collective-permute-done.31.refs_2_) | copy-start | bytes 2162692
  115.2 17.9 %collective-permute-start.39 = (bf16[256,1408]{1,0:T(8,128)(2,1)S(1)}, bf16[256,1408]{1,0:T(8,128)(2,1)S(1)}, u32[]{:S(2)}, u32[]{:S(2)}) collective-permute-start(bf16[256,1408]{1,0:T(8,128)(2,1)S(1)} %copy-done.2), channel_id=1, source_target_pairs={{12,0},{0,4},{4,8},{8,12},{13,1},{1,5},{5,9},{9,13},{14,2},{2,6},{... | collective-permute-start | bytes 2162696 | tf_op jit(solution)/shard_map/ppermute | solution.py:20
  123.9 31.5 %copy-start.3 = (bf16[256,1408]{1,0:T(8,128)(2,1)}, bf16[256,1408]{1,0:T(8,128)(2,1)S(1)}, u32[]{:S(2)}) copy-start(bf16[256,1408]{1,0:T(8,128)(2,1)S(1)} %collective-permute-done.27.refs_8_) | copy-start | bytes 2162692
  123.9 16.9 %collective-permute-start.33 = (bf16[256,1408]{1,0:T(8,128)(2,1)S(1)}, bf16[256,1408]{1,0:T(8,128)(2,1)S(1)}, u32[]{:S(2)}, u32[]{:S(2)}) collective-permute-start(bf16[256,1408]{1,0:T(8,128)(2,1)S(1)} %copy-done.1), channel_id=1, source_target_pairs={{3,0},{0,1},{1,2},{2,3},{7,4},{4,5},{5,6},{6,7},{11,8},{8,9},{9,10... | collective-permute-start | bytes 2162696 | tf_op jit(solution)/shard_map/ppermute | solution.py:20
  125.4 30.0 %copy-start.4 = (bf16[256,1408]{1,0:T(8,128)(2,1)}, bf16[256,1408]{1,0:T(8,128)(2,1)S(1)}, u32[]{:S(2)}) copy-start(bf16[256,1408]{1,0:T(8,128)(2,1)S(1)} %collective-permute-done.29.refs_11_) | copy-start | bytes 2162692
  125.4 19.9 %collective-permute-start.38 = (bf16[256,1408]{1,0:T(8,128)(2,1)S(1)}, bf16[256,1408]{1,0:T(8,128)(2,1)S(1)}, u32[]{:S(2)}, u32[]{:S(2)}) collective-permute-start(bf16[256,1408]{1,0:T(8,128)(2,1)S(1)} %collective-permute-done.37.refs_7_), channel_id=1, source_target_pairs={{4,0},{8,4},{12,8},{0,12},{5,1},{9,5},{13,9},{1,13},{6,2},{10,6},{... | collective-permute-start | bytes 2162696 | tf_op jit(solution)/shard_map/ppermute | solution.py:20
  128.8 26.7 %copy-start.5 = (bf16[256,1408]{1,0:T(8,128)(2,1)}, bf16[256,1408]{1,0:T(8,128)(2,1)S(1)}, u32[]{:S(2)}) copy-start(bf16[256,1408]{1,0:T(8,128)(2,1)S(1)} %collective-permute-done.20.refs_2_) | copy-start | bytes 2162692
  128.8 19.1 %collective-permute-start.32 = (bf16[256,1408]{1,0:T(8,128)(2,1)S(1)}, bf16[256,1408]{1,0:T(8,128)(2,1)S(1)}, u32[]{:S(2)}, u32[]{:S(2)}) collective-permute-start(bf16[256,1408]{1,0:T(8,128)(2,1)S(1)} %collective-permute-done.31.refs_2_), channel_id=1, source_target_pairs={{1,0},{2,1},{3,2},{0,3},{5,4},{6,5},{7,6},{4,7},{9,8},{10,9},{11,1... | collective-permute-start | bytes 2162696 | tf_op jit(solution)/shard_map/ppermute | solution.py:20
  132.1 23.4 %copy-start.6 = (bf16[256,1408]{1,0:T(8,128)(2,1)}, bf16[256,1408]{1,0:T(8,128)(2,1)S(1)}, u32[]{:S(2)}) copy-start(bf16[256,1408]{1,0:T(8,128)(2,1)S(1)} %collective-permute-done.22.refs_5_) | copy-start | bytes 2162692
  132.1 23.4 %collective-permute-start.28 = (bf16[128,1408]{1,0:T(8,128)(2,1)}, bf16[128,1408]{1,0:T(8,128)(2,1)}, u32[]{:S(2)}, u32[]{:S(2)}) collective-permute-start(bf16[128,1408]{1,0:T(8,128)(2,1)} %slice.58), channel_id=1, source_target_pairs={{4,0},{8,4},{12,8},{0,12},{5,1},{9,5},{13,9},{1,13},{6,2},{10,6},{... | collective-permute-start | bytes 1081352 | tf_op jit(solution)/shard_map/ppermute | solution.py:20
  133.1 22.4 %collective-permute-start.30 = (bf16[128,1408]{1,0:T(8,128)(2,1)}, bf16[128,1408]{1,0:T(8,128)(2,1)S(1)}, u32[]{:S(2)}, u32[]{:S(2)}) collective-permute-start(bf16[128,1408]{1,0:T(8,128)(2,1)} %slice.59), channel_id=1, source_target_pairs={{12,0},{0,4},{4,8},{8,12},{13,1},{1,5},{5,9},{9,13},{14,2},{2,6},{... | collective-permute-start | bytes 1081352 | tf_op jit(solution)/shard_map/ppermute | solution.py:20
  140.9 14.7 %collective-permute-start.21 = (bf16[128,1408]{1,0:T(8,128)(2,1)S(1)}, bf16[128,1408]{1,0:T(8,128)(2,1)S(1)}, u32[]{:S(2)}, u32[]{:S(2)}) collective-permute-start(bf16[128,1408]{1,0:T(8,128)(2,1)S(1)} %slice.56), channel_id=1, source_target_pairs={{1,0},{2,1},{3,2},{0,3},{5,4},{6,5},{7,6},{4,7},{9,8},{10,9},{11,1... | collective-permute-start | bytes 1081352 | tf_op jit(solution)/shard_map/ppermute | solution.py:20
  145.4 10.2 %collective-permute-start.23 = (bf16[128,1408]{1,0:T(8,128)(2,1)}, bf16[128,1408]{1,0:T(8,128)(2,1)S(1)}, u32[]{:S(2)}, u32[]{:S(2)}) collective-permute-start(bf16[128,1408]{1,0:T(8,128)(2,1)} %slice.57), channel_id=1, source_target_pairs={{3,0},{0,1},{1,2},{2,3},{7,4},{4,5},{5,6},{6,7},{11,8},{8,9},{9,10... | collective-permute-start | bytes 1081352 | tf_op jit(solution)/shard_map/ppermute | solution.py:20
  (28 other events, 103.6 us)
